TPU v7x, 32 devices: a whole 2x2x4 slice. The times are simulated.
32 devices in a mesh: gx: 4 (over z), gy: 4 (over y, core), gz: 2 (over x).
Axes of the slice: x: 2, y: 2, z: 4, core: 2. Of those that a mesh axis runs over, the one named last changes fastest.
Arguments:
- basis: bfloat16 [32, 32, 16, 8192], P('gx', 'gy', 'gz'), may hold values from -0.1875 to 0.1875
- classes: int32 [32, 32, 16], P('gx', 'gy', 'gz'), may hold values from 0 to 15
- cond_table: float32 [16], replicated, may hold values from 0.5 to 2
- ground_table: float32 [16], replicated, may hold values from 4 to 40
- port_cells: int32 [2048], replicated, may hold values from 0 to 16383
- port_load: float32 [2048], replicated, may hold values from 20 to 200
Outputs:
- reduced: float32 [8192, 1024], P(('gx', 'gz'), 'gy')
- factor: float32 [8192, 1024], P(('gx', 'gz'), 'gy')
Inputs may be any that keep to these rules, and one draw needn't show every extreme that they name: `port_cells`: several ports may name the same cell; their loads add.
All inputs are finite; a program needn't handle non-finite values.
Results may differ from a plain program's by a relative error of at most 0.0024.
Values may be sent and summed in bfloat16 or wider, within the bound.
No kernel may reach another device: no remote copies, remote signals or barrier semaphores. Data moves between devices by JAX's collectives and lax.ppermute only.
A program may use at most 256 MiB of HBM per device.

v0:
```python
import functools

import jax
import jax.numpy as jnp
from jax import lax
from jax.experimental import pallas as pl
from jax.experimental.pallas import tpu as pltpu
from jax.sharding import PartitionSpec as P

NB = 512
PANELS = 2
LEAF = 128
SUB = 8


def dot3(a, b, dims):
    a_hi = a.astype(jnp.bfloat16)
    b_hi = b.astype(jnp.bfloat16)
    a_lo = (a - a_hi.astype(jnp.float32)).astype(jnp.bfloat16)
    b_lo = (b - b_hi.astype(jnp.float32)).astype(jnp.bfloat16)

    def dot(x, y):
        return lax.dot_general(x, y, (dims, ((), ())), preferred_element_type=jnp.float32)

    return dot(a_hi, b_hi) + (dot(a_hi, b_lo) + dot(a_lo, b_hi))


def inverse_of(d):
    guess = pl.reciprocal(d, approx=True)
    return guess * (2.0 - d * guess)


def leaf_inverse(block_ref):
    lanes = lax.broadcasted_iota(jnp.int32, (SUB, LEAF), 1)
    subs = lax.broadcasted_iota(jnp.int32, (SUB, LEAF), 0)
    shape = (SUB, LEAF)
    for t in range(LEAF // SUB):
        j0 = t * SUB
        rows = block_ref[j0 : j0 + SUB, :]
        cols = [jnp.broadcast_to(rows[:, j0 + k : j0 + k + 1], shape) for k in range(SUB)]
        p = [[jnp.broadcast_to(cols[k][i : i + 1, :], shape) for k in range(i + 1)] for i in range(SUB)]
        in_block = jnp.logical_and(lanes >= j0, lanes < j0 + SUB)
        start = jnp.where(in_block, (lanes - j0 == subs).astype(jnp.float32), rows)
        u = [jnp.broadcast_to(start[k : k + 1, :], shape) for k in range(SUB)]
        inv = [None] * SUB
        factor = [[None] * SUB for _ in range(SUB)]
        for k in range(SUB):
            inv[k] = inverse_of(p[k][k])
            for i in range(k + 1, SUB):
                factor[i][k] = p[i][k] * inv[k]
                for j in range(k + 1, i + 1):
                    p[i][j] = p[i][j] - factor[i][k] * p[j][k] if j < i else p[i][j] - factor[i][k] * p[i][k]
                u[i] = u[i] - factor[i][k] * u[k]
        out = u[0] * lax.rsqrt(p[0][0])
        for k in range(1, SUB):
            out = jnp.where(subs == k, u[k] * lax.rsqrt(p[k][k]), out)
        block_ref[j0 : j0 + SUB, :] = out
        if t + 1 == LEAF // SUB:
            break
        z = [None] * SUB
        for k in reversed(range(SUB)):
            z[k] = u[k] * inv[k]
            for i in range(k + 1, SUB):
                z[k] = z[k] - factor[i][k] * z[i]
        for v in range(t + 1, LEAF // SUB):
            below = block_ref[v * SUB : (v + 1) * SUB, :]
            upd = jnp.where(in_block, 0.0, below)
            for k in range(SUB):
                upd = upd - jnp.broadcast_to(below[:, j0 + k : j0 + k + 1], shape) * z[k]
            block_ref[v * SUB : (v + 1) * SUB, :] = upd


def factor_inverse(s_ref, d_ref):
    width = s_ref.shape[0]
    row_ids = lax.broadcasted_iota(jnp.int32, (width, width), 0)
    col_ids = lax.broadcasted_iota(jnp.int32, (width, width), 1)
    wide_cols = lax.broadcasted_iota(jnp.int32, (LEAF, width), 1)
    leaf_rows = lax.broadcasted_iota(jnp.int32, (LEAF, LEAF), 0)
    leaf_cols = lax.broadcasted_iota(jnp.int32, (LEAF, LEAF), 1)

    def step(b, carry):
        off = pl.multiple_of(b * LEAF, LEAF)
        span = pl.ds(off, LEAF)
        d_ref[...] = s_ref[span, span]
        leaf_inverse(d_ref)
        inverse = jnp.where(leaf_rows >= leaf_cols, d_ref[...], 0.0)
        s_ref[span, span] = (leaf_rows == leaf_cols).astype(jnp.float32)
        upper = dot3(inverse, s_ref[span, :], ((1,), (0,)))
        s_ref[span, :] = upper
        tail = jnp.where(wide_cols >= off + LEAF, upper, 0.0)
        current = s_ref[...]
        dead = jnp.logical_and(
            row_ids >= off + LEAF, jnp.logical_and(col_ids >= off, col_ids < off + LEAF)
        )
        s_ref[...] = jnp.where(dead, 0.0, current) - dot3(tail, upper, ((0,), (0,)))
        return carry

    lax.fori_loop(0, width // LEAF, step, 0)
    s_ref[...] = jnp.where(row_ids >= col_ids, s_ref[...], 0.0)


def unpack_symmetric(packed_ref, s_ref, first=0):
    at = first
    for i in range(s_ref.shape[0] // LEAF):
        for j in range(i + 1):
            block = packed_ref[at * LEAF : (at + 1) * LEAF, :]
            s_ref[i * LEAF : (i + 1) * LEAF, j * LEAF : (j + 1) * LEAF] = block
            if j < i:
                s_ref[j * LEAF : (j + 1) * LEAF, i * LEAF : (i + 1) * LEAF] = block.T
            at += 1


def first_panel_kernel(packed_ref, w_ref, d_ref):
    unpack_symmetric(packed_ref, w_ref)
    factor_inverse(w_ref, d_ref)


def next_panel_kernel(packed_ref, w0_ref, f_ref, w_ref, d_ref):
    unpack_symmetric(packed_ref, w_ref)
    nb = w0_ref.shape[0]
    start = packed_ref.shape[0] - nb // LEAF * nb
    below = jnp.concatenate(
        [packed_ref[start + i * nb : start + (i + 1) * nb, :] for i in range(nb // LEAF)], 1
    )
    below = dot3(below, w0_ref[...], ((1,), (1,)))
    f_ref[...] = below
    w_ref[...] = w_ref[...] - dot3(below, below, ((1,), (1,)))
    factor_inverse(w_ref, d_ref)


def factor_kernel(first_ref, rows_ref, w0_ref, f_ref, w1_ref, out_ref):
    nb = w0_ref.shape[0]
    ids = first_ref[0] + lax.broadcasted_iota(jnp.int32, (rows_ref.shape[0], nb), 0)
    cols = lax.broadcasted_iota(jnp.int32, (rows_ref.shape[0], nb), 1)
    part = dot3(rows_ref[:, :nb], w0_ref[...], ((1,), (1,)))
    out_ref[:, :nb] = jnp.where(cols <= ids, part, 0.0)
    rest = rows_ref[:, nb:] - dot3(part, f_ref[...], ((1,), (1,)))
    rest = dot3(rest, w1_ref[...], ((1,), (1,)))
    out_ref[:, nb:] = jnp.where(cols + nb <= ids, rest, 0.0)


def panel_call(kernel, outputs, nb, *operands):
    return pl.pallas_call(
        kernel,
        out_shape=[jax.ShapeDtypeStruct((nb, nb), jnp.float32)] * outputs,
        in_specs=[pl.BlockSpec(memory_space=pltpu.VMEM)] * len(operands),
        out_specs=[pl.BlockSpec(memory_space=pltpu.VMEM)] * outputs,
        scratch_shapes=[pltpu.VMEM((LEAF, LEAF), jnp.float32)],
        compiler_params=pltpu.CompilerParams(vmem_limit_bytes=24 * 2**20),
        cost_estimate=pl.CostEstimate(
            flops=24 * nb**3 * 8, transcendentals=0, bytes_accessed=8 * nb * nb
        ),
    )(*operands)


def first_panel(packed, nb):
    return panel_call(first_panel_kernel, 1, nb, packed)[0]


def next_panel(packed, w0):
    return panel_call(next_panel_kernel, 2, w0.shape[0], packed, w0)


def whole(memory=pltpu.VMEM):
    return pl.BlockSpec(memory_space=memory)


def faces_kernel(cond_ref, ground_ref, info_ref, cells_ref, load_ref, panel_ref, *refs, sides):
    outs, (conduct_ref, grounds_ref, scaled_ref) = refs[:6], refs[6:]
    size_x, size_y, size_z = sides
    count, width = panel_ref.shape
    tile = 64
    classes = cond_ref.shape[0]
    ports = cells_ref.shape[1]

    def by_tile(t, carry):
        rows = pl.ds(pl.multiple_of(t * tile, tile), tile)
        kind = jnp.broadcast_to(info_ref[rows, 0:1], (tile, LEAF))
        ids = jnp.broadcast_to(info_ref[rows, 1:2], (tile, LEAF))
        conduct = jnp.zeros((tile, LEAF), jnp.float32)
        grounds = jnp.zeros((tile, LEAF), jnp.float32)
        for c in range(classes):
            conduct = jnp.where(kind == c, cond_ref[c], conduct)
            grounds = jnp.where(kind == c, ground_ref[c], grounds)
        loads = jnp.zeros((tile, LEAF), jnp.float32)
        for p in range(0, ports, LEAF):
            hit = ids == cells_ref[:, p : p + LEAF]
            loads = loads + jnp.where(hit, load_ref[:, p : p + LEAF], 0.0)
        conduct_ref[rows, :] = conduct
        grounds_ref[rows, :] = grounds + jnp.sum(loads, axis=1, keepdims=True)
        for p in range(0, width, LEAF):
            part = panel_ref[rows, p : p + LEAF].astype(jnp.float32)
            scaled_ref[p // LEAF, rows, :] = (
                (conduct * part).astype(jnp.bfloat16).astype(jnp.float32)
            )
        return carry

    lax.fori_loop(0, count // tile, by_tile, 0)
    plane = size_y * size_z
    for p in range(width // LEAF):
        lanes = slice(p * LEAF, (p + 1) * LEAF)
        outs[0][:, lanes] = scaled_ref[p, 0:plane, :].astype(jnp.bfloat16)
        outs[1][:, lanes] = scaled_ref[p, count - plane : count, :].astype(jnp.bfloat16)
        for out, at in ((outs[2], 0), (outs[3], plane - size_z)):
            face = [
                scaled_ref[p, x * plane + at : x * plane + at + size_z, :] for x in range(size_x)
            ]
            out[:, lanes] = jnp.concatenate(face, 0).astype(jnp.bfloat16)
        for out, at in ((outs[4], 0), (outs[5], size_z - 1)):
            face = scaled_ref[p, pl.ds(at, size_x * size_y, stride=size_z), :]
            out[:, lanes] = face.astype(jnp.bfloat16)


def image_kernel(panel_ref, conduct_ref, grounds_ref, *refs, sides, nb):
    halos, (image_ref, first_ref, later_ref, scaled_ref, square_ref) = refs[:6], refs[6:]
    size_x, size_y, size_z = sides
    width = panel_ref.shape[1]
    plane = size_y * size_z
    subs = lax.broadcasted_iota(jnp.int32, (size_z, LEAF), 0)

    def by_lane(p, carry):
        lanes = pl.ds(pl.multiple_of(p * LEAF, LEAF), LEAF)
        x_low, x_high, y_low, y_high, z_low, z_high = (
            h[:, lanes].astype(jnp.float32) for h in halos
        )
        scaled_ref[...] = (
            (conduct_ref[...] * panel_ref[:, lanes].astype(jnp.float32))
            .astype(jnp.bfloat16)
            .astype(jnp.float32)
        )

        def cell_rows(x, y):
            at = x * plane + y * size_z
            return scaled_ref[at : at + size_z, :]

        for x in range(size_x):
            done = []
            for y in range(size_y):
                at = x * plane + y * size_z
                here = cell_rows(x, y)
                span = slice(y * size_z, (y + 1) * size_z)
                total = cell_rows(x + 1, y) if x + 1 < size_x else x_high[span, :]
                total = total + (cell_rows(x - 1, y) if x > 0 else x_low[span, :])
                span = slice(x * size_z, (x + 1) * size_z)
                total = total + (cell_rows(x, y + 1) if y + 1 < size_y else y_high[span, :])
                total = total + (cell_rows(x, y - 1) if y > 0 else y_low[span, :])
                k = x * size_y + y
                up = jnp.where(
                    subs == size_z - 1, z_high[k : k + 1, :], pltpu.roll(here, size_z - 1, 0)
                )
                down = jnp.where(subs == 0, z_low[k : k + 1, :], pltpu.roll(here, 1, 0))
                total = total + up + down
                own = slice(at, at + size_z)
                done.append(
                    conduct_ref[own, :] * (6.0 * here - total)
                    + grounds_ref[own, :] * panel_ref[at : at + size_z, lanes].astype(jnp.float32)
                )
            image_ref[x * plane : (x + 1) * plane, lanes] = jnp.concatenate(done, 0).astype(
                jnp.bfloat16
            )
        return carry

    lax.fori_loop(0, width // LEAF, by_lane, 0)

    def product(rows, cols):
        return lax.dot_general(
            panel_ref[:, rows],
            image_ref[:, cols],
            (((0,), (0,)), ((), ())),
            preferred_element_type=jnp.float32,
        )

    blocks = nb // LEAF

    def lower(out_ref):
        at = 0
        for i in range(blocks):
            for j in range(i + 1):
                row, col = slice(i * LEAF, (i + 1) * LEAF), slice(j * LEAF, (j + 1) * LEAF)
                out_ref[at : at + LEAF, :] = 0.5 * (square_ref[row, col] + square_ref[col, row].T)
                at += LEAF
        return at

    head, tail = slice(0, nb), slice(nb, 2 * nb)
    square_ref[...] = product(head, head)
    lower(first_ref)
    square_ref[...] = product(tail, tail)
    at = lower(later_ref)
    below = product(tail, head)
    for i in range(blocks):
        later_ref[at + i * nb : at + (i + 1) * nb, :] = below[:, i * LEAF : (i + 1) * LEAF]


def pieces_kernel(index_ref, *refs, groups):
    del index_ref
    total = sum(groups)
    ins, outs = refs[:total], refs[total:]
    at = 0
    for out, count in zip(outs, groups):
        width = out.shape[1] // count
        for i in range(count):
            out[:, i * width : (i + 1) * width] = ins[at][...]
            at += 1


def take_pieces(flat_basis, lists):
    rows = flat_basis.shape[0]
    tile = min(128, rows)
    index = jnp.stack([jnp.asarray(b, jnp.int32) for blocks, _ in lists for b in blocks])
    in_specs, out_specs, out_shape = [], [], []
    for blocks, width in lists:
        for _ in blocks:
            k = len(in_specs)
            in_specs.append(pl.BlockSpec((tile, width), lambda t, idx, k=k: (t, idx[k])))
        out_specs.append(pl.BlockSpec((tile, width * len(blocks)), lambda t, idx: (t, 0)))
        out_shape.append(jax.ShapeDtypeStruct((rows, width * len(blocks)), flat_basis.dtype))
    kernel = functools.partial(pieces_kernel, groups=[len(blocks) for blocks, _ in lists])
    return pl.pallas_call(
        kernel,
        grid_spec=pltpu.PrefetchScalarGridSpec(
            num_scalar_prefetch=1, grid=(rows // tile,), in_specs=in_specs, out_specs=out_specs
        ),
        out_shape=out_shape,
        compiler_params=pltpu.CompilerParams(vmem_limit_bytes=32 * 2**20),
        cost_estimate=pl.CostEstimate(
            flops=0, transcendentals=0, bytes_accessed=4 * rows * flat_basis.shape[1]
        ),
    )(index, *([flat_basis] * len(in_specs)))


def products_kernel(index_ref, *refs):
    del index_ref
    out, count = refs[-1], len(refs) // 2
    total = None
    for b, image in zip(refs[:count], refs[count:-1]):
        term = lax.dot_general(
            b[...], image[...], (((0,), (0,)), ((), ())), preferred_element_type=jnp.float32
        )
        total = term if total is None else total + term
    out[...] = total.astype(out.dtype)


def products(bases, images, blocks, width, dtype):
    rows, cols = images[0].shape
    step = 256 if width % 256 == 0 else width
    parts = width // step
    index = jnp.stack([jnp.asarray(b * parts + i, jnp.int32) for b in blocks for i in range(parts)])
    in_specs = [pl.BlockSpec((rows, step), lambda t, idx: (0, idx[t]))] * len(bases)
    in_specs += [pl.BlockSpec((rows, cols), lambda t, idx: (0, 0))] * len(images)
    total = len(blocks) * width
    return pl.pallas_call(
        products_kernel,
        grid_spec=pltpu.PrefetchScalarGridSpec(
            num_scalar_prefetch=1,
            grid=(len(blocks) * parts,),
            in_specs=in_specs,
            out_specs=pl.BlockSpec((step, cols), lambda t, idx: (t, 0)),
        ),
        out_shape=jax.ShapeDtypeStruct((total, cols), dtype),
        compiler_params=pltpu.CompilerParams(vmem_limit_bytes=48 * 2**20),
        cost_estimate=pl.CostEstimate(
            flops=2 * total * cols * rows * len(bases),
            transcendentals=0,
            bytes_accessed=2 * rows * (total + cols) * len(bases) + 4 * total * cols,
        ),
    )(index, *bases, *images)


def swap_everywhere(rows, axes, devices):
    count = rows.shape[0]
    share = -(-count // devices)
    if share * devices > count:
        rows = jnp.pad(rows, ((0, share * devices - count), (0, 0)))
    rows = rows.reshape(devices, share, LEAF)
    terms = lax.all_to_all(rows, axes, split_axis=0, concat_axis=0, tiled=True)
    own = jnp.broadcast_to(jnp.sum(terms, axis=0), (devices, share, LEAF))
    sums = lax.all_to_all(own, axes, split_axis=0, concat_axis=0, tiled=True)
    return sums.reshape(devices * share, LEAF)[:count]


def local(basis, classes, cond_table, ground_table, port_cells, port_load):
    sides = classes.shape
    cells_x, cells_y, cells_z = sides
    width_k = basis.shape[3]
    devices_x = lax.axis_size("gx")
    devices_y = lax.axis_size("gy")
    devices_z = lax.axis_size("gz")
    devices = devices_x * devices_y * devices_z
    chips_y = devices_y // 2
    spans = devices_x // 2
    split = spans // 2
    count = cells_x * cells_y * cells_z
    cols = PANELS * NB
    at_x, at_y, at_z = (lax.axis_index(axis) for axis in ("gx", "gy", "gz"))
    core = at_y % 2
    chip = at_y // 2
    axes = ("gx", "gy", "gz")
    f32, bf16 = jnp.float32, jnp.bfloat16

    flat_basis = basis.reshape(count, width_k)
    panel = flat_basis[:, :cols]
    global_x = at_x * cells_x + jnp.arange(cells_x, dtype=jnp.int32)
    global_y = at_y * cells_y + jnp.arange(cells_y, dtype=jnp.int32)
    global_z = at_z * cells_z + jnp.arange(cells_z, dtype=jnp.int32)
    flat_ids = (
        (global_x[:, None, None] * (cells_y * devices_y) + global_y[None, :, None])
        * (cells_z * devices_z)
        + global_z[None, None, :]
    )
    info = jnp.stack([classes, flat_ids], -1).reshape(count, 2)

    face_rows = [cells_y * cells_z] * 2 + [cells_x * cells_z] * 2 + [cells_x * cells_y] * 2
    *faces, conduct, grounds = pl.pallas_call(
        functools.partial(faces_kernel, sides=sides),
        out_shape=[jax.ShapeDtypeStruct((n, cols), bf16) for n in face_rows]
        + [jax.ShapeDtypeStruct((count, LEAF), f32)] * 2,
        in_specs=[whole(pltpu.SMEM)] * 2 + [whole()] * 4,
        out_specs=[whole()] * 8,
        scratch_shapes=[pltpu.VMEM((cols // LEAF, count, LEAF), f32)],
        compiler_params=pltpu.CompilerParams(vmem_limit_bytes=24 * 2**20),
    )(cond_table, ground_table, info, port_cells[None, :], port_load[None, :], panel)
    halos = []
    for i, (axis, size) in enumerate((("gx", devices_x), ("gy", devices_y), ("gz", devices_z))):
        low, high = faces[2 * i : 2 * i + 2]
        halos.append(lax.ppermute(high, axis, [(k, k + 1) for k in range(size - 1)]))
        halos.append(lax.ppermute(low, axis, [(k + 1, k) for k in range(size - 1)]))

    wide = width_k // (devices_x * devices_z)
    narrow = wide // chips_y

    def over_z_blocks(s, x):
        return [(s * spans + zz) * devices_z + x for zz in range(split)]

    def over_y_blocks(s, y):
        return [
            ((s * spans + zz) * devices_z + x) * chips_y + y
            for zz in range(split, spans)
            for x in range(devices_z)
        ]

    z_steps = [(ds, d) for d in range(devices_z) for ds in (0, 1)]
    y_steps = [(ds, d) for d in range(chips_y) for ds in (0, 1)]
    lists = [(over_z_blocks(core ^ ds, (at_z + d) % devices_z), wide) for ds, d in z_steps]
    lists += [(over_y_blocks(core ^ ds, (chip + d) % chips_y), narrow) for ds, d in y_steps]
    pieces = take_pieces(flat_basis, lists)

    def z_pairs(ds, d):
        return [
            (y * devices_z + z, (y ^ ds) * devices_z + (z + d) % devices_z)
            for y in range(devices_y)
            for z in range(devices_z)
        ]

    def y_pairs(ds, d):
        return [(2 * y + c, 2 * ((y + d) % chips_y) + (c ^ ds)) for y in range(chips_y) for c in (0, 1)]

    def move_z(array, ds, d):
        return array if (ds, d) == (0, 0) else lax.ppermute(array, ("gy", "gz"), z_pairs(ds, d))

    def move_y(array, ds, d):
        return array if (ds, d) == (0, 0) else lax.ppermute(array, "gy", y_pairs(ds, d))

    z_bases = [move_z(p, ds, d) for p, (ds, d) in zip(pieces, z_steps)]
    y_bases = [move_y(p, ds, d) for p, (ds, d) in zip(pieces[len(z_steps) :], y_steps)]

    blocks = NB // LEAF
    lower_rows = blocks * (blocks + 1) // 2 * LEAF
    image, first_rows, later_rows = pl.pallas_call(
        functools.partial(image_kernel, sides=sides, nb=NB),
        out_shape=[
            jax.ShapeDtypeStruct((count, cols), bf16),
            jax.ShapeDtypeStruct((lower_rows, LEAF), f32),
            jax.ShapeDtypeStruct((lower_rows + blocks * NB, LEAF), f32),
        ],
        in_specs=[whole()] * 9,
        out_specs=[whole()] * 3,
        scratch_shapes=[pltpu.VMEM((count, LEAF), f32), pltpu.VMEM((NB, NB), f32)],
        compiler_params=pltpu.CompilerParams(vmem_limit_bytes=32 * 2**20),
    )(panel, conduct, grounds, *halos)

    by_z = {(0, d): move_z(image, 0, d) for d in range(devices_z)}
    by_y = {(0, d): move_y(image, 0, d) for d in range(1, chips_y)}
    by_z.update({(1, d): move_y(by_z[0, d], 1, 0) for d in range(devices_z)})
    by_y.update({(1, d): move_y(by_y[0, d], 1, 0) for d in range(1, chips_y)})
    by_y.update({(ds, 0): by_z[ds, 0] for ds in (0, 1)})
    z_images = [by_z[key] for key in z_steps]
    y_images = [by_y[key] for key in y_steps]

    first_rows = swap_everywhere(first_rows, axes, devices)
    later_rows = swap_everywhere(later_rows, axes, devices)
    inverse_0 = first_panel(first_rows, NB)
    factor_10, inverse_1 = next_panel(later_rows, inverse_0)

    part = narrow // 2

    def y_block(d):
        return [zz * chips_y + (chip + d) % chips_y for zz in range(split)]

    def z_block(d):
        return [zz * devices_z + (at_z + d) % devices_z for zz in range(spans - split)]

    y_sent = [products(z_bases, z_images, y_block(d), narrow, bf16) for d in range(1, chips_y)]
    y_got = [move_y(a, 0, d) for d, a in zip(range(1, chips_y), y_sent)]
    z_sent = [products(y_bases, y_images, z_block(d), narrow, bf16) for d in range(1, devices_z)]
    z_got = [move_z(a, 0, d) for d, a in zip(range(1, devices_z), z_sent)]
    sums_a = products(z_bases, z_images, y_block(0), narrow, f32)
    sums_b = products(y_bases, y_images, z_block(0), narrow, f32)
    y_got, z_got, inverse_0 = lax.optimization_barrier((y_got, z_got, inverse_0))
    for got in y_got:
        sums_a = sums_a + got.astype(f32)
    for got in z_got:
        sums_b = sums_b + got.astype(f32)
    plane = jnp.concatenate([sums_a.astype(bf16), sums_b.astype(bf16)], 0)
    plane = plane.reshape(devices_x, part, cols)
    rows = jnp.zeros((part, cols), f32)
    for step in range(devices_x):
        sent = lax.dynamic_index_in_dim(plane, (at_x + step) % devices_x, 0, keepdims=False)
        pairs = []
        for x in range(devices_x):
            for y in range(devices_y):
                to = (x + step) % devices_x
                dest_x = (y % 2) * spans + to // 2
                dest_y = (y // 2) * 2 + to % 2
                pairs.append((x * devices_y + y, dest_x * devices_y + dest_y))
        rows = rows + lax.ppermute(sent, ("gx", "gy"), pairs).astype(f32)
    reduced = lax.all_to_all(rows, "gy", split_axis=1, concat_axis=0, tiled=True)

    first_row = ((at_x * devices_z + at_z) * devices_y + at_y) * part
    factor = pl.pallas_call(
        factor_kernel,
        out_shape=jax.ShapeDtypeStruct((part, cols), f32),
        in_specs=[whole(pltpu.SMEM)] + [whole()] * 4,
        out_specs=whole(),
        compiler_params=pltpu.CompilerParams(vmem_limit_bytes=32 * 2**20),
    )(first_row[None], rows, inverse_0, factor_10, inverse_1)
    factor = lax.all_to_all(factor, "gy", split_axis=1, concat_axis=0, tiled=True)
    return (reduced, factor)


def solution(mesh):
    placed = (P("gx", "gy", "gz", None), P("gx", "gy", "gz"), P(), P(), P(), P())
    return jax.shard_map(
        local,
        mesh=mesh,
        in_specs=placed,
        out_specs=(P(("gx", "gz"), "gy"), P(("gx", "gz"), "gy")),
        check_vma=False,
    )
```

profile of v0, /device:TPU:1, one launch (start us, length us, event | category | flops | bytes accessed | tf_op | source)
XLA Modules:
  0.0 372.1 jit_solution(6498921902500057401)
XLA Ops:
  2.0 1.3 slice.4.panel_ref
  3.3 2.4 shard_map.78
  5.8 4.0 %collective-permute-start.3 = (bf16[64,1024]{1,0:T(8,128)(2,1)S(1)}, bf16[64,1024]{1,0:T(8,128)(2,1)S(1)}, u32[]{:S(2)}, u32[]{:S(2)}) collective-permute-start(bf16[64,1024]{1,0:T(8,128)(2,1)S(1)} %get-tuple-element.32), channel_id=1, source_target_pairs={{0,8},{8,16},{16,24},{1,9},{9,17},{17,25},{2,10},{10,18},{18,26},{... | collective-permute-start | bytes 393224 | tf_op jit(solution)/shard_map/ppermute | solution.py:425
  11.1 4.0 %collective-permute-start.5 = (bf16[64,1024]{1,0:T(8,128)(2,1)S(1)}, bf16[64,1024]{1,0:T(8,128)(2,1)S(1)}, u32[]{:S(2)}, u32[]{:S(2)}) collective-permute-start(bf16[64,1024]{1,0:T(8,128)(2,1)S(1)} %get-tuple-element.34), channel_id=1, source_target_pairs={{0,2},{2,4},{4,6},{1,3},{3,5},{5,7},{8,10},{10,12},{12,14},{9,11},... | collective-permute-start | bytes 393224 | tf_op jit(solution)/shard_map/ppermute | solution.py:425
  15.1 1.9 collective-permute-start.6
  17.0 3.1 collective-permute-start.7
  22.1 3.8 %collective-permute-done.8.refs_5_ = bf16[64,1024]{1,0:T(8,128)(2,1)S(1)} collective-permute-done((bf16[64,1024]{1,0:T(8,128)(2,1)S(1)}, bf16[64,1024]{1,0:T(8,128)(2,1)S(1)}, u32[]{:S(2)}, u32[]{:S(2)}) %collective-permute-start.8) | collective-permute-done | bytes 131104 | tf_op jit(solution)/shard_map/ppermute | solution.py:426
  25.9 3.9 %shard_map.79 = (bf16[512,1024]{1,0:T(8,128)(2,1)S(1)}, f32[1280,128]{1,0:T(8,128)S(1)}, f32[3328,128]{1,0:T(8,128)}) custom-call(bf16[512,1024]{1,0:T(8,128)(2,1)S(1)} %slice.4.panel_ref, f32[512,128]{1,0:T(8,128)S(1)} %get-tuple-element.30.conduct_ref, f32[512,128]{1,0:T(8,128)S(1)} %get-tuple-element.31.grounds_ref, ...), custom_call_target="tpu_custom_call" | custom-call | tf_op jit(solution)/shard_map/pallas_call | solution.py:468
  29.8 26.0 %all_to_all.58 = f32[32,40,128]{2,1,0:T(8,128)} all-to-all(f32[32,40,128]{2,1,0:T(8,128)S(1)} %bitcast.67), channel_id=1, replica_groups=mesh['gx'=4,'gy'=4,'gz'=2] {'gx','gy','gz'}, dimensions={0} | all-to-all | bytes 1310720 | tf_op jit(solution)/shard_map/all_to_all | solution.py:375
  55.8 3.2 all-to-all-start.3
  59.2 3.4 copy-done
  62.5 3.4 shard_map.77
  66.2 1.4 collective-permute-start.10
  67.7 2.0 collective-permute-start.2
  72.0 30.5 %collective-permute-done.10.refs_6_ = bf16[512,1024]{1,0:T(8,128)(2,1)} collective-permute-done((bf16[512,1024]{1,0:T(8,128)(2,1)S(1)}, bf16[512,1024]{1,0:T(8,128)(2,1)}, u32[]{:S(2)}, u32[]{:S(2)}) %collective-permute-start.10) | collective-permute-done | bytes 1048608 | tf_op jit(solution)/shard_map/ppermute | solution.py:458
  102.5 1.4 collective-permute-start.11
  103.9 21.0 %collective-permute-done.1.refs_2_ = bf16[512,1024]{1,0:T(8,128)(2,1)S(1)} collective-permute-done((bf16[512,1024]{1,0:T(8,128)(2,1)S(1)}, bf16[512,1024]{1,0:T(8,128)(2,1)S(1)}, u32[]{:S(2)}, u32[]{:S(2)}) %collective-permute-start.1) | collective-permute-done | bytes 1048608 | tf_op jit(solution)/shard_map/ppermute | solution.py:458
  125.9 1.4 collective-permute-start.13
  127.2 20.3 %collective-permute-done.2.refs_3_ = bf16[512,1024]{1,0:T(8,128)(2,1)S(1)} collective-permute-done((bf16[512,1024]{1,0:T(8,128)(2,1)S(1)}, bf16[512,1024]{1,0:T(8,128)(2,1)S(1)}, u32[]{:S(2)}, u32[]{:S(2)}) %collective-permute-start.2) | collective-permute-done | bytes 1048608 | tf_op jit(solution)/shard_map/ppermute | solution.py:458
  153.5 5.0 %all-to-all-start.1 = ((f32[32,40,128]{2,1,0:T(8,128)}), f32[32,40,128]{2,1,0:T(8,128)}, u32[]{:S(2)}, u32[]{:S(2)}) async-start(f32[32,40,128]{2,1,0:T(8,128)} %broadcast_in_dim.20), calls=%async_computation.1 | async-start | bytes 1310720 | tf_op jit(solution)/shard_map/all_to_all | solution.py:377
  161.4 6.3 %shard_map.81 = bf16[512,1024]{1,0:T(8,128)(2,1)} custom-call(s32[2]{0:T(128)S(1)} %pad_add_fusion.2.index_ref, bf16[512,1024]{1,0:T(8,128)(2,1)S(1)} %get-tuple-element.26.refs_0_, bf16[512,1024]{1,0:T(8,128)(2,1)S(1)} %copy-done.4, bf16[512,1024]{1,0:T(8,128)(2,1)S(1)} %copy-done.6, bf16[512,1024]{1,0:T(8,128)(2,1)S(1)} %copy-done.8, ...), custom_call_target="tpu_custom_call" | custom-call | flops 2147483648 | bytes 8388608 | tf_op jit(solution)/shard_map/pallas_call | solution.py:351
  167.7 1.4 collective-permute-start.12
  169.1 10.5 %collective-permute-done.14.refs_2_ = bf16[512,1024]{1,0:T(8,128)(2,1)} collective-permute-done((bf16[512,1024]{1,0:T(8,128)(2,1)}, bf16[512,1024]{1,0:T(8,128)(2,1)}, u32[]{:S(2)}, u32[]{:S(2)}) %collective-permute-start.14) | collective-permute-done | bytes 1048608 | tf_op jit(solution)/shard_map/ppermute | solution.py:461
  179.6 23.4 %collective-permute-done.15.refs_3_ = bf16[512,1024]{1,0:T(8,128)(2,1)} collective-permute-done((bf16[512,1024]{1,0:T(8,128)(2,1)}, bf16[512,1024]{1,0:T(8,128)(2,1)}, u32[]{:S(2)}, u32[]{:S(2)}) %collective-permute-start.15) | collective-permute-done | bytes 1048608 | tf_op jit(solution)/shard_map/ppermute | solution.py:461
  203.0 6.5 %shard_map.82 = bf16[512,1024]{1,0:T(8,128)(2,1)} custom-call(s32[2]{0:T(128)S(1)} %pad_add_fusion.3.index_ref, bf16[512,1024]{1,0:T(8,128)(2,1)S(1)} %get-tuple-element.39.refs_0_, bf16[512,1024]{1,0:T(8,128)(2,1)} %collective-permute-done.13.refs_1_, bf16[512,1024]{1,0:T(8,128)(2,1)} %collective-permute-done.14.refs_2_, ...), custom_call_target="tpu_custom_call" | custom-call | flops 2147483648 | bytes 8388608 | tf_op jit(solution)/shard_map/pallas_call | solution.py:351
  209.5 6.2 %shard_map.80 = f32[512,1024]{1,0:T(8,128)} custom-call(s32[2]{0:T(128)S(1)} %pad_add_fusion.1.index_ref, bf16[512,1024]{1,0:T(8,128)(2,1)S(1)} %get-tuple-element.26.refs_0_, bf16[512,1024]{1,0:T(8,128)(2,1)S(1)} %copy-done.4, bf16[512,1024]{1,0:T(8,128)(2,1)S(1)} %copy-done.6, bf16[512,1024]{1,0:T(8,128)(2,1)S(1)} %copy-done.9, ...), custom_call_target="tpu_custom_call" | custom-call | flops 2147483648 | bytes 8388608 | tf_op jit(solution)/shard_map/pallas_call | solution.py:351
  215.6 6.3 %shard_map.84 = f32[512,1024]{1,0:T(8,128)} custom-call(s32[2]{0:T(128)S(1)} %pad_add_fusion.4.index_ref, bf16[512,1024]{1,0:T(8,128)(2,1)S(1)} %get-tuple-element.39.refs_0_, bf16[512,1024]{1,0:T(8,128)(2,1)} %collective-permute-done.13.refs_1_, bf16[512,1024]{1,0:T(8,128)(2,1)} %collective-permute-done.14.refs_2_, ...), custom_call_target="tpu_custom_call" | custom-call | flops 2147483648 | bytes 8388608 | tf_op jit(solution)/shard_map/pallas_call | solution.py:351
  222.0 1.5 reduce_sum.19
  223.5 1.4 broadcast_in_dim.22
  224.9 5.9 %all-to-all-start.4 = ((f32[32,104,128]{2,1,0:T(8,128)}), f32[32,104,128]{2,1,0:T(8,128)S(1)}, u32[]{:S(2)}, u32[]{:S(2)}) async-start(f32[32,104,128]{2,1,0:T(8,128)} %broadcast_in_dim.22), calls=%async_computation.4 | async-start | bytes 3407872 | tf_op jit(solution)/shard_map/all_to_all | solution.py:377
  230.8 28.3 %shard_map.83.w0_ref = f32[512,512]{1,0:T(8,128)S(1)} custom-call(f32[1280,128]{1,0:T(8,128)} %bitcast.22.packed_ref), custom_call_target="tpu_custom_call" | custom-call | flops 25769803776 | bytes 2097152 | tf_op jit(solution)/shard_map/pallas_call | solution.py:143
  259.1 2.0 add_convert_fusion
  261.4 1.6 add_convert_fusion.1
  263.2 1.4 dynamic-slice_bitcast_fusion.3
  264.5 4.4 %collective-permute-start.19 = (bf16[256,1024]{1,0:T(8,128)(2,1)}, bf16[256,1024]{1,0:T(8,128)(2,1)S(1)}, u32[]{:S(2)}, u32[]{:S(2)}) collective-permute-start(bf16[256,1024]{1,0:T(8,128)(2,1)} %get-tuple-element.50), channel_id=1, source_target_pairs={{0,0},{2,16},{4,4},{6,20},{8,2},{10,18},{12,6},{14,22},{16,8},{18,... | collective-permute-start | bytes 1572872 | tf_op jit(solution)/shard_map/ppermute | solution.py:525
  269.0 2.4 collective-permute-start.22
  272.5 3.1 collective-permute-start.20
  275.6 2.9 collective-permute-done.19
  278.5 16.9 %collective-permute-done.22 = bf16[256,1024]{1,0:T(8,128)(2,1)S(1)} collective-permute-done((bf16[256,1024]{1,0:T(8,128)(2,1)}, bf16[256,1024]{1,0:T(8,128)(2,1)S(1)}, u32[]{:S(2)}, u32[]{:S(2)}) %collective-permute-start.22) | collective-permute-done | bytes 524320 | tf_op jit(solution)/shard_map/ppermute | solution.py:525
  295.4 4.4 %collective-permute-done.21 = bf16[256,1024]{1,0:T(8,128)(2,1)S(1)} collective-permute-done((bf16[256,1024]{1,0:T(8,128)(2,1)}, bf16[256,1024]{1,0:T(8,128)(2,1)S(1)}, u32[]{:S(2)}, u32[]{:S(2)}) %collective-permute-start.21) | collective-permute-done | bytes 524320 | tf_op jit(solution)/shard_map/ppermute | solution.py:525
  300.6 3.0 collective-permute-done.20
  303.5 1.7 convert_add_fusion.rows_ref
  306.3 12.5 %all-to-all-start.2 = ((f32[256,4,256]{2,0,1:T(8,128)}), f32[256,4,256]{2,0,1:T(8,128)}, u32[]{:S(2)}, u32[]{:S(2)}) async-start(f32[256,4,256]{2,0,1:T(8,128)} %bitcast.71), calls=%async_computation.2 | async-start | bytes 2097152 | tf_op jit(solution)/shard_map/all_to_all | solution.py:526
  320.0 28.8 %shard_map.85 = (f32[512,512]{1,0:T(8,128)S(1)}, f32[512,512]{1,0:T(8,128)S(1)}) custom-call(f32[3328,128]{1,0:T(8,128)S(1)} %bitcast.66, f32[512,512]{1,0:T(8,128)S(1)} %copy-done.11), custom_call_target="tpu_custom_call" | custom-call | flops 25769803776 | bytes 2097152 | tf_op jit(solution)/shard_map/pallas_call | solution.py:143
  348.8 1.6 shard_map.86
  351.5 3.8 %all-to-all-start.5 = ((f32[256,4,256]{2,0,1:T(8,128)}), f32[256,4,256]{2,0,1:T(8,128)S(1)}, u32[]{:S(2)}, u32[]{:S(2)}) async-start(f32[256,4,256]{2,0,1:T(8,128)} %bitcast.49), calls=%async_computation.5 | async-start | bytes 2097152 | tf_op jit(solution)/shard_map/all_to_all | solution.py:536
  355.2 13.6 %all-to-all-done.5 = f32[256,4,256]{2,0,1:T(8,128)S(1)} async-done(((f32[256,4,256]{2,0,1:T(8,128)}), f32[256,4,256]{2,0,1:T(8,128)S(1)}, u32[]{:S(2)}, u32[]{:S(2)}) %all-to-all-start.5) | async-done | bytes 1048608 | tf_op jit(solution)/shard_map/all_to_all | solution.py:536
  368.8 2.3 copy.25
  (90 shorter events, 23.6 us)
Async XLA Ops:
  0.6 2.6 copy-start.14
  0.6 2.6 copy-start.13
  0.7 2.6 copy-start.16
  0.7 2.6 copy-start.15
  5.8 14.4 %collective-permute-start.3 = (bf16[64,1024]{1,0:T(8,128)(2,1)S(1)}, bf16[64,1024]{1,0:T(8,128)(2,1)S(1)}, u32[]{:S(2)}, u32[]{:S(2)}) collective-permute-start(bf16[64,1024]{1,0:T(8,128)(2,1)S(1)} %get-tuple-element.32), channel_id=1, source_target_pairs={{0,8},{8,16},{16,24},{1,9},{9,17},{17,25},{2,10},{10,18},{18,26},{... | collective-permute-start | bytes 393224 | tf_op jit(solution)/shard_map/ppermute | solution.py:425
  9.8 11.7 %collective-permute-start.4 = (bf16[64,1024]{1,0:T(8,128)(2,1)S(1)}, bf16[64,1024]{1,0:T(8,128)(2,1)S(1)}, u32[]{:S(2)}, u32[]{:S(2)}) collective-permute-start(bf16[64,1024]{1,0:T(8,128)(2,1)S(1)} %get-tuple-element.33), channel_id=1, source_target_pairs={{8,0},{16,8},{24,16},{9,1},{17,9},{25,17},{10,2},{18,10},{26,18},{... | collective-permute-start | bytes 393224 | tf_op jit(solution)/shard_map/ppermute | solution.py:426
  11.1 10.4 %collective-permute-start.5 = (bf16[64,1024]{1,0:T(8,128)(2,1)S(1)}, bf16[64,1024]{1,0:T(8,128)(2,1)S(1)}, u32[]{:S(2)}, u32[]{:S(2)}) collective-permute-start(bf16[64,1024]{1,0:T(8,128)(2,1)S(1)} %get-tuple-element.34), channel_id=1, source_target_pairs={{0,2},{2,4},{4,6},{1,3},{3,5},{5,7},{8,10},{10,12},{12,14},{9,11},... | collective-permute-start | bytes 393224 | tf_op jit(solution)/shard_map/ppermute | solution.py:425
  15.1 6.4 %collective-permute-start.6 = (bf16[64,1024]{1,0:T(8,128)(2,1)S(1)}, bf16[64,1024]{1,0:T(8,128)(2,1)S(1)}, u32[]{:S(2)}, u32[]{:S(2)}) collective-permute-start(bf16[64,1024]{1,0:T(8,128)(2,1)S(1)} %get-tuple-element.35), channel_id=1, source_target_pairs={{2,0},{4,2},{6,4},{3,1},{5,3},{7,5},{10,8},{12,10},{14,12},{11,9},... | collective-permute-start | bytes 393224 | tf_op jit(solution)/shard_map/ppermute | solution.py:426
  17.0 5.1 %collective-permute-start.7 = (bf16[64,1024]{1,0:T(8,128)(2,1)S(1)}, bf16[64,1024]{1,0:T(8,128)(2,1)S(1)}, u32[]{:S(2)}, u32[]{:S(2)}) collective-permute-start(bf16[64,1024]{1,0:T(8,128)(2,1)S(1)} %get-tuple-element.36), channel_id=1, source_target_pairs={{0,1},{2,3},{4,5},{6,7},{8,9},{10,11},{12,13},{14,15},{16,17},{18,... | collective-permute-start | bytes 393224 | tf_op jit(solution)/shard_map/ppermute | solution.py:425
  20.2 5.7 %collective-permute-start.8 = (bf16[64,1024]{1,0:T(8,128)(2,1)S(1)}, bf16[64,1024]{1,0:T(8,128)(2,1)S(1)}, u32[]{:S(2)}, u32[]{:S(2)}) collective-permute-start(bf16[64,1024]{1,0:T(8,128)(2,1)S(1)} %get-tuple-element.37), channel_id=1, source_target_pairs={{1,0},{3,2},{5,4},{7,6},{9,8},{11,10},{13,12},{15,14},{17,16},{19,... | collective-permute-start | bytes 393224 | tf_op jit(solution)/shard_map/ppermute | solution.py:426
  29.8 41.2 %copy-start.1 = (bf16[512,1024]{1,0:T(8,128)(2,1)}, bf16[512,1024]{1,0:T(8,128)(2,1)S(1)}, u32[]{:S(2)}) copy-start(bf16[512,1024]{1,0:T(8,128)(2,1)S(1)} %get-tuple-element.38.refs_4_) | copy-start | bytes 3145732
  55.8 96.8 %all-to-all-start.3 = ((f32[32,104,128]{2,1,0:T(8,128)}), f32[32,104,128]{2,1,0:T(8,128)}, u32[]{:S(2)}, u32[]{:S(2)}) async-start(f32[32,104,128]{2,1,0:T(8,128)} %bitcast.33), calls=%async_computation.3 | async-start | bytes 3407872 | tf_op jit(solution)/shard_map/all_to_all | solution.py:375
  59.1 3.4 copy-start
  66.0 5.0 %collective-permute-start = (bf16[512,1024]{1,0:T(8,128)(2,1)S(1)}, bf16[512,1024]{1,0:T(8,128)(2,1)S(1)}, u32[]{:S(2)}, u32[]{:S(2)}) collective-permute-start(bf16[512,1024]{1,0:T(8,128)(2,1)S(1)} %get-tuple-element.27), channel_id=1, source_target_pairs={{0,2},{1,3},{2,0},{3,1},{4,6},{5,7},{6,4},{7,5},{8,10},{9,11},{10,... | collective-permute-start | bytes 3145736 | tf_op jit(solution)/shard_map/ppermute | solution.py:458
  66.2 36.3 %collective-permute-start.10 = (bf16[512,1024]{1,0:T(8,128)(2,1)S(1)}, bf16[512,1024]{1,0:T(8,128)(2,1)}, u32[]{:S(2)}, u32[]{:S(2)}) collective-permute-start(bf16[512,1024]{1,0:T(8,128)(2,1)S(1)} %get-tuple-element.38.refs_4_), channel_id=1, source_target_pairs={{0,1},{1,0},{2,3},{3,2},{4,5},{5,4},{6,7},{7,6},{8,9},{9,8},{10,11... | collective-permute-start | bytes 3145736 | tf_op jit(solution)/shard_map/ppermute | solution.py:458
  67.7 57.2 %collective-permute-start.1 = (bf16[512,1024]{1,0:T(8,128)(2,1)S(1)}, bf16[512,1024]{1,0:T(8,128)(2,1)S(1)}, u32[]{:S(2)}, u32[]{:S(2)}) collective-permute-start(bf16[512,1024]{1,0:T(8,128)(2,1)S(1)} %get-tuple-element.28), channel_id=1, source_target_pairs={{0,1},{1,0},{2,3},{3,2},{4,5},{5,4},{6,7},{7,6},{8,9},{9,8},{10,11... | collective-permute-start | bytes 3145736 | tf_op jit(solution)/shard_map/ppermute | solution.py:458
  67.7 79.8 %collective-permute-start.2 = (bf16[512,1024]{1,0:T(8,128)(2,1)S(1)}, bf16[512,1024]{1,0:T(8,128)(2,1)S(1)}, u32[]{:S(2)}, u32[]{:S(2)}) collective-permute-start(bf16[512,1024]{1,0:T(8,128)(2,1)S(1)} %get-tuple-element.29), channel_id=1, source_target_pairs={{0,3},{1,2},{2,1},{3,0},{4,7},{5,6},{6,5},{7,4},{8,11},{9,10},{10,... | collective-permute-start | bytes 3145736 | tf_op jit(solution)/shard_map/ppermute | solution.py:458
  69.7 79.6 %collective-permute-start.16 = (bf16[512,1024]{1,0:T(8,128)(2,1)S(1)}, bf16[512,1024]{1,0:T(8,128)(2,1)}, u32[]{:S(2)}, u32[]{:S(2)}) collective-permute-start(bf16[512,1024]{1,0:T(8,128)(2,1)S(1)} %get-tuple-element.38.refs_4_), channel_id=1, source_target_pairs={{0,4},{2,6},{4,0},{6,2},{1,5},{3,7},{5,1},{7,3},{8,12},{10,14},{12... | collective-permute-start | bytes 3145736 | tf_op jit(solution)/shard_map/ppermute | solution.py:461
  70.9 1.0 copy-start.3
  71.9 78.5 %collective-permute-start.9 = (bf16[512,1024]{1,0:T(8,128)(2,1)S(1)}, bf16[512,1024]{1,0:T(8,128)(2,1)S(1)}, u32[]{:S(2)}, u32[]{:S(2)}) collective-permute-start(bf16[512,1024]{1,0:T(8,128)(2,1)S(1)} %get-tuple-element.38.refs_4_), channel_id=1, source_target_pairs={{0,2},{2,0},{4,6},{6,4},{1,3},{3,1},{5,7},{7,5},{8,10},{10,8},{12,... | collective-permute-start | bytes 3145736 | tf_op jit(solution)/shard_map/ppermute | solution.py:461
  102.5 56.4 %collective-permute-start.11 = (bf16[512,1024]{1,0:T(8,128)(2,1)}, bf16[512,1024]{1,0:T(8,128)(2,1)}, u32[]{:S(2)}, u32[]{:S(2)}) collective-permute-start(bf16[512,1024]{1,0:T(8,128)(2,1)} %collective-permute-done.10.refs_6_), channel_id=1, source_target_pairs={{0,2},{2,0},{4,6},{6,4},{1,3},{3,1},{5,7},{7,5},{8,10},{10,8},{12,... | collective-permute-start | bytes 3145736 | tf_op jit(solution)/shard_map/ppermute | solution.py:461
  124.9 1.0 copy-start.5
  125.9 43.3 %collective-permute-start.13 = (bf16[512,1024]{1,0:T(8,128)(2,1)}, bf16[512,1024]{1,0:T(8,128)(2,1)}, u32[]{:S(2)}, u32[]{:S(2)}) collective-permute-start(bf16[512,1024]{1,0:T(8,128)(2,1)} %get-tuple-element.40), channel_id=1, source_target_pairs={{0,2},{2,0},{4,6},{6,4},{1,3},{3,1},{5,7},{7,5},{8,10},{10,8},{12,... | collective-permute-start | bytes 3145736 | tf_op jit(solution)/shard_map/ppermute | solution.py:461
  147.5 1.0 copy-start.7
  148.5 31.0 %collective-permute-start.14 = (bf16[512,1024]{1,0:T(8,128)(2,1)}, bf16[512,1024]{1,0:T(8,128)(2,1)}, u32[]{:S(2)}, u32[]{:S(2)}) collective-permute-start(bf16[512,1024]{1,0:T(8,128)(2,1)} %get-tuple-element.41), channel_id=1, source_target_pairs={{0,4},{2,6},{4,0},{6,2},{1,5},{3,7},{5,1},{7,3},{8,12},{10,14},{12... | collective-permute-start | bytes 3145736 | tf_op jit(solution)/shard_map/ppermute | solution.py:461
  149.4 53.6 %collective-permute-start.15 = (bf16[512,1024]{1,0:T(8,128)(2,1)}, bf16[512,1024]{1,0:T(8,128)(2,1)}, u32[]{:S(2)}, u32[]{:S(2)}) collective-permute-start(bf16[512,1024]{1,0:T(8,128)(2,1)} %get-tuple-element.42), channel_id=1, source_target_pairs={{0,6},{2,4},{4,2},{6,0},{1,7},{3,5},{5,3},{7,1},{8,14},{10,12},{12... | collective-permute-start | bytes 3145736 | tf_op jit(solution)/shard_map/ppermute | solution.py:461
  151.4 7.6 %copy-start.4 = (bf16[512,1024]{1,0:T(8,128)(2,1)S(1)}, bf16[512,1024]{1,0:T(8,128)(2,1)}, u32[]{:S(2)}) copy-start(bf16[512,1024]{1,0:T(8,128)(2,1)} %copy-done.3) | copy-start | bytes 3145732
  151.4 51.6 %collective-permute-start.17 = (bf16[512,1024]{1,0:T(8,128)(2,1)}, bf16[512,1024]{1,0:T(8,128)(2,1)}, u32[]{:S(2)}, u32[]{:S(2)}) collective-permute-start(bf16[512,1024]{1,0:T(8,128)(2,1)} %collective-permute-done.16.refs_6_), channel_id=1, source_target_pairs={{0,2},{2,0},{4,6},{6,4},{1,3},{3,1},{5,7},{7,5},{8,10},{10,8},{12,... | collective-permute-start | bytes 3145736 | tf_op jit(solution)/shard_map/ppermute | solution.py:461
  153.5 70.0 %all-to-all-start.1 = ((f32[32,40,128]{2,1,0:T(8,128)}), f32[32,40,128]{2,1,0:T(8,128)}, u32[]{:S(2)}, u32[]{:S(2)}) async-start(f32[32,40,128]{2,1,0:T(8,128)} %broadcast_in_dim.20), calls=%async_computation.1 | async-start | bytes 1310720 | tf_op jit(solution)/shard_map/all_to_all | solution.py:377
  158.9 1.2 copy-start.6
  160.2 1.2 copy-start.8
  167.7 91.4 %collective-permute-start.12 = (bf16[512,1024]{1,0:T(8,128)(2,1)}, bf16[512,1024]{1,0:T(8,128)(2,1)}, u32[]{:S(2)}, u32[]{:S(2)}) collective-permute-start(bf16[512,1024]{1,0:T(8,128)(2,1)} %shard_map.81), channel_id=1, source_target_pairs={{0,4},{2,6},{4,0},{6,2},{1,5},{3,7},{5,1},{7,3},{8,12},{10,14},{12... | collective-permute-start | bytes 3145736 | tf_op jit(solution)/shard_map/ppermute | solution.py:461
  203.0 6.5 %copy-start.2 = (bf16[512,1024]{1,0:T(8,128)(2,1)S(1)}, bf16[512,1024]{1,0:T(8,128)(2,1)}, u32[]{:S(2)}) copy-start(bf16[512,1024]{1,0:T(8,128)(2,1)} %copy-done.1) | copy-start | bytes 3145732
  203.0 6.5 %copy-start.9 = (bf16[512,1024]{1,0:T(8,128)(2,1)S(1)}, bf16[512,1024]{1,0:T(8,128)(2,1)}, u32[]{:S(2)}) copy-start(bf16[512,1024]{1,0:T(8,128)(2,1)} %copy-done.7) | copy-start | bytes 3145732
  209.4 49.6 %collective-permute-start.18 = (bf16[512,1024]{1,0:T(8,128)(2,1)}, bf16[512,1024]{1,0:T(8,128)(2,1)}, u32[]{:S(2)}, u32[]{:S(2)}) collective-permute-start(bf16[512,1024]{1,0:T(8,128)(2,1)} %shard_map.82), channel_id=1, source_target_pairs={{0,1},{1,0},{2,3},{3,2},{4,5},{5,4},{6,7},{7,6},{8,9},{9,8},{10,11... | collective-permute-start | bytes 3145736 | tf_op jit(solution)/shard_map/ppermute | solution.py:458
  224.9 81.4 %all-to-all-start.4 = ((f32[32,104,128]{2,1,0:T(8,128)}), f32[32,104,128]{2,1,0:T(8,128)S(1)}, u32[]{:S(2)}, u32[]{:S(2)}) async-start(f32[32,104,128]{2,1,0:T(8,128)} %broadcast_in_dim.22), calls=%async_computation.4 | async-start | bytes 3407872 | tf_op jit(solution)/shard_map/all_to_all | solution.py:377
  230.8 28.3 %copy-start.19 = (f32[512,1024]{1,0:T(8,128)S(1)}, f32[512,1024]{1,0:T(8,128)}, u32[]{:S(2)}) copy-start(f32[512,1024]{1,0:T(8,128)} %shard_map.84) | copy-start | bytes 6291460
  259.1 2.0 copy-start.10
  259.1 2.3 copy-start.18
  264.5 14.0 %collective-permute-start.19 = (bf16[256,1024]{1,0:T(8,128)(2,1)}, bf16[256,1024]{1,0:T(8,128)(2,1)S(1)}, u32[]{:S(2)}, u32[]{:S(2)}) collective-permute-start(bf16[256,1024]{1,0:T(8,128)(2,1)} %get-tuple-element.50), channel_id=1, source_target_pairs={{0,0},{2,16},{4,4},{6,20},{8,2},{10,18},{12,6},{14,22},{16,8},{18,... | collective-permute-start | bytes 1572872 | tf_op jit(solution)/shard_map/ppermute | solution.py:525
  269.0 26.4 %collective-permute-start.22 = (bf16[256,1024]{1,0:T(8,128)(2,1)}, bf16[256,1024]{1,0:T(8,128)(2,1)S(1)}, u32[]{:S(2)}, u32[]{:S(2)}) collective-permute-start(bf16[256,1024]{1,0:T(8,128)(2,1)} %get-tuple-element.51), channel_id=1, source_target_pairs={{0,10},{2,26},{4,14},{6,30},{8,0},{10,16},{12,4},{14,20},{16,2},{1... | collective-permute-start | bytes 1572872 | tf_op jit(solution)/shard_map/ppermute | solution.py:525
  271.4 28.4 %collective-permute-start.21 = (bf16[256,1024]{1,0:T(8,128)(2,1)}, bf16[256,1024]{1,0:T(8,128)(2,1)S(1)}, u32[]{:S(2)}, u32[]{:S(2)}) collective-permute-start(bf16[256,1024]{1,0:T(8,128)(2,1)} %get-tuple-element.52), channel_id=1, source_target_pairs={{0,8},{2,24},{4,12},{6,28},{8,10},{10,26},{12,14},{14,30},{16,0},{... | collective-permute-start | bytes 1572872 | tf_op jit(solution)/shard_map/ppermute | solution.py:525
  272.5 31.0 %collective-permute-start.20 = (bf16[256,1024]{1,0:T(8,128)(2,1)}, bf16[256,1024]{1,0:T(8,128)(2,1)}, u32[]{:S(2)}, u32[]{:S(2)}) collective-permute-start(bf16[256,1024]{1,0:T(8,128)(2,1)} %get-tuple-element.53), channel_id=1, source_target_pairs={{0,2},{2,18},{4,6},{6,22},{8,8},{10,24},{12,12},{14,28},{16,10},{1... | collective-permute-start | bytes 1572872 | tf_op jit(solution)/shard_map/ppermute | solution.py:525
  295.4 4.4 %copy-start.20 = (bf16[256,1024]{1,0:T(8,128)(2,1)}, bf16[256,1024]{1,0:T(8,128)(2,1)S(1)}, u32[]{:S(2)}) copy-start(bf16[256,1024]{1,0:T(8,128)(2,1)S(1)} %collective-permute-done.22) | copy-start | bytes 1572868
  306.3 45.2 %all-to-all-start.2 = ((f32[256,4,256]{2,0,1:T(8,128)}), f32[256,4,256]{2,0,1:T(8,128)}, u32[]{:S(2)}, u32[]{:S(2)}) async-start(f32[256,4,256]{2,0,1:T(8,128)} %bitcast.71), calls=%async_computation.2 | async-start | bytes 2097152 | tf_op jit(solution)/shard_map/all_to_all | solution.py:526
  318.7 1.2 copy-start.11
  320.0 28.8 %copy-start.12 = (f32[512,512]{1,0:T(8,128)S(1)}, f32[512,512]{1,0:T(8,128)}, u32[]{:S(2)}) copy-start(f32[512,512]{1,0:T(8,128)} %copy-done.10) | copy-start | bytes 3145732
  351.5 17.4 %all-to-all-start.5 = ((f32[256,4,256]{2,0,1:T(8,128)}), f32[256,4,256]{2,0,1:T(8,128)S(1)}, u32[]{:S(2)}, u32[]{:S(2)}) async-start(f32[256,4,256]{2,0,1:T(8,128)} %bitcast.49), calls=%async_computation.5 | async-start | bytes 2097152 | tf_op jit(solution)/shard_map/all_to_all | solution.py:536
  (2 other events, 1.8 us)
where the time goes:
time: 376 us; the launch traced here: 372 us
  waiting for transfers between devices  151 us (40%)
  Pallas kernels  93.7 us (25%)
  starting transfers between devices  68 us (18%)
  blocking collectives  26 us (7%)
  local copies, waits for them, and re-layouts  23.6 us (6%)
  other arithmetic  8.7 us (2%)
    ppermute x5, waiting for transfers between devices, move_z(): lax.ppermute(array, ('gy', 'gz'), z_pairs(ds, d))  71.9 us
    pallas_call x2, Pallas kernels, panel_call(): pl.pallas_call(kernel, out_shape=[jax.ShapeDtypeStruct((nb, nb), jnp.floa...  57 us
    ppermute x8, waiting for transfers between devices, move_y(): lax.ppermute(array, 'gy', y_pairs(ds, d))  33.9 us
    ppermute x4, waiting for transfers between devices, local(): rows = rows + lax.ppermute(sent, ('gx', 'gy'), pairs).astype(f32)  27.1 us
    all_to_all x1, blocking collectives, swap_everywhere(): terms = lax.all_to_all(rows, axes, split_axis=0, concat_axis=0, tiled=True)  26 us
    pallas_call x4, Pallas kernels, products(): pl.pallas_call(products_kernel, grid_spec=pltpu.PrefetchScalarGridSpec(nu...  25.3 us
    unnamed x46, local copies, waits for them, and re-layouts  15.4 us
    all_to_all x1, waiting for transfers between devices, local(): lax.all_to_all(factor, 'gy', split_axis=1, concat_axis=0, tiled=True)  13.6 us
  transfers between devices with their start and end apart: 28, of which 12 were waited for; matrix products, arithmetic and copies ran while one was open for 4% of the time, Pallas kernels for 23%

commit v1 on v0

--- a/solution.py
+++ b/solution.py
@@ -133,10 +133,13 @@
     ids = first_ref[0] + lax.broadcasted_iota(jnp.int32, (rows_ref.shape[0], nb), 0)
     cols = lax.broadcasted_iota(jnp.int32, (rows_ref.shape[0], nb), 1)
     part = dot3(rows_ref[:, :nb], w0_ref[...], ((1,), (1,)))
-    out_ref[:, :nb] = jnp.where(cols <= ids, part, 0.0)
     rest = rows_ref[:, nb:] - dot3(part, f_ref[...], ((1,), (1,)))
     rest = dot3(rest, w1_ref[...], ((1,), (1,)))
-    out_ref[:, nb:] = jnp.where(cols + nb <= ids, rest, 0.0)
+    width = out_ref.shape[2]
+    for at, value in ((0, part), (nb, rest)):
+        value = jnp.where(cols + at <= ids, value, 0.0)
+        for i in range(nb // width):
+            out_ref[at // width + i] = value[:, i * width : (i + 1) * width]
 
 
 def panel_call(kernel, outputs, nb, *operands):
@@ -340,19 +343,25 @@
     out[...] = total.astype(out.dtype)
 
 
-def products(bases, images, blocks, width, dtype):
+def products(bases, images, lists, width, dtype):
     rows, cols = images[0].shape
-    step = 256 if width % 256 == 0 else width
+    step = 512 if width % 512 == 0 else width
     parts = width // step
-    index = jnp.stack([jnp.asarray(b * parts + i, jnp.int32) for b in blocks for i in range(parts)])
-    in_specs = [pl.BlockSpec((rows, step), lambda t, idx: (0, idx[t]))] * len(bases)
+    steps = len(lists[0]) * parts
+    index = jnp.stack(
+        [jnp.asarray(b * parts + i, jnp.int32) for blocks in lists for b in blocks for i in range(parts)]
+    )
+    in_specs = [
+        pl.BlockSpec((rows, step), lambda t, idx, k=k: (0, idx[k * steps + t]))
+        for k in range(len(bases))
+    ]
     in_specs += [pl.BlockSpec((rows, cols), lambda t, idx: (0, 0))] * len(images)
-    total = len(blocks) * width
+    total = steps * step
     return pl.pallas_call(
         products_kernel,
         grid_spec=pltpu.PrefetchScalarGridSpec(
             num_scalar_prefetch=1,
-            grid=(len(blocks) * parts,),
+            grid=(steps,),
             in_specs=in_specs,
             out_specs=pl.BlockSpec((step, cols), lambda t, idx: (t, 0)),
         ),
@@ -366,16 +375,116 @@
     )(index, *bases, *images)
 
 
-def swap_everywhere(rows, axes, devices):
-    count = rows.shape[0]
-    share = -(-count // devices)
-    if share * devices > count:
-        rows = jnp.pad(rows, ((0, share * devices - count), (0, 0)))
-    rows = rows.reshape(devices, share, LEAF)
-    terms = lax.all_to_all(rows, axes, split_axis=0, concat_axis=0, tiled=True)
+def add_kernel(index_ref, *refs):
+    del index_ref
+    total = refs[0][...].astype(jnp.float32)
+    for got in refs[1:-1]:
+        total = total + got[...].astype(jnp.float32)
+    refs[-1][...] = total.astype(refs[-1].dtype)
+
+
+def add_blocks(arrays, lists, height, dtype):
+    cols = arrays[0].shape[1]
+    step = min(128, height)
+    parts = height // step
+    steps = len(lists[0]) * parts
+    index = jnp.stack(
+        [jnp.asarray(b * parts + i, jnp.int32) for blocks in lists for b in blocks for i in range(parts)]
+    )
+    return pl.pallas_call(
+        add_kernel,
+        grid_spec=pltpu.PrefetchScalarGridSpec(
+            num_scalar_prefetch=1,
+            grid=(steps,),
+            in_specs=[
+                pl.BlockSpec((step, cols), lambda t, idx, k=k: (idx[k * steps + t], 0))
+                for k in range(len(arrays))
+            ],
+            out_specs=pl.BlockSpec((step, cols), lambda t, idx: (t, 0)),
+        ),
+        out_shape=jax.ShapeDtypeStruct((steps * step, cols), dtype),
+        compiler_params=pltpu.CompilerParams(vmem_limit_bytes=24 * 2**20),
+        cost_estimate=pl.CostEstimate(
+            flops=steps * step * cols,
+            transcendentals=0,
+            bytes_accessed=steps * step * cols * 4 * len(arrays),
+        ),
+    )(index, *arrays)
+
+
+def pick_kernel(index_ref, *refs):
+    half = (len(refs) - 1) // 2
+
+    def total(group):
+        out = group[0][...].astype(jnp.float32)
+        for got in group[1:]:
+            out = out + got[...].astype(jnp.float32)
+        refs[-1][...] = out.astype(refs[-1].dtype)
+
+    @pl.when(index_ref[0] == 0)
+    def _():
+        total(refs[:half])
+
+    @pl.when(index_ref[0] != 0)
+    def _():
+        total(refs[half:-1])
+
+
+def pick_block(second, arrays_a, arrays_b, at_a, at_b, height, dtype):
+    cols = arrays_a[0].shape[1]
+    step = min(128, height)
+    parts = height // step
+    arrays = [*arrays_a, *arrays_b]
+    index = jnp.stack([jnp.asarray(v, jnp.int32) for v in (second, *at_a, *at_b)])
+    return pl.pallas_call(
+        pick_kernel,
+        grid_spec=pltpu.PrefetchScalarGridSpec(
+            num_scalar_prefetch=1,
+            grid=(parts,),
+            in_specs=[
+                pl.BlockSpec((step, cols), lambda t, idx, k=k: (idx[1 + k] * parts + t, 0))
+                for k in range(len(arrays))
+            ],
+            out_specs=pl.BlockSpec((step, cols), lambda t, idx: (t, 0)),
+        ),
+        out_shape=jax.ShapeDtypeStruct((height, cols), dtype),
+        compiler_params=pltpu.CompilerParams(vmem_limit_bytes=24 * 2**20),
+        cost_estimate=pl.CostEstimate(
+            flops=height * cols, transcendentals=0, bytes_accessed=height * cols * 18
+        ),
+    )(index, *arrays)
+
+
+def swap_pairs():
+    return [(0, 1), (1, 0)]
+
+
+def sum_everywhere(rows, core, axes, devices):
+    half = rows.shape[0] // 2
+    share = half // devices
+    both = rows.reshape(2, half, LEAF)
+    kept = lax.dynamic_index_in_dim(both, core, 0, keepdims=False)
+    sent = lax.dynamic_index_in_dim(both, 1 - core, 0, keepdims=False)
+    mine = kept + lax.ppermute(sent, "core", swap_pairs())
+    terms = lax.all_to_all(
+        mine.reshape(devices, share, LEAF), axes, split_axis=0, concat_axis=0, tiled=True
+    )
     own = jnp.broadcast_to(jnp.sum(terms, axis=0), (devices, share, LEAF))
-    sums = lax.all_to_all(own, axes, split_axis=0, concat_axis=0, tiled=True)
-    return sums.reshape(devices * share, LEAF)[:count]
+    own = lax.all_to_all(own, axes, split_axis=0, concat_axis=0, tiled=True).reshape(half, LEAF)
+    other = lax.ppermute(own, "core", swap_pairs())
+    first = core == 0
+    return jnp.concatenate([jnp.where(first, own, other), jnp.where(first, other, own)], 0)
+
+
+def sums_kernel(home_ref, own_ref, swapped_ref, *refs):
+    ins, (rows_ref, blocks_ref) = refs[:-2], refs[-2:]
+    total = jnp.where(home_ref[0] != 0, own_ref[...], swapped_ref[...])
+    for got in ins:
+        total = total + got[...].astype(jnp.float32)
+    rows_ref[...] = total
+    width = blocks_ref.shape[2]
+    for i in range(blocks_ref.shape[0]):
+        blocks_ref[i] = total[:, i * width : (i + 1) * width]
 
 
 def local(basis, classes, cond_table, ground_table, port_cells, port_load):
@@ -383,21 +492,27 @@
     cells_x, cells_y, cells_z = sides
     width_k = basis.shape[3]
     devices_x = lax.axis_size("gx")
-    devices_y = lax.axis_size("gy")
+    chips_y = lax.axis_size("gy")
     devices_z = lax.axis_size("gz")
-    devices = devices_x * devices_y * devices_z
-    chips_y = devices_y // 2
+    devices_y = 2 * chips_y
     spans = devices_x // 2
     split = spans // 2
     count = cells_x * cells_y * cells_z
     cols = PANELS * NB
-    at_x, at_y, at_z = (lax.axis_index(axis) for axis in ("gx", "gy", "gz"))
-    core = at_y % 2
-    chip = at_y // 2
-    axes = ("gx", "gy", "gz")
+    at_x, chip, core, at_z = (lax.axis_index(axis) for axis in ("gx", "gy", "core", "gz"))
+    at_y = 2 * chip + core
     f32, bf16 = jnp.float32, jnp.bfloat16
 
     flat_basis = basis.reshape(count, width_k)
+    wide = width_k // (devices_x * devices_z)
+    narrow = wide // chips_y
+    part = narrow // 2
+    (given,) = take_pieces(flat_basis, [([1 - core], width_k // 2)])
+
+    def move(array, axis, d):
+        size = lax.axis_size(axis)
+        return lax.ppermute(array, axis, [(i, (i + d) % size) for i in range(size)])
+
     panel = flat_basis[:, :cols]
     global_x = at_x * cells_x + jnp.arange(cells_x, dtype=jnp.int32)
     global_y = at_y * cells_y + jnp.arange(cells_y, dtype=jnp.int32)
@@ -408,7 +523,6 @@
         + global_z[None, None, :]
     )
     info = jnp.stack([classes, flat_ids], -1).reshape(count, 2)
-
     face_rows = [cells_y * cells_z] * 2 + [cells_x * cells_z] * 2 + [cells_x * cells_y] * 2
     *faces, conduct, grounds = pl.pallas_call(
         functools.partial(faces_kernel, sides=sides),
@@ -420,51 +534,23 @@
         compiler_params=pltpu.CompilerParams(vmem_limit_bytes=24 * 2**20),
     )(cond_table, ground_table, info, port_cells[None, :], port_load[None, :], panel)
     halos = []
-    for i, (axis, size) in enumerate((("gx", devices_x), ("gy", devices_y), ("gz", devices_z))):
+    for i, (axis, size) in enumerate(
+        (("gx", devices_x), (("gy", "core"), devices_y), ("gz", devices_z))
+    ):
         low, high = faces[2 * i : 2 * i + 2]
-        halos.append(lax.ppermute(high, axis, [(k, k + 1) for k in range(size - 1)]))
-        halos.append(lax.ppermute(low, axis, [(k + 1, k) for k in range(size - 1)]))
-
-    wide = width_k // (devices_x * devices_z)
-    narrow = wide // chips_y
-
-    def over_z_blocks(s, x):
-        return [(s * spans + zz) * devices_z + x for zz in range(split)]
-
-    def over_y_blocks(s, y):
-        return [
-            ((s * spans + zz) * devices_z + x) * chips_y + y
-            for zz in range(split, spans)
-            for x in range(devices_z)
-        ]
-
-    z_steps = [(ds, d) for d in range(devices_z) for ds in (0, 1)]
-    y_steps = [(ds, d) for d in range(chips_y) for ds in (0, 1)]
-    lists = [(over_z_blocks(core ^ ds, (at_z + d) % devices_z), wide) for ds, d in z_steps]
-    lists += [(over_y_blocks(core ^ ds, (chip + d) % chips_y), narrow) for ds, d in y_steps]
-    pieces = take_pieces(flat_basis, lists)
-
-    def z_pairs(ds, d):
-        return [
-            (y * devices_z + z, (y ^ ds) * devices_z + (z + d) % devices_z)
-            for y in range(devices_y)
-            for z in range(devices_z)
-        ]
-
-    def y_pairs(ds, d):
-        return [(2 * y + c, 2 * ((y + d) % chips_y) + (c ^ ds)) for y in range(chips_y) for c in (0, 1)]
-
-    def move_z(array, ds, d):
-        return array if (ds, d) == (0, 0) else lax.ppermute(array, ("gy", "gz"), z_pairs(ds, d))
-
-    def move_y(array, ds, d):
-        return array if (ds, d) == (0, 0) else lax.ppermute(array, "gy", y_pairs(ds, d))
-
-    z_bases = [move_z(p, ds, d) for p, (ds, d) in zip(pieces, z_steps)]
-    y_bases = [move_y(p, ds, d) for p, (ds, d) in zip(pieces[len(z_steps) :], y_steps)]
+        if size == 2:
+            last = lax.axis_index(axis) == 1
+            got = lax.ppermute(jnp.where(last, low, high), axis, swap_pairs())
+            halos.append(jnp.where(last, got, 0))
+            halos.append(jnp.where(last, 0, got))
+        else:
+            halos.append(lax.ppermute(high, axis, [(k, k + 1) for k in range(size - 1)]))
+            halos.append(lax.ppermute(low, axis, [(k + 1, k) for k in range(size - 1)]))
+    other_basis = lax.ppermute(given, "core", swap_pairs())
 
     blocks = NB // LEAF
     lower_rows = blocks * (blocks + 1) // 2 * LEAF
+    halos, _ = lax.optimization_barrier((halos, given))
     image, first_rows, later_rows = pl.pallas_call(
         functools.partial(image_kernel, sides=sides, nb=NB),
         out_shape=[
@@ -478,71 +564,115 @@
         compiler_params=pltpu.CompilerParams(vmem_limit_bytes=32 * 2**20),
     )(panel, conduct, grounds, *halos)
 
-    by_z = {(0, d): move_z(image, 0, d) for d in range(devices_z)}
-    by_y = {(0, d): move_y(image, 0, d) for d in range(1, chips_y)}
-    by_z.update({(1, d): move_y(by_z[0, d], 1, 0) for d in range(devices_z)})
-    by_y.update({(1, d): move_y(by_y[0, d], 1, 0) for d in range(1, chips_y)})
-    by_y.update({(ds, 0): by_z[ds, 0] for ds in (0, 1)})
-    z_images = [by_z[key] for key in z_steps]
-    y_images = [by_y[key] for key in y_steps]
-
-    first_rows = swap_everywhere(first_rows, axes, devices)
-    later_rows = swap_everywhere(later_rows, axes, devices)
+    other_image = lax.ppermute(image, "core", swap_pairs())
+
+    axes = ("gx", "gy", "gz")
+    chips = devices_x * chips_y * devices_z
+    first_rows = sum_everywhere(first_rows, core, axes, chips)
     inverse_0 = first_panel(first_rows, NB)
-    factor_10, inverse_1 = next_panel(later_rows, inverse_0)
-
-    part = narrow // 2
-
-    def y_block(d):
-        return [zz * chips_y + (chip + d) % chips_y for zz in range(split)]
-
-    def z_block(d):
-        return [zz * devices_z + (at_z + d) % devices_z for zz in range(spans - split)]
-
-    y_sent = [products(z_bases, z_images, y_block(d), narrow, bf16) for d in range(1, chips_y)]
-    y_got = [move_y(a, 0, d) for d, a in zip(range(1, chips_y), y_sent)]
-    z_sent = [products(y_bases, y_images, z_block(d), narrow, bf16) for d in range(1, devices_z)]
-    z_got = [move_z(a, 0, d) for d, a in zip(range(1, devices_z), z_sent)]
-    sums_a = products(z_bases, z_images, y_block(0), narrow, f32)
-    sums_b = products(y_bases, y_images, z_block(0), narrow, f32)
-    y_got, z_got, inverse_0 = lax.optimization_barrier((y_got, z_got, inverse_0))
-    for got in y_got:
-        sums_a = sums_a + got.astype(f32)
-    for got in z_got:
-        sums_b = sums_b + got.astype(f32)
-    plane = jnp.concatenate([sums_a.astype(bf16), sums_b.astype(bf16)], 0)
-    plane = plane.reshape(devices_x, part, cols)
-    rows = jnp.zeros((part, cols), f32)
+
+    shift = core * spans * devices_z * chips_y
+
+    def chip_products(blocks, dtype):
+        lists = [[b + shift for b in blocks], blocks]
+        return products([flat_basis, other_basis], [image, other_image], lists, narrow, dtype)
+
+    def products_a(d, dtype):
+        x = (at_z + d) % devices_z
+        blocks = [(zz * devices_z + x) * chips_y + y for zz in range(split) for y in range(chips_y)]
+        return chip_products(blocks, dtype)
+
+    def products_b(d, dtype):
+        y = (chip + d) % chips_y
+        blocks = [
+            (zz * devices_z + x) * chips_y + y for zz in range(split, spans) for x in range(devices_z)
+        ]
+        return chip_products(blocks, dtype)
+
+    got_a = [move(products_a(d, bf16), "gz", d) for d in range(1, devices_z)]
+    got_b = [move(products_b(d, bf16), "gy", d) for d in range(1, chips_y)]
+    own_a, own_b = products_a(0, f32), products_b(0, f32)
+    (got_a, got_b, own_a, own_b, later_rows), inverse_0 = lax.optimization_barrier(
+        ((got_a, got_b, own_a, own_b, later_rows), inverse_0)
+    )
+    later_rows = sum_everywhere(later_rows, core, axes, chips)
+    sums_a, sums_b = [own_a, *got_a], [own_b, *got_b]
+
+    def further(arrays, axis, mine, size, groups):
+        got = []
+        for d in range(1, size):
+            blocks = [zz * size + (mine + d) % size for zz in range(groups)]
+            got.append(move(add_blocks(arrays, [blocks] * len(arrays), narrow, bf16), axis, d))
+        return got
+
+    further_a = further(sums_a, "gy", chip, chips_y, split)
+    further_b = further(sums_b, "gz", at_z, devices_z, spans - split)
+
+    def plane_block(zz, c, dtype):
+        in_b = zz >= split
+        zz_a, zz_b = jnp.minimum(zz, split - 1), jnp.maximum(zz - split, 0)
+        at_a = [(zz_a * chips_y + chip) * 2 + c] * len(sums_a) + [zz_a * 2 + c] * len(further_a)
+        at_b = [(zz_b * devices_z + at_z) * 2 + c] * len(sums_b) + [zz_b * 2 + c] * len(further_b)
+        return pick_block(
+            in_b, sums_a + further_a, sums_b + further_b, at_a, at_b, part, dtype
+        )
+
+    x_got, x_sent = [], []
     for step in range(devices_x):
-        sent = lax.dynamic_index_in_dim(plane, (at_x + step) % devices_x, 0, keepdims=False)
+        to = (at_x + step) % devices_x
+        x_sent.append(plane_block(to // 2, to % 2, bf16))
         pairs = []
         for x in range(devices_x):
             for y in range(devices_y):
                 to = (x + step) % devices_x
                 dest_x = (y % 2) * spans + to // 2
                 dest_y = (y // 2) * 2 + to % 2
-                pairs.append((x * devices_y + y, dest_x * devices_y + dest_y))
-        rows = rows + lax.ppermute(sent, ("gx", "gy"), pairs).astype(f32)
-    reduced = lax.all_to_all(rows, "gy", split_axis=1, concat_axis=0, tiled=True)
-
+                if dest_x != x:
+                    pairs.append((x * devices_y + y, dest_x * devices_y + dest_y))
+        x_got.append(lax.ppermute(x_sent[-1], ("gx", "gy", "core"), pairs))
+    home = at_x // spans == core
+    own = plane_block(at_x % spans, core, f32)
+    swapped = lax.ppermute(plane_block(at_x % spans, 1 - core, f32), "core", swap_pairs())
+    later_rows, x_sent, own = lax.optimization_barrier((later_rows, x_sent, own))
+    factor_10, inverse_1 = next_panel(later_rows, inverse_0)
+    (x_got, swapped), inverse_1 = lax.optimization_barrier(((x_got, swapped), inverse_1))
+    by_blocks = jax.ShapeDtypeStruct((devices_y, part, cols // devices_y), f32)
+    rows, reduced = pl.pallas_call(
+        sums_kernel,
+        out_shape=[jax.ShapeDtypeStruct((part, cols), f32), by_blocks],
+        in_specs=[whole(pltpu.SMEM)] + [whole()] * (devices_x + 2),
+        out_specs=[whole()] * 2,
+        compiler_params=pltpu.CompilerParams(vmem_limit_bytes=32 * 2**20),
+    )(home.astype(jnp.int32)[None], own, swapped, *x_got)
+
+    def to_columns(array):
+        array = lax.all_to_all(array, ("gy", "core"), split_axis=0, concat_axis=0, tiled=True)
+        return array.reshape(devices_y * part, cols // devices_y)
+
+    reduced = to_columns(reduced)
     first_row = ((at_x * devices_z + at_z) * devices_y + at_y) * part
     factor = pl.pallas_call(
         factor_kernel,
-        out_shape=jax.ShapeDtypeStruct((part, cols), f32),
+        out_shape=by_blocks,
         in_specs=[whole(pltpu.SMEM)] + [whole()] * 4,
         out_specs=whole(),
         compiler_params=pltpu.CompilerParams(vmem_limit_bytes=32 * 2**20),
     )(first_row[None], rows, inverse_0, factor_10, inverse_1)
-    factor = lax.all_to_all(factor, "gy", split_axis=1, concat_axis=0, tiled=True)
-    return (reduced, factor)
+    return (reduced, to_columns(factor))
 
 
 def solution(mesh):
-    placed = (P("gx", "gy", "gz", None), P("gx", "gy", "gz"), P(), P(), P(), P())
+    sizes = mesh.shape
+    fine = jax.sharding.Mesh(
+        mesh.devices.reshape(sizes["gx"], sizes["gy"] // 2, 2, sizes["gz"]),
+        ("gx", "gy", "core", "gz"),
+    )
+    grid = ("gx", ("gy", "core"), "gz")
+    out = P(("gx", "gz"), ("gy", "core"))
     return jax.shard_map(
         local,
-        mesh=mesh,
-        in_specs=placed,
-        out_specs=(P(("gx", "gz"), "gy"), P(("gx", "gz"), "gy")),
+        mesh=fine,
+        in_specs=(P(*grid, None), P(*grid), P(), P(), P(), P()),
+        out_specs=(out, out),
         check_vma=False,
     )

time: 376 us -> 306 us (0.81)
  waiting for transfers between devices: 151 us -> 69.9 us
  blocking collectives: 26 us -> 40.5 us
  starting transfers between devices: 68 us -> 58 us
  Pallas kernels: 93.7 us -> 102 us
  other arithmetic: 8.7 us -> 2.29 us
  local copies, waits for them, and re-layouts: 23.6 us -> 29.7 us
    ppermute x17 -> x16, waiting for transfers between devices: 133 us -> 26.5 us  [the longest x4 21.8 us: move(): return lax.ppermute(array, axis, [(i, (i + d) % size) for i in range(size)])]
    all_to_all x5 -> x4, waiting for transfers between devices: 13.6 us -> 39.7 us  [the longest x2 23.4 us: to_columns(): lax.all_to_all(array, ('gy', 'core'), split_axis=0, concat_axis=0, tiled=...]
    pallas_call x1 -> x10, Pallas kernels: 1.62 us -> 18.6 us  [the longest x6 10.3 us: pick_block(): pl.pallas_call(pick_kernel, grid_spec=pltpu.PrefetchScalarGridSpec(num_sc...]
    all_to_all x1 -> x2, blocking collectives: 26 us -> 40.5 us  [sum_everywhere(): lax.all_to_all(mine.reshape(devices, share, LEAF), axes, split_axis=0, co...]
    all_to_all x5 -> x4, starting transfers between devices: 30.3 us -> 17.4 us  [the longest x2 8.76 us: sum_everywhere(): lax.all_to_all(own, axes, split_axis=0, concat_axis=0, tiled=True)]
    unnamed x46 -> x54, local copies, waits for them, and re-layouts: 15.4 us -> 25.6 us
    ppermute x17 -> x16, starting transfers between devices: 22 us -> 30.6 us  [the longest x4 13.3 us: local(): x_got.append(lax.ppermute(x_sent[-1], ('gx', 'gy', 'core'), pairs))]
    pallas_call x4, Pallas kernels: 25.3 us -> 20.2 us  [products(): pl.pallas_call(products_kernel, grid_spec=pltpu.PrefetchScalarGridSpec(nu...]
  transfers between devices with their start and end apart: 28 -> 24, of which waited for: 12 -> 12; matrix products, arithmetic and copies ran while one was open for 4% -> 2% of each run, Pallas kernels for 23% -> 31%
where the time goes in v1:
time: 306 us; the launch traced here: 304 us
  Pallas kernels  102 us (33%)
  waiting for transfers between devices  69.9 us (23%)
  starting transfers between devices  58 us (19%)
  blocking collectives  40.5 us (13%)
  local copies, waits for them, and re-layouts  29.7 us (10%)
    pallas_call x2, Pallas kernels, panel_call(): pl.pallas_call(kernel, out_shape=[jax.ShapeDtypeStruct((nb, nb), jnp.floa...  55.8 us
    all_to_all x2, blocking collectives, sum_everywhere(): lax.all_to_all(mine.reshape(devices, share, LEAF), axes, split_axis=0, co...  40.5 us
    unnamed x54, local copies, waits for them, and re-layouts  25.6 us
    all_to_all x2, waiting for transfers between devices, to_columns(): lax.all_to_all(array, ('gy', 'core'), split_axis=0, concat_axis=0, tiled=...  23.4 us
    ppermute x4, waiting for transfers between devices, move(): return lax.ppermute(array, axis, [(i, (i + d) % size) for i in range(size)])  21.8 us
    pallas_call x4, Pallas kernels, products(): pl.pallas_call(products_kernel, grid_spec=pltpu.PrefetchScalarGridSpec(nu...  20.2 us
    all_to_all x2, waiting for transfers between devices, sum_everywhere(): lax.all_to_all(own, axes, split_axis=0, concat_axis=0, tiled=True)  16.3 us
    ppermute x4, starting transfers between devices, local(): x_got.append(lax.ppermute(x_sent[-1], ('gx', 'gy', 'core'), pairs))  13.3 us
  transfers between devices with their start and end apart: 24, of which 12 were waited for; matrix products, arithmetic and copies ran while one was open for 2% of the time, Pallas kernels for 31%

profile of v1, /device:TPU:1, one launch (start us, length us, event | category | flops | bytes accessed | tf_op | source)
XLA Modules:
  0.0 304.0 jit_solution(1936733601949042712)
XLA Ops:
  0.6 3.4 %copy-done.4 = bf16[8,8,8,8192]{3,2,1,0:T(8,128)(2,1)S(1)} copy-done((bf16[8,8,8,8192]{3,2,1,0:T(8,128)(2,1)S(1)}, bf16[8,8,8,8192]{3,2,1,0:T(8,128)(2,1)}, u32[]{:S(2)}) %copy-start.4) | copy-done | bytes 8388632
  4.0 2.8 shard_map.77
  8.8 2.4 shard_map.78
  12.0 2.7 collective-permute-start.5
  14.7 3.2 %collective-permute-start.1 = (bf16[64,1024]{1,0:T(8,128)(2,1)S(1)}, bf16[64,1024]{1,0:T(8,128)(2,1)S(1)}, u32[]{:S(2)}, u32[]{:S(2)}) collective-permute-start(bf16[64,1024]{1,0:T(8,128)(2,1)S(1)} %get-tuple-element.39), channel_id=1, source_target_pairs={{0,8},{8,16},{16,24},{1,9},{9,17},{17,25},{2,10},{10,18},{18,26},{... | collective-permute-start | bytes 393224 | tf_op jit(solution)/shard_map/ppermute | solution.py:547
  19.2 3.6 %collective-permute-start.3 = (bf16[64,1024]{1,0:T(8,128)(2,1)S(1)}, bf16[64,1024]{1,0:T(8,128)(2,1)S(1)}, u32[]{:S(2)}, u32[]{:S(2)}) collective-permute-start(bf16[64,1024]{1,0:T(8,128)(2,1)S(1)} %get-tuple-element.41), channel_id=1, source_target_pairs={{0,2},{2,4},{4,6},{1,3},{3,5},{5,7},{8,10},{10,12},{12,14},{9,11},... | collective-permute-start | bytes 393224 | tf_op jit(solution)/shard_map/ppermute | solution.py:547
  22.8 1.9 collective-permute-start.4
  25.5 3.6 %collective-permute-done.4.refs_3_ = bf16[64,1024]{1,0:T(8,128)(2,1)S(1)} collective-permute-done((bf16[64,1024]{1,0:T(8,128)(2,1)S(1)}, bf16[64,1024]{1,0:T(8,128)(2,1)S(1)}, u32[]{:S(2)}, u32[]{:S(2)}) %collective-permute-start.4) | collective-permute-done | bytes 131104 | tf_op jit(solution)/shard_map/ppermute | solution.py:548
  31.0 2.6 shard_map.79
  36.5 15.5 %all_to_all.30 = f32[16,40,128]{2,1,0:T(8,128)S(1)} all-to-all(f32[16,40,128]{2,1,0:T(8,128)S(1)} %bitcast.93), channel_id=1, replica_groups=mesh['gx'=4,'gy'=2,'core'=2,'gz'=2] {'gx','gy','gz'}, dimensions={0} | all-to-all | bytes 655360 | tf_op jit(solution)/shard_map/all_to_all | solution.py:469
  52.8 4.4 %all-to-all-start.1 = ((f32[16,40,128]{2,1,0:T(8,128)}), f32[16,40,128]{2,1,0:T(8,128)S(1)}, u32[]{:S(2)}, u32[]{:S(2)}) async-start(f32[16,40,128]{2,1,0:T(8,128)} %broadcast_in_dim.34), calls=%async_computation.1 | async-start | bytes 655360 | tf_op jit(solution)/shard_map/all_to_all | solution.py:473
  58.8 7.0 %all-to-all-done.1 = f32[16,40,128]{2,1,0:T(8,128)S(1)} async-done(((f32[16,40,128]{2,1,0:T(8,128)}), f32[16,40,128]{2,1,0:T(8,128)S(1)}, u32[]{:S(2)}, u32[]{:S(2)}) %all-to-all-start.1) | async-done | bytes 327712 | tf_op jit(solution)/shard_map/all_to_all | solution.py:473
  65.8 3.7 %collective-permute-start.10 = (f32[640,128]{1,0:T(8,128)S(1)}, f32[640,128]{1,0:T(8,128)S(1)}, u32[]{:S(2)}, u32[]{:S(2)}) collective-permute-start(f32[640,128]{1,0:T(8,128)S(1)} %bitcast.94), channel_id=1, source_target_pairs={{0,2},{2,0},{1,3},{3,1},{4,6},{6,4},{5,7},{7,5},{8,10},{10,8},{9,1... | collective-permute-start | bytes 983048 | tf_op jit(solution)/shard_map/ppermute | solution.py:474
  70.9 4.4 %shard_map.80 = bf16[1024,1024]{1,0:T(8,128)(2,1)S(1)} custom-call(s32[4]{0:T(128)S(1)} %get-tuple-element.78.index_ref, bf16[512,8192]{1,0:T(8,128)(2,1)} %bitcast.80, bf16[512,4096]{1,0:T(8,128)(2,1)} %collective-permute-done.refs_1_, bf16[512,1024]{1,0:T(8,128)(2,1)S(1)} %get-tuple-element.51.refs_2_, bf16[512,1024]{1,0:T(8,128)(2,1)S(1)} %collective-permute-done.6.refs_3_), custom_call_target="tpu_custom_call" | custom-call | flops 2147483648 | bytes 8388608 | tf_op jit(solution)/shard_map/pallas_call | solution.py:360
  77.8 4.4 %shard_map.81 = bf16[1024,1024]{1,0:T(8,128)(2,1)S(1)} custom-call(s32[4]{0:T(128)S(1)} %get-tuple-element.79.index_ref, bf16[512,8192]{1,0:T(8,128)(2,1)} %bitcast.81, bf16[512,4096]{1,0:T(8,128)(2,1)} %collective-permute-done.refs_1_, bf16[512,1024]{1,0:T(8,128)(2,1)S(1)} %get-tuple-element.51.refs_2_, bf16[512,1024]{1,0:T(8,128)(2,1)S(1)} %copy-done.9), custom_call_target="tpu_custom_call" | custom-call | flops 2147483648 | bytes 8388608 | tf_op jit(solution)/shard_map/pallas_call | solution.py:360
  82.7 27.0 %shard_map.84.w0_ref = f32[512,512]{1,0:T(8,128)S(1)} custom-call(f32[1280,128]{1,0:T(8,128)S(1)} %pad_maximum_fusion.1.packed_ref), custom_call_target="tpu_custom_call" | custom-call | flops 25769803776 | bytes 2097152 | tf_op jit(solution)/shard_map/pallas_call | solution.py:146
  110.7 5.7 %shard_map.82.refs_0_ = f32[1024,1024]{1,0:T(8,128)} custom-call(s32[4]{0:T(128)S(1)} %get-tuple-element.80.index_ref, bf16[512,8192]{1,0:T(8,128)(2,1)} %bitcast.82, bf16[512,4096]{1,0:T(8,128)(2,1)} %collective-permute-done.refs_1_, bf16[512,1024]{1,0:T(8,128)(2,1)S(1)} %get-tuple-element.51.refs_2_, bf16[512,1024]{1,0:T(8,128)(2,1)S(1)} %copy-done.10), custom_call_target="tpu_custom_call" | custom-call | flops 2147483648 | bytes 8388608 | tf_op jit(solution)/shard_map/pallas_call | solution.py:360
  116.4 5.7 %shard_map.83.refs_0_.refs_3_ = f32[1024,1024]{1,0:T(8,128)} custom-call(s32[4]{0:T(128)S(1)} %get-tuple-element.81.index_ref, bf16[512,8192]{1,0:T(8,128)(2,1)} %bitcast.83, bf16[512,4096]{1,0:T(8,128)(2,1)} %collective-permute-done.refs_1_, bf16[512,1024]{1,0:T(8,128)(2,1)S(1)} %get-tuple-element.51.refs_2_, bf16[512,1024]{1,0:T(8,128)(2,1)S(1)} %copy-done.10), custom_call_target="tpu_custom_call" | custom-call | flops 2147483648 | bytes 8388608 | tf_op jit(solution)/shard_map/pallas_call | solution.py:360
  123.1 5.6 %collective-permute-done.8.refs_1_.refs_4_ = bf16[1024,1024]{1,0:T(8,128)(2,1)S(1)} collective-permute-done((bf16[1024,1024]{1,0:T(8,128)(2,1)S(1)}, bf16[1024,1024]{1,0:T(8,128)(2,1)S(1)}, u32[]{:S(2)}, u32[]{:S(2)}) %collective-permute-start.8) | collective-permute-done | bytes 2097184 | tf_op jit(solution)/shard_map/ppermute | solution.py:514
  130.4 2.0 collective-permute-done.11
  132.5 25.1 %all_to_all.31 = f32[16,104,128]{2,1,0:T(8,128)S(1)} all-to-all(f32[16,104,128]{2,1,0:T(8,128)S(1)} %bitcast.92), channel_id=1, replica_groups=mesh['gx'=4,'gy'=2,'core'=2,'gz'=2] {'gx','gy','gz'}, dimensions={0} | all-to-all | bytes 1703936 | tf_op jit(solution)/shard_map/all_to_all | solution.py:469
  158.6 4.3 %all-to-all-start.3 = ((f32[16,104,128]{2,1,0:T(8,128)}), f32[16,104,128]{2,1,0:T(8,128)}, u32[]{:S(2)}, u32[]{:S(2)}) async-start(f32[16,104,128]{2,1,0:T(8,128)} %broadcast_in_dim.35), calls=%async_computation.3 | async-start | bytes 1703936 | tf_op jit(solution)/shard_map/all_to_all | solution.py:473
  163.1 2.2 copy-done
  165.3 2.1 shard_map.85
  168.7 2.1 shard_map.86
  172.0 9.3 %all-to-all-done.3 = f32[16,104,128]{2,1,0:T(8,128)} async-done(((f32[16,104,128]{2,1,0:T(8,128)}), f32[16,104,128]{2,1,0:T(8,128)}, u32[]{:S(2)}, u32[]{:S(2)}) %all-to-all-start.3) | async-done | bytes 852000 | tf_op jit(solution)/shard_map/all_to_all | solution.py:473
  181.4 3.4 %collective-permute-start.12 = (f32[1664,128]{1,0:T(8,128)}, f32[1664,128]{1,0:T(8,128)}, u32[]{:S(2)}, u32[]{:S(2)}) collective-permute-start(f32[1664,128]{1,0:T(8,128)} %bitcast.30), channel_id=1, source_target_pairs={{0,2},{2,0},{1,3},{3,1},{4,6},{6,4},{5,7},{7,5},{8,10},{10,8},{9,1... | collective-permute-start | bytes 2555912 | tf_op jit(solution)/shard_map/ppermute | solution.py:474
  185.3 11.5 %collective-permute-done.13.refs_2_ = bf16[512,1024]{1,0:T(8,128)(2,1)S(1)} collective-permute-done((bf16[512,1024]{1,0:T(8,128)(2,1)}, bf16[512,1024]{1,0:T(8,128)(2,1)S(1)}, u32[]{:S(2)}, u32[]{:S(2)}) %collective-permute-start.13) | collective-permute-done | bytes 1048608 | tf_op jit(solution)/shard_map/ppermute | solution.py:514
  196.8 3.7 %collective-permute-done.14.refs_5_ = bf16[512,1024]{1,0:T(8,128)(2,1)} collective-permute-done((bf16[512,1024]{1,0:T(8,128)(2,1)}, bf16[512,1024]{1,0:T(8,128)(2,1)}, u32[]{:S(2)}, u32[]{:S(2)}) %collective-permute-start.14) | collective-permute-done | bytes 1048608 | tf_op jit(solution)/shard_map/ppermute | solution.py:514
  200.5 2.2 copy-done.1
  202.7 2.2 copy-done.3
  206.5 1.7 shard_map.87
  208.2 6.0 %collective-permute-start.15 = (bf16[256,1024]{1,0:T(8,128)(2,1)S(1)}, bf16[256,1024]{1,0:T(8,128)(2,1)S(1)}, u32[]{:S(2)}, u32[]{:S(2)}) collective-permute-start(bf16[256,1024]{1,0:T(8,128)(2,1)S(1)} %shard_map.87), channel_id=1, source_target_pairs={{2,16},{6,20},{8,2},{10,18},{12,6},{14,22},{16,8},{18,24},{20,12},... | collective-permute-start | bytes 1572872 | tf_op jit(solution)/shard_map/ppermute | solution.py:632
  214.2 1.7 shard_map.88
  216.0 1.8 collective-permute-start.16
  217.8 1.7 shard_map.89
  219.5 1.9 collective-permute-start.17
  221.4 1.7 shard_map.90
  223.1 3.6 %collective-permute-start.18 = (bf16[256,1024]{1,0:T(8,128)(2,1)S(1)}, bf16[256,1024]{1,0:T(8,128)(2,1)S(1)}, u32[]{:S(2)}, u32[]{:S(2)}) collective-permute-start(bf16[256,1024]{1,0:T(8,128)(2,1)S(1)} %shard_map.90), channel_id=1, source_target_pairs={{0,10},{2,26},{4,14},{6,30},{8,0},{10,16},{12,4},{14,20},{16,2},{2... | collective-permute-start | bytes 1572872 | tf_op jit(solution)/shard_map/ppermute | solution.py:632
  226.8 1.7 shard_map.91.own_ref
  228.5 1.7 shard_map.92
  233.7 28.8 %shard_map.93 = (f32[512,512]{1,0:T(8,128)S(1)}, f32[512,512]{1,0:T(8,128)S(1)}) custom-call(f32[3328,128]{1,0:T(8,128)S(1)} %pad_maximum_fusion.packed_ref, f32[512,512]{1,0:T(8,128)S(1)} %copy-done.14), custom_call_target="tpu_custom_call" | custom-call | flops 25769803776 | bytes 2097152 | tf_op jit(solution)/shard_map/pallas_call | solution.py:146
  264.9 4.2 %all-to-all-start.4 = ((f32[4,256,256]{2,1,0:T(8,128)}), f32[4,256,256]{2,1,0:T(8,128)}, u32[]{:S(2)}, u32[]{:S(2)}) async-start(f32[4,256,256]{2,1,0:T(8,128)} %get-tuple-element.68), calls=%async_computation.4 | async-start | bytes 2097152 | tf_op jit(solution)/shard_map/all_to_all | solution.py:649
  270.4 2.6 shard_map.95
  273.0 9.8 %all-to-all-done.4 = f32[4,256,256]{2,1,0:T(8,128)} async-done(((f32[4,256,256]{2,1,0:T(8,128)}), f32[4,256,256]{2,1,0:T(8,128)}, u32[]{:S(2)}, u32[]{:S(2)}) %all-to-all-start.4) | async-done | bytes 1048608 | tf_op jit(solution)/shard_map/all_to_all | solution.py:649
  282.8 4.4 %all-to-all-start.5 = ((f32[4,256,256]{2,1,0:T(8,128)}), f32[4,256,256]{2,1,0:T(8,128)S(1)}, u32[]{:S(2)}, u32[]{:S(2)}) async-start(f32[4,256,256]{2,1,0:T(8,128)} %shard_map.95), calls=%async_computation.5 | async-start | bytes 2097152 | tf_op jit(solution)/shard_map/all_to_all | solution.py:649
  287.2 13.6 %all-to-all-done.5 = f32[4,256,256]{2,1,0:T(8,128)S(1)} async-done(((f32[4,256,256]{2,1,0:T(8,128)}), f32[4,256,256]{2,1,0:T(8,128)S(1)}, u32[]{:S(2)}, u32[]{:S(2)}) %all-to-all-start.5) | async-done | bytes 1048608 | tf_op jit(solution)/shard_map/all_to_all | solution.py:649
  300.8 2.3 copy.13
  (108 shorter events, 33.6 us)
Async XLA Ops:
  0.6 3.4 %copy-start.4 = (bf16[8,8,8,8192]{3,2,1,0:T(8,128)(2,1)S(1)}, bf16[8,8,8,8192]{3,2,1,0:T(8,128)(2,1)}, u32[]{:S(2)}) copy-start(bf16[8,8,8,8192]{3,2,1,0:T(8,128)(2,1)} %param.6) | copy-start | bytes 25165828
  6.8 1.7 copy-start.25
  6.8 2.0 copy-start.21
  6.8 2.0 copy-start.22
  6.8 2.0 copy-start.23
  6.8 2.0 copy-start.24
  6.8 64.1 %collective-permute-start = (bf16[512,4096]{1,0:T(8,128)(2,1)}, bf16[512,4096]{1,0:T(8,128)(2,1)}, u32[]{:S(2)}, u32[]{:S(2)}) collective-permute-start(bf16[512,4096]{1,0:T(8,128)(2,1)} %shard_map.77), channel_id=1, source_target_pairs={{0,2},{2,0},{1,3},{3,1},{4,6},{6,4},{5,7},{7,5},{8,10},{10,8},{9,1... | collective-permute-start | bytes 12582920 | tf_op jit(solution)/shard_map/ppermute | solution.py:549
  12.0 10.9 %collective-permute-start.5 = (bf16[64,1024]{1,0:T(8,128)(2,1)S(1)}, bf16[64,1024]{1,0:T(8,128)(2,1)S(1)}, u32[]{:S(2)}, u32[]{:S(2)}) collective-permute-start(bf16[64,1024]{1,0:T(8,128)(2,1)S(1)} %broadcast_select_fusion.6), channel_id=1, source_target_pairs={{0,1},{1,0},{2,3},{3,2},{4,5},{5,4},{6,7},{7,6},{8,9},{9,8},{10,11... | collective-permute-start | bytes 393224 | tf_op jit(solution)/shard_map/ppermute | solution.py:543
  14.7 10.1 %collective-permute-start.1 = (bf16[64,1024]{1,0:T(8,128)(2,1)S(1)}, bf16[64,1024]{1,0:T(8,128)(2,1)S(1)}, u32[]{:S(2)}, u32[]{:S(2)}) collective-permute-start(bf16[64,1024]{1,0:T(8,128)(2,1)S(1)} %get-tuple-element.39), channel_id=1, source_target_pairs={{0,8},{8,16},{16,24},{1,9},{9,17},{17,25},{2,10},{10,18},{18,26},{... | collective-permute-start | bytes 393224 | tf_op jit(solution)/shard_map/ppermute | solution.py:547
  17.9 6.9 %collective-permute-start.2 = (bf16[64,1024]{1,0:T(8,128)(2,1)S(1)}, bf16[64,1024]{1,0:T(8,128)(2,1)S(1)}, u32[]{:S(2)}, u32[]{:S(2)}) collective-permute-start(bf16[64,1024]{1,0:T(8,128)(2,1)S(1)} %get-tuple-element.40), channel_id=1, source_target_pairs={{8,0},{16,8},{24,16},{9,1},{17,9},{25,17},{10,2},{18,10},{26,18},{... | collective-permute-start | bytes 393224 | tf_op jit(solution)/shard_map/ppermute | solution.py:548
  19.2 5.6 %collective-permute-start.3 = (bf16[64,1024]{1,0:T(8,128)(2,1)S(1)}, bf16[64,1024]{1,0:T(8,128)(2,1)S(1)}, u32[]{:S(2)}, u32[]{:S(2)}) collective-permute-start(bf16[64,1024]{1,0:T(8,128)(2,1)S(1)} %get-tuple-element.41), channel_id=1, source_target_pairs={{0,2},{2,4},{4,6},{1,3},{3,5},{5,7},{8,10},{10,12},{12,14},{9,11},... | collective-permute-start | bytes 393224 | tf_op jit(solution)/shard_map/ppermute | solution.py:547
  22.8 6.3 %collective-permute-start.4 = (bf16[64,1024]{1,0:T(8,128)(2,1)S(1)}, bf16[64,1024]{1,0:T(8,128)(2,1)S(1)}, u32[]{:S(2)}, u32[]{:S(2)}) collective-permute-start(bf16[64,1024]{1,0:T(8,128)(2,1)S(1)} %get-tuple-element.42), channel_id=1, source_target_pairs={{2,0},{4,2},{6,4},{3,1},{5,3},{7,5},{10,8},{12,10},{14,12},{11,9},... | collective-permute-start | bytes 393224 | tf_op jit(solution)/shard_map/ppermute | solution.py:548
  29.1 1.0 copy-start.18
  30.1 0.9 copy-start.20
  33.6 1.2 copy-start.11
  34.8 1.7 collective-permute-start.9
  52.8 13.0 %all-to-all-start.1 = ((f32[16,40,128]{2,1,0:T(8,128)}), f32[16,40,128]{2,1,0:T(8,128)S(1)}, u32[]{:S(2)}, u32[]{:S(2)}) async-start(f32[16,40,128]{2,1,0:T(8,128)} %broadcast_in_dim.34), calls=%async_computation.1 | async-start | bytes 655360 | tf_op jit(solution)/shard_map/all_to_all | solution.py:473
  57.2 13.6 %collective-permute-start.6 = (bf16[512,1024]{1,0:T(8,128)(2,1)S(1)}, bf16[512,1024]{1,0:T(8,128)(2,1)S(1)}, u32[]{:S(2)}, u32[]{:S(2)}) collective-permute-start(bf16[512,1024]{1,0:T(8,128)(2,1)S(1)} %get-tuple-element.51.refs_2_), channel_id=1, source_target_pairs={{0,2},{2,0},{1,3},{3,1},{4,6},{6,4},{5,7},{7,5},{8,10},{10,8},{9,1... | collective-permute-start | bytes 3145736 | tf_op jit(solution)/shard_map/ppermute | solution.py:567
  65.8 5.0 %collective-permute-start.10 = (f32[640,128]{1,0:T(8,128)S(1)}, f32[640,128]{1,0:T(8,128)S(1)}, u32[]{:S(2)}, u32[]{:S(2)}) collective-permute-start(f32[640,128]{1,0:T(8,128)S(1)} %bitcast.94), channel_id=1, source_target_pairs={{0,2},{2,0},{1,3},{3,1},{4,6},{6,4},{5,7},{7,5},{8,10},{10,8},{9,1... | collective-permute-start | bytes 983048 | tf_op jit(solution)/shard_map/ppermute | solution.py:474
  75.3 1.0 copy-start.8
  76.3 46.8 %collective-permute-start.7 = (bf16[1024,1024]{1,0:T(8,128)(2,1)S(1)}, bf16[1024,1024]{1,0:T(8,128)(2,1)S(1)}, u32[]{:S(2)}, u32[]{:S(2)}) collective-permute-start(bf16[1024,1024]{1,0:T(8,128)(2,1)S(1)} %shard_map.80), channel_id=1, source_target_pairs={{0,1},{1,0},{2,3},{3,2},{4,5},{5,4},{6,7},{7,6},{8,9},{9,8},{10,11... | collective-permute-start | bytes 6291464 | tf_op jit(solution)/shard_map/ppermute | solution.py:514
  76.5 1.2 copy-start.9
  82.1 28.6 %copy-start.10 = (bf16[512,1024]{1,0:T(8,128)(2,1)S(1)}, bf16[512,1024]{1,0:T(8,128)(2,1)}, u32[]{:S(2)}) copy-start(bf16[512,1024]{1,0:T(8,128)(2,1)} %copy-done.8) | copy-start | bytes 3145732
  82.1 46.6 %collective-permute-start.8 = (bf16[1024,1024]{1,0:T(8,128)(2,1)S(1)}, bf16[1024,1024]{1,0:T(8,128)(2,1)S(1)}, u32[]{:S(2)}, u32[]{:S(2)}) collective-permute-start(bf16[1024,1024]{1,0:T(8,128)(2,1)S(1)} %shard_map.81), channel_id=1, source_target_pairs={{0,4},{4,0},{1,5},{5,1},{2,6},{6,2},{3,7},{7,3},{8,12},{12,8},{9,1... | collective-permute-start | bytes 6291464 | tf_op jit(solution)/shard_map/ppermute | solution.py:514
  109.7 1.0 copy-start.13
  116.4 12.3 %copy-start.12 = (f32[3328,128]{1,0:T(8,128)S(1)}, f32[3328,128]{1,0:T(8,128)}, u32[]{:S(2)}) copy-start(f32[3328,128]{1,0:T(8,128)} %copy-done.11) | copy-start | bytes 5111812
  128.7 3.7 %copy-start.5 = (bf16[1024,1024]{1,0:T(8,128)(2,1)}, bf16[1024,1024]{1,0:T(8,128)(2,1)S(1)}, u32[]{:S(2)}) copy-start(bf16[1024,1024]{1,0:T(8,128)(2,1)S(1)} %collective-permute-done.8.refs_1_.refs_4_) | copy-start | bytes 6291460
  128.8 3.6 %collective-permute-start.11 = (f32[1664,128]{1,0:T(8,128)S(1)}, f32[1664,128]{1,0:T(8,128)S(1)}, u32[]{:S(2)}, u32[]{:S(2)}) collective-permute-start(f32[1664,128]{1,0:T(8,128)S(1)} %dynamic-slice_bitcast_fusion), channel_id=1, source_target_pairs={{0,2},{2,0},{1,3},{3,1},{4,6},{6,4},{5,7},{7,5},{8,10},{10,8},{9,1... | collective-permute-start | bytes 2555912 | tf_op jit(solution)/shard_map/ppermute | solution.py:468
  158.6 22.8 %all-to-all-start.3 = ((f32[16,104,128]{2,1,0:T(8,128)}), f32[16,104,128]{2,1,0:T(8,128)}, u32[]{:S(2)}, u32[]{:S(2)}) async-start(f32[16,104,128]{2,1,0:T(8,128)} %broadcast_in_dim.35), calls=%async_computation.3 | async-start | bytes 1703936 | tf_op jit(solution)/shard_map/all_to_all | solution.py:473
  163.1 2.2 copy-start
  165.3 3.4 %copy-start.2 = (f32[1024,1024]{1,0:T(8,128)S(1)}, f32[1024,1024]{1,0:T(8,128)}, u32[]{:S(2)}) copy-start(f32[1024,1024]{1,0:T(8,128)} %shard_map.83.refs_0_.refs_3_) | copy-start | bytes 12582916
  165.3 3.4 %copy-start.6 = (bf16[1024,1024]{1,0:T(8,128)(2,1)S(1)}, bf16[1024,1024]{1,0:T(8,128)(2,1)}, u32[]{:S(2)}) copy-start(bf16[1024,1024]{1,0:T(8,128)(2,1)} %copy-done.5) | copy-start | bytes 6291460
  167.4 29.4 %collective-permute-start.13 = (bf16[512,1024]{1,0:T(8,128)(2,1)}, bf16[512,1024]{1,0:T(8,128)(2,1)S(1)}, u32[]{:S(2)}, u32[]{:S(2)}) collective-permute-start(bf16[512,1024]{1,0:T(8,128)(2,1)} %shard_map.85), channel_id=1, source_target_pairs={{0,4},{4,0},{1,5},{5,1},{2,6},{6,2},{3,7},{7,3},{8,12},{12,8},{9,1... | collective-permute-start | bytes 3145736 | tf_op jit(solution)/shard_map/ppermute | solution.py:514
  170.9 29.7 %collective-permute-start.14 = (bf16[512,1024]{1,0:T(8,128)(2,1)}, bf16[512,1024]{1,0:T(8,128)(2,1)}, u32[]{:S(2)}, u32[]{:S(2)}) collective-permute-start(bf16[512,1024]{1,0:T(8,128)(2,1)} %shard_map.86), channel_id=1, source_target_pairs={{0,1},{1,0},{2,3},{3,2},{4,5},{5,4},{6,7},{7,6},{8,9},{9,8},{10,11... | collective-permute-start | bytes 3145736 | tf_op jit(solution)/shard_map/ppermute | solution.py:514
  181.4 48.8 %collective-permute-start.12 = (f32[1664,128]{1,0:T(8,128)}, f32[1664,128]{1,0:T(8,128)}, u32[]{:S(2)}, u32[]{:S(2)}) collective-permute-start(f32[1664,128]{1,0:T(8,128)} %bitcast.30), channel_id=1, source_target_pairs={{0,2},{2,0},{1,3},{3,1},{4,6},{6,4},{5,7},{7,5},{8,10},{10,8},{9,1... | collective-permute-start | bytes 2555912 | tf_op jit(solution)/shard_map/ppermute | solution.py:474
  200.5 2.2 copy-start.1
  202.7 2.2 copy-start.3
  204.9 1.6 copy-start.7
  208.2 54.3 %collective-permute-start.15 = (bf16[256,1024]{1,0:T(8,128)(2,1)S(1)}, bf16[256,1024]{1,0:T(8,128)(2,1)S(1)}, u32[]{:S(2)}, u32[]{:S(2)}) collective-permute-start(bf16[256,1024]{1,0:T(8,128)(2,1)S(1)} %shard_map.87), channel_id=1, source_target_pairs={{2,16},{6,20},{8,2},{10,18},{12,6},{14,22},{16,8},{18,24},{20,12},... | collective-permute-start | bytes 1572872 | tf_op jit(solution)/shard_map/ppermute | solution.py:632
  216.0 46.6 %collective-permute-start.16 = (bf16[256,1024]{1,0:T(8,128)(2,1)S(1)}, bf16[256,1024]{1,0:T(8,128)(2,1)S(1)}, u32[]{:S(2)}, u32[]{:S(2)}) collective-permute-start(bf16[256,1024]{1,0:T(8,128)(2,1)S(1)} %shard_map.88), channel_id=1, source_target_pairs={{2,18},{6,22},{10,24},{14,28},{16,10},{18,26},{20,14},{22,30},{24,... | collective-permute-start | bytes 1572872 | tf_op jit(solution)/shard_map/ppermute | solution.py:632
  219.5 43.0 %collective-permute-start.17 = (bf16[256,1024]{1,0:T(8,128)(2,1)S(1)}, bf16[256,1024]{1,0:T(8,128)(2,1)S(1)}, u32[]{:S(2)}, u32[]{:S(2)}) collective-permute-start(bf16[256,1024]{1,0:T(8,128)(2,1)S(1)} %shard_map.89), channel_id=1, source_target_pairs={{0,8},{2,24},{4,12},{6,28},{10,26},{14,30},{16,0},{20,4},{24,2},{2... | collective-permute-start | bytes 1572872 | tf_op jit(solution)/shard_map/ppermute | solution.py:632
  223.1 39.4 %collective-permute-start.18 = (bf16[256,1024]{1,0:T(8,128)(2,1)S(1)}, bf16[256,1024]{1,0:T(8,128)(2,1)S(1)}, u32[]{:S(2)}, u32[]{:S(2)}) collective-permute-start(bf16[256,1024]{1,0:T(8,128)(2,1)S(1)} %shard_map.90), channel_id=1, source_target_pairs={{0,10},{2,26},{4,14},{6,30},{8,0},{10,16},{12,4},{14,20},{16,2},{2... | collective-permute-start | bytes 1572872 | tf_op jit(solution)/shard_map/ppermute | solution.py:632
  230.2 32.4 %collective-permute-start.19 = (f32[256,1024]{1,0:T(8,128)S(1)}, f32[256,1024]{1,0:T(8,128)S(1)}, u32[]{:S(2)}, u32[]{:S(2)}) collective-permute-start(f32[256,1024]{1,0:T(8,128)S(1)} %shard_map.92), channel_id=1, source_target_pairs={{0,2},{2,0},{1,3},{3,1},{4,6},{6,4},{5,7},{7,5},{8,10},{10,8},{9,1... | collective-permute-start | bytes 3145736 | tf_op jit(solution)/shard_map/ppermute | solution.py:635
  232.5 1.2 copy-start.14
  263.9 1.0 copy-start.15
  264.9 17.9 %all-to-all-start.4 = ((f32[4,256,256]{2,1,0:T(8,128)}), f32[4,256,256]{2,1,0:T(8,128)}, u32[]{:S(2)}, u32[]{:S(2)}) async-start(f32[4,256,256]{2,1,0:T(8,128)} %get-tuple-element.68), calls=%async_computation.4 | async-start | bytes 2097152 | tf_op jit(solution)/shard_map/all_to_all | solution.py:649
  269.2 1.2 copy-start.16
  282.8 18.0 %all-to-all-start.5 = ((f32[4,256,256]{2,1,0:T(8,128)}), f32[4,256,256]{2,1,0:T(8,128)S(1)}, u32[]{:S(2)}, u32[]{:S(2)}) async-start(f32[4,256,256]{2,1,0:T(8,128)} %shard_map.95), calls=%async_computation.5 | async-start | bytes 2097152 | tf_op jit(solution)/shard_map/all_to_all | solution.py:649
  (2 other events, 1.4 us)

commit v2 on v1

--- a/solution.py
+++ b/solution.py
@@ -116,9 +116,10 @@
 
 
 def next_panel_kernel(packed_ref, w0_ref, f_ref, w_ref, d_ref):
-    unpack_symmetric(packed_ref, w_ref)
     nb = w0_ref.shape[0]
-    start = packed_ref.shape[0] - nb // LEAF * nb
+    blocks = nb // LEAF
+    unpack_symmetric(packed_ref, w_ref, blocks * (blocks + 1) // 2)
+    start = packed_ref.shape[0] - blocks * nb
     below = jnp.concatenate(
         [packed_ref[start + i * nb : start + (i + 1) * nb, :] for i in range(nb // LEAF)], 1
     )
@@ -128,18 +129,19 @@
     factor_inverse(w_ref, d_ref)
 
 
-def factor_kernel(first_ref, rows_ref, w0_ref, f_ref, w1_ref, out_ref):
+def factor_kernel(first_ref, rows_ref, w0_ref, f_ref, w1_ref, *refs):
+    blocks, all_ref = refs[:-1], refs[-1]
     nb = w0_ref.shape[0]
     ids = first_ref[0] + lax.broadcasted_iota(jnp.int32, (rows_ref.shape[0], nb), 0)
     cols = lax.broadcasted_iota(jnp.int32, (rows_ref.shape[0], nb), 1)
     part = dot3(rows_ref[:, :nb], w0_ref[...], ((1,), (1,)))
     rest = rows_ref[:, nb:] - dot3(part, f_ref[...], ((1,), (1,)))
     rest = dot3(rest, w1_ref[...], ((1,), (1,)))
-    width = out_ref.shape[2]
-    for at, value in ((0, part), (nb, rest)):
-        value = jnp.where(cols + at <= ids, value, 0.0)
-        for i in range(nb // width):
-            out_ref[at // width + i] = value[:, i * width : (i + 1) * width]
+    all_ref[:, :nb] = jnp.where(cols <= ids, part, 0.0)
+    all_ref[:, nb:] = jnp.where(cols + nb <= ids, rest, 0.0)
+    for d, block in enumerate(blocks):
+        width = block.shape[1]
+        block[...] = all_ref[:, pl.ds(pl.multiple_of(first_ref[1 + d] * width, width), width)]
 
 
 def panel_call(kernel, outputs, nb, *operands):
@@ -151,7 +153,7 @@
         scratch_shapes=[pltpu.VMEM((LEAF, LEAF), jnp.float32)],
         compiler_params=pltpu.CompilerParams(vmem_limit_bytes=24 * 2**20),
         cost_estimate=pl.CostEstimate(
-            flops=24 * nb**3 * 8, transcendentals=0, bytes_accessed=8 * nb * nb
+            flops=24 * nb**3 * 4, transcendentals=0, bytes_accessed=8 * nb * nb
         ),
     )(*operands)
 
@@ -366,7 +368,7 @@
             out_specs=pl.BlockSpec((step, cols), lambda t, idx: (t, 0)),
         ),
         out_shape=jax.ShapeDtypeStruct((total, cols), dtype),
-        compiler_params=pltpu.CompilerParams(vmem_limit_bytes=48 * 2**20),
+        compiler_params=pltpu.CompilerParams(vmem_limit_bytes=56 * 2**20),
         cost_estimate=pl.CostEstimate(
             flops=2 * total * cols * rows * len(bases),
             transcendentals=0,
@@ -403,7 +405,7 @@
             out_specs=pl.BlockSpec((step, cols), lambda t, idx: (t, 0)),
         ),
         out_shape=jax.ShapeDtypeStruct((steps * step, cols), dtype),
-        compiler_params=pltpu.CompilerParams(vmem_limit_bytes=24 * 2**20),
+        compiler_params=pltpu.CompilerParams(vmem_limit_bytes=56 * 2**20),
         cost_estimate=pl.CostEstimate(
             flops=steps * step * cols,
             transcendentals=0,
@@ -448,7 +450,7 @@
             out_specs=pl.BlockSpec((step, cols), lambda t, idx: (t, 0)),
         ),
         out_shape=jax.ShapeDtypeStruct((height, cols), dtype),
-        compiler_params=pltpu.CompilerParams(vmem_limit_bytes=24 * 2**20),
+        compiler_params=pltpu.CompilerParams(vmem_limit_bytes=56 * 2**20),
         cost_estimate=pl.CostEstimate(
             flops=height * cols, transcendentals=0, bytes_accessed=height * cols * 18
         ),
@@ -459,32 +461,29 @@
     return [(0, 1), (1, 0)]
 
 
-def sum_everywhere(rows, core, axes, devices):
-    half = rows.shape[0] // 2
-    share = half // devices
-    both = rows.reshape(2, half, LEAF)
-    kept = lax.dynamic_index_in_dim(both, core, 0, keepdims=False)
-    sent = lax.dynamic_index_in_dim(both, 1 - core, 0, keepdims=False)
-    mine = kept + lax.ppermute(sent, "core", swap_pairs())
-    terms = lax.all_to_all(
-        mine.reshape(devices, share, LEAF), axes, split_axis=0, concat_axis=0, tiled=True
-    )
-    own = jnp.broadcast_to(jnp.sum(terms, axis=0), (devices, share, LEAF))
-    own = lax.all_to_all(own, axes, split_axis=0, concat_axis=0, tiled=True).reshape(half, LEAF)
-    other = lax.ppermute(own, "core", swap_pairs())
+def other_half(half, core):
+    other = lax.ppermute(half, "core", swap_pairs())
     first = core == 0
-    return jnp.concatenate([jnp.where(first, own, other), jnp.where(first, other, own)], 0)
+    return jnp.concatenate([jnp.where(first, half, other), jnp.where(first, other, half)], 0)
+
+
+def join_kernel(place_ref, *refs):
+    out = refs[-1]
+    part = refs[0].shape[0]
+    for d, block in enumerate(refs[:-1]):
+        out[pl.ds(pl.multiple_of(place_ref[d] * part, part), part), :] = block[...]
 
 
 def sums_kernel(home_ref, own_ref, swapped_ref, *refs):
-    ins, (rows_ref, blocks_ref) = refs[:-2], refs[-2:]
+    cols, width = own_ref.shape[1], refs[-1].shape[1]
+    ins, rows_ref, blocks = refs[: -1 - cols // width], refs[-1 - cols // width], refs[-(cols // width) :]
     total = jnp.where(home_ref[0] != 0, own_ref[...], swapped_ref[...])
     for got in ins:
         total = total + got[...].astype(jnp.float32)
     rows_ref[...] = total
-    width = blocks_ref.shape[2]
-    for i in range(blocks_ref.shape[0]):
-        blocks_ref[i] = total[:, i * width : (i + 1) * width]
+    for d, block in enumerate(blocks):
+        at = pl.multiple_of(home_ref[1 + d] * width, width)
+        block[...] = rows_ref[:, pl.ds(at, width)]
 
 
 def local(basis, classes, cond_table, ground_table, port_cells, port_load):
@@ -507,13 +506,12 @@
     wide = width_k // (devices_x * devices_z)
     narrow = wide // chips_y
     part = narrow // 2
-    (given,) = take_pieces(flat_basis, [([1 - core], width_k // 2)])
 
     def move(array, axis, d):
         size = lax.axis_size(axis)
         return lax.ppermute(array, axis, [(i, (i + d) % size) for i in range(size)])
 
-    panel = flat_basis[:, :cols]
+    panel_spec = pl.BlockSpec((count, cols), lambda i: (0, 0))
     global_x = at_x * cells_x + jnp.arange(cells_x, dtype=jnp.int32)
     global_y = at_y * cells_y + jnp.arange(cells_y, dtype=jnp.int32)
     global_z = at_z * cells_z + jnp.arange(cells_z, dtype=jnp.int32)
@@ -528,11 +526,14 @@
         functools.partial(faces_kernel, sides=sides),
         out_shape=[jax.ShapeDtypeStruct((n, cols), bf16) for n in face_rows]
         + [jax.ShapeDtypeStruct((count, LEAF), f32)] * 2,
-        in_specs=[whole(pltpu.SMEM)] * 2 + [whole()] * 4,
+        grid=(1,),
+        in_specs=[whole(pltpu.SMEM)] * 2 + [whole()] * 3 + [panel_spec],
         out_specs=[whole()] * 8,
         scratch_shapes=[pltpu.VMEM((cols // LEAF, count, LEAF), f32)],
         compiler_params=pltpu.CompilerParams(vmem_limit_bytes=24 * 2**20),
-    )(cond_table, ground_table, info, port_cells[None, :], port_load[None, :], panel)
+    )(cond_table, ground_table, info, port_cells[None, :], port_load[None, :], flat_basis)
+    faces, other_core = lax.optimization_barrier((faces, 1 - core))
+    (given,) = take_pieces(flat_basis, [([other_core], width_k // 2)])
     halos = []
     for i, (axis, size) in enumerate(
         (("gx", devices_x), (("gy", "core"), devices_y), ("gz", devices_z))
@@ -558,18 +559,20 @@
             jax.ShapeDtypeStruct((lower_rows, LEAF), f32),
             jax.ShapeDtypeStruct((lower_rows + blocks * NB, LEAF), f32),
         ],
-        in_specs=[whole()] * 9,
+        grid=(1,),
+        in_specs=[panel_spec] + [whole()] * 8,
         out_specs=[whole()] * 3,
         scratch_shapes=[pltpu.VMEM((count, LEAF), f32), pltpu.VMEM((NB, NB), f32)],
         compiler_params=pltpu.CompilerParams(vmem_limit_bytes=32 * 2**20),
-    )(panel, conduct, grounds, *halos)
+    )(flat_basis, conduct, grounds, *halos)
 
     other_image = lax.ppermute(image, "core", swap_pairs())
 
     axes = ("gx", "gy", "gz")
-    chips = devices_x * chips_y * devices_z
-    first_rows = sum_everywhere(first_rows, core, axes, chips)
-    inverse_0 = first_panel(first_rows, NB)
+    both = jnp.concatenate([first_rows, later_rows], 0).reshape(2, -1, LEAF)
+    kept = lax.dynamic_index_in_dim(both, core, 0, keepdims=False)
+    sent = lax.dynamic_index_in_dim(both, 1 - core, 0, keepdims=False)
+    lead_half = lax.psum(kept + lax.ppermute(sent, "core", swap_pairs()), axes)
 
     shift = core * spans * devices_z * chips_y
 
@@ -592,21 +595,25 @@
     got_a = [move(products_a(d, bf16), "gz", d) for d in range(1, devices_z)]
     got_b = [move(products_b(d, bf16), "gy", d) for d in range(1, chips_y)]
     own_a, own_b = products_a(0, f32), products_b(0, f32)
-    (got_a, got_b, own_a, own_b, later_rows), inverse_0 = lax.optimization_barrier(
-        ((got_a, got_b, own_a, own_b, later_rows), inverse_0)
-    )
-    later_rows = sum_everywhere(later_rows, core, axes, chips)
     sums_a, sums_b = [own_a, *got_a], [own_b, *got_b]
 
-    def further(arrays, axis, mine, size, groups):
-        got = []
+    def further(arrays, mine, size, groups):
+        sent = []
         for d in range(1, size):
             blocks = [zz * size + (mine + d) % size for zz in range(groups)]
-            got.append(move(add_blocks(arrays, [blocks] * len(arrays), narrow, bf16), axis, d))
-        return got
-
-    further_a = further(sums_a, "gy", chip, chips_y, split)
-    further_b = further(sums_b, "gz", at_z, devices_z, spans - split)
+            sent.append(add_blocks(arrays, [blocks] * len(arrays), narrow, bf16))
+        return sent
+
+    further_a = further(sums_a, chip, chips_y, split)
+    further_b = further(sums_b, at_z, devices_z, spans - split)
+    lead_half, _ = lax.optimization_barrier((lead_half, (further_a, further_b)))
+    further_a = [move(a, "gy", d) for d, a in enumerate(further_a, 1)]
+    further_b = [move(a, "gz", d) for d, a in enumerate(further_b, 1)]
+    lead_rows = other_half(lead_half, core)
+    inverse_0 = first_panel(lead_rows, NB)
+    (further_a, further_b), inverse_0 = lax.optimization_barrier(
+        ((further_a, further_b), inverse_0)
+    )
 
     def plane_block(zz, c, dtype):
         in_b = zz >= split
@@ -633,21 +640,35 @@
     home = at_x // spans == core
     own = plane_block(at_x % spans, core, f32)
     swapped = lax.ppermute(plane_block(at_x % spans, 1 - core, f32), "core", swap_pairs())
-    later_rows, x_sent, own = lax.optimization_barrier((later_rows, x_sent, own))
-    factor_10, inverse_1 = next_panel(later_rows, inverse_0)
+    lead_rows, _ = lax.optimization_barrier((lead_rows, (x_sent, own)))
+    factor_10, inverse_1 = next_panel(lead_rows, inverse_0)
     (x_got, swapped), inverse_1 = lax.optimization_barrier(((x_got, swapped), inverse_1))
-    by_blocks = jax.ShapeDtypeStruct((devices_y, part, cols // devices_y), f32)
-    rows, reduced = pl.pallas_call(
+    by_blocks = [jax.ShapeDtypeStruct((part, cols // devices_y), f32)] * devices_y
+    order = jnp.stack([(at_y + d) % devices_y for d in range(devices_y)])
+    home = jnp.concatenate([home.astype(jnp.int32)[None], order])
+    rows, *reduced = pl.pallas_call(
         sums_kernel,
-        out_shape=[jax.ShapeDtypeStruct((part, cols), f32), by_blocks],
+        out_shape=[jax.ShapeDtypeStruct((part, cols), f32), *by_blocks],
         in_specs=[whole(pltpu.SMEM)] + [whole()] * (devices_x + 2),
-        out_specs=[whole()] * 2,
+        out_specs=[whole()] * (1 + devices_y),
         compiler_params=pltpu.CompilerParams(vmem_limit_bytes=32 * 2**20),
-    )(home.astype(jnp.int32)[None], own, swapped, *x_got)
-
-    def to_columns(array):
-        array = lax.all_to_all(array, ("gy", "core"), split_axis=0, concat_axis=0, tiled=True)
-        return array.reshape(devices_y * part, cols // devices_y)
+    )(home, own, swapped, *x_got)
+
+    block = jax.ShapeDtypeStruct((devices_y * part, cols // devices_y), f32)
+    places = jnp.stack([(at_y - d) % devices_y for d in range(devices_y)])
+
+    def to_columns(blocks):
+        got = [blocks[0]]
+        for d in range(1, devices_y):
+            pairs = [(i, (i + d) % devices_y) for i in range(devices_y)]
+            got.append(lax.ppermute(blocks[d], ("gy", "core"), pairs))
+        return pl.pallas_call(
+            join_kernel,
+            out_shape=block,
+            in_specs=[whole(pltpu.SMEM)] + [whole()] * devices_y,
+            out_specs=whole(),
+            compiler_params=pltpu.CompilerParams(vmem_limit_bytes=24 * 2**20),
+        )(places, *got)
 
     reduced = to_columns(reduced)
     first_row = ((at_x * devices_z + at_z) * devices_y + at_y) * part
@@ -655,9 +676,10 @@
         factor_kernel,
         out_shape=by_blocks,
         in_specs=[whole(pltpu.SMEM)] + [whole()] * 4,
-        out_specs=whole(),
+        out_specs=[whole()] * devices_y,
+        scratch_shapes=[pltpu.VMEM((part, cols), f32)],
         compiler_params=pltpu.CompilerParams(vmem_limit_bytes=32 * 2**20),
-    )(first_row[None], rows, inverse_0, factor_10, inverse_1)
+    )(jnp.concatenate([first_row[None], order]), rows, inverse_0, factor_10, inverse_1)
     return (reduced, to_columns(factor))
 
 

time: 306 us -> 323 us (1.056)
  waiting for transfers between devices: 69.9 us -> 115 us
  blocking collectives: 40.5 us -> 0 us
  Pallas kernels: 102 us -> 127 us
  starting transfers between devices: 58 us -> 34.5 us
  between operations: 1.21 us -> 14.5 us
  local copies, waits for them, and re-layouts: 29.7 us -> 23.3 us
  other arithmetic: 2.29 us -> 7.24 us
    psum x0 -> x1, waiting for transfers between devices: none -> 65.8 us  [local(): lead_half = lax.psum(kept + lax.ppermute(sent, 'core', swap_pairs()), axes)]
    all_to_all x2 -> x0, blocking collectives: 40.5 us -> none  [sum_everywhere(): lax.all_to_all(mine.reshape(devices, share, LEAF), axes, split_axis=0, co...]
    all_to_all x4 -> x0, waiting for transfers between devices: 39.7 us -> none  [the longest x2 23.4 us: to_columns(): lax.all_to_all(array, ('gy', 'core'), split_axis=0, concat_axis=0, tiled=...]
    all_to_all x4 -> x0, starting transfers between devices: 17.4 us -> none  [the longest x2 8.76 us: sum_everywhere(): lax.all_to_all(own, axes, split_axis=0, concat_axis=0, tiled=True)]
    ppermute x4 -> x8, waiting for transfers between devices: 4.73 us -> 17.4 us  [the longest x6 17.4 us: to_columns(): got.append(lax.ppermute(blocks[d], ('gy', 'core'), pairs))]
    pallas_call x6, Pallas kernels: 10.3 us -> 22 us  [pick_block(): pl.pallas_call(pick_kernel, grid_spec=pltpu.PrefetchScalarGridSpec(num_sc...]
    unnamed x54 -> x28, local copies, waits for them, and re-layouts: 25.6 us -> 16.8 us
    ppermute x4, waiting for transfers between devices: 21.8 us -> 27.4 us  [move(): return lax.ppermute(array, axis, [(i, (i + d) % size) for i in range(size)])]
  transfers between devices with their start and end apart: 24 -> 25, of which waited for: 12 -> 10; matrix products, arithmetic and copies ran while one was open for 2% -> 4% of each run, Pallas kernels for 31% -> 35%
where the time goes in v2:
time: 323 us; the launch traced here: 322 us
  Pallas kernels  127 us (39%)
  waiting for transfers between devices  115 us (36%)
  starting transfers between devices  34.5 us (11%)
  local copies, waits for them, and re-layouts  23.3 us (7%)
  between operations  14.5 us (4%)
  other arithmetic  7.24 us (2%)
    psum x1, waiting for transfers between devices, local(): lead_half = lax.psum(kept + lax.ppermute(sent, 'core', swap_pairs()), axes)  65.8 us
    pallas_call x2, Pallas kernels, panel_call(): pl.pallas_call(kernel, out_shape=[jax.ShapeDtypeStruct((nb, nb), jnp.floa...  55.8 us
    ppermute x4, waiting for transfers between devices, move(): return lax.ppermute(array, axis, [(i, (i + d) % size) for i in range(size)])  27.4 us
    pallas_call x4, Pallas kernels, products(): pl.pallas_call(products_kernel, grid_spec=pltpu.PrefetchScalarGridSpec(nu...  25.3 us
    pallas_call x6, Pallas kernels, pick_block(): pl.pallas_call(pick_kernel, grid_spec=pltpu.PrefetchScalarGridSpec(num_sc...  22 us
    ppermute x6, waiting for transfers between devices, to_columns(): got.append(lax.ppermute(blocks[d], ('gy', 'core'), pairs))  17.4 us
    unnamed x28, local copies, waits for them, and re-layouts  16.8 us
    ppermute x4, starting transfers between devices, local(): x_got.append(lax.ppermute(x_sent[-1], ('gx', 'gy', 'core'), pairs))  11.7 us
  transfers between devices with their start and end apart: 25, of which 10 were waited for; matrix products, arithmetic and copies ran while one was open for 4% of the time, Pallas kernels for 35%

profile of v2, /device:TPU:1, one launch (start us, length us, event | category | flops | bytes accessed | tf_op | source)
XLA Modules:
  0.0 321.6 jit_solution(11414374675803465875)
XLA Ops:
  8.5 3.4 %copy-done = bf16[8,8,8,8192]{3,2,1,0:T(8,128)(2,1)S(1)} copy-done((bf16[8,8,8,8192]{3,2,1,0:T(8,128)(2,1)S(1)}, bf16[8,8,8,8192]{3,2,1,0:T(8,128)(2,1)}, u32[]{:S(2)}) %copy-start) | copy-done | bytes 8388632
  14.6 2.4 shard_map.77
  18.0 2.7 shard_map.78
  20.8 2.7 collective-permute-start.5
  23.5 3.2 collective-permute-start.1
  26.7 1.3 collective-permute-start.2
  28.0 3.6 %collective-permute-start.3 = (bf16[64,1024]{1,0:T(8,128)(2,1)S(1)}, bf16[64,1024]{1,0:T(8,128)(2,1)S(1)}, u32[]{:S(2)}, u32[]{:S(2)}) collective-permute-start(bf16[64,1024]{1,0:T(8,128)(2,1)S(1)} %get-tuple-element.59), channel_id=1, source_target_pairs={{0,2},{2,4},{4,6},{1,3},{3,5},{5,7},{8,10},{10,12},{12,14},{9,11},... | collective-permute-start | bytes 393224 | tf_op jit(solution)/shard_map/ppermute | solution.py:548
  31.6 1.9 collective-permute-start.4
  33.6 4.3 %collective-permute-done.4.refs_3_ = bf16[64,1024]{1,0:T(8,128)(2,1)S(1)} collective-permute-done((bf16[64,1024]{1,0:T(8,128)(2,1)S(1)}, bf16[64,1024]{1,0:T(8,128)(2,1)S(1)}, u32[]{:S(2)}, u32[]{:S(2)}) %collective-permute-start.4) | collective-permute-done | bytes 131104 | tf_op jit(solution)/shard_map/ppermute | solution.py:549
  37.9 3.4 %copy-done.2 = bf16[8,8,8,8192]{3,2,1,0:T(8,128)(2,1)S(1)} copy-done((bf16[8,8,8,8192]{3,2,1,0:T(8,128)(2,1)S(1)}, bf16[8,8,8,8192]{3,2,1,0:T(8,128)(2,1)}, u32[]{:S(2)}) %copy-start.2) | copy-done | bytes 8388632
  41.3 2.7 shard_map.79
  45.0 1.4 copy-done.13
  48.8 6.1 %shard_map.84 = bf16[1024,1024]{1,0:T(8,128)(2,1)} custom-call(s32[4]{0:T(128)} %pad_add_fusion.5.index_ref, bf16[512,8192]{1,0:T(8,128)(2,1)} %bitcast.71, bf16[512,4096]{1,0:T(8,128)(2,1)} %collective-permute-done.refs_1_, bf16[512,1024]{1,0:T(8,128)(2,1)} %copy-done.3, bf16[512,1024]{1,0:T(8,128)(2,1)} %copy-done.12), custom_call_target="tpu_custom_call" | custom-call | flops 2147483648 | bytes 8388608 | tf_op jit(solution)/shard_map/pallas_call | solution.py:362
  54.9 6.1 %shard_map.81 = bf16[1024,1024]{1,0:T(8,128)(2,1)} custom-call(s32[4]{0:T(128)} %pad_add_fusion.3.index_ref, bf16[512,8192]{1,0:T(8,128)(2,1)} %bitcast.72, bf16[512,4096]{1,0:T(8,128)(2,1)} %collective-permute-done.refs_1_, bf16[512,1024]{1,0:T(8,128)(2,1)} %copy-done.3, bf16[512,1024]{1,0:T(8,128)(2,1)} %copy-done.12), custom_call_target="tpu_custom_call" | custom-call | flops 2147483648 | bytes 8388608 | tf_op jit(solution)/shard_map/pallas_call | solution.py:362
  61.3 2.8 bitcast_add_fusion
  66.7 6.5 %shard_map.83.refs_0_.refs_3_ = f32[1024,1024]{1,0:T(8,128)} custom-call(s32[4]{0:T(128)} %pad_add_fusion.4.index_ref, bf16[512,8192]{1,0:T(8,128)(2,1)} %bitcast.73, bf16[512,4096]{1,0:T(8,128)(2,1)} %collective-permute-done.refs_1_, bf16[512,1024]{1,0:T(8,128)(2,1)} %copy-done.3, bf16[512,1024]{1,0:T(8,128)(2,1)} %copy-done.12), custom_call_target="tpu_custom_call" | custom-call | flops 2147483648 | bytes 8388608 | tf_op jit(solution)/shard_map/pallas_call | solution.py:362
  73.2 6.6 %shard_map.80.refs_0_ = f32[1024,1024]{1,0:T(8,128)} custom-call(s32[4]{0:T(128)} %pad_add_fusion.2.index_ref, bf16[512,8192]{1,0:T(8,128)(2,1)} %bitcast.74, bf16[512,4096]{1,0:T(8,128)(2,1)} %collective-permute-done.refs_1_, bf16[512,1024]{1,0:T(8,128)(2,1)} %copy-done.3, bf16[512,1024]{1,0:T(8,128)(2,1)} %copy-done.12), custom_call_target="tpu_custom_call" | custom-call | flops 2147483648 | bytes 8388608 | tf_op jit(solution)/shard_map/pallas_call | solution.py:362
  79.7 27.0 %collective-permute-done.9.refs_1_.refs_4_ = bf16[1024,1024]{1,0:T(8,128)(2,1)S(1)} collective-permute-done((bf16[1024,1024]{1,0:T(8,128)(2,1)}, bf16[1024,1024]{1,0:T(8,128)(2,1)S(1)}, u32[]{:S(2)}, u32[]{:S(2)}) %collective-permute-start.9) | collective-permute-done | bytes 2097184 | tf_op jit(solution)/shard_map/ppermute | solution.py:512
  106.8 1.3 copy-done.9
  108.1 4.4 %shard_map.85 = bf16[512,1024]{1,0:T(8,128)(2,1)} custom-call(s32[8]{0:T(128)} %stack.304.index_ref, f32[1024,1024]{1,0:T(8,128)} %shard_map.83.refs_0_.refs_3_, bf16[1024,1024]{1,0:T(8,128)(2,1)} %copy-done.9), custom_call_target="tpu_custom_call" | custom-call | flops 524288 | bytes 4194304 | tf_op jit(solution)/shard_map/pallas_call | solution.py:396
  112.9 4.5 %shard_map.82 = bf16[512,1024]{1,0:T(8,128)(2,1)} custom-call(s32[8]{0:T(128)} %stack.299.index_ref, f32[1024,1024]{1,0:T(8,128)} %shard_map.80.refs_0_, bf16[1024,1024]{1,0:T(8,128)(2,1)} %collective-permute-done.7.refs_1_), custom_call_target="tpu_custom_call" | custom-call | flops 524288 | bytes 4194304 | tf_op jit(solution)/shard_map/pallas_call | solution.py:396
  117.3 65.8 %all-reduce.2.cloned.1.call-done = f32[2304,128]{1,0:T(8,128)} async-done(((f32[2304,128]{1,0:T(8,128)}), f32[2304,128]{1,0:T(8,128)}) %all-reduce.2.cloned.1.call-update) | async-done | bytes 1179664 | tf_op jit(solution)/shard_map/psum | solution.py:575
  183.1 1.6 collective-permute-start.12
  188.8 1.2 collective-permute-start.10
  190.5 1.4 broadcast_select_fusion.1
  192.1 27.0 %shard_map.86.w0_ref = f32[512,512]{1,0:T(8,128)S(1)} custom-call(f32[4608,128]{1,0:T(8,128)S(1)} %pad_maximum_fusion.1.packed_ref), custom_call_target="tpu_custom_call" | custom-call | flops 12884901888 | bytes 2097152 | tf_op jit(solution)/shard_map/pallas_call | solution.py:148
  221.0 3.6 %shard_map.91 = bf16[256,1024]{1,0:T(8,128)(2,1)} custom-call(s32[7]{0:T(128)} %stack.342.index_ref, f32[1024,1024]{1,0:T(8,128)} %shard_map.80.refs_0_, bf16[1024,1024]{1,0:T(8,128)(2,1)} %collective-permute-done.7.refs_1_, bf16[512,1024]{1,0:T(8,128)(2,1)} %copy-done.11, f32[1024,1024]{1,0:T(8,128)} %shard_map.83.refs_0_.refs_3_, ...), custom_call_target="tpu_custom_call" | custom-call | flops 262144 | bytes 4718592 | tf_op jit(solution)/shard_map/pallas_call | solution.py:441
  224.7 3.7 %collective-permute-start.16 = (bf16[256,1024]{1,0:T(8,128)(2,1)}, bf16[256,1024]{1,0:T(8,128)(2,1)S(1)}, u32[]{:S(2)}, u32[]{:S(2)}) collective-permute-start(bf16[256,1024]{1,0:T(8,128)(2,1)} %shard_map.91), channel_id=1, source_target_pairs={{0,10},{2,26},{4,14},{6,30},{8,0},{10,16},{12,4},{14,20},{16,2},{2... | collective-permute-start | bytes 1572872 | tf_op jit(solution)/shard_map/ppermute | solution.py:639
  228.3 3.6 %shard_map.90 = bf16[256,1024]{1,0:T(8,128)(2,1)} custom-call(s32[7]{0:T(128)} %stack.335.index_ref, f32[1024,1024]{1,0:T(8,128)} %shard_map.80.refs_0_, bf16[1024,1024]{1,0:T(8,128)(2,1)} %collective-permute-done.7.refs_1_, bf16[512,1024]{1,0:T(8,128)(2,1)} %copy-done.11, f32[1024,1024]{1,0:T(8,128)} %shard_map.83.refs_0_.refs_3_, ...), custom_call_target="tpu_custom_call" | custom-call | flops 262144 | bytes 4718592 | tf_op jit(solution)/shard_map/pallas_call | solution.py:441
  232.0 4.2 %collective-permute-start.15 = (bf16[256,1024]{1,0:T(8,128)(2,1)}, bf16[256,1024]{1,0:T(8,128)(2,1)S(1)}, u32[]{:S(2)}, u32[]{:S(2)}) collective-permute-start(bf16[256,1024]{1,0:T(8,128)(2,1)} %shard_map.90), channel_id=1, source_target_pairs={{0,8},{2,24},{4,12},{6,28},{10,26},{14,30},{16,0},{20,4},{24,2},{2... | collective-permute-start | bytes 1572872 | tf_op jit(solution)/shard_map/ppermute | solution.py:639
  236.2 3.6 %shard_map.89 = bf16[256,1024]{1,0:T(8,128)(2,1)} custom-call(s32[7]{0:T(128)} %stack.328.index_ref, f32[1024,1024]{1,0:T(8,128)} %shard_map.80.refs_0_, bf16[1024,1024]{1,0:T(8,128)(2,1)} %collective-permute-done.7.refs_1_, bf16[512,1024]{1,0:T(8,128)(2,1)} %copy-done.11, f32[1024,1024]{1,0:T(8,128)} %shard_map.83.refs_0_.refs_3_, ...), custom_call_target="tpu_custom_call" | custom-call | flops 262144 | bytes 4718592 | tf_op jit(solution)/shard_map/pallas_call | solution.py:441
  239.8 1.3 collective-permute-start.14
  241.1 3.7 %shard_map.88 = bf16[256,1024]{1,0:T(8,128)(2,1)} custom-call(s32[7]{0:T(128)} %stack.321.index_ref, f32[1024,1024]{1,0:T(8,128)} %shard_map.80.refs_0_, bf16[1024,1024]{1,0:T(8,128)(2,1)} %collective-permute-done.7.refs_1_, bf16[512,1024]{1,0:T(8,128)(2,1)} %copy-done.11, f32[1024,1024]{1,0:T(8,128)} %shard_map.83.refs_0_.refs_3_, ...), custom_call_target="tpu_custom_call" | custom-call | flops 262144 | bytes 4718592 | tf_op jit(solution)/shard_map/pallas_call | solution.py:441
  244.8 2.6 collective-permute-start.13
  247.4 3.7 %shard_map.87.own_ref = f32[256,1024]{1,0:T(8,128)} custom-call(s32[7]{0:T(128)} %stack.281.index_ref, f32[1024,1024]{1,0:T(8,128)} %shard_map.80.refs_0_, bf16[1024,1024]{1,0:T(8,128)(2,1)} %collective-permute-done.7.refs_1_, bf16[512,1024]{1,0:T(8,128)(2,1)} %copy-done.11, f32[1024,1024]{1,0:T(8,128)} %shard_map.83.refs_0_.refs_3_, ...), custom_call_target="tpu_custom_call" | custom-call | flops 262144 | bytes 4718592 | tf_op jit(solution)/shard_map/pallas_call | solution.py:441
  251.1 3.7 %shard_map.92 = f32[256,1024]{1,0:T(8,128)} custom-call(s32[7]{0:T(128)} %stack.347.index_ref, f32[1024,1024]{1,0:T(8,128)} %shard_map.80.refs_0_, bf16[1024,1024]{1,0:T(8,128)(2,1)} %collective-permute-done.7.refs_1_, bf16[512,1024]{1,0:T(8,128)(2,1)} %copy-done.11, f32[1024,1024]{1,0:T(8,128)} %shard_map.83.refs_0_.refs_3_, bf16[1024,1024]{1,0:T(8,128)(2,1)} %copy-done.9, ...), custom_call_target="tpu_custom_call" | custom-call | flops 262144 | bytes 4718592 | tf_op jit(solution)/shard_map/pallas_call | solution.py:441
  254.9 28.8 %shard_map.93 = (f32[512,512]{1,0:T(8,128)S(1)}, f32[512,512]{1,0:T(8,128)S(1)}) custom-call(f32[4608,128]{1,0:T(8,128)S(1)} %pad_maximum_fusion.1.packed_ref, f32[512,512]{1,0:T(8,128)S(1)} %shard_map.86.w0_ref), custom_call_target="tpu_custom_call" | custom-call | flops 12884901888 | bytes 2097152 | tf_op jit(solution)/shard_map/pallas_call | solution.py:148
  283.7 1.3 shard_map.94
  285.0 3.0 shard_map.96
  288.5 1.3 collective-permute-start.22
  289.8 1.7 collective-permute-start.18
  291.7 2.1 collective-permute-done.21.refs_1_
  293.8 2.4 collective-permute-start.20
  296.3 4.8 %collective-permute-done.22.refs_2_ = f32[256,256]{1,0:T(8,128)S(1)} collective-permute-done((f32[256,256]{1,0:T(8,128)}, f32[256,256]{1,0:T(8,128)S(1)}, u32[]{:S(2)}, u32[]{:S(2)}) %collective-permute-start.22) | collective-permute-done | bytes 262176 | tf_op jit(solution)/shard_map/ppermute | solution.py:664
  301.2 1.9 collective-permute-done.23.refs_3_
  303.1 1.6 shard_map.97
  305.1 7.4 %collective-permute-done.19.refs_2_ = f32[256,256]{1,0:T(8,128)S(1)} collective-permute-done((f32[256,256]{1,0:T(8,128)S(1)}, f32[256,256]{1,0:T(8,128)S(1)}, u32[]{:S(2)}, u32[]{:S(2)}) %collective-permute-start.19) | collective-permute-done | bytes 262176 | tf_op jit(solution)/shard_map/ppermute | solution.py:664
  313.2 1.6 shard_map.95
  (82 shorter events, 20.2 us)
Async XLA Ops:
  7.2 175.9 %all-reduce.2.cloned.1.call-start = ((), (), s32[]{:S(2)}) async-start(), calls=%async_computation | async-start | bytes 2359296 | tf_op jit(solution)/shard_map/psum | solution.py:575
  8.5 3.4 %copy-start = (bf16[8,8,8,8192]{3,2,1,0:T(8,128)(2,1)S(1)}, bf16[8,8,8,8192]{3,2,1,0:T(8,128)(2,1)}, u32[]{:S(2)}) copy-start(bf16[8,8,8,8192]{3,2,1,0:T(8,128)(2,1)} %param.6) | copy-start | bytes 25165828
  11.9 0.7 copy-start.5
  12.6 0.7 copy-start.6
  13.3 0.7 copy-start.7
  14.0 0.7 copy-start.8
  14.6 3.4 %copy-start.1 = (bf16[8,8,8,8192]{3,2,1,0:T(8,128)(2,1)S(1)}, bf16[8,8,8,8192]{3,2,1,0:T(8,128)(2,1)}, u32[]{:S(2)}) copy-start(bf16[8,8,8,8192]{3,2,1,0:T(8,128)(2,1)} %param.6) | copy-start | bytes 25165828
  20.7 27.1 %collective-permute-start = (bf16[512,4096]{1,0:T(8,128)(2,1)}, bf16[512,4096]{1,0:T(8,128)(2,1)}, u32[]{:S(2)}, u32[]{:S(2)}) collective-permute-start(bf16[512,4096]{1,0:T(8,128)(2,1)} %shard_map.78), channel_id=1, source_target_pairs={{0,2},{2,0},{1,3},{3,1},{4,6},{6,4},{5,7},{7,5},{8,10},{10,8},{9,1... | collective-permute-start | bytes 12582920 | tf_op jit(solution)/shard_map/ppermute | solution.py:550
  20.8 10.8 %collective-permute-start.5 = (bf16[64,1024]{1,0:T(8,128)(2,1)S(1)}, bf16[64,1024]{1,0:T(8,128)(2,1)S(1)}, u32[]{:S(2)}, u32[]{:S(2)}) collective-permute-start(bf16[64,1024]{1,0:T(8,128)(2,1)S(1)} %broadcast_select_fusion.4), channel_id=1, source_target_pairs={{0,1},{1,0},{2,3},{3,2},{4,5},{5,4},{6,7},{7,6},{8,9},{9,8},{10,11... | collective-permute-start | bytes 393224 | tf_op jit(solution)/shard_map/ppermute | solution.py:544
  23.5 10.1 %collective-permute-start.1 = (bf16[64,1024]{1,0:T(8,128)(2,1)S(1)}, bf16[64,1024]{1,0:T(8,128)(2,1)S(1)}, u32[]{:S(2)}, u32[]{:S(2)}) collective-permute-start(bf16[64,1024]{1,0:T(8,128)(2,1)S(1)} %get-tuple-element.57), channel_id=1, source_target_pairs={{0,8},{8,16},{16,24},{1,9},{9,17},{17,25},{2,10},{10,18},{18,26},{... | collective-permute-start | bytes 393224 | tf_op jit(solution)/shard_map/ppermute | solution.py:548
  26.7 6.9 %collective-permute-start.2 = (bf16[64,1024]{1,0:T(8,128)(2,1)S(1)}, bf16[64,1024]{1,0:T(8,128)(2,1)S(1)}, u32[]{:S(2)}, u32[]{:S(2)}) collective-permute-start(bf16[64,1024]{1,0:T(8,128)(2,1)S(1)} %get-tuple-element.58), channel_id=1, source_target_pairs={{8,0},{16,8},{24,16},{9,1},{17,9},{25,17},{10,2},{18,10},{26,18},{... | collective-permute-start | bytes 393224 | tf_op jit(solution)/shard_map/ppermute | solution.py:549
  28.0 5.6 %collective-permute-start.3 = (bf16[64,1024]{1,0:T(8,128)(2,1)S(1)}, bf16[64,1024]{1,0:T(8,128)(2,1)S(1)}, u32[]{:S(2)}, u32[]{:S(2)}) collective-permute-start(bf16[64,1024]{1,0:T(8,128)(2,1)S(1)} %get-tuple-element.59), channel_id=1, source_target_pairs={{0,2},{2,4},{4,6},{1,3},{3,5},{5,7},{8,10},{10,12},{12,14},{9,11},... | collective-permute-start | bytes 393224 | tf_op jit(solution)/shard_map/ppermute | solution.py:548
  31.6 6.3 %collective-permute-start.4 = (bf16[64,1024]{1,0:T(8,128)(2,1)S(1)}, bf16[64,1024]{1,0:T(8,128)(2,1)S(1)}, u32[]{:S(2)}, u32[]{:S(2)}) collective-permute-start(bf16[64,1024]{1,0:T(8,128)(2,1)S(1)} %get-tuple-element.60), channel_id=1, source_target_pairs={{2,0},{4,2},{6,4},{3,1},{5,3},{7,5},{10,8},{12,10},{14,12},{11,9},... | collective-permute-start | bytes 393224 | tf_op jit(solution)/shard_map/ppermute | solution.py:549
  37.9 3.4 %copy-start.2 = (bf16[8,8,8,8192]{3,2,1,0:T(8,128)(2,1)S(1)}, bf16[8,8,8,8192]{3,2,1,0:T(8,128)(2,1)}, u32[]{:S(2)}) copy-start(bf16[8,8,8,8192]{3,2,1,0:T(8,128)(2,1)} %param.6) | copy-start | bytes 25165828
  44.0 1.0 copy-start.3
  44.0 3.8 %collective-permute-start.6 = (bf16[512,1024]{1,0:T(8,128)(2,1)S(1)}, bf16[512,1024]{1,0:T(8,128)(2,1)S(1)}, u32[]{:S(2)}, u32[]{:S(2)}) collective-permute-start(bf16[512,1024]{1,0:T(8,128)(2,1)S(1)} %get-tuple-element.69.refs_2_), channel_id=1, source_target_pairs={{0,2},{2,0},{1,3},{3,1},{4,6},{6,4},{5,7},{7,5},{8,10},{10,8},{9,1... | collective-permute-start | bytes 3145736 | tf_op jit(solution)/shard_map/ppermute | solution.py:569
  45.0 1.4 copy-start.13
  46.5 14.8 %collective-permute-start.11 = (f32[2304,128]{1,0:T(8,128)S(1)}, f32[2304,128]{1,0:T(8,128)}, u32[]{:S(2)}, u32[]{:S(2)}) collective-permute-start(f32[2304,128]{1,0:T(8,128)S(1)} %dynamic-slice_bitcast_fusion), channel_id=1, source_target_pairs={{0,2},{2,0},{1,3},{3,1},{4,6},{6,4},{5,7},{7,5},{8,10},{10,8},{9,1... | collective-permute-start | bytes 3538952 | tf_op jit(solution)/shard_map/ppermute | solution.py:575
  47.8 1.0 copy-start.12
  54.9 51.8 %collective-permute-start.9 = (bf16[1024,1024]{1,0:T(8,128)(2,1)}, bf16[1024,1024]{1,0:T(8,128)(2,1)S(1)}, u32[]{:S(2)}, u32[]{:S(2)}) collective-permute-start(bf16[1024,1024]{1,0:T(8,128)(2,1)} %shard_map.84), channel_id=1, source_target_pairs={{0,4},{4,0},{1,5},{5,1},{2,6},{6,2},{3,7},{7,3},{8,12},{12,8},{9,1... | collective-permute-start | bytes 6291464 | tf_op jit(solution)/shard_map/ppermute | solution.py:512
  61.1 51.8 %collective-permute-start.7 = (bf16[1024,1024]{1,0:T(8,128)(2,1)}, bf16[1024,1024]{1,0:T(8,128)(2,1)}, u32[]{:S(2)}, u32[]{:S(2)}) collective-permute-start(bf16[1024,1024]{1,0:T(8,128)(2,1)} %shard_map.81), channel_id=1, source_target_pairs={{0,1},{1,0},{2,3},{3,2},{4,5},{5,4},{6,7},{7,6},{8,9},{9,8},{10,11... | collective-permute-start | bytes 6291464 | tf_op jit(solution)/shard_map/ppermute | solution.py:512
  106.8 1.3 copy-start.9
  183.1 7.4 %collective-permute-start.12 = (f32[2304,128]{1,0:T(8,128)}, f32[2304,128]{1,0:T(8,128)S(1)}, u32[]{:S(2)}, u32[]{:S(2)}) collective-permute-start(f32[2304,128]{1,0:T(8,128)} %all-reduce.2.cloned.1.call-done), channel_id=1, source_target_pairs={{0,2},{2,0},{1,3},{3,1},{4,6},{6,4},{5,7},{7,5},{8,10},{10,8},{9,1... | collective-permute-start | bytes 3538952 | tf_op jit(solution)/shard_map/ppermute | solution.py:465
  188.8 30.3 %collective-permute-start.10 = (bf16[512,1024]{1,0:T(8,128)(2,1)}, bf16[512,1024]{1,0:T(8,128)(2,1)S(1)}, u32[]{:S(2)}, u32[]{:S(2)}) collective-permute-start(bf16[512,1024]{1,0:T(8,128)(2,1)} %shard_map.85), channel_id=1, source_target_pairs={{0,1},{1,0},{2,3},{3,2},{4,5},{5,4},{6,7},{7,6},{8,9},{9,8},{10,11... | collective-permute-start | bytes 3145736 | tf_op jit(solution)/shard_map/ppermute | solution.py:512
  190.0 29.1 %collective-permute-start.8 = (bf16[512,1024]{1,0:T(8,128)(2,1)}, bf16[512,1024]{1,0:T(8,128)(2,1)S(1)}, u32[]{:S(2)}, u32[]{:S(2)}) collective-permute-start(bf16[512,1024]{1,0:T(8,128)(2,1)} %shard_map.82), channel_id=1, source_target_pairs={{0,4},{4,0},{1,5},{5,1},{2,6},{6,2},{3,7},{7,3},{8,12},{12,8},{9,1... | collective-permute-start | bytes 3145736 | tf_op jit(solution)/shard_map/ppermute | solution.py:512
  219.1 1.0 copy-start.10
  220.1 1.0 copy-start.11
  224.7 59.0 %collective-permute-start.16 = (bf16[256,1024]{1,0:T(8,128)(2,1)}, bf16[256,1024]{1,0:T(8,128)(2,1)S(1)}, u32[]{:S(2)}, u32[]{:S(2)}) collective-permute-start(bf16[256,1024]{1,0:T(8,128)(2,1)} %shard_map.91), channel_id=1, source_target_pairs={{0,10},{2,26},{4,14},{6,30},{8,0},{10,16},{12,4},{14,20},{16,2},{2... | collective-permute-start | bytes 1572872 | tf_op jit(solution)/shard_map/ppermute | solution.py:639
  232.0 51.7 %collective-permute-start.15 = (bf16[256,1024]{1,0:T(8,128)(2,1)}, bf16[256,1024]{1,0:T(8,128)(2,1)S(1)}, u32[]{:S(2)}, u32[]{:S(2)}) collective-permute-start(bf16[256,1024]{1,0:T(8,128)(2,1)} %shard_map.90), channel_id=1, source_target_pairs={{0,8},{2,24},{4,12},{6,28},{10,26},{14,30},{16,0},{20,4},{24,2},{2... | collective-permute-start | bytes 1572872 | tf_op jit(solution)/shard_map/ppermute | solution.py:639
  239.8 43.9 %collective-permute-start.14 = (bf16[256,1024]{1,0:T(8,128)(2,1)}, bf16[256,1024]{1,0:T(8,128)(2,1)S(1)}, u32[]{:S(2)}, u32[]{:S(2)}) collective-permute-start(bf16[256,1024]{1,0:T(8,128)(2,1)} %shard_map.89), channel_id=1, source_target_pairs={{2,18},{6,22},{10,24},{14,28},{16,10},{18,26},{20,14},{22,30},{24,... | collective-permute-start | bytes 1572872 | tf_op jit(solution)/shard_map/ppermute | solution.py:639
  244.8 38.9 %collective-permute-start.13 = (bf16[256,1024]{1,0:T(8,128)(2,1)}, bf16[256,1024]{1,0:T(8,128)(2,1)S(1)}, u32[]{:S(2)}, u32[]{:S(2)}) collective-permute-start(bf16[256,1024]{1,0:T(8,128)(2,1)} %shard_map.88), channel_id=1, source_target_pairs={{2,16},{6,20},{8,2},{10,18},{12,6},{14,22},{16,8},{18,24},{20,12},... | collective-permute-start | bytes 1572872 | tf_op jit(solution)/shard_map/ppermute | solution.py:639
  254.8 28.9 %copy-start.4 = (f32[256,1024]{1,0:T(8,128)S(1)}, f32[256,1024]{1,0:T(8,128)}, u32[]{:S(2)}) copy-start(f32[256,1024]{1,0:T(8,128)} %shard_map.87.own_ref) | copy-start | bytes 3145732
  254.9 28.8 %collective-permute-start.17 = (f32[256,1024]{1,0:T(8,128)}, f32[256,1024]{1,0:T(8,128)S(1)}, u32[]{:S(2)}, u32[]{:S(2)}) collective-permute-start(f32[256,1024]{1,0:T(8,128)} %shard_map.92), channel_id=1, source_target_pairs={{0,2},{2,0},{1,3},{3,1},{4,6},{6,4},{5,7},{7,5},{8,10},{10,8},{9,1... | collective-permute-start | bytes 3145736 | tf_op jit(solution)/shard_map/ppermute | solution.py:642
  287.9 5.9 %collective-permute-start.21 = (f32[256,256]{1,0:T(8,128)S(1)}, f32[256,256]{1,0:T(8,128)S(1)}, u32[]{:S(2)}, u32[]{:S(2)}) collective-permute-start(f32[256,256]{1,0:T(8,128)S(1)} %get-tuple-element.91), channel_id=1, source_target_pairs={{0,2},{2,4},{4,6},{6,0},{1,3},{3,5},{5,7},{7,1},{8,10},{10,12},{12... | collective-permute-start | bytes 786440 | tf_op jit(solution)/shard_map/ppermute | solution.py:664
  288.5 12.7 %collective-permute-start.22 = (f32[256,256]{1,0:T(8,128)}, f32[256,256]{1,0:T(8,128)S(1)}, u32[]{:S(2)}, u32[]{:S(2)}) collective-permute-start(f32[256,256]{1,0:T(8,128)} %get-tuple-element.92), channel_id=1, source_target_pairs={{0,4},{2,6},{4,0},{6,2},{1,5},{3,7},{5,1},{7,3},{8,12},{10,14},{12... | collective-permute-start | bytes 786440 | tf_op jit(solution)/shard_map/ppermute | solution.py:664
  289.8 13.3 %collective-permute-start.23 = (f32[256,256]{1,0:T(8,128)S(1)}, f32[256,256]{1,0:T(8,128)S(1)}, u32[]{:S(2)}, u32[]{:S(2)}) collective-permute-start(f32[256,256]{1,0:T(8,128)S(1)} %get-tuple-element.93), channel_id=1, source_target_pairs={{0,6},{2,0},{4,2},{6,4},{1,7},{3,1},{5,3},{7,5},{8,14},{10,8},{12,... | collective-permute-start | bytes 786440 | tf_op jit(solution)/shard_map/ppermute | solution.py:664
  289.8 15.3 %collective-permute-start.18 = (f32[256,256]{1,0:T(8,128)S(1)}, f32[256,256]{1,0:T(8,128)S(1)}, u32[]{:S(2)}, u32[]{:S(2)}) collective-permute-start(f32[256,256]{1,0:T(8,128)S(1)} %get-tuple-element.84), channel_id=1, source_target_pairs={{0,2},{2,4},{4,6},{6,0},{1,3},{3,5},{5,7},{7,1},{8,10},{10,12},{12... | collective-permute-start | bytes 786440 | tf_op jit(solution)/shard_map/ppermute | solution.py:664
  291.5 20.9 %collective-permute-start.19 = (f32[256,256]{1,0:T(8,128)S(1)}, f32[256,256]{1,0:T(8,128)S(1)}, u32[]{:S(2)}, u32[]{:S(2)}) collective-permute-start(f32[256,256]{1,0:T(8,128)S(1)} %get-tuple-element.85), channel_id=1, source_target_pairs={{0,4},{2,6},{4,0},{6,2},{1,5},{3,7},{5,1},{7,3},{8,12},{10,14},{12... | collective-permute-start | bytes 786440 | tf_op jit(solution)/shard_map/ppermute | solution.py:664
  293.8 19.4 %collective-permute-start.20 = (f32[256,256]{1,0:T(8,128)S(1)}, f32[256,256]{1,0:T(8,128)S(1)}, u32[]{:S(2)}, u32[]{:S(2)}) collective-permute-start(f32[256,256]{1,0:T(8,128)S(1)} %get-tuple-element.86), channel_id=1, source_target_pairs={{0,6},{2,0},{4,2},{6,4},{1,7},{3,1},{5,3},{7,5},{8,14},{10,8},{12,... | collective-permute-start | bytes 786440 | tf_op jit(solution)/shard_map/ppermute | solution.py:664
Sparse Core Ops, SparseCore 0:
  64.2 118.8 all-reduce.1

commit v3 on v2

--- a/solution.py
+++ b/solution.py
@@ -99,8 +99,8 @@
     s_ref[...] = jnp.where(row_ids >= col_ids, s_ref[...], 0.0)
 
 
-def unpack_symmetric(packed_ref, s_ref, first=0):
-    at = first
+def unpack_symmetric(packed_ref, s_ref):
+    at = 0
     for i in range(s_ref.shape[0] // LEAF):
         for j in range(i + 1):
             block = packed_ref[at * LEAF : (at + 1) * LEAF, :]
@@ -118,7 +118,7 @@
 def next_panel_kernel(packed_ref, w0_ref, f_ref, w_ref, d_ref):
     nb = w0_ref.shape[0]
     blocks = nb // LEAF
-    unpack_symmetric(packed_ref, w_ref, blocks * (blocks + 1) // 2)
+    unpack_symmetric(packed_ref, w_ref)
     start = packed_ref.shape[0] - blocks * nb
     below = jnp.concatenate(
         [packed_ref[start + i * nb : start + (i + 1) * nb, :] for i in range(nb // LEAF)], 1
@@ -296,45 +296,32 @@
         later_ref[at + i * nb : at + (i + 1) * nb, :] = below[:, i * LEAF : (i + 1) * LEAF]
 
 
-def pieces_kernel(index_ref, *refs, groups):
-    del index_ref
-    total = sum(groups)
-    ins, outs = refs[:total], refs[total:]
-    at = 0
-    for out, count in zip(outs, groups):
-        width = out.shape[1] // count
-        for i in range(count):
-            out[:, i * width : (i + 1) * width] = ins[at][...]
-            at += 1
-
-
-def take_pieces(flat_basis, lists):
-    rows = flat_basis.shape[0]
-    tile = min(128, rows)
-    index = jnp.stack([jnp.asarray(b, jnp.int32) for blocks, _ in lists for b in blocks])
-    in_specs, out_specs, out_shape = [], [], []
-    for blocks, width in lists:
-        for _ in blocks:
-            k = len(in_specs)
-            in_specs.append(pl.BlockSpec((tile, width), lambda t, idx, k=k: (t, idx[k])))
-        out_specs.append(pl.BlockSpec((tile, width * len(blocks)), lambda t, idx: (t, 0)))
-        out_shape.append(jax.ShapeDtypeStruct((rows, width * len(blocks)), flat_basis.dtype))
-    kernel = functools.partial(pieces_kernel, groups=[len(blocks) for blocks, _ in lists])
+def copy_kernel(table_ref, in_ref, out_ref):
+    del table_ref
+    out_ref[...] = in_ref[...]
+
+
+def take_columns(table, at, array, width):
+    rows = array.shape[0]
+    tile = min(64, rows)
     return pl.pallas_call(
-        kernel,
+        copy_kernel,
         grid_spec=pltpu.PrefetchScalarGridSpec(
-            num_scalar_prefetch=1, grid=(rows // tile,), in_specs=in_specs, out_specs=out_specs
-        ),
-        out_shape=out_shape,
+            num_scalar_prefetch=1,
+            grid=(rows // tile,),
+            in_specs=[pl.BlockSpec((tile, width), lambda t, tab: (t, tab[at]))],
+            out_specs=pl.BlockSpec((tile, width), lambda t, tab: (t, 0)),
+        ),
+        out_shape=jax.ShapeDtypeStruct((rows, width), array.dtype),
         compiler_params=pltpu.CompilerParams(vmem_limit_bytes=32 * 2**20),
         cost_estimate=pl.CostEstimate(
-            flops=0, transcendentals=0, bytes_accessed=4 * rows * flat_basis.shape[1]
-        ),
-    )(index, *([flat_basis] * len(in_specs)))
-
-
-def products_kernel(index_ref, *refs):
-    del index_ref
+            flops=0, transcendentals=0, bytes_accessed=4 * rows * width
+        ),
+    )(table, array)
+
+
+def products_kernel(table_ref, *refs):
+    del table_ref
     out, count = refs[-1], len(refs) // 2
     total = None
     for b, image in zip(refs[:count], refs[count:-1]):
@@ -345,19 +332,18 @@
     out[...] = total.astype(out.dtype)
 
 
-def products(bases, images, lists, width, dtype):
+def products(table, bases, images, lists, width, dtype):
     rows, cols = images[0].shape
     step = 512 if width % 512 == 0 else width
     parts = width // step
-    steps = len(lists[0]) * parts
-    index = jnp.stack(
-        [jnp.asarray(b * parts + i, jnp.int32) for blocks in lists for b in blocks for i in range(parts)]
-    )
+    steps = lists[0][1] * parts
     in_specs = [
-        pl.BlockSpec((rows, step), lambda t, idx, k=k: (0, idx[k * steps + t]))
-        for k in range(len(bases))
+        pl.BlockSpec(
+            (rows, step), lambda t, tab, at=at: (0, tab[at + t // parts] * parts + t % parts)
+        )
+        for at, _ in lists
     ]
-    in_specs += [pl.BlockSpec((rows, cols), lambda t, idx: (0, 0))] * len(images)
+    in_specs += [pl.BlockSpec((rows, cols), lambda t, tab: (0, 0))] * len(images)
     total = steps * step
     return pl.pallas_call(
         products_kernel,
@@ -365,96 +351,89 @@
             num_scalar_prefetch=1,
             grid=(steps,),
             in_specs=in_specs,
-            out_specs=pl.BlockSpec((step, cols), lambda t, idx: (t, 0)),
+            out_specs=pl.BlockSpec((step, cols), lambda t, tab: (t, 0)),
         ),
         out_shape=jax.ShapeDtypeStruct((total, cols), dtype),
-        compiler_params=pltpu.CompilerParams(vmem_limit_bytes=56 * 2**20),
+        compiler_params=pltpu.CompilerParams(vmem_limit_bytes=48 * 2**20),
         cost_estimate=pl.CostEstimate(
             flops=2 * total * cols * rows * len(bases),
             transcendentals=0,
             bytes_accessed=2 * rows * (total + cols) * len(bases) + 4 * total * cols,
         ),
-    )(index, *bases, *images)
-
-
-def add_kernel(index_ref, *refs):
-    del index_ref
+    )(table, *bases, *images)
+
+
+def add_kernel(table_ref, *refs):
+    del table_ref
     total = refs[0][...].astype(jnp.float32)
     for got in refs[1:-1]:
         total = total + got[...].astype(jnp.float32)
     refs[-1][...] = total.astype(refs[-1].dtype)
 
 
-def add_blocks(arrays, lists, height, dtype):
+def add_blocks(table, arrays, at, count, height, dtype):
     cols = arrays[0].shape[1]
-    step = min(128, height)
+    step = min(256, height)
     parts = height // step
-    steps = len(lists[0]) * parts
-    index = jnp.stack(
-        [jnp.asarray(b * parts + i, jnp.int32) for blocks in lists for b in blocks for i in range(parts)]
-    )
+    steps = count * parts
+    spec = pl.BlockSpec((step, cols), lambda t, tab: (tab[at + t // parts] * parts + t % parts, 0))
     return pl.pallas_call(
         add_kernel,
         grid_spec=pltpu.PrefetchScalarGridSpec(
             num_scalar_prefetch=1,
             grid=(steps,),
-            in_specs=[
-                pl.BlockSpec((step, cols), lambda t, idx, k=k: (idx[k * steps + t], 0))
-                for k in range(len(arrays))
-            ],
-            out_specs=pl.BlockSpec((step, cols), lambda t, idx: (t, 0)),
+            in_specs=[spec] * len(arrays),
+            out_specs=pl.BlockSpec((step, cols), lambda t, tab: (t, 0)),
         ),
         out_shape=jax.ShapeDtypeStruct((steps * step, cols), dtype),
-        compiler_params=pltpu.CompilerParams(vmem_limit_bytes=56 * 2**20),
+        compiler_params=pltpu.CompilerParams(vmem_limit_bytes=24 * 2**20),
         cost_estimate=pl.CostEstimate(
             flops=steps * step * cols,
             transcendentals=0,
             bytes_accessed=steps * step * cols * 4 * len(arrays),
         ),
-    )(index, *arrays)
-
-
-def pick_kernel(index_ref, *refs):
-    half = (len(refs) - 1) // 2
-
-    def total(group):
-        out = group[0][...].astype(jnp.float32)
-        for got in group[1:]:
-            out = out + got[...].astype(jnp.float32)
-        refs[-1][...] = out.astype(refs[-1].dtype)
-
-    @pl.when(index_ref[0] == 0)
-    def _():
-        total(refs[:half])
-
-    @pl.when(index_ref[0] != 0)
-    def _():
-        total(refs[half:-1])
-
-
-def pick_block(second, arrays_a, arrays_b, at_a, at_b, height, dtype):
-    cols = arrays_a[0].shape[1]
-    step = min(128, height)
-    parts = height // step
-    arrays = [*arrays_a, *arrays_b]
-    index = jnp.stack([jnp.asarray(v, jnp.int32) for v in (second, *at_a, *at_b)])
+    )(table, *arrays)
+
+
+def plane_kernel(table_ref, *refs, groups, at):
+    ins, outs, plane_ref = refs[: sum(groups)], refs[sum(groups) : -1], refs[-1]
+    height = ins[0].shape[0]
+    done = 0
+    for i, count in enumerate(groups):
+        total = ins[done][...].astype(jnp.float32)
+        for got in ins[done + 1 : done + count]:
+            total = total + got[...].astype(jnp.float32)
+        plane_ref[i * height : (i + 1) * height, :] = total
+        done += count
+    for i, out in enumerate(outs):
+        part = out.shape[0]
+        rows = pl.ds(pl.multiple_of(table_ref[at + i] * part, part), part)
+        out[...] = plane_ref[rows, :].astype(out.dtype)
+
+
+def plane_parts(table, sums, height, at, outs):
+    cols = sums[0][0][0].shape[1]
+
+    def spec(place, block):
+        if place is None:
+            return pl.BlockSpec((height, cols), lambda t, tab: (block, 0))
+        return pl.BlockSpec((height, cols), lambda t, tab: (tab[place], 0))
+
     return pl.pallas_call(
-        pick_kernel,
+        functools.partial(plane_kernel, groups=[len(terms) for terms in sums], at=at),
         grid_spec=pltpu.PrefetchScalarGridSpec(
             num_scalar_prefetch=1,
-            grid=(parts,),
-            in_specs=[
-                pl.BlockSpec((step, cols), lambda t, idx, k=k: (idx[1 + k] * parts + t, 0))
-                for k in range(len(arrays))
-            ],
-            out_specs=pl.BlockSpec((step, cols), lambda t, idx: (t, 0)),
-        ),
-        out_shape=jax.ShapeDtypeStruct((height, cols), dtype),
-        compiler_params=pltpu.CompilerParams(vmem_limit_bytes=56 * 2**20),
+            grid=(1,),
+            in_specs=[spec(place, block) for terms in sums for _, place, block in terms],
+            out_specs=[pl.BlockSpec(out.shape, lambda t, tab: (0, 0)) for out in outs],
+            scratch_shapes=[pltpu.VMEM((height * len(sums), cols), jnp.float32)],
+        ),
+        out_shape=outs,
+        compiler_params=pltpu.CompilerParams(vmem_limit_bytes=44 * 2**20),
         cost_estimate=pl.CostEstimate(
-            flops=height * cols, transcendentals=0, bytes_accessed=height * cols * 18
-        ),
-    )(index, *arrays)
+            flops=0, transcendentals=0, bytes_accessed=height * len(sums) * cols * 14
+        ),
+    )(table, *(array for terms in sums for array, _, _ in terms))
 
 
 def swap_pairs():
@@ -506,6 +485,39 @@
     wide = width_k // (devices_x * devices_z)
     narrow = wide // chips_y
     part = narrow // 2
+
+    entries = []
+
+    def put(values):
+        entries.extend(values)
+        return len(entries) - len(values), len(values)
+
+    shift = core * spans * devices_z * chips_y
+
+    def put_products(blocks):
+        return [put([b + shift for b in blocks]), put(blocks)]
+
+    lists_a, lists_b, next_a, next_b = [], [], [], []
+    for d in range(devices_z):
+        x = (at_z + d) % devices_z
+        lists_a.append(
+            put_products(
+                [(zz * devices_z + x) * chips_y + y for zz in range(split) for y in range(chips_y)]
+            )
+        )
+        next_b.append(put([zz * devices_z + x for zz in range(spans - split)]))
+    for d in range(chips_y):
+        y = (chip + d) % chips_y
+        lists_b.append(
+            put_products(
+                [(zz * devices_z + x) * chips_y + y for zz in range(split, spans) for x in range(devices_z)]
+            )
+        )
+        next_a.append(put([zz * chips_y + y for zz in range(split)]))
+    leaving = [(at_x + step) % devices_x for step in range(devices_x)]
+    leaving_at, _ = put(leaving + [at_x % spans * 2 + core, at_x % spans * 2 + 1 - core])
+    given_at, _ = put([1 - core])
+    table = jnp.stack([jnp.asarray(e, jnp.int32) for e in entries])
 
     def move(array, axis, d):
         size = lax.axis_size(axis)
@@ -532,8 +544,8 @@
         scratch_shapes=[pltpu.VMEM((cols // LEAF, count, LEAF), f32)],
         compiler_params=pltpu.CompilerParams(vmem_limit_bytes=24 * 2**20),
     )(cond_table, ground_table, info, port_cells[None, :], port_load[None, :], flat_basis)
-    faces, other_core = lax.optimization_barrier((faces, 1 - core))
-    (given,) = take_pieces(flat_basis, [([other_core], width_k // 2)])
+    later_table, _ = lax.optimization_barrier((table, faces))
+    given = take_columns(later_table, given_at, flat_basis, width_k // 2)
     halos = []
     for i, (axis, size) in enumerate(
         (("gx", devices_x), (("gy", "core"), devices_y), ("gz", devices_z))
@@ -569,65 +581,68 @@
     other_image = lax.ppermute(image, "core", swap_pairs())
 
     axes = ("gx", "gy", "gz")
-    both = jnp.concatenate([first_rows, later_rows], 0).reshape(2, -1, LEAF)
-    kept = lax.dynamic_index_in_dim(both, core, 0, keepdims=False)
-    sent = lax.dynamic_index_in_dim(both, 1 - core, 0, keepdims=False)
-    lead_half = lax.psum(kept + lax.ppermute(sent, "core", swap_pairs()), axes)
-
-    shift = core * spans * devices_z * chips_y
-
-    def chip_products(blocks, dtype):
-        lists = [[b + shift for b in blocks], blocks]
-        return products([flat_basis, other_basis], [image, other_image], lists, narrow, dtype)
-
-    def products_a(d, dtype):
-        x = (at_z + d) % devices_z
-        blocks = [(zz * devices_z + x) * chips_y + y for zz in range(split) for y in range(chips_y)]
-        return chip_products(blocks, dtype)
-
-    def products_b(d, dtype):
-        y = (chip + d) % chips_y
-        blocks = [
-            (zz * devices_z + x) * chips_y + y for zz in range(split, spans) for x in range(devices_z)
-        ]
-        return chip_products(blocks, dtype)
-
-    got_a = [move(products_a(d, bf16), "gz", d) for d in range(1, devices_z)]
-    got_b = [move(products_b(d, bf16), "gy", d) for d in range(1, chips_y)]
-    own_a, own_b = products_a(0, f32), products_b(0, f32)
+    chips = devices_x * chips_y * devices_z
+
+    def halved(rows):
+        both = rows.reshape(2, -1, LEAF)
+        kept = lax.dynamic_index_in_dim(both, core, 0, keepdims=False)
+        sent = lax.dynamic_index_in_dim(both, 1 - core, 0, keepdims=False)
+        return kept + lax.ppermute(sent, "core", swap_pairs())
+
+    def exchanged(rows):
+        rows = rows.reshape(chips, -1, LEAF)
+        return lax.all_to_all(rows, axes, split_axis=0, concat_axis=0, tiled=True)
+
+    def spread(terms):
+        own = jnp.sum(terms, axis=0)
+        return own, exchanged(jnp.broadcast_to(own, terms.shape)).reshape(-1, LEAF)
+
+    first_half, later_half = halved(first_rows), halved(later_rows)
+    first_terms = exchanged(first_half)
+
+    def chip_products(images, lists, dtype):
+        return products(table, [flat_basis, other_basis], images, lists, narrow, dtype)
+
+    images, _ = lax.optimization_barrier(([image, other_image], first_half))
+    sent_a = [chip_products(images, lists_a[d], bf16) for d in range(1, devices_z)]
+    sent_b = [chip_products(images, lists_b[d], bf16) for d in range(1, chips_y)]
+    got_a = [move(a, "gz", d) for d, a in enumerate(sent_a, 1)]
+    got_b = [move(a, "gy", d) for d, a in enumerate(sent_b, 1)]
+    first_terms, _ = lax.optimization_barrier((first_terms, (sent_a, sent_b)))
+    own, first_half = spread(first_terms)
+    images, _ = lax.optimization_barrier((images, own))
+    own_a, own_b = (chip_products(images, lists[0], f32) for lists in (lists_a, lists_b))
+    first_half, later_half, _ = lax.optimization_barrier((first_half, later_half, (own_a, own_b)))
+    first_rows = other_half(first_half, core)
+    later_half, _ = lax.optimization_barrier((later_half, first_half))
+    later_terms = exchanged(later_half)
     sums_a, sums_b = [own_a, *got_a], [own_b, *got_b]
 
-    def further(arrays, mine, size, groups):
-        sent = []
-        for d in range(1, size):
-            blocks = [zz * size + (mine + d) % size for zz in range(groups)]
-            sent.append(add_blocks(arrays, [blocks] * len(arrays), narrow, bf16))
-        return sent
-
-    further_a = further(sums_a, chip, chips_y, split)
-    further_b = further(sums_b, at_z, devices_z, spans - split)
-    lead_half, _ = lax.optimization_barrier((lead_half, (further_a, further_b)))
+    further_a = [add_blocks(table, sums_a, *next_a[d], narrow, bf16) for d in range(1, chips_y)]
+    further_b = [add_blocks(table, sums_b, *next_b[d], narrow, bf16) for d in range(1, devices_z)]
+    later_terms, _ = lax.optimization_barrier((later_terms, (further_a, further_b)))
     further_a = [move(a, "gy", d) for d, a in enumerate(further_a, 1)]
     further_b = [move(a, "gz", d) for d, a in enumerate(further_b, 1)]
-    lead_rows = other_half(lead_half, core)
-    inverse_0 = first_panel(lead_rows, NB)
-    (further_a, further_b), inverse_0 = lax.optimization_barrier(
-        ((further_a, further_b), inverse_0)
+    own, later_half = spread(later_terms)
+    first_rows, _ = lax.optimization_barrier((first_rows, own))
+    inverse_0 = first_panel(first_rows, NB)
+    (further_a, further_b, later_half), inverse_0 = lax.optimization_barrier(
+        ((further_a, further_b, later_half), inverse_0)
     )
-
-    def plane_block(zz, c, dtype):
-        in_b = zz >= split
-        zz_a, zz_b = jnp.minimum(zz, split - 1), jnp.maximum(zz - split, 0)
-        at_a = [(zz_a * chips_y + chip) * 2 + c] * len(sums_a) + [zz_a * 2 + c] * len(further_a)
-        at_b = [(zz_b * devices_z + at_z) * 2 + c] * len(sums_b) + [zz_b * 2 + c] * len(further_b)
-        return pick_block(
-            in_b, sums_a + further_a, sums_b + further_b, at_a, at_b, part, dtype
-        )
-
-    x_got, x_sent = [], []
+    later_rows = other_half(later_half, core)
+
+    terms = []
+    for zz in range(split):
+        at = next_a[0][0] + zz
+        terms.append([(a, at, None) for a in sums_a] + [(a, None, zz) for a in further_a])
+    for zz in range(spans - split):
+        at = next_b[0][0] + zz
+        terms.append([(a, at, None) for a in sums_b] + [(a, None, zz) for a in further_b])
+    outs = [jax.ShapeDtypeStruct((part, cols), bf16)] * devices_x
+    outs += [jax.ShapeDtypeStruct((part, cols), f32)] * 2
+    *x_sent, own, swapped = plane_parts(table, terms, narrow, leaving_at, outs)
+    x_got = []
     for step in range(devices_x):
-        to = (at_x + step) % devices_x
-        x_sent.append(plane_block(to // 2, to % 2, bf16))
         pairs = []
         for x in range(devices_x):
             for y in range(devices_y):
@@ -636,12 +651,11 @@
                 dest_y = (y // 2) * 2 + to % 2
                 if dest_x != x:
                     pairs.append((x * devices_y + y, dest_x * devices_y + dest_y))
-        x_got.append(lax.ppermute(x_sent[-1], ("gx", "gy", "core"), pairs))
+        x_got.append(lax.ppermute(x_sent[step], ("gx", "gy", "core"), pairs))
+    swapped = lax.ppermute(swapped, "core", swap_pairs())
     home = at_x // spans == core
-    own = plane_block(at_x % spans, core, f32)
-    swapped = lax.ppermute(plane_block(at_x % spans, 1 - core, f32), "core", swap_pairs())
-    lead_rows, _ = lax.optimization_barrier((lead_rows, (x_sent, own)))
-    factor_10, inverse_1 = next_panel(lead_rows, inverse_0)
+    later_rows, _ = lax.optimization_barrier((later_rows, x_sent))
+    factor_10, inverse_1 = next_panel(later_rows, inverse_0)
     (x_got, swapped), inverse_1 = lax.optimization_barrier(((x_got, swapped), inverse_1))
     by_blocks = [jax.ShapeDtypeStruct((part, cols // devices_y), f32)] * devices_y
     order = jnp.stack([(at_y + d) % devices_y for d in range(devices_y)])

time: 323 us -> 266 us (0.82)
  waiting for transfers between devices: 115 us -> 66.1 us
  starting transfers between devices: 34.5 us -> 60.4 us
  Pallas kernels: 127 us -> 106 us
  between operations: 14.5 us -> 1.13 us
    psum x1 -> x0, waiting for transfers between devices: 65.8 us -> none  [local(): lead_half = lax.psum(kept + lax.ppermute(sent, 'core', swap_pairs()), axes)]
    all_to_all x0 -> x4, waiting for transfers between devices: none -> 37.9 us  [exchanged(): return lax.all_to_all(rows, axes, split_axis=0, concat_axis=0, tiled=True)]
    ppermute x4, waiting for transfers between devices: 27.4 us -> 4.34 us  [move(): return lax.ppermute(array, axis, [(i, (i + d) % size) for i in range(size)])]
    all_to_all x0 -> x4, starting transfers between devices: none -> 21.7 us  [exchanged(): return lax.all_to_all(rows, axes, split_axis=0, concat_axis=0, tiled=True)]
    pallas_call x7 -> x2, Pallas kernels: 24.7 us -> 8.91 us  [the longest x1 4.64 us: plane_parts(): pl.pallas_call(functools.partial(plane_kernel, groups=[len(terms) for ter...]
    ppermute x6 -> x7, waiting for transfers between devices: 0.02 us -> 8.17 us  [the longest x4 7.77 us: local(): x_got.append(lax.ppermute(x_sent[step], ('gx', 'gy', 'core'), pairs))]
    another operation x8 -> x1, local copies, waits for them, and re-layouts: 5.2 us -> 0.11 us  [local(): table = jnp.stack([jnp.asarray(e, jnp.int32) for e in entries])]
    unnamed x28 -> x32, local copies, waits for them, and re-layouts: 16.8 us -> 20.7 us
  transfers between devices with their start and end apart: 25 -> 30, of which waited for: 10 -> 12; matrix products, arithmetic and copies ran while one was open for 4% -> 3% of each run, Pallas kernels for 35% -> 36%
where the time goes in v3:
time: 266 us; the launch traced here: 265 us
  Pallas kernels  106 us (40%)
  waiting for transfers between devices  66.1 us (25%)
  starting transfers between devices  60.4 us (23%)
  local copies, waits for them, and re-layouts  25.9 us (10%)
  other arithmetic  5.28 us (2%)
    pallas_call x2, Pallas kernels, panel_call(): pl.pallas_call(kernel, out_shape=[jax.ShapeDtypeStruct((nb, nb), jnp.floa...  55.8 us
    all_to_all x4, waiting for transfers between devices, exchanged(): return lax.all_to_all(rows, axes, split_axis=0, concat_axis=0, tiled=True)  37.9 us
    pallas_call x4, Pallas kernels, products(): pl.pallas_call(products_kernel, grid_spec=pltpu.PrefetchScalarGridSpec(nu...  22.1 us
    all_to_all x4, starting transfers between devices, exchanged(): return lax.all_to_all(rows, axes, split_axis=0, concat_axis=0, tiled=True)  21.7 us
    unnamed x32, local copies, waits for them, and re-layouts  20.7 us
    ppermute x6, waiting for transfers between devices, to_columns(): got.append(lax.ppermute(blocks[d], ('gy', 'core'), pairs))  13.9 us
    ppermute x4, starting transfers between devices, local(): x_got.append(lax.ppermute(x_sent[step], ('gx', 'gy', 'core'), pairs))  12.2 us
    ppermute x4, waiting for transfers between devices, local(): x_got.append(lax.ppermute(x_sent[step], ('gx', 'gy', 'core'), pairs))  7.77 us
  transfers between devices with their start and end apart: 30, of which 12 were waited for; matrix products, arithmetic and copies ran while one was open for 3% of the time, Pallas kernels for 36%

profile of v3, /device:TPU:1, one launch (start us, length us, event | category | flops | bytes accessed | tf_op | source)
XLA Modules:
  0.0 264.9 jit_solution(11852626659032526857)
XLA Ops:
  2.1 3.4 %copy-done = bf16[8,8,8,8192]{3,2,1,0:T(8,128)(2,1)S(1)} copy-done((bf16[8,8,8,8192]{3,2,1,0:T(8,128)(2,1)S(1)}, bf16[8,8,8,8192]{3,2,1,0:T(8,128)(2,1)}, u32[]{:S(2)}) %copy-start) | copy-done | bytes 8388632
  8.2 2.4 shard_map.77
  10.7 3.4 %copy-done.1 = bf16[8,8,8,8192]{3,2,1,0:T(8,128)(2,1)S(1)} copy-done((bf16[8,8,8,8192]{3,2,1,0:T(8,128)(2,1)S(1)}, bf16[8,8,8,8192]{3,2,1,0:T(8,128)(2,1)}, u32[]{:S(2)}) %copy-start.1) | copy-done | bytes 8388632
  14.1 4.3 %shard_map.78 = bf16[512,4096]{1,0:T(8,128)(2,1)} custom-call(s32[27]{0:T(128)S(1)} %stack.152.table_ref, bf16[512,8192]{1,0:T(8,128)(2,1)S(1)} %bitcast.58), custom_call_target="tpu_custom_call" | custom-call | bytes 8388608 | tf_op jit(solution)/shard_map/pallas_call | solution.py:307
  18.4 2.7 %collective-permute-start.5 = (bf16[64,1024]{1,0:T(8,128)(2,1)S(1)}, bf16[64,1024]{1,0:T(8,128)(2,1)S(1)}, u32[]{:S(2)}, u32[]{:S(2)}) collective-permute-start(bf16[64,1024]{1,0:T(8,128)(2,1)S(1)} %broadcast_select_fusion.6), channel_id=1, source_target_pairs={{0,1},{1,0},{2,3},{3,2},{4,5},{5,4},{6,7},{7,6},{8,9},{9,8},{10,11... | collective-permute-start | bytes 393224 | tf_op jit(solution)/shard_map/ppermute | solution.py:556
  21.1 1.3 collective-permute-start.2
  22.4 4.0 %collective-permute-start.1 = (bf16[64,1024]{1,0:T(8,128)(2,1)S(1)}, bf16[64,1024]{1,0:T(8,128)(2,1)S(1)}, u32[]{:S(2)}, u32[]{:S(2)}) collective-permute-start(bf16[64,1024]{1,0:T(8,128)(2,1)S(1)} %get-tuple-element.59), channel_id=1, source_target_pairs={{0,8},{8,16},{16,24},{1,9},{9,17},{17,25},{2,10},{10,18},{18,26},{... | collective-permute-start | bytes 393224 | tf_op jit(solution)/shard_map/ppermute | solution.py:560
  26.4 2.8 %collective-permute-start.4 = (bf16[64,1024]{1,0:T(8,128)(2,1)S(1)}, bf16[64,1024]{1,0:T(8,128)(2,1)S(1)}, u32[]{:S(2)}, u32[]{:S(2)}) collective-permute-start(bf16[64,1024]{1,0:T(8,128)(2,1)S(1)} %get-tuple-element.60), channel_id=1, source_target_pairs={{2,0},{4,2},{6,4},{3,1},{5,3},{7,5},{10,8},{12,10},{14,12},{11,9},... | collective-permute-start | bytes 393224 | tf_op jit(solution)/shard_map/ppermute | solution.py:561
  29.2 3.0 %collective-permute-start.3 = (bf16[64,1024]{1,0:T(8,128)(2,1)S(1)}, bf16[64,1024]{1,0:T(8,128)(2,1)S(1)}, u32[]{:S(2)}, u32[]{:S(2)}) collective-permute-start(bf16[64,1024]{1,0:T(8,128)(2,1)S(1)} %get-tuple-element.61), channel_id=1, source_target_pairs={{0,2},{2,4},{4,6},{1,3},{3,5},{5,7},{8,10},{10,12},{12,14},{9,11},... | collective-permute-start | bytes 393224 | tf_op jit(solution)/shard_map/ppermute | solution.py:560
  34.2 3.4 %copy-done.2 = bf16[8,8,8,8192]{3,2,1,0:T(8,128)(2,1)S(1)} copy-done((bf16[8,8,8,8192]{3,2,1,0:T(8,128)(2,1)S(1)}, bf16[8,8,8,8192]{3,2,1,0:T(8,128)(2,1)}, u32[]{:S(2)}) %copy-start.2) | copy-done | bytes 8388632
  37.6 2.7 %shard_map.79 = (bf16[512,1024]{1,0:T(8,128)(2,1)S(1)}, f32[1280,128]{1,0:T(8,128)S(1)}, f32[3328,128]{1,0:T(8,128)S(1)}) custom-call(bf16[512,8192]{1,0:T(8,128)(2,1)S(1)} %bitcast.59, f32[512,128]{1,0:T(8,128)S(1)} %get-tuple-element.65.conduct_ref, f32[512,128]{1,0:T(8,128)S(1)} %get-tuple-element.66.grounds_ref, ...), custom_call_target="tpu_custom_call" | custom-call | tf_op jit(solution)/shard_map/pallas_call | solution.py:567
  42.1 2.1 dynamic-slice_bitcast_fusion
  45.4 5.6 %all-to-all-start = ((f32[16,40,128]{2,1,0:T(8,128)}), f32[16,40,128]{2,1,0:T(8,128)S(1)}, u32[]{:S(2)}, u32[]{:S(2)}) async-start(f32[16,40,128]{2,1,0:T(8,128)} %bitcast.41), calls=%async_computation | async-start | bytes 655360 | tf_op jit(solution)/shard_map/all_to_all | solution.py:594
  51.0 5.3 %shard_map.80 = bf16[1024,1024]{1,0:T(8,128)(2,1)} custom-call(s32[27]{0:T(128)S(1)} %stack.152.table_ref, bf16[512,8192]{1,0:T(8,128)(2,1)} %bitcast.53, bf16[512,4096]{1,0:T(8,128)(2,1)} %collective-permute-done.refs_1_, bf16[512,1024]{1,0:T(8,128)(2,1)S(1)} %get-tuple-element.78.refs_2_, bf16[512,1024]{1,0:T(8,128)(2,1)S(1)} %collective-permute-done.6.refs_3_), custom_call_target="tpu_custom_call" | custom-call | flops 2147483648 | bytes 8388608 | tf_op jit(solution)/shard_map/pallas_call | solution.py:348
  56.4 1.4 collective-permute-start.8
  57.7 5.3 %shard_map.81 = bf16[1024,1024]{1,0:T(8,128)(2,1)} custom-call(s32[27]{0:T(128)S(1)} %stack.152.table_ref, bf16[512,8192]{1,0:T(8,128)(2,1)} %bitcast.54, bf16[512,4096]{1,0:T(8,128)(2,1)} %collective-permute-done.refs_1_, bf16[512,1024]{1,0:T(8,128)(2,1)S(1)} %get-tuple-element.78.refs_2_, bf16[512,1024]{1,0:T(8,128)(2,1)S(1)} %collective-permute-done.6.refs_3_), custom_call_target="tpu_custom_call" | custom-call | flops 2147483648 | bytes 8388608 | tf_op jit(solution)/shard_map/pallas_call | solution.py:348
  65.0 4.4 %all-to-all-start.1 = ((f32[16,40,128]{2,1,0:T(8,128)}), f32[16,40,128]{2,1,0:T(8,128)S(1)}, u32[]{:S(2)}, u32[]{:S(2)}) async-start(f32[16,40,128]{2,1,0:T(8,128)} %broadcast_in_dim.35), calls=%async_computation.1 | async-start | bytes 655360 | tf_op jit(solution)/shard_map/all_to_all | solution.py:594
  69.4 2.4 bitcast_add_fusion
  71.8 5.7 %shard_map.84.refs_0_.refs_3_ = f32[1024,1024]{1,0:T(8,128)} custom-call(s32[27]{0:T(128)S(1)} %stack.152.table_ref, bf16[512,8192]{1,0:T(8,128)(2,1)} %bitcast.55, bf16[512,4096]{1,0:T(8,128)(2,1)} %collective-permute-done.refs_1_, bf16[512,1024]{1,0:T(8,128)(2,1)S(1)} %get-tuple-element.78.refs_2_, bf16[512,1024]{1,0:T(8,128)(2,1)S(1)} %collective-permute-done.6.refs_3_), custom_call_target="tpu_custom_call" | custom-call | flops 2147483648 | bytes 8388608 | tf_op jit(solution)/shard_map/pallas_call | solution.py:348
  77.6 5.7 %shard_map.82.refs_0_ = f32[1024,1024]{1,0:T(8,128)} custom-call(s32[27]{0:T(128)S(1)} %stack.152.table_ref, bf16[512,8192]{1,0:T(8,128)(2,1)} %bitcast.56, bf16[512,4096]{1,0:T(8,128)(2,1)} %collective-permute-done.refs_1_, bf16[512,1024]{1,0:T(8,128)(2,1)S(1)} %get-tuple-element.78.refs_2_, bf16[512,1024]{1,0:T(8,128)(2,1)S(1)} %collective-permute-done.6.refs_3_), custom_call_target="tpu_custom_call" | custom-call | flops 2147483648 | bytes 8388608 | tf_op jit(solution)/shard_map/pallas_call | solution.py:348
  83.3 29.5 %all-to-all-done.1 = f32[16,40,128]{2,1,0:T(8,128)S(1)} async-done(((f32[16,40,128]{2,1,0:T(8,128)}), f32[16,40,128]{2,1,0:T(8,128)S(1)}, u32[]{:S(2)}, u32[]{:S(2)}) %all-to-all-start.1) | async-done | bytes 327712 | tf_op jit(solution)/shard_map/all_to_all | solution.py:594
  112.8 5.3 %all-to-all-start.2 = ((f32[16,104,128]{2,1,0:T(8,128)}), f32[16,104,128]{2,1,0:T(8,128)S(1)}, u32[]{:S(2)}, u32[]{:S(2)}) async-start(f32[16,104,128]{2,1,0:T(8,128)} %bitcast.46), calls=%async_computation.2 | async-start | bytes 1703936 | tf_op jit(solution)/shard_map/all_to_all | solution.py:594
  118.1 2.4 collective-permute-start.13
  120.4 2.3 copy-done.4
  122.8 2.7 %shard_map.83 = bf16[512,1024]{1,0:T(8,128)(2,1)} custom-call(s32[27]{0:T(128)S(1)} %stack.152.table_ref, f32[1024,1024]{1,0:T(8,128)S(1)} %copy-done.4, bf16[1024,1024]{1,0:T(8,128)(2,1)} %collective-permute-done.8.refs_1_), custom_call_target="tpu_custom_call" | custom-call | flops 524288 | bytes 4194304 | tf_op jit(solution)/shard_map/pallas_call | solution.py:380
  125.5 2.7 %shard_map.85 = bf16[512,1024]{1,0:T(8,128)(2,1)} custom-call(s32[27]{0:T(128)S(1)} %stack.152.table_ref, f32[1024,1024]{1,0:T(8,128)S(1)} %copy-done.3, bf16[1024,1024]{1,0:T(8,128)(2,1)} %collective-permute-done.10.refs_1_.refs_4_), custom_call_target="tpu_custom_call" | custom-call | flops 524288 | bytes 4194304 | tf_op jit(solution)/shard_map/pallas_call | solution.py:380
  128.1 8.4 %all-to-all-done.2 = f32[16,104,128]{2,1,0:T(8,128)S(1)} async-done(((f32[16,104,128]{2,1,0:T(8,128)}), f32[16,104,128]{2,1,0:T(8,128)S(1)}, u32[]{:S(2)}, u32[]{:S(2)}) %all-to-all-start.2) | async-done | bytes 852000 | tf_op jit(solution)/shard_map/all_to_all | solution.py:594
  137.6 6.4 %all-to-all-start.3 = ((f32[16,104,128]{2,1,0:T(8,128)}), f32[16,104,128]{2,1,0:T(8,128)}, u32[]{:S(2)}, u32[]{:S(2)}) async-start(f32[16,104,128]{2,1,0:T(8,128)} %broadcast_in_dim.36), calls=%async_computation.3 | async-start | bytes 1703936 | tf_op jit(solution)/shard_map/all_to_all | solution.py:594
  144.1 1.4 collective-permute-start.11
  146.7 27.0 %shard_map.86.w0_ref = f32[512,512]{1,0:T(8,128)S(1)} custom-call(f32[1280,128]{1,0:T(8,128)S(1)} %pad_maximum_fusion.1.packed_ref), custom_call_target="tpu_custom_call" | custom-call | flops 12884901888 | bytes 2097152 | tf_op jit(solution)/shard_map/pallas_call | solution.py:148
  173.7 2.0 collective-permute-done.11.refs_5_
  175.6 2.4 collective-permute-done.9.refs_2_
  179.2 4.6 %shard_map.87 = (bf16[256,1024]{1,0:T(8,128)(2,1)S(1)}, bf16[256,1024]{1,0:T(8,128)(2,1)S(1)}, bf16[256,1024]{1,0:T(8,128)(2,1)S(1)}, bf16[256,1024]{1,0:T(8,128...) custom-call(s32[27]{0:T(128)S(1)} %stack.152.table_ref, f32[1024,1024]{1,0:T(8,128)} %shard_map.82.refs_0_, ...), custom_call_target="tpu_custom_call" | custom-call | bytes 14680064 | tf_op jit(solution)/shard_map/pallas_call | solution.py:422
  183.8 3.6 %collective-permute-start.14 = (bf16[256,1024]{1,0:T(8,128)(2,1)S(1)}, bf16[256,1024]{1,0:T(8,128)(2,1)S(1)}, u32[]{:S(2)}, u32[]{:S(2)}) collective-permute-start(bf16[256,1024]{1,0:T(8,128)(2,1)S(1)} %get-tuple-element.89), channel_id=1, source_target_pairs={{2,16},{6,20},{8,2},{10,18},{12,6},{14,22},{16,8},{18,24},{20,12},... | collective-permute-start | bytes 1572872 | tf_op jit(solution)/shard_map/ppermute | solution.py:654
  187.5 3.4 %collective-permute-start.15 = (bf16[256,1024]{1,0:T(8,128)(2,1)S(1)}, bf16[256,1024]{1,0:T(8,128)(2,1)S(1)}, u32[]{:S(2)}, u32[]{:S(2)}) collective-permute-start(bf16[256,1024]{1,0:T(8,128)(2,1)S(1)} %get-tuple-element.90), channel_id=1, source_target_pairs={{2,18},{6,22},{10,24},{14,28},{16,10},{18,26},{20,14},{22,30},{24,... | collective-permute-start | bytes 1572872 | tf_op jit(solution)/shard_map/ppermute | solution.py:654
  190.8 2.5 collective-permute-start.16
  193.3 2.7 %collective-permute-start.17 = (bf16[256,1024]{1,0:T(8,128)(2,1)S(1)}, bf16[256,1024]{1,0:T(8,128)(2,1)S(1)}, u32[]{:S(2)}, u32[]{:S(2)}) collective-permute-start(bf16[256,1024]{1,0:T(8,128)(2,1)S(1)} %get-tuple-element.92), channel_id=1, source_target_pairs={{0,10},{2,26},{4,14},{6,30},{8,0},{10,16},{12,4},{14,20},{16,2},{2... | collective-permute-start | bytes 1572872 | tf_op jit(solution)/shard_map/ppermute | solution.py:654
  196.4 1.5 broadcast_select_fusion.1
  198.0 28.8 %shard_map.88 = (f32[512,512]{1,0:T(8,128)S(1)}, f32[512,512]{1,0:T(8,128)S(1)}) custom-call(f32[3328,128]{1,0:T(8,128)S(1)} %pad_maximum_fusion.packed_ref, f32[512,512]{1,0:T(8,128)S(1)} %shard_map.86.w0_ref), custom_call_target="tpu_custom_call" | custom-call | flops 12884901888 | bytes 2097152 | tf_op jit(solution)/shard_map/pallas_call | solution.py:148
  226.9 7.8 %collective-permute-done.17.refs_3_ = bf16[256,1024]{1,0:T(8,128)(2,1)S(1)} collective-permute-done((bf16[256,1024]{1,0:T(8,128)(2,1)S(1)}, bf16[256,1024]{1,0:T(8,128)(2,1)S(1)}, u32[]{:S(2)}, u32[]{:S(2)}) %collective-permute-start.17) | collective-permute-done | bytes 524320 | tf_op jit(solution)/shard_map/ppermute | solution.py:654
  234.6 2.0 shard_map.89
  241.8 3.1 %shard_map.91 = (f32[256,256]{1,0:T(8,128)S(1)}, f32[256,256]{1,0:T(8,128)}, f32[256,256]{1,0:T(8,128)}, f32[256,256]{1,0:T(8,128)}) custom-call(s32[5]{0:T(128)S(1)} %concatenate.18.first_ref, f32[256,1024]{1,0:T(8,128)S(1)} %copy-done.7, f32[512,512]{1,0:T(8,128)S(1)} %shard_map.86.w0_ref, f32[512,512]{1,0:T(8,128)S(1)} %get-tuple-element.108.f_ref, ...), custom_call_target="tpu_custom_call" | custom-call | tf_op jit(solution)/shard_map/pallas_call | solution.py:689
  247.3 3.0 %collective-permute-done.21.refs_2_ = f32[256,256]{1,0:T(8,128)} collective-permute-done((f32[256,256]{1,0:T(8,128)}, f32[256,256]{1,0:T(8,128)}, u32[]{:S(2)}, u32[]{:S(2)}) %collective-permute-start.21) | collective-permute-done | bytes 262176 | tf_op jit(solution)/shard_map/ppermute | solution.py:678
  250.4 3.9 %collective-permute-done.22.refs_3_ = f32[256,256]{1,0:T(8,128)} collective-permute-done((f32[256,256]{1,0:T(8,128)}, f32[256,256]{1,0:T(8,128)}, u32[]{:S(2)}, u32[]{:S(2)}) %collective-permute-start.22) | collective-permute-done | bytes 262176 | tf_op jit(solution)/shard_map/ppermute | solution.py:678
  254.2 2.2 shard_map.90
  256.4 5.1 %collective-permute-done.24.refs_2_ = f32[256,256]{1,0:T(8,128)S(1)} collective-permute-done((f32[256,256]{1,0:T(8,128)}, f32[256,256]{1,0:T(8,128)S(1)}, u32[]{:S(2)}, u32[]{:S(2)}) %collective-permute-start.24) | collective-permute-done | bytes 262176 | tf_op jit(solution)/shard_map/ppermute | solution.py:678
  261.5 1.8 collective-permute-done.25.refs_3_
  263.3 1.6 shard_map.92
  (86 shorter events, 22.6 us)
Async XLA Ops:
  2.1 3.4 %copy-start = (bf16[8,8,8,8192]{3,2,1,0:T(8,128)(2,1)S(1)}, bf16[8,8,8,8192]{3,2,1,0:T(8,128)(2,1)}, u32[]{:S(2)}) copy-start(bf16[8,8,8,8192]{3,2,1,0:T(8,128)(2,1)} %param.6) | copy-start | bytes 25165828
  5.4 0.7 copy-start.10
  6.1 0.7 copy-start.11
  6.8 0.7 copy-start.12
  7.5 0.7 copy-start.13
  10.7 3.4 %copy-start.1 = (bf16[8,8,8,8192]{3,2,1,0:T(8,128)(2,1)S(1)}, bf16[8,8,8,8192]{3,2,1,0:T(8,128)(2,1)}, u32[]{:S(2)}) copy-start(bf16[8,8,8,8192]{3,2,1,0:T(8,128)(2,1)} %param.6) | copy-start | bytes 25165828
  18.3 32.7 %collective-permute-start = (bf16[512,4096]{1,0:T(8,128)(2,1)}, bf16[512,4096]{1,0:T(8,128)(2,1)}, u32[]{:S(2)}, u32[]{:S(2)}) collective-permute-start(bf16[512,4096]{1,0:T(8,128)(2,1)} %shard_map.78), channel_id=1, source_target_pairs={{0,2},{2,0},{1,3},{3,1},{4,6},{6,4},{5,7},{7,5},{8,10},{10,8},{9,1... | collective-permute-start | bytes 12582920 | tf_op jit(solution)/shard_map/ppermute | solution.py:562
  18.4 10.8 %collective-permute-start.5 = (bf16[64,1024]{1,0:T(8,128)(2,1)S(1)}, bf16[64,1024]{1,0:T(8,128)(2,1)S(1)}, u32[]{:S(2)}, u32[]{:S(2)}) collective-permute-start(bf16[64,1024]{1,0:T(8,128)(2,1)S(1)} %broadcast_select_fusion.6), channel_id=1, source_target_pairs={{0,1},{1,0},{2,3},{3,2},{4,5},{5,4},{6,7},{7,6},{8,9},{9,8},{10,11... | collective-permute-start | bytes 393224 | tf_op jit(solution)/shard_map/ppermute | solution.py:556
  21.1 11.1 %collective-permute-start.2 = (bf16[64,1024]{1,0:T(8,128)(2,1)S(1)}, bf16[64,1024]{1,0:T(8,128)(2,1)S(1)}, u32[]{:S(2)}, u32[]{:S(2)}) collective-permute-start(bf16[64,1024]{1,0:T(8,128)(2,1)S(1)} %get-tuple-element.58), channel_id=1, source_target_pairs={{8,0},{16,8},{24,16},{9,1},{17,9},{25,17},{10,2},{18,10},{26,18},{... | collective-permute-start | bytes 393224 | tf_op jit(solution)/shard_map/ppermute | solution.py:561
  22.4 9.9 %collective-permute-start.1 = (bf16[64,1024]{1,0:T(8,128)(2,1)S(1)}, bf16[64,1024]{1,0:T(8,128)(2,1)S(1)}, u32[]{:S(2)}, u32[]{:S(2)}) collective-permute-start(bf16[64,1024]{1,0:T(8,128)(2,1)S(1)} %get-tuple-element.59), channel_id=1, source_target_pairs={{0,8},{8,16},{16,24},{1,9},{9,17},{17,25},{2,10},{10,18},{18,26},{... | collective-permute-start | bytes 393224 | tf_op jit(solution)/shard_map/ppermute | solution.py:560
  26.4 6.5 %collective-permute-start.4 = (bf16[64,1024]{1,0:T(8,128)(2,1)S(1)}, bf16[64,1024]{1,0:T(8,128)(2,1)S(1)}, u32[]{:S(2)}, u32[]{:S(2)}) collective-permute-start(bf16[64,1024]{1,0:T(8,128)(2,1)S(1)} %get-tuple-element.60), channel_id=1, source_target_pairs={{2,0},{4,2},{6,4},{3,1},{5,3},{7,5},{10,8},{12,10},{14,12},{11,9},... | collective-permute-start | bytes 393224 | tf_op jit(solution)/shard_map/ppermute | solution.py:561
  29.2 5.0 %collective-permute-start.3 = (bf16[64,1024]{1,0:T(8,128)(2,1)S(1)}, bf16[64,1024]{1,0:T(8,128)(2,1)S(1)}, u32[]{:S(2)}, u32[]{:S(2)}) collective-permute-start(bf16[64,1024]{1,0:T(8,128)(2,1)S(1)} %get-tuple-element.61), channel_id=1, source_target_pairs={{0,2},{2,4},{4,6},{1,3},{3,5},{5,7},{8,10},{10,12},{12,14},{9,11},... | collective-permute-start | bytes 393224 | tf_op jit(solution)/shard_map/ppermute | solution.py:560
  34.2 3.4 %copy-start.2 = (bf16[8,8,8,8192]{3,2,1,0:T(8,128)(2,1)S(1)}, bf16[8,8,8,8192]{3,2,1,0:T(8,128)(2,1)}, u32[]{:S(2)}) copy-start(bf16[8,8,8,8192]{3,2,1,0:T(8,128)(2,1)} %param.6) | copy-start | bytes 25165828
  40.3 1.2 copy-start.5
  41.5 9.5 %collective-permute-start.6 = (bf16[512,1024]{1,0:T(8,128)(2,1)S(1)}, bf16[512,1024]{1,0:T(8,128)(2,1)S(1)}, u32[]{:S(2)}, u32[]{:S(2)}) collective-permute-start(bf16[512,1024]{1,0:T(8,128)(2,1)S(1)} %get-tuple-element.78.refs_2_), channel_id=1, source_target_pairs={{0,2},{2,0},{1,3},{3,1},{4,6},{6,4},{5,7},{7,5},{8,10},{10,8},{9,1... | collective-permute-start | bytes 3145736 | tf_op jit(solution)/shard_map/ppermute | solution.py:581
  41.5 3.1 %collective-permute-start.7 = (f32[640,128]{1,0:T(8,128)S(1)}, f32[640,128]{1,0:T(8,128)S(1)}, u32[]{:S(2)}, u32[]{:S(2)}) collective-permute-start(f32[640,128]{1,0:T(8,128)S(1)} %dynamic-slice_bitcast_fusion.1), channel_id=1, source_target_pairs={{0,2},{2,0},{1,3},{3,1},{4,6},{6,4},{5,7},{7,5},{8,10},{10,8},{9,1... | collective-permute-start | bytes 983048 | tf_op jit(solution)/shard_map/ppermute | solution.py:590
  44.2 25.2 %collective-permute-start.12 = (f32[1664,128]{1,0:T(8,128)}, f32[1664,128]{1,0:T(8,128)}, u32[]{:S(2)}, u32[]{:S(2)}) collective-permute-start(f32[1664,128]{1,0:T(8,128)} %dynamic-slice_bitcast_fusion), channel_id=1, source_target_pairs={{0,2},{2,0},{1,3},{3,1},{4,6},{6,4},{5,7},{7,5},{8,10},{10,8},{9,1... | collective-permute-start | bytes 2555912 | tf_op jit(solution)/shard_map/ppermute | solution.py:590
  45.4 18.8 %all-to-all-start = ((f32[16,40,128]{2,1,0:T(8,128)}), f32[16,40,128]{2,1,0:T(8,128)S(1)}, u32[]{:S(2)}, u32[]{:S(2)}) async-start(f32[16,40,128]{2,1,0:T(8,128)} %bitcast.41), calls=%async_computation | async-start | bytes 655360 | tf_op jit(solution)/shard_map/all_to_all | solution.py:594
  56.4 64.1 %collective-permute-start.8 = (bf16[1024,1024]{1,0:T(8,128)(2,1)}, bf16[1024,1024]{1,0:T(8,128)(2,1)}, u32[]{:S(2)}, u32[]{:S(2)}) collective-permute-start(bf16[1024,1024]{1,0:T(8,128)(2,1)} %shard_map.80), channel_id=1, source_target_pairs={{0,1},{1,0},{2,3},{3,2},{4,5},{5,4},{6,7},{7,6},{8,9},{9,8},{10,11... | collective-permute-start | bytes 6291464 | tf_op jit(solution)/shard_map/ppermute | solution.py:524
  63.1 62.4 %collective-permute-start.10 = (bf16[1024,1024]{1,0:T(8,128)(2,1)}, bf16[1024,1024]{1,0:T(8,128)(2,1)}, u32[]{:S(2)}, u32[]{:S(2)}) collective-permute-start(bf16[1024,1024]{1,0:T(8,128)(2,1)} %shard_map.81), channel_id=1, source_target_pairs={{0,4},{4,0},{1,5},{5,1},{2,6},{6,2},{3,7},{7,3},{8,12},{12,8},{9,1... | collective-permute-start | bytes 6291464 | tf_op jit(solution)/shard_map/ppermute | solution.py:524
  65.0 47.8 %all-to-all-start.1 = ((f32[16,40,128]{2,1,0:T(8,128)}), f32[16,40,128]{2,1,0:T(8,128)S(1)}, u32[]{:S(2)}, u32[]{:S(2)}) async-start(f32[16,40,128]{2,1,0:T(8,128)} %broadcast_in_dim.35), calls=%async_computation.1 | async-start | bytes 655360 | tf_op jit(solution)/shard_map/all_to_all | solution.py:594
  112.8 23.7 %all-to-all-start.2 = ((f32[16,104,128]{2,1,0:T(8,128)}), f32[16,104,128]{2,1,0:T(8,128)S(1)}, u32[]{:S(2)}, u32[]{:S(2)}) async-start(f32[16,104,128]{2,1,0:T(8,128)} %bitcast.46), calls=%async_computation.2 | async-start | bytes 1703936 | tf_op jit(solution)/shard_map/all_to_all | solution.py:594
  118.1 25.9 %collective-permute-start.13 = (f32[640,128]{1,0:T(8,128)S(1)}, f32[640,128]{1,0:T(8,128)S(1)}, u32[]{:S(2)}, u32[]{:S(2)}) collective-permute-start(f32[640,128]{1,0:T(8,128)S(1)} %bitcast.66), channel_id=1, source_target_pairs={{0,2},{2,0},{1,3},{3,1},{4,6},{6,4},{5,7},{7,5},{8,10},{10,8},{9,1... | collective-permute-start | bytes 983048 | tf_op jit(solution)/shard_map/ppermute | solution.py:444
  120.4 5.0 %copy-start.3 = (f32[1024,1024]{1,0:T(8,128)S(1)}, f32[1024,1024]{1,0:T(8,128)}, u32[]{:S(2)}) copy-start(f32[1024,1024]{1,0:T(8,128)} %shard_map.84.refs_0_.refs_3_) | copy-start | bytes 12582916
  120.4 2.3 copy-start.4
  137.6 40.5 %all-to-all-start.3 = ((f32[16,104,128]{2,1,0:T(8,128)}), f32[16,104,128]{2,1,0:T(8,128)}, u32[]{:S(2)}, u32[]{:S(2)}) async-start(f32[16,104,128]{2,1,0:T(8,128)} %broadcast_in_dim.36), calls=%async_computation.3 | async-start | bytes 1703936 | tf_op jit(solution)/shard_map/all_to_all | solution.py:594
  144.1 31.5 %collective-permute-start.11 = (bf16[512,1024]{1,0:T(8,128)(2,1)}, bf16[512,1024]{1,0:T(8,128)(2,1)S(1)}, u32[]{:S(2)}, u32[]{:S(2)}) collective-permute-start(bf16[512,1024]{1,0:T(8,128)(2,1)} %shard_map.85), channel_id=1, source_target_pairs={{0,1},{1,0},{2,3},{3,2},{4,5},{5,4},{6,7},{7,6},{8,9},{9,8},{10,11... | collective-permute-start | bytes 3145736 | tf_op jit(solution)/shard_map/ppermute | solution.py:524
  145.5 32.5 %collective-permute-start.9 = (bf16[512,1024]{1,0:T(8,128)(2,1)}, bf16[512,1024]{1,0:T(8,128)(2,1)S(1)}, u32[]{:S(2)}, u32[]{:S(2)}) collective-permute-start(bf16[512,1024]{1,0:T(8,128)(2,1)} %shard_map.83), channel_id=1, source_target_pairs={{0,4},{4,0},{1,5},{5,1},{2,6},{6,2},{3,7},{7,3},{8,12},{12,8},{9,1... | collective-permute-start | bytes 3145736 | tf_op jit(solution)/shard_map/ppermute | solution.py:524
  178.0 18.0 %collective-permute-start.19 = (f32[1664,128]{1,0:T(8,128)}, f32[1664,128]{1,0:T(8,128)}, u32[]{:S(2)}, u32[]{:S(2)}) collective-permute-start(f32[1664,128]{1,0:T(8,128)} %bitcast.47), channel_id=1, source_target_pairs={{0,2},{2,0},{1,3},{3,1},{4,6},{6,4},{5,7},{7,5},{8,10},{10,8},{9,1... | collective-permute-start | bytes 2555912 | tf_op jit(solution)/shard_map/ppermute | solution.py:444
  183.8 43.0 %collective-permute-start.14 = (bf16[256,1024]{1,0:T(8,128)(2,1)S(1)}, bf16[256,1024]{1,0:T(8,128)(2,1)S(1)}, u32[]{:S(2)}, u32[]{:S(2)}) collective-permute-start(bf16[256,1024]{1,0:T(8,128)(2,1)S(1)} %get-tuple-element.89), channel_id=1, source_target_pairs={{2,16},{6,20},{8,2},{10,18},{12,6},{14,22},{16,8},{18,24},{20,12},... | collective-permute-start | bytes 1572872 | tf_op jit(solution)/shard_map/ppermute | solution.py:654
  187.5 39.4 %collective-permute-start.15 = (bf16[256,1024]{1,0:T(8,128)(2,1)S(1)}, bf16[256,1024]{1,0:T(8,128)(2,1)S(1)}, u32[]{:S(2)}, u32[]{:S(2)}) collective-permute-start(bf16[256,1024]{1,0:T(8,128)(2,1)S(1)} %get-tuple-element.90), channel_id=1, source_target_pairs={{2,18},{6,22},{10,24},{14,28},{16,10},{18,26},{20,14},{22,30},{24,... | collective-permute-start | bytes 1572872 | tf_op jit(solution)/shard_map/ppermute | solution.py:654
  190.8 36.0 %collective-permute-start.16 = (bf16[256,1024]{1,0:T(8,128)(2,1)S(1)}, bf16[256,1024]{1,0:T(8,128)(2,1)S(1)}, u32[]{:S(2)}, u32[]{:S(2)}) collective-permute-start(bf16[256,1024]{1,0:T(8,128)(2,1)S(1)} %get-tuple-element.91), channel_id=1, source_target_pairs={{0,8},{2,24},{4,12},{6,28},{10,26},{14,30},{16,0},{20,4},{24,2},{2... | collective-permute-start | bytes 1572872 | tf_op jit(solution)/shard_map/ppermute | solution.py:654
  193.3 41.3 %collective-permute-start.17 = (bf16[256,1024]{1,0:T(8,128)(2,1)S(1)}, bf16[256,1024]{1,0:T(8,128)(2,1)S(1)}, u32[]{:S(2)}, u32[]{:S(2)}) collective-permute-start(bf16[256,1024]{1,0:T(8,128)(2,1)S(1)} %get-tuple-element.92), channel_id=1, source_target_pairs={{0,10},{2,26},{4,14},{6,30},{8,0},{10,16},{12,4},{14,20},{16,2},{2... | collective-permute-start | bytes 1572872 | tf_op jit(solution)/shard_map/ppermute | solution.py:654
  196.1 38.5 %collective-permute-start.18 = (f32[256,1024]{1,0:T(8,128)S(1)}, f32[256,1024]{1,0:T(8,128)S(1)}, u32[]{:S(2)}, u32[]{:S(2)}) collective-permute-start(f32[256,1024]{1,0:T(8,128)S(1)} %get-tuple-element.93), channel_id=1, source_target_pairs={{0,2},{2,0},{1,3},{3,1},{4,6},{6,4},{5,7},{7,5},{8,10},{10,8},{9,1... | collective-permute-start | bytes 3145736 | tf_op jit(solution)/shard_map/ppermute | solution.py:655
  236.6 1.0 copy-start.6
  237.6 0.7 copy-start.14
  238.3 0.7 copy-start.15
  239.0 8.3 %collective-permute-start.20 = (f32[256,256]{1,0:T(8,128)}, f32[256,256]{1,0:T(8,128)}, u32[]{:S(2)}, u32[]{:S(2)}) collective-permute-start(f32[256,256]{1,0:T(8,128)} %get-tuple-element.104), channel_id=1, source_target_pairs={{0,2},{2,4},{4,6},{6,0},{1,3},{3,5},{5,7},{7,1},{8,10},{10,12},{12... | collective-permute-start | bytes 786440 | tf_op jit(solution)/shard_map/ppermute | solution.py:678
  239.0 11.3 %collective-permute-start.21 = (f32[256,256]{1,0:T(8,128)}, f32[256,256]{1,0:T(8,128)}, u32[]{:S(2)}, u32[]{:S(2)}) collective-permute-start(f32[256,256]{1,0:T(8,128)} %copy-done.15), channel_id=1, source_target_pairs={{0,4},{2,6},{4,0},{6,2},{1,5},{3,7},{5,1},{7,3},{8,12},{10,14},{12... | collective-permute-start | bytes 786440 | tf_op jit(solution)/shard_map/ppermute | solution.py:678
  239.8 14.4 %collective-permute-start.22 = (f32[256,256]{1,0:T(8,128)}, f32[256,256]{1,0:T(8,128)}, u32[]{:S(2)}, u32[]{:S(2)}) collective-permute-start(f32[256,256]{1,0:T(8,128)} %copy-done.14), channel_id=1, source_target_pairs={{0,6},{2,0},{4,2},{6,4},{1,7},{3,1},{5,3},{7,5},{8,14},{10,8},{12,... | collective-permute-start | bytes 786440 | tf_op jit(solution)/shard_map/ppermute | solution.py:678
  240.6 1.2 copy-start.7
  244.9 0.7 copy-start.8
  245.6 17.8 %copy-start.9 = (f32[256,256]{1,0:T(8,128)S(1)}, f32[256,256]{1,0:T(8,128)}, u32[]{:S(2)}) copy-start(f32[256,256]{1,0:T(8,128)} %copy-done.8) | copy-start | bytes 786436
  245.6 10.8 %collective-permute-start.23 = (f32[256,256]{1,0:T(8,128)}, f32[256,256]{1,0:T(8,128)S(1)}, u32[]{:S(2)}, u32[]{:S(2)}) collective-permute-start(f32[256,256]{1,0:T(8,128)} %get-tuple-element.111), channel_id=1, source_target_pairs={{0,2},{2,4},{4,6},{6,0},{1,3},{3,5},{5,7},{7,1},{8,10},{10,12},{12... | collective-permute-start | bytes 786440 | tf_op jit(solution)/shard_map/ppermute | solution.py:678
  246.5 15.0 %collective-permute-start.24 = (f32[256,256]{1,0:T(8,128)}, f32[256,256]{1,0:T(8,128)S(1)}, u32[]{:S(2)}, u32[]{:S(2)}) collective-permute-start(f32[256,256]{1,0:T(8,128)} %get-tuple-element.112), channel_id=1, source_target_pairs={{0,4},{2,6},{4,0},{6,2},{1,5},{3,7},{5,1},{7,3},{8,12},{10,14},{12... | collective-permute-start | bytes 786440 | tf_op jit(solution)/shard_map/ppermute | solution.py:678
  247.2 16.1 %collective-permute-start.25 = (f32[256,256]{1,0:T(8,128)}, f32[256,256]{1,0:T(8,128)S(1)}, u32[]{:S(2)}, u32[]{:S(2)}) collective-permute-start(f32[256,256]{1,0:T(8,128)} %get-tuple-element.113), channel_id=1, source_target_pairs={{0,6},{2,0},{4,2},{6,4},{1,7},{3,1},{5,3},{7,5},{8,14},{10,8},{12,... | collective-permute-start | bytes 786440 | tf_op jit(solution)/shard_map/ppermute | solution.py:678

commit v4 on v3

--- a/solution.py
+++ b/solution.py
@@ -129,19 +129,30 @@
     factor_inverse(w_ref, d_ref)
 
 
-def factor_kernel(first_ref, rows_ref, w0_ref, f_ref, w1_ref, *refs):
-    blocks, all_ref = refs[:-1], refs[-1]
+def factor_kernel(table_ref, own_ref, swapped_ref, *refs, at):
+    home_at, order_at, first_at = at
+    cols = own_ref.shape[1]
+    *ins, rows_ref, all_ref = refs
+    count = cols // ins[-1].shape[2]
+    ins, blocks = ins[:-count], ins[-count:]
+    *ins, w0_ref, f_ref, w1_ref = ins
+    total = jnp.where(table_ref[home_at] != 0, own_ref[...], swapped_ref[...])
+    for got in ins:
+        total = total + got[...].astype(jnp.float32)
+    rows_ref[...] = total
     nb = w0_ref.shape[0]
-    ids = first_ref[0] + lax.broadcasted_iota(jnp.int32, (rows_ref.shape[0], nb), 0)
-    cols = lax.broadcasted_iota(jnp.int32, (rows_ref.shape[0], nb), 1)
+    ids = table_ref[first_at] + lax.broadcasted_iota(jnp.int32, (rows_ref.shape[0], nb), 0)
+    columns = lax.broadcasted_iota(jnp.int32, (rows_ref.shape[0], nb), 1)
     part = dot3(rows_ref[:, :nb], w0_ref[...], ((1,), (1,)))
     rest = rows_ref[:, nb:] - dot3(part, f_ref[...], ((1,), (1,)))
     rest = dot3(rest, w1_ref[...], ((1,), (1,)))
-    all_ref[:, :nb] = jnp.where(cols <= ids, part, 0.0)
-    all_ref[:, nb:] = jnp.where(cols + nb <= ids, rest, 0.0)
+    all_ref[:, :nb] = jnp.where(columns <= ids, part, 0.0)
+    all_ref[:, nb:] = jnp.where(columns + nb <= ids, rest, 0.0)
     for d, block in enumerate(blocks):
-        width = block.shape[1]
-        block[...] = all_ref[:, pl.ds(pl.multiple_of(first_ref[1 + d] * width, width), width)]
+        width = block.shape[2]
+        span = pl.ds(pl.multiple_of(table_ref[order_at + d] * width, width), width)
+        block[0] = rows_ref[:, span]
+        block[1] = all_ref[:, span]
 
 
 def panel_call(kernel, outputs, nb, *operands):
@@ -153,7 +164,7 @@
         scratch_shapes=[pltpu.VMEM((LEAF, LEAF), jnp.float32)],
         compiler_params=pltpu.CompilerParams(vmem_limit_bytes=24 * 2**20),
         cost_estimate=pl.CostEstimate(
-            flops=24 * nb**3 * 4, transcendentals=0, bytes_accessed=8 * nb * nb
+            flops=nb, transcendentals=0, bytes_accessed=nb
         ),
     )(*operands)
 
@@ -168,6 +179,10 @@
 
 def whole(memory=pltpu.VMEM):
     return pl.BlockSpec(memory_space=memory)
+
+
+def block_of(array, memory=pltpu.VMEM):
+    return pl.BlockSpec(array.shape, lambda *_: (0,) * array.ndim, memory_space=memory)
 
 
 def faces_kernel(cond_ref, ground_ref, info_ref, cells_ref, load_ref, panel_ref, *refs, sides):
@@ -216,8 +231,9 @@
             out[:, lanes] = face.astype(jnp.bfloat16)
 
 
-def image_kernel(panel_ref, conduct_ref, grounds_ref, *refs, sides, nb):
-    halos, (image_ref, first_ref, later_ref, scaled_ref, square_ref) = refs[:6], refs[6:]
+def image_kernel(table_ref, panel_ref, conduct_ref, grounds_ref, *refs, sides, nb, at):
+    halos, (image_ref, *lead_refs, scaled_ref, square_ref) = refs[:6], refs[6:]
+    core = table_ref[at]
     size_x, size_y, size_z = sides
     width = panel_ref.shape[1]
     plane = size_y * size_z
@@ -277,23 +293,38 @@
 
     blocks = nb // LEAF
 
-    def lower(out_ref):
-        at = 0
+    def put_block(refs, number, value):
+        half = refs[0].shape[0] // LEAF
+        rows = slice(number % half * LEAF, (number % half + 1) * LEAF)
+        kept = core == number // half
+
+        @pl.when(kept)
+        def _():
+            refs[0][rows, :] = value
+
+        @pl.when(jnp.logical_not(kept))
+        def _():
+            refs[1][rows, :] = value
+
+    def lower(refs):
+        number = 0
         for i in range(blocks):
             for j in range(i + 1):
                 row, col = slice(i * LEAF, (i + 1) * LEAF), slice(j * LEAF, (j + 1) * LEAF)
-                out_ref[at : at + LEAF, :] = 0.5 * (square_ref[row, col] + square_ref[col, row].T)
-                at += LEAF
-        return at
+                put_block(refs, number, 0.5 * (square_ref[row, col] + square_ref[col, row].T))
+                number += 1
+        return number
 
     head, tail = slice(0, nb), slice(nb, 2 * nb)
     square_ref[...] = product(head, head)
-    lower(first_ref)
+    lower(lead_refs[:2])
     square_ref[...] = product(tail, tail)
-    at = lower(later_ref)
-    below = product(tail, head)
-    for i in range(blocks):
-        later_ref[at + i * nb : at + (i + 1) * nb, :] = below[:, i * LEAF : (i + 1) * LEAF]
+    number = lower(lead_refs[2:])
+    square_ref[...] = product(tail, head)
+    for j in range(blocks):
+        for i in range(blocks):
+            row, col = slice(i * LEAF, (i + 1) * LEAF), slice(j * LEAF, (j + 1) * LEAF)
+            put_block(lead_refs[2:], number + j * blocks + i, square_ref[row, col])
 
 
 def copy_kernel(table_ref, in_ref, out_ref):
@@ -303,7 +334,7 @@
 
 def take_columns(table, at, array, width):
     rows = array.shape[0]
-    tile = min(64, rows)
+    tile = min(128, rows)
     return pl.pallas_call(
         copy_kernel,
         grid_spec=pltpu.PrefetchScalarGridSpec(
@@ -313,7 +344,7 @@
             out_specs=pl.BlockSpec((tile, width), lambda t, tab: (t, 0)),
         ),
         out_shape=jax.ShapeDtypeStruct((rows, width), array.dtype),
-        compiler_params=pltpu.CompilerParams(vmem_limit_bytes=32 * 2**20),
+        compiler_params=pltpu.CompilerParams(vmem_limit_bytes=58 * 2**20),
         cost_estimate=pl.CostEstimate(
             flops=0, transcendentals=0, bytes_accessed=4 * rows * width
         ),
@@ -446,23 +477,13 @@
     return jnp.concatenate([jnp.where(first, half, other), jnp.where(first, other, half)], 0)
 
 
-def join_kernel(place_ref, *refs):
-    out = refs[-1]
-    part = refs[0].shape[0]
-    for d, block in enumerate(refs[:-1]):
-        out[pl.ds(pl.multiple_of(place_ref[d] * part, part), part), :] = block[...]
-
-
-def sums_kernel(home_ref, own_ref, swapped_ref, *refs):
-    cols, width = own_ref.shape[1], refs[-1].shape[1]
-    ins, rows_ref, blocks = refs[: -1 - cols // width], refs[-1 - cols // width], refs[-(cols // width) :]
-    total = jnp.where(home_ref[0] != 0, own_ref[...], swapped_ref[...])
-    for got in ins:
-        total = total + got[...].astype(jnp.float32)
-    rows_ref[...] = total
-    for d, block in enumerate(blocks):
-        at = pl.multiple_of(home_ref[1 + d] * width, width)
-        block[...] = rows_ref[:, pl.ds(at, width)]
+def join_kernel(table_ref, *refs, at):
+    ins, outs = refs[:-2], refs[-2:]
+    part = ins[0].shape[1]
+    for d, block in enumerate(ins):
+        rows = pl.ds(pl.multiple_of(table_ref[at + d] * part, part), part)
+        for i, out in enumerate(outs):
+            out[rows, :] = block[i]
 
 
 def local(basis, classes, cond_table, ground_table, port_cells, port_load):
@@ -517,13 +538,19 @@
     leaving = [(at_x + step) % devices_x for step in range(devices_x)]
     leaving_at, _ = put(leaving + [at_x % spans * 2 + core, at_x % spans * 2 + 1 - core])
     given_at, _ = put([1 - core])
+    core_at, _ = put([core])
+    places_at, _ = put([(at_y - d) % devices_y for d in range(devices_y)])
+    order_at, _ = put([(at_y + d) % devices_y for d in range(devices_y)])
+    home_at, _ = put([at_x // spans == core])
+    first_at, _ = put([((at_x * devices_z + at_z) * devices_y + at_y) * part])
     table = jnp.stack([jnp.asarray(e, jnp.int32) for e in entries])
 
     def move(array, axis, d):
         size = lax.axis_size(axis)
         return lax.ppermute(array, axis, [(i, (i + d) % size) for i in range(size)])
 
-    panel_spec = pl.BlockSpec((count, cols), lambda i: (0, 0))
+    panel_spec = pl.BlockSpec((count, cols), lambda *_: (0, 0))
+    port_rows, load_rows = port_cells[None, :], port_load[None, :]
     global_x = at_x * cells_x + jnp.arange(cells_x, dtype=jnp.int32)
     global_y = at_y * cells_y + jnp.arange(cells_y, dtype=jnp.int32)
     global_z = at_z * cells_z + jnp.arange(cells_z, dtype=jnp.int32)
@@ -534,16 +561,18 @@
     )
     info = jnp.stack([classes, flat_ids], -1).reshape(count, 2)
     face_rows = [cells_y * cells_z] * 2 + [cells_x * cells_z] * 2 + [cells_x * cells_y] * 2
+    outs = [jax.ShapeDtypeStruct((n, cols), bf16) for n in face_rows]
+    outs += [jax.ShapeDtypeStruct((count, LEAF), f32)] * 2
     *faces, conduct, grounds = pl.pallas_call(
         functools.partial(faces_kernel, sides=sides),
-        out_shape=[jax.ShapeDtypeStruct((n, cols), bf16) for n in face_rows]
-        + [jax.ShapeDtypeStruct((count, LEAF), f32)] * 2,
+        out_shape=outs,
         grid=(1,),
-        in_specs=[whole(pltpu.SMEM)] * 2 + [whole()] * 3 + [panel_spec],
-        out_specs=[whole()] * 8,
+        in_specs=[block_of(cond_table, pltpu.SMEM), block_of(ground_table, pltpu.SMEM)]
+        + [block_of(info), block_of(port_rows), block_of(load_rows), panel_spec],
+        out_specs=[block_of(a) for a in outs],
         scratch_shapes=[pltpu.VMEM((cols // LEAF, count, LEAF), f32)],
-        compiler_params=pltpu.CompilerParams(vmem_limit_bytes=24 * 2**20),
-    )(cond_table, ground_table, info, port_cells[None, :], port_load[None, :], flat_basis)
+        compiler_params=pltpu.CompilerParams(vmem_limit_bytes=58 * 2**20),
+    )(cond_table, ground_table, info, port_rows, load_rows, flat_basis)
     later_table, _ = lax.optimization_barrier((table, faces))
     given = take_columns(later_table, given_at, flat_basis, width_k // 2)
     halos = []
@@ -564,40 +593,39 @@
     blocks = NB // LEAF
     lower_rows = blocks * (blocks + 1) // 2 * LEAF
     halos, _ = lax.optimization_barrier((halos, given))
-    image, first_rows, later_rows = pl.pallas_call(
-        functools.partial(image_kernel, sides=sides, nb=NB),
-        out_shape=[
-            jax.ShapeDtypeStruct((count, cols), bf16),
-            jax.ShapeDtypeStruct((lower_rows, LEAF), f32),
-            jax.ShapeDtypeStruct((lower_rows + blocks * NB, LEAF), f32),
-        ],
-        grid=(1,),
-        in_specs=[panel_spec] + [whole()] * 8,
-        out_specs=[whole()] * 3,
-        scratch_shapes=[pltpu.VMEM((count, LEAF), f32), pltpu.VMEM((NB, NB), f32)],
-        compiler_params=pltpu.CompilerParams(vmem_limit_bytes=32 * 2**20),
-    )(flat_basis, conduct, grounds, *halos)
+    first_part = jax.ShapeDtypeStruct((lower_rows // 2, LEAF), f32)
+    later_part = jax.ShapeDtypeStruct(((lower_rows + blocks * NB) // 2, LEAF), f32)
+    lead_parts = [first_part] * 2 + [later_part] * 2
+    outs = [jax.ShapeDtypeStruct((count, cols), bf16), *lead_parts]
+    image, first_kept, first_sent, later_kept, later_sent = pl.pallas_call(
+        functools.partial(image_kernel, sides=sides, nb=NB, at=core_at),
+        out_shape=outs,
+        grid_spec=pltpu.PrefetchScalarGridSpec(
+            num_scalar_prefetch=1,
+            grid=(1,),
+            in_specs=[panel_spec] + [block_of(a) for a in (conduct, grounds, *halos)],
+            out_specs=[block_of(a) for a in outs],
+            scratch_shapes=[pltpu.VMEM((count, LEAF), f32), pltpu.VMEM((NB, NB), f32)],
+        ),
+        compiler_params=pltpu.CompilerParams(vmem_limit_bytes=58 * 2**20),
+    )(table, flat_basis, conduct, grounds, *halos)
 
     other_image = lax.ppermute(image, "core", swap_pairs())
 
     axes = ("gx", "gy", "gz")
     chips = devices_x * chips_y * devices_z
 
-    def halved(rows):
-        both = rows.reshape(2, -1, LEAF)
-        kept = lax.dynamic_index_in_dim(both, core, 0, keepdims=False)
-        sent = lax.dynamic_index_in_dim(both, 1 - core, 0, keepdims=False)
+    def halved(kept, sent):
         return kept + lax.ppermute(sent, "core", swap_pairs())
 
     def exchanged(rows):
         rows = rows.reshape(chips, -1, LEAF)
         return lax.all_to_all(rows, axes, split_axis=0, concat_axis=0, tiled=True)
 
-    def spread(terms):
-        own = jnp.sum(terms, axis=0)
-        return own, exchanged(jnp.broadcast_to(own, terms.shape)).reshape(-1, LEAF)
-
-    first_half, later_half = halved(first_rows), halved(later_rows)
+    def for_all(own):
+        return jnp.broadcast_to(own, (chips, *own.shape))
+
+    first_half, later_half = halved(first_kept, first_sent), halved(later_kept, later_sent)
     first_terms = exchanged(first_half)
 
     def chip_products(images, lists, dtype):
@@ -609,22 +637,22 @@
     got_a = [move(a, "gz", d) for d, a in enumerate(sent_a, 1)]
     got_b = [move(a, "gy", d) for d, a in enumerate(sent_b, 1)]
     first_terms, _ = lax.optimization_barrier((first_terms, (sent_a, sent_b)))
-    own, first_half = spread(first_terms)
+    own = jnp.sum(first_terms, axis=0)
+    share = own.shape[0]
     images, _ = lax.optimization_barrier((images, own))
     own_a, own_b = (chip_products(images, lists[0], f32) for lists in (lists_a, lists_b))
-    first_half, later_half, _ = lax.optimization_barrier((first_half, later_half, (own_a, own_b)))
-    first_rows = other_half(first_half, core)
-    later_half, _ = lax.optimization_barrier((later_half, first_half))
-    later_terms = exchanged(later_half)
+    both = jnp.concatenate([for_all(own), later_half.reshape(chips, -1, LEAF)], 1)
+    both = lax.all_to_all(both, axes, split_axis=0, concat_axis=0, tiled=True)
+    both, _ = lax.optimization_barrier((both, (own_a, own_b)))
     sums_a, sums_b = [own_a, *got_a], [own_b, *got_b]
 
     further_a = [add_blocks(table, sums_a, *next_a[d], narrow, bf16) for d in range(1, chips_y)]
     further_b = [add_blocks(table, sums_b, *next_b[d], narrow, bf16) for d in range(1, devices_z)]
-    later_terms, _ = lax.optimization_barrier((later_terms, (further_a, further_b)))
+    both, _ = lax.optimization_barrier((both, (further_a, further_b)))
     further_a = [move(a, "gy", d) for d, a in enumerate(further_a, 1)]
     further_b = [move(a, "gz", d) for d, a in enumerate(further_b, 1)]
-    own, later_half = spread(later_terms)
-    first_rows, _ = lax.optimization_barrier((first_rows, own))
+    first_rows = other_half(both[:, :share].reshape(-1, LEAF), core)
+    later_half = exchanged(for_all(jnp.sum(both[:, share:], axis=0))).reshape(-1, LEAF)
     inverse_0 = first_panel(first_rows, NB)
     (further_a, further_b, later_half), inverse_0 = lax.optimization_barrier(
         ((further_a, further_b, later_half), inverse_0)
@@ -653,48 +681,38 @@
                     pairs.append((x * devices_y + y, dest_x * devices_y + dest_y))
         x_got.append(lax.ppermute(x_sent[step], ("gx", "gy", "core"), pairs))
     swapped = lax.ppermute(swapped, "core", swap_pairs())
-    home = at_x // spans == core
     later_rows, _ = lax.optimization_barrier((later_rows, x_sent))
     factor_10, inverse_1 = next_panel(later_rows, inverse_0)
     (x_got, swapped), inverse_1 = lax.optimization_barrier(((x_got, swapped), inverse_1))
-    by_blocks = [jax.ShapeDtypeStruct((part, cols // devices_y), f32)] * devices_y
-    order = jnp.stack([(at_y + d) % devices_y for d in range(devices_y)])
-    home = jnp.concatenate([home.astype(jnp.int32)[None], order])
-    rows, *reduced = pl.pallas_call(
-        sums_kernel,
-        out_shape=[jax.ShapeDtypeStruct((part, cols), f32), *by_blocks],
-        in_specs=[whole(pltpu.SMEM)] + [whole()] * (devices_x + 2),
-        out_specs=[whole()] * (1 + devices_y),
-        compiler_params=pltpu.CompilerParams(vmem_limit_bytes=32 * 2**20),
-    )(home, own, swapped, *x_got)
-
-    block = jax.ShapeDtypeStruct((devices_y * part, cols // devices_y), f32)
-    places = jnp.stack([(at_y - d) % devices_y for d in range(devices_y)])
-
-    def to_columns(blocks):
-        got = [blocks[0]]
-        for d in range(1, devices_y):
-            pairs = [(i, (i + d) % devices_y) for i in range(devices_y)]
-            got.append(lax.ppermute(blocks[d], ("gy", "core"), pairs))
-        return pl.pallas_call(
-            join_kernel,
-            out_shape=block,
-            in_specs=[whole(pltpu.SMEM)] + [whole()] * devices_y,
-            out_specs=whole(),
-            compiler_params=pltpu.CompilerParams(vmem_limit_bytes=24 * 2**20),
-        )(places, *got)
-
-    reduced = to_columns(reduced)
-    first_row = ((at_x * devices_z + at_z) * devices_y + at_y) * part
-    factor = pl.pallas_call(
-        factor_kernel,
-        out_shape=by_blocks,
-        in_specs=[whole(pltpu.SMEM)] + [whole()] * 4,
-        out_specs=[whole()] * devices_y,
-        scratch_shapes=[pltpu.VMEM((part, cols), f32)],
-        compiler_params=pltpu.CompilerParams(vmem_limit_bytes=32 * 2**20),
-    )(jnp.concatenate([first_row[None], order]), rows, inverse_0, factor_10, inverse_1)
-    return (reduced, to_columns(factor))
+    pair = jax.ShapeDtypeStruct((2, part, cols // devices_y), f32)
+    ins = [own, swapped, *x_got, inverse_0, factor_10, inverse_1]
+    pairs = list(pl.pallas_call(
+        functools.partial(factor_kernel, at=(home_at, order_at, first_at)),
+        out_shape=[pair] * devices_y,
+        grid_spec=pltpu.PrefetchScalarGridSpec(
+            num_scalar_prefetch=1,
+            grid=(1,),
+            in_specs=[block_of(a) for a in ins],
+            out_specs=[block_of(pair)] * devices_y,
+            scratch_shapes=[pltpu.VMEM((part, cols), f32)] * 2,
+        ),
+        compiler_params=pltpu.CompilerParams(vmem_limit_bytes=44 * 2**20),
+    )(table, *ins))
+    for d in range(1, devices_y):
+        route = [(i, (i + d) % devices_y) for i in range(devices_y)]
+        pairs[d] = lax.ppermute(pairs[d], ("gy", "core"), route)
+    out = jax.ShapeDtypeStruct((devices_y * part, cols // devices_y), f32)
+    return pl.pallas_call(
+        functools.partial(join_kernel, at=places_at),
+        out_shape=(out, out),
+        grid_spec=pltpu.PrefetchScalarGridSpec(
+            num_scalar_prefetch=1,
+            grid=(1,),
+            in_specs=[block_of(a) for a in pairs],
+            out_specs=[block_of(out)] * 2,
+        ),
+        compiler_params=pltpu.CompilerParams(vmem_limit_bytes=44 * 2**20),
+    )(table, *pairs)
 
 
 def solution(mesh):

time: 266 us -> 269 us (1.011)
  waiting for transfers between devices: 66.1 us -> 81.6 us
  local copies, waits for them, and re-layouts: 25.9 us -> 13.9 us
  starting transfers between devices: 60.4 us -> 54.9 us
  other arithmetic: 5.28 us -> 8.01 us
    ppermute x4, waiting for transfers between devices: 4.34 us -> 44.5 us  [move(): return lax.ppermute(array, axis, [(i, (i + d) % size) for i in range(size)])]
    all_to_all x4 -> x2, waiting for transfers between devices: 37.9 us -> 0.01 us  [exchanged(): return lax.all_to_all(rows, axes, split_axis=0, concat_axis=0, tiled=True)]
    unnamed x32 -> x40, local copies, waits for them, and re-layouts: 20.7 us -> 9.4 us
    all_to_all x4 -> x2, starting transfers between devices: 21.7 us -> 11.8 us  [exchanged(): return lax.all_to_all(rows, axes, split_axis=0, concat_axis=0, tiled=True)]
    ppermute x6 -> x3, waiting for transfers between devices: 13.9 us -> 22.6 us  [local(): pairs[d] = lax.ppermute(pairs[d], ('gy', 'core'), route)]
    all_to_all x0 -> x1, starting transfers between devices: none -> 6.36 us  [local(): both = lax.all_to_all(both, axes, split_axis=0, concat_axis=0, tiled=True)]
    pallas_call x6 -> x4, Pallas kernels: 13.9 us -> 17.8 us  [the longest x1 9.15 us: local(): pl.pallas_call(functools.partial(image_kernel, sides=sides, nb=NB, at=cor...]
    ppermute x2, waiting for transfers between devices: 0.4 us -> 4.05 us  [halved(): return kept + lax.ppermute(sent, 'core', swap_pairs())]
  transfers between devices with their start and end apart: 30 -> 26, of which waited for: 12 -> 8; matrix products, arithmetic and copies ran while one was open for 3% -> 2% of each run, Pallas kernels for 36% -> 35%
where the time goes in v4:
time: 269 us; the launch traced here: 268 us
  Pallas kernels  108 us (40%)
  waiting for transfers between devices  81.6 us (30%)
  starting transfers between devices  54.9 us (20%)
  local copies, waits for them, and re-layouts  13.9 us (5%)
  other arithmetic  8.01 us (3%)
    pallas_call x2, Pallas kernels, panel_call(): pl.pallas_call(kernel, out_shape=[jax.ShapeDtypeStruct((nb, nb), jnp.floa...  55.8 us
    ppermute x4, waiting for transfers between devices, move(): return lax.ppermute(array, axis, [(i, (i + d) % size) for i in range(size)])  44.5 us
    ppermute x3, waiting for transfers between devices, local(): pairs[d] = lax.ppermute(pairs[d], ('gy', 'core'), route)  22.6 us
    pallas_call x4, Pallas kernels, products(): pl.pallas_call(products_kernel, grid_spec=pltpu.PrefetchScalarGridSpec(nu...  20.5 us
    ppermute x4, starting transfers between devices, local(): x_got.append(lax.ppermute(x_sent[step], ('gx', 'gy', 'core'), pairs))  12.2 us
    all_to_all x2, starting transfers between devices, exchanged(): return lax.all_to_all(rows, axes, split_axis=0, concat_axis=0, tiled=True)  11.8 us
    unnamed x40, local copies, waits for them, and re-layouts  9.4 us
    pallas_call x1, Pallas kernels, local(): pl.pallas_call(functools.partial(image_kernel, sides=sides, nb=NB, at=cor...  9.15 us
  transfers between devices with their start and end apart: 26, of which 8 were waited for; matrix products, arithmetic and copies ran while one was open for 2% of the time, Pallas kernels for 35%

profile of v4, /device:TPU:1, one launch (start us, length us, event | category | flops | bytes accessed | tf_op | source)
XLA Modules:
  0.0 267.5 jit_solution(3752912369232674976)
XLA Ops:
  2.8 4.0 %shard_map.77 = (bf16[64,1024]{1,0:T(8,128)(2,1)}, bf16[64,1024]{1,0:T(8,128)(2,1)}, bf16[64,1024]{1,0:T(8,128)(2,1)}, bf16[64,1024]{1,0:T(8,128)(2,1)}, bf16[64...) custom-call(f32[16]{0:T(128)} %cond_ref.1, f32[16]{0:T(128)} %ground_ref.1, ...), custom_call_target="tpu_custom_call" | custom-call | tf_op jit(solution)/shard_map/pallas_call | solution.py:566
  7.6 5.6 %shard_map.78 = bf16[512,4096]{1,0:T(8,128)(2,1)} custom-call(s32[38]{0:T(128)} %stack.163.table_ref, bf16[512,8192]{1,0:T(8,128)(2,1)} %bitcast.47), custom_call_target="tpu_custom_call" | custom-call | bytes 8388608 | tf_op jit(solution)/shard_map/pallas_call | solution.py:338
  13.3 2.7 %collective-permute-start.5 = (bf16[64,1024]{1,0:T(8,128)(2,1)S(1)}, bf16[64,1024]{1,0:T(8,128)(2,1)S(1)}, u32[]{:S(2)}, u32[]{:S(2)}) collective-permute-start(bf16[64,1024]{1,0:T(8,128)(2,1)S(1)} %broadcast_select_fusion.6), channel_id=1, source_target_pairs={{0,1},{1,0},{2,3},{3,2},{4,5},{5,4},{6,7},{7,6},{8,9},{9,8},{10,11... | collective-permute-start | bytes 393224 | tf_op jit(solution)/shard_map/ppermute | solution.py:585
  16.0 1.3 collective-permute-start.2
  17.3 4.0 %collective-permute-start.1 = (bf16[64,1024]{1,0:T(8,128)(2,1)S(1)}, bf16[64,1024]{1,0:T(8,128)(2,1)S(1)}, u32[]{:S(2)}, u32[]{:S(2)}) collective-permute-start(bf16[64,1024]{1,0:T(8,128)(2,1)S(1)} %copy-done.18), channel_id=1, source_target_pairs={{0,8},{8,16},{16,24},{1,9},{9,17},{17,25},{2,10},{10,18},{18,26},{... | collective-permute-start | bytes 393224 | tf_op jit(solution)/shard_map/ppermute | solution.py:589
  21.4 2.8 %collective-permute-start.4 = (bf16[64,1024]{1,0:T(8,128)(2,1)S(1)}, bf16[64,1024]{1,0:T(8,128)(2,1)S(1)}, u32[]{:S(2)}, u32[]{:S(2)}) collective-permute-start(bf16[64,1024]{1,0:T(8,128)(2,1)S(1)} %copy-done.17), channel_id=1, source_target_pairs={{2,0},{4,2},{6,4},{3,1},{5,3},{7,5},{10,8},{12,10},{14,12},{11,9},... | collective-permute-start | bytes 393224 | tf_op jit(solution)/shard_map/ppermute | solution.py:590
  24.1 3.0 %collective-permute-start.3 = (bf16[64,1024]{1,0:T(8,128)(2,1)S(1)}, bf16[64,1024]{1,0:T(8,128)(2,1)S(1)}, u32[]{:S(2)}, u32[]{:S(2)}) collective-permute-start(bf16[64,1024]{1,0:T(8,128)(2,1)S(1)} %copy-done.16), channel_id=1, source_target_pairs={{0,2},{2,4},{4,6},{1,3},{3,5},{5,7},{8,10},{10,12},{12,14},{9,11},... | collective-permute-start | bytes 393224 | tf_op jit(solution)/shard_map/ppermute | solution.py:589
  28.0 1.2 collective-permute-done.3.refs_2_
  29.8 9.1 %shard_map.79 = (bf16[512,1024]{1,0:T(8,128)(2,1)}, f32[640,128]{1,0:T(8,128)}, f32[640,128]{1,0:T(8,128)}, f32[1664,128]{1,0:T(8,128)}, f32[1664,128]{1,0:T(8,128)}) custom-call(s32[38]{0:T(128)} %stack.163.table_ref, bf16[512,8192]{1,0:T(8,128)(2,1)} %bitcast.48, f32[512,128]{1,0:T(8,128)} %get-tuple-element.59.conduct_ref, ...), custom_call_target="tpu_custom_call" | custom-call | tf_op jit(solution)/shard_map/pallas_call | solution.py:600
  39.4 4.0 %collective-permute-done.7 = f32[640,128]{1,0:T(8,128)S(1)} collective-permute-done((f32[640,128]{1,0:T(8,128)}, f32[640,128]{1,0:T(8,128)S(1)}, u32[]{:S(2)}, u32[]{:S(2)}) %collective-permute-start.7) | collective-permute-done | bytes 327712 | tf_op jit(solution)/shard_map/ppermute | solution.py:619
  43.5 1.8 add.270
  45.3 5.7 %all-to-all-start = ((f32[16,40,128]{2,1,0:T(8,128)}), f32[16,40,128]{2,1,0:T(8,128)S(1)}, u32[]{:S(2)}, u32[]{:S(2)}) async-start(f32[16,40,128]{2,1,0:T(8,128)} %bitcast.40), calls=%async_computation | async-start | bytes 655360 | tf_op jit(solution)/shard_map/all_to_all | solution.py:623
  51.9 1.5 add.271
  53.4 4.4 %shard_map.81 = bf16[1024,1024]{1,0:T(8,128)(2,1)S(1)} custom-call(s32[38]{0:T(128)S(1)} %copy-done.8, bf16[512,8192]{1,0:T(8,128)(2,1)} %bitcast.49, bf16[512,4096]{1,0:T(8,128)(2,1)} %collective-permute-done.refs_1_, bf16[512,1024]{1,0:T(8,128)(2,1)S(1)} %copy-done.2, bf16[512,1024]{1,0:T(8,128)(2,1)S(1)} %collective-permute-done.6.refs_3_), custom_call_target="tpu_custom_call" | custom-call | flops 2147483648 | bytes 8388608 | tf_op jit(solution)/shard_map/pallas_call | solution.py:379
  57.9 1.3 copy-done.6
  59.2 4.4 %shard_map.80 = bf16[1024,1024]{1,0:T(8,128)(2,1)S(1)} custom-call(s32[38]{0:T(128)S(1)} %copy-done.8, bf16[512,8192]{1,0:T(8,128)(2,1)} %bitcast.50, bf16[512,4096]{1,0:T(8,128)(2,1)} %collective-permute-done.refs_1_, bf16[512,1024]{1,0:T(8,128)(2,1)S(1)} %copy-done.2, bf16[512,1024]{1,0:T(8,128)(2,1)S(1)} %collective-permute-done.6.refs_3_), custom_call_target="tpu_custom_call" | custom-call | flops 2147483648 | bytes 8388608 | tf_op jit(solution)/shard_map/pallas_call | solution.py:379
  63.6 1.3 copy-done.7
  66.1 6.4 %all-to-all-start.1 = ((f32[16,144,128]{2,1,0:T(8,128)}), f32[16,144,128]{2,1,0:T(8,128)}, u32[]{:S(2)}, u32[]{:S(2)}) async-start(f32[16,144,128]{2,1,0:T(8,128)} %pad_maximum_fusion.1), calls=%async_computation.1 | async-start | bytes 2359296 | tf_op jit(solution)/shard_map/all_to_all | solution.py:645
  72.4 1.3 collective-permute-start.8
  73.8 1.2 collective-permute-start.10
  75.0 5.8 %shard_map.84.refs_0_.refs_3_ = f32[1024,1024]{1,0:T(8,128)} custom-call(s32[38]{0:T(128)S(1)} %copy-done.8, bf16[512,8192]{1,0:T(8,128)(2,1)} %bitcast.51, bf16[512,4096]{1,0:T(8,128)(2,1)} %collective-permute-done.refs_1_, bf16[512,1024]{1,0:T(8,128)(2,1)S(1)} %copy-done.2, bf16[512,1024]{1,0:T(8,128)(2,1)S(1)} %collective-permute-done.6.refs_3_), custom_call_target="tpu_custom_call" | custom-call | flops 2147483648 | bytes 8388608 | tf_op jit(solution)/shard_map/pallas_call | solution.py:379
  80.8 5.8 %shard_map.82.refs_0_ = f32[1024,1024]{1,0:T(8,128)} custom-call(s32[38]{0:T(128)S(1)} %copy-done.8, bf16[512,8192]{1,0:T(8,128)(2,1)} %bitcast.52, bf16[512,4096]{1,0:T(8,128)(2,1)} %collective-permute-done.refs_1_, bf16[512,1024]{1,0:T(8,128)(2,1)S(1)} %copy-done.2, bf16[512,1024]{1,0:T(8,128)(2,1)S(1)} %collective-permute-done.6.refs_3_), custom_call_target="tpu_custom_call" | custom-call | flops 2147483648 | bytes 8388608 | tf_op jit(solution)/shard_map/pallas_call | solution.py:379
  86.6 44.5 %collective-permute-done.8.refs_1_ = bf16[1024,1024]{1,0:T(8,128)(2,1)S(1)} collective-permute-done((bf16[1024,1024]{1,0:T(8,128)(2,1)}, bf16[1024,1024]{1,0:T(8,128)(2,1)S(1)}, u32[]{:S(2)}, u32[]{:S(2)}) %collective-permute-start.8) | collective-permute-done | bytes 2097184 | tf_op jit(solution)/shard_map/ppermute | solution.py:550
  131.0 2.2 copy-done.1
  133.2 1.6 shard_map.83
  134.9 1.6 copy-done
  136.6 1.6 shard_map.85
  138.2 1.3 copy-done.5
  139.5 1.2 slice_reduce_fusion
  141.7 6.1 %all-to-all-start.2 = ((f32[16,104,128]{2,1,0:T(8,128)}), f32[16,104,128]{2,1,0:T(8,128)}, u32[]{:S(2)}, u32[]{:S(2)}) async-start(f32[16,104,128]{2,1,0:T(8,128)} %broadcast_in_dim.25), calls=%async_computation.2 | async-start | bytes 1703936 | tf_op jit(solution)/shard_map/all_to_all | solution.py:623
  147.8 1.4 collective-permute-start.11
  149.2 1.2 collective-permute-start.9
  151.4 2.5 collective-permute-start.13
  153.9 1.3 collective-permute-done.13
  155.3 27.0 %shard_map.86.w0_ref.refs_4_ = f32[512,512]{1,0:T(8,128)S(1)} custom-call(f32[1280,128]{1,0:T(8,128)S(1)} %pad_maximum_fusion.2.packed_ref), custom_call_target="tpu_custom_call" | custom-call | flops 512 | bytes 512 | tf_op jit(solution)/shard_map/pallas_call | solution.py:159
  183.0 4.9 %shard_map.87 = (bf16[256,1024]{1,0:T(8,128)(2,1)S(1)}, bf16[256,1024]{1,0:T(8,128)(2,1)S(1)}, bf16[256,1024]{1,0:T(8,128)(2,1)S(1)}, bf16[256,1024]{1,0:T(8,128...) custom-call(s32[38]{0:T(128)S(1)} %copy-done.8, f32[1024,1024]{1,0:T(8,128)} %shard_map.82.refs_0_, ...), custom_call_target="tpu_custom_call" | custom-call | bytes 14680064 | tf_op jit(solution)/shard_map/pallas_call | solution.py:453
  188.0 3.8 %collective-permute-start.14 = (bf16[256,1024]{1,0:T(8,128)(2,1)S(1)}, bf16[256,1024]{1,0:T(8,128)(2,1)S(1)}, u32[]{:S(2)}, u32[]{:S(2)}) collective-permute-start(bf16[256,1024]{1,0:T(8,128)(2,1)S(1)} %get-tuple-element.82), channel_id=1, source_target_pairs={{2,16},{6,20},{8,2},{10,18},{12,6},{14,22},{16,8},{18,24},{20,12},... | collective-permute-start | bytes 1572872 | tf_op jit(solution)/shard_map/ppermute | solution.py:682
  191.8 3.2 %collective-permute-start.15 = (bf16[256,1024]{1,0:T(8,128)(2,1)S(1)}, bf16[256,1024]{1,0:T(8,128)(2,1)S(1)}, u32[]{:S(2)}, u32[]{:S(2)}) collective-permute-start(bf16[256,1024]{1,0:T(8,128)(2,1)S(1)} %get-tuple-element.83), channel_id=1, source_target_pairs={{2,18},{6,22},{10,24},{14,28},{16,10},{18,26},{20,14},{22,30},{24,... | collective-permute-start | bytes 1572872 | tf_op jit(solution)/shard_map/ppermute | solution.py:682
  194.9 2.4 collective-permute-start.16
  197.3 2.8 %collective-permute-start.17 = (bf16[256,1024]{1,0:T(8,128)(2,1)S(1)}, bf16[256,1024]{1,0:T(8,128)(2,1)S(1)}, u32[]{:S(2)}, u32[]{:S(2)}) collective-permute-start(bf16[256,1024]{1,0:T(8,128)(2,1)S(1)} %get-tuple-element.85), channel_id=1, source_target_pairs={{0,10},{2,26},{4,14},{6,30},{8,0},{10,16},{12,4},{14,20},{16,2},{2... | collective-permute-start | bytes 1572872 | tf_op jit(solution)/shard_map/ppermute | solution.py:682
  200.4 1.3 broadcast_select_fusion.1
  201.8 28.8 %shard_map.88 = (f32[512,512]{1,0:T(8,128)S(1)}, f32[512,512]{1,0:T(8,128)S(1)}) custom-call(f32[3328,128]{1,0:T(8,128)S(1)} %pad_maximum_fusion.packed_ref, f32[512,512]{1,0:T(8,128)S(1)} %shard_map.86.w0_ref.refs_4_), custom_call_target="tpu_custom_call" | custom-call | flops 512 | bytes 512 | tf_op jit(solution)/shard_map/pallas_call | solution.py:159
  230.7 8.0 %collective-permute-done.17.refs_3_ = bf16[256,1024]{1,0:T(8,128)(2,1)S(1)} collective-permute-done((bf16[256,1024]{1,0:T(8,128)(2,1)S(1)}, bf16[256,1024]{1,0:T(8,128)(2,1)S(1)}, u32[]{:S(2)}, u32[]{:S(2)}) %collective-permute-start.17) | collective-permute-done | bytes 524320 | tf_op jit(solution)/shard_map/ppermute | solution.py:682
  238.6 2.6 shard_map.89
  242.9 8.3 %collective-permute-done.20.refs_1_ = f32[2,256,256]{2,1,0:T(8,128)S(1)} collective-permute-done((f32[2,256,256]{2,1,0:T(8,128)S(1)}, f32[2,256,256]{2,1,0:T(8,128)S(1)}, u32[]{:S(2)}, u32[]{:S(2)}) %collective-permute-start.20) | collective-permute-done | bytes 524320 | tf_op jit(solution)/shard_map/ppermute | solution.py:703
  251.2 12.7 %collective-permute-done.21.refs_2_ = f32[2,256,256]{2,1,0:T(8,128)S(1)} collective-permute-done((f32[2,256,256]{2,1,0:T(8,128)S(1)}, f32[2,256,256]{2,1,0:T(8,128)S(1)}, u32[]{:S(2)}, u32[]{:S(2)}) %collective-permute-start.21) | collective-permute-done | bytes 524320 | tf_op jit(solution)/shard_map/ppermute | solution.py:703
  263.8 1.7 collective-permute-done.22.refs_3_
  265.5 2.0 shard_map.90
  (81 shorter events, 11.6 us)
Async XLA Ops:
  7.6 5.7 %copy-start.14 = (bf16[64,1024]{1,0:T(8,128)(2,1)S(1)}, bf16[64,1024]{1,0:T(8,128)(2,1)}, u32[]{:S(2)}) copy-start(bf16[64,1024]{1,0:T(8,128)(2,1)} %get-tuple-element.56) | copy-start | bytes 393220
  7.6 5.7 %copy-start.15 = (bf16[64,1024]{1,0:T(8,128)(2,1)S(1)}, bf16[64,1024]{1,0:T(8,128)(2,1)}, u32[]{:S(2)}) copy-start(bf16[64,1024]{1,0:T(8,128)(2,1)} %get-tuple-element.57) | copy-start | bytes 393220
  7.6 8.5 %copy-start.19 = (bf16[64,1024]{1,0:T(8,128)(2,1)S(1)}, bf16[64,1024]{1,0:T(8,128)(2,1)}, u32[]{:S(2)}) copy-start(bf16[64,1024]{1,0:T(8,128)(2,1)} %get-tuple-element.52) | copy-start | bytes 393220
  7.6 9.7 %copy-start.18 = (bf16[64,1024]{1,0:T(8,128)(2,1)S(1)}, bf16[64,1024]{1,0:T(8,128)(2,1)}, u32[]{:S(2)}) copy-start(bf16[64,1024]{1,0:T(8,128)(2,1)} %get-tuple-element.53) | copy-start | bytes 393220
  7.6 13.8 %copy-start.17 = (bf16[64,1024]{1,0:T(8,128)(2,1)S(1)}, bf16[64,1024]{1,0:T(8,128)(2,1)}, u32[]{:S(2)}) copy-start(bf16[64,1024]{1,0:T(8,128)(2,1)} %get-tuple-element.54) | copy-start | bytes 393220
  7.6 16.5 %copy-start.16 = (bf16[64,1024]{1,0:T(8,128)(2,1)S(1)}, bf16[64,1024]{1,0:T(8,128)(2,1)}, u32[]{:S(2)}) copy-start(bf16[64,1024]{1,0:T(8,128)(2,1)} %get-tuple-element.55) | copy-start | bytes 393220
  13.2 40.2 %collective-permute-start = (bf16[512,4096]{1,0:T(8,128)(2,1)}, bf16[512,4096]{1,0:T(8,128)(2,1)}, u32[]{:S(2)}, u32[]{:S(2)}) collective-permute-start(bf16[512,4096]{1,0:T(8,128)(2,1)} %shard_map.78), channel_id=1, source_target_pairs={{0,2},{2,0},{1,3},{3,1},{4,6},{6,4},{5,7},{7,5},{8,10},{10,8},{9,1... | collective-permute-start | bytes 12582920 | tf_op jit(solution)/shard_map/ppermute | solution.py:591
  13.3 10.8 %collective-permute-start.5 = (bf16[64,1024]{1,0:T(8,128)(2,1)S(1)}, bf16[64,1024]{1,0:T(8,128)(2,1)S(1)}, u32[]{:S(2)}, u32[]{:S(2)}) collective-permute-start(bf16[64,1024]{1,0:T(8,128)(2,1)S(1)} %broadcast_select_fusion.6), channel_id=1, source_target_pairs={{0,1},{1,0},{2,3},{3,2},{4,5},{5,4},{6,7},{7,6},{8,9},{9,8},{10,11... | collective-permute-start | bytes 393224 | tf_op jit(solution)/shard_map/ppermute | solution.py:585
  16.0 11.9 %collective-permute-start.2 = (bf16[64,1024]{1,0:T(8,128)(2,1)S(1)}, bf16[64,1024]{1,0:T(8,128)(2,1)S(1)}, u32[]{:S(2)}, u32[]{:S(2)}) collective-permute-start(bf16[64,1024]{1,0:T(8,128)(2,1)S(1)} %copy-done.19), channel_id=1, source_target_pairs={{8,0},{16,8},{24,16},{9,1},{17,9},{25,17},{10,2},{18,10},{26,18},{... | collective-permute-start | bytes 393224 | tf_op jit(solution)/shard_map/ppermute | solution.py:590
  17.3 10.6 %collective-permute-start.1 = (bf16[64,1024]{1,0:T(8,128)(2,1)S(1)}, bf16[64,1024]{1,0:T(8,128)(2,1)S(1)}, u32[]{:S(2)}, u32[]{:S(2)}) collective-permute-start(bf16[64,1024]{1,0:T(8,128)(2,1)S(1)} %copy-done.18), channel_id=1, source_target_pairs={{0,8},{8,16},{16,24},{1,9},{9,17},{17,25},{2,10},{10,18},{18,26},{... | collective-permute-start | bytes 393224 | tf_op jit(solution)/shard_map/ppermute | solution.py:589
  21.4 6.6 %collective-permute-start.4 = (bf16[64,1024]{1,0:T(8,128)(2,1)S(1)}, bf16[64,1024]{1,0:T(8,128)(2,1)S(1)}, u32[]{:S(2)}, u32[]{:S(2)}) collective-permute-start(bf16[64,1024]{1,0:T(8,128)(2,1)S(1)} %copy-done.17), channel_id=1, source_target_pairs={{2,0},{4,2},{6,4},{3,1},{5,3},{7,5},{10,8},{12,10},{14,12},{11,9},... | collective-permute-start | bytes 393224 | tf_op jit(solution)/shard_map/ppermute | solution.py:590
  24.1 5.0 %collective-permute-start.3 = (bf16[64,1024]{1,0:T(8,128)(2,1)S(1)}, bf16[64,1024]{1,0:T(8,128)(2,1)S(1)}, u32[]{:S(2)}, u32[]{:S(2)}) collective-permute-start(bf16[64,1024]{1,0:T(8,128)(2,1)S(1)} %copy-done.16), channel_id=1, source_target_pairs={{0,2},{2,4},{4,6},{1,3},{3,5},{5,7},{8,10},{10,12},{12,14},{9,11},... | collective-permute-start | bytes 393224 | tf_op jit(solution)/shard_map/ppermute | solution.py:589
  27.9 1.2 copy-start.10
  27.9 1.2 copy-start.11
  28.0 1.2 copy-start.12
  29.1 0.6 copy-start.13
  38.9 14.5 %collective-permute-start.6 = (bf16[512,1024]{1,0:T(8,128)(2,1)}, bf16[512,1024]{1,0:T(8,128)(2,1)S(1)}, u32[]{:S(2)}, u32[]{:S(2)}) collective-permute-start(bf16[512,1024]{1,0:T(8,128)(2,1)} %get-tuple-element.73.refs_2_), channel_id=1, source_target_pairs={{0,2},{2,0},{1,3},{3,1},{4,6},{6,4},{5,7},{7,5},{8,10},{10,8},{9,1... | collective-permute-start | bytes 3145736 | tf_op jit(solution)/shard_map/ppermute | solution.py:613
  38.9 12.0 %collective-permute-start.12 = (f32[1664,128]{1,0:T(8,128)}, f32[1664,128]{1,0:T(8,128)S(1)}, u32[]{:S(2)}, u32[]{:S(2)}) collective-permute-start(f32[1664,128]{1,0:T(8,128)} %get-tuple-element.76), channel_id=1, source_target_pairs={{0,2},{2,0},{1,3},{3,1},{4,6},{6,4},{5,7},{7,5},{8,10},{10,8},{9,1... | collective-permute-start | bytes 2555912 | tf_op jit(solution)/shard_map/ppermute | solution.py:619
  39.4 4.0 %collective-permute-start.7 = (f32[640,128]{1,0:T(8,128)}, f32[640,128]{1,0:T(8,128)S(1)}, u32[]{:S(2)}, u32[]{:S(2)}) collective-permute-start(f32[640,128]{1,0:T(8,128)} %get-tuple-element.69), channel_id=1, source_target_pairs={{0,2},{2,0},{1,3},{3,1},{4,6},{6,4},{5,7},{7,5},{8,10},{10,8},{9,1... | collective-permute-start | bytes 983048 | tf_op jit(solution)/shard_map/ppermute | solution.py:619
  45.3 8.1 %copy-start.2 = (bf16[512,1024]{1,0:T(8,128)(2,1)S(1)}, bf16[512,1024]{1,0:T(8,128)(2,1)}, u32[]{:S(2)}) copy-start(bf16[512,1024]{1,0:T(8,128)(2,1)} %get-tuple-element.73.refs_2_) | copy-start | bytes 3145732
  45.3 8.2 %copy-start.8 = (s32[38]{0:T(128)S(1)}, s32[38]{0:T(128)}, u32[]{:S(2)}) copy-start(s32[38]{0:T(128)} %stack.163.table_ref) | copy-start | bytes 460
  45.3 19.6 %all-to-all-start = ((f32[16,40,128]{2,1,0:T(8,128)}), f32[16,40,128]{2,1,0:T(8,128)S(1)}, u32[]{:S(2)}, u32[]{:S(2)}) async-start(f32[16,40,128]{2,1,0:T(8,128)} %bitcast.40), calls=%async_computation | async-start | bytes 655360 | tf_op jit(solution)/shard_map/all_to_all | solution.py:623
  51.0 0.9 copy-start.9
  57.9 1.3 copy-start.6
  63.6 1.3 copy-start.7
  66.1 73.4 %all-to-all-start.1 = ((f32[16,144,128]{2,1,0:T(8,128)}), f32[16,144,128]{2,1,0:T(8,128)}, u32[]{:S(2)}, u32[]{:S(2)}) async-start(f32[16,144,128]{2,1,0:T(8,128)} %pad_maximum_fusion.1), calls=%async_computation.1 | async-start | bytes 2359296 | tf_op jit(solution)/shard_map/all_to_all | solution.py:645
  72.4 58.6 %collective-permute-start.8 = (bf16[1024,1024]{1,0:T(8,128)(2,1)}, bf16[1024,1024]{1,0:T(8,128)(2,1)S(1)}, u32[]{:S(2)}, u32[]{:S(2)}) collective-permute-start(bf16[1024,1024]{1,0:T(8,128)(2,1)} %copy-done.7), channel_id=1, source_target_pairs={{0,1},{1,0},{2,3},{3,2},{4,5},{5,4},{6,7},{7,6},{8,9},{9,8},{10,11... | collective-permute-start | bytes 6291464 | tf_op jit(solution)/shard_map/ppermute | solution.py:550
  73.8 61.1 %collective-permute-start.10 = (bf16[1024,1024]{1,0:T(8,128)(2,1)}, bf16[1024,1024]{1,0:T(8,128)(2,1)S(1)}, u32[]{:S(2)}, u32[]{:S(2)}) collective-permute-start(bf16[1024,1024]{1,0:T(8,128)(2,1)} %copy-done.6), channel_id=1, source_target_pairs={{0,4},{4,0},{1,5},{5,1},{2,6},{6,2},{3,7},{7,3},{8,12},{12,8},{9,1... | collective-permute-start | bytes 6291464 | tf_op jit(solution)/shard_map/ppermute | solution.py:550
  131.0 2.2 copy-start.1
  133.2 1.7 copy-start.3
  133.2 3.3 %copy-start = (f32[1024,1024]{1,0:T(8,128)S(1)}, f32[1024,1024]{1,0:T(8,128)}, u32[]{:S(2)}) copy-start(f32[1024,1024]{1,0:T(8,128)} %shard_map.84.refs_0_.refs_3_) | copy-start | bytes 12582916
  138.2 1.3 copy-start.5
  141.7 40.7 %all-to-all-start.2 = ((f32[16,104,128]{2,1,0:T(8,128)}), f32[16,104,128]{2,1,0:T(8,128)}, u32[]{:S(2)}, u32[]{:S(2)}) async-start(f32[16,104,128]{2,1,0:T(8,128)} %broadcast_in_dim.25), calls=%async_computation.2 | async-start | bytes 1703936 | tf_op jit(solution)/shard_map/all_to_all | solution.py:623
  147.8 34.5 %collective-permute-start.11 = (bf16[512,1024]{1,0:T(8,128)(2,1)}, bf16[512,1024]{1,0:T(8,128)(2,1)}, u32[]{:S(2)}, u32[]{:S(2)}) collective-permute-start(bf16[512,1024]{1,0:T(8,128)(2,1)} %shard_map.85), channel_id=1, source_target_pairs={{0,1},{1,0},{2,3},{3,2},{4,5},{5,4},{6,7},{7,6},{8,9},{9,8},{10,11... | collective-permute-start | bytes 3145736 | tf_op jit(solution)/shard_map/ppermute | solution.py:550
  149.2 33.2 %collective-permute-start.9 = (bf16[512,1024]{1,0:T(8,128)(2,1)}, bf16[512,1024]{1,0:T(8,128)(2,1)}, u32[]{:S(2)}, u32[]{:S(2)}) collective-permute-start(bf16[512,1024]{1,0:T(8,128)(2,1)} %shard_map.83), channel_id=1, source_target_pairs={{0,4},{4,0},{1,5},{5,1},{2,6},{6,2},{3,7},{7,3},{8,12},{12,8},{9,1... | collective-permute-start | bytes 3145736 | tf_op jit(solution)/shard_map/ppermute | solution.py:550
  151.4 3.8 %collective-permute-start.13 = (f32[640,128]{1,0:T(8,128)S(1)}, f32[640,128]{1,0:T(8,128)S(1)}, u32[]{:S(2)}, u32[]{:S(2)}) collective-permute-start(f32[640,128]{1,0:T(8,128)S(1)} %bitcast.54), channel_id=1, source_target_pairs={{0,2},{2,0},{1,3},{3,1},{4,6},{6,4},{5,7},{7,5},{8,10},{10,8},{9,1... | collective-permute-start | bytes 983048 | tf_op jit(solution)/shard_map/ppermute | solution.py:475
  155.2 27.8 %copy-start.4 = (bf16[1024,1024]{1,0:T(8,128)(2,1)S(1)}, bf16[1024,1024]{1,0:T(8,128)(2,1)}, u32[]{:S(2)}) copy-start(bf16[1024,1024]{1,0:T(8,128)(2,1)} %copy-done.3) | copy-start | bytes 6291460
  182.4 17.8 %collective-permute-start.19 = (f32[1664,128]{1,0:T(8,128)}, f32[1664,128]{1,0:T(8,128)S(1)}, u32[]{:S(2)}, u32[]{:S(2)}) collective-permute-start(f32[1664,128]{1,0:T(8,128)} %bitcast.42), channel_id=1, source_target_pairs={{0,2},{2,0},{1,3},{3,1},{4,6},{6,4},{5,7},{7,5},{8,10},{10,8},{9,1... | collective-permute-start | bytes 2555912 | tf_op jit(solution)/shard_map/ppermute | solution.py:475
  188.0 42.7 %collective-permute-start.14 = (bf16[256,1024]{1,0:T(8,128)(2,1)S(1)}, bf16[256,1024]{1,0:T(8,128)(2,1)S(1)}, u32[]{:S(2)}, u32[]{:S(2)}) collective-permute-start(bf16[256,1024]{1,0:T(8,128)(2,1)S(1)} %get-tuple-element.82), channel_id=1, source_target_pairs={{2,16},{6,20},{8,2},{10,18},{12,6},{14,22},{16,8},{18,24},{20,12},... | collective-permute-start | bytes 1572872 | tf_op jit(solution)/shard_map/ppermute | solution.py:682
  191.8 38.9 %collective-permute-start.15 = (bf16[256,1024]{1,0:T(8,128)(2,1)S(1)}, bf16[256,1024]{1,0:T(8,128)(2,1)S(1)}, u32[]{:S(2)}, u32[]{:S(2)}) collective-permute-start(bf16[256,1024]{1,0:T(8,128)(2,1)S(1)} %get-tuple-element.83), channel_id=1, source_target_pairs={{2,18},{6,22},{10,24},{14,28},{16,10},{18,26},{20,14},{22,30},{24,... | collective-permute-start | bytes 1572872 | tf_op jit(solution)/shard_map/ppermute | solution.py:682
  194.9 35.7 %collective-permute-start.16 = (bf16[256,1024]{1,0:T(8,128)(2,1)S(1)}, bf16[256,1024]{1,0:T(8,128)(2,1)S(1)}, u32[]{:S(2)}, u32[]{:S(2)}) collective-permute-start(bf16[256,1024]{1,0:T(8,128)(2,1)S(1)} %get-tuple-element.84), channel_id=1, source_target_pairs={{0,8},{2,24},{4,12},{6,28},{10,26},{14,30},{16,0},{20,4},{24,2},{2... | collective-permute-start | bytes 1572872 | tf_op jit(solution)/shard_map/ppermute | solution.py:682
  197.3 41.3 %collective-permute-start.17 = (bf16[256,1024]{1,0:T(8,128)(2,1)S(1)}, bf16[256,1024]{1,0:T(8,128)(2,1)S(1)}, u32[]{:S(2)}, u32[]{:S(2)}) collective-permute-start(bf16[256,1024]{1,0:T(8,128)(2,1)S(1)} %get-tuple-element.85), channel_id=1, source_target_pairs={{0,10},{2,26},{4,14},{6,30},{8,0},{10,16},{12,4},{14,20},{16,2},{2... | collective-permute-start | bytes 1572872 | tf_op jit(solution)/shard_map/ppermute | solution.py:682
  200.2 38.5 %collective-permute-start.18 = (f32[256,1024]{1,0:T(8,128)S(1)}, f32[256,1024]{1,0:T(8,128)S(1)}, u32[]{:S(2)}, u32[]{:S(2)}) collective-permute-start(f32[256,1024]{1,0:T(8,128)S(1)} %get-tuple-element.86), channel_id=1, source_target_pairs={{0,2},{2,0},{1,3},{3,1},{4,6},{6,4},{5,7},{7,5},{8,10},{10,8},{9,1... | collective-permute-start | bytes 3145736 | tf_op jit(solution)/shard_map/ppermute | solution.py:683
  241.2 10.0 %collective-permute-start.20 = (f32[2,256,256]{2,1,0:T(8,128)S(1)}, f32[2,256,256]{2,1,0:T(8,128)S(1)}, u32[]{:S(2)}, u32[]{:S(2)}) collective-permute-start(f32[2,256,256]{2,1,0:T(8,128)S(1)} %get-tuple-element.99), channel_id=1, source_target_pairs={{0,2},{2,4},{4,6},{6,0},{1,3},{3,5},{5,7},{7,1},{8,10},{10,12},{12... | collective-permute-start | bytes 1572872 | tf_op jit(solution)/shard_map/ppermute | solution.py:703
  241.3 22.5 %collective-permute-start.21 = (f32[2,256,256]{2,1,0:T(8,128)S(1)}, f32[2,256,256]{2,1,0:T(8,128)S(1)}, u32[]{:S(2)}, u32[]{:S(2)}) collective-permute-start(f32[2,256,256]{2,1,0:T(8,128)S(1)} %get-tuple-element.100), channel_id=1, source_target_pairs={{0,4},{2,6},{4,0},{6,2},{1,5},{3,7},{5,1},{7,3},{8,12},{10,14},{12... | collective-permute-start | bytes 1572872 | tf_op jit(solution)/shard_map/ppermute | solution.py:703
  242.2 23.3 %collective-permute-start.22 = (f32[2,256,256]{2,1,0:T(8,128)S(1)}, f32[2,256,256]{2,1,0:T(8,128)S(1)}, u32[]{:S(2)}, u32[]{:S(2)}) collective-permute-start(f32[2,256,256]{2,1,0:T(8,128)S(1)} %get-tuple-element.101), channel_id=1, source_target_pairs={{0,6},{2,0},{4,2},{6,4},{1,7},{3,1},{5,3},{7,5},{8,14},{10,8},{12,... | collective-permute-start | bytes 1572872 | tf_op jit(solution)/shard_map/ppermute | solution.py:703

commit v5 on v4

--- a/solution.py
+++ b/solution.py
@@ -10,6 +10,7 @@
 NB = 512
 PANELS = 2
 LEAF = 128
+LIGHT = pl.CostEstimate(flops=1, transcendentals=0, bytes_accessed=1)
 SUB = 8
 
 
@@ -163,9 +164,7 @@
         out_specs=[pl.BlockSpec(memory_space=pltpu.VMEM)] * outputs,
         scratch_shapes=[pltpu.VMEM((LEAF, LEAF), jnp.float32)],
         compiler_params=pltpu.CompilerParams(vmem_limit_bytes=24 * 2**20),
-        cost_estimate=pl.CostEstimate(
-            flops=nb, transcendentals=0, bytes_accessed=nb
-        ),
+        cost_estimate=LIGHT,
     )(*operands)
 
 
@@ -345,9 +344,7 @@
         ),
         out_shape=jax.ShapeDtypeStruct((rows, width), array.dtype),
         compiler_params=pltpu.CompilerParams(vmem_limit_bytes=58 * 2**20),
-        cost_estimate=pl.CostEstimate(
-            flops=0, transcendentals=0, bytes_accessed=4 * rows * width
-        ),
+        cost_estimate=LIGHT,
     )(table, array)
 
 
@@ -386,11 +383,7 @@
         ),
         out_shape=jax.ShapeDtypeStruct((total, cols), dtype),
         compiler_params=pltpu.CompilerParams(vmem_limit_bytes=48 * 2**20),
-        cost_estimate=pl.CostEstimate(
-            flops=2 * total * cols * rows * len(bases),
-            transcendentals=0,
-            bytes_accessed=2 * rows * (total + cols) * len(bases) + 4 * total * cols,
-        ),
+        cost_estimate=LIGHT,
     )(table, *bases, *images)
 
 
@@ -418,11 +411,7 @@
         ),
         out_shape=jax.ShapeDtypeStruct((steps * step, cols), dtype),
         compiler_params=pltpu.CompilerParams(vmem_limit_bytes=24 * 2**20),
-        cost_estimate=pl.CostEstimate(
-            flops=steps * step * cols,
-            transcendentals=0,
-            bytes_accessed=steps * step * cols * 4 * len(arrays),
-        ),
+        cost_estimate=LIGHT,
     )(table, *arrays)
 
 
@@ -461,9 +450,7 @@
         ),
         out_shape=outs,
         compiler_params=pltpu.CompilerParams(vmem_limit_bytes=44 * 2**20),
-        cost_estimate=pl.CostEstimate(
-            flops=0, transcendentals=0, bytes_accessed=height * len(sums) * cols * 14
-        ),
+        cost_estimate=LIGHT,
     )(table, *(array for terms in sums for array, _, _ in terms))
 
 
@@ -572,9 +559,8 @@
         out_specs=[block_of(a) for a in outs],
         scratch_shapes=[pltpu.VMEM((cols // LEAF, count, LEAF), f32)],
         compiler_params=pltpu.CompilerParams(vmem_limit_bytes=58 * 2**20),
+        cost_estimate=LIGHT,
     )(cond_table, ground_table, info, port_rows, load_rows, flat_basis)
-    later_table, _ = lax.optimization_barrier((table, faces))
-    given = take_columns(later_table, given_at, flat_basis, width_k // 2)
     halos = []
     for i, (axis, size) in enumerate(
         (("gx", devices_x), (("gy", "core"), devices_y), ("gz", devices_z))
@@ -588,11 +574,8 @@
         else:
             halos.append(lax.ppermute(high, axis, [(k, k + 1) for k in range(size - 1)]))
             halos.append(lax.ppermute(low, axis, [(k + 1, k) for k in range(size - 1)]))
-    other_basis = lax.ppermute(given, "core", swap_pairs())
-
     blocks = NB // LEAF
     lower_rows = blocks * (blocks + 1) // 2 * LEAF
-    halos, _ = lax.optimization_barrier((halos, given))
     first_part = jax.ShapeDtypeStruct((lower_rows // 2, LEAF), f32)
     later_part = jax.ShapeDtypeStruct(((lower_rows + blocks * NB) // 2, LEAF), f32)
     lead_parts = [first_part] * 2 + [later_part] * 2
@@ -603,14 +586,18 @@
         grid_spec=pltpu.PrefetchScalarGridSpec(
             num_scalar_prefetch=1,
             grid=(1,),
-            in_specs=[panel_spec] + [block_of(a) for a in (conduct, grounds, *halos)],
-            out_specs=[block_of(a) for a in outs],
+            in_specs=[panel_spec] + [whole()] * 8,
+            out_specs=[whole()] * 5,
             scratch_shapes=[pltpu.VMEM((count, LEAF), f32), pltpu.VMEM((NB, NB), f32)],
         ),
-        compiler_params=pltpu.CompilerParams(vmem_limit_bytes=58 * 2**20),
+        compiler_params=pltpu.CompilerParams(vmem_limit_bytes=54 * 2**20),
+        cost_estimate=LIGHT,
     )(table, flat_basis, conduct, grounds, *halos)
 
     other_image = lax.ppermute(image, "core", swap_pairs())
+    later_table, _ = lax.optimization_barrier((table, image))
+    given = take_columns(later_table, given_at, flat_basis, width_k // 2)
+    other_basis = lax.ppermute(given, "core", swap_pairs())
 
     axes = ("gx", "gy", "gz")
     chips = devices_x * chips_y * devices_z
@@ -652,7 +639,10 @@
     further_a = [move(a, "gy", d) for d, a in enumerate(further_a, 1)]
     further_b = [move(a, "gz", d) for d, a in enumerate(further_b, 1)]
     first_rows = other_half(both[:, :share].reshape(-1, LEAF), core)
-    later_half = exchanged(for_all(jnp.sum(both[:, share:], axis=0))).reshape(-1, LEAF)
+    later_terms, _ = lax.optimization_barrier((both[:, share:], first_rows))
+    later_sums = for_all(jnp.sum(later_terms, axis=0))
+    later_half = exchanged(later_sums).reshape(-1, LEAF)
+    first_rows, _ = lax.optimization_barrier((first_rows, later_sums))
     inverse_0 = first_panel(first_rows, NB)
     (further_a, further_b, later_half), inverse_0 = lax.optimization_barrier(
         ((further_a, further_b, later_half), inverse_0)
@@ -697,6 +687,7 @@
             scratch_shapes=[pltpu.VMEM((part, cols), f32)] * 2,
         ),
         compiler_params=pltpu.CompilerParams(vmem_limit_bytes=44 * 2**20),
+        cost_estimate=LIGHT,
     )(table, *ins))
     for d in range(1, devices_y):
         route = [(i, (i + d) % devices_y) for i in range(devices_y)]
@@ -712,6 +703,7 @@
             out_specs=[block_of(out)] * 2,
         ),
         compiler_params=pltpu.CompilerParams(vmem_limit_bytes=44 * 2**20),
+        cost_estimate=LIGHT,
     )(table, *pairs)
 
 

time: 269 us -> 280 us (1.041)
  waiting for transfers between devices: 81.6 us -> 89.5 us
  local copies, waits for them, and re-layouts: 13.9 us -> 18.8 us
    ppermute x2, waiting for transfers between devices: 4.05 us -> 8.81 us  [halved(): return kept + lax.ppermute(sent, 'core', swap_pairs())]
    unnamed x40 -> x42, local copies, waits for them, and re-layouts: 9.4 us -> 13.2 us
    ppermute x2, waiting for transfers between devices: 0.01 us -> 2.93 us  [local(): halos.append(lax.ppermute(low, axis, [(k + 1, k) for k in range(size - 1)]))]
  transfers between devices with their start and end apart: 26 -> 26, of which waited for: 8 -> 8; matrix products, arithmetic and copies ran while one was open for 2% -> 2% of each run, Pallas kernels for 35% -> 30%
where the time goes in v5:
time: 280 us; the launch traced here: 279 us
  Pallas kernels  107 us (38%)
  waiting for transfers between devices  89.5 us (32%)
  starting transfers between devices  54.5 us (19%)
  local copies, waits for them, and re-layouts  18.8 us (7%)
  other arithmetic  7.62 us (3%)
    pallas_call x2, Pallas kernels, panel_call(): pl.pallas_call(kernel, out_shape=[jax.ShapeDtypeStruct((nb, nb), jnp.floa...  55.8 us
    ppermute x4, waiting for transfers between devices, move(): return lax.ppermute(array, axis, [(i, (i + d) % size) for i in range(size)])  47.1 us
    ppermute x3, waiting for transfers between devices, local(): pairs[d] = lax.ppermute(pairs[d], ('gy', 'core'), route)  22.6 us
    pallas_call x4, Pallas kernels, products(): pl.pallas_call(products_kernel, grid_spec=pltpu.PrefetchScalarGridSpec(nu...  20.4 us
    unnamed x42, local copies, waits for them, and re-layouts  13.2 us
    ppermute x4, starting transfers between devices, local(): x_got.append(lax.ppermute(x_sent[step], ('gx', 'gy', 'core'), pairs))  12.2 us
    all_to_all x2, starting transfers between devices, exchanged(): return lax.all_to_all(rows, axes, split_axis=0, concat_axis=0, tiled=True)  11.1 us
    pallas_call x1, Pallas kernels, local(): pl.pallas_call(functools.partial(image_kernel, sides=sides, nb=NB, at=cor...  9.16 us
  transfers between devices with their start and end apart: 26, of which 8 were waited for; matrix products, arithmetic and copies ran while one was open for 2% of the time, Pallas kernels for 30%

profile of v5, /device:TPU:1, one launch (start us, length us, event | category | flops | bytes accessed | tf_op | source)
XLA Modules:
  0.0 278.9 jit_solution(10019260156818977139)
XLA Ops:
  2.6 4.0 %shard_map.77 = (bf16[64,1024]{1,0:T(8,128)(2,1)}, bf16[64,1024]{1,0:T(8,128)(2,1)}, bf16[64,1024]{1,0:T(8,128)(2,1)}, bf16[64,1024]{1,0:T(8,128)(2,1)}, bf16[64...) custom-call(f32[16]{0:T(128)} %cond_ref.1, f32[16]{0:T(128)} %ground_ref.1, ...), custom_call_target="tpu_custom_call" | custom-call | flops 1 | bytes 1 | tf_op jit(solution)/shard_map/pallas_call | solution.py:553
  7.6 2.1 collective-permute-start.4
  9.7 3.2 %collective-permute-start = (bf16[64,1024]{1,0:T(8,128)(2,1)}, bf16[64,1024]{1,0:T(8,128)(2,1)S(1)}, u32[]{:S(2)}, u32[]{:S(2)}) collective-permute-start(bf16[64,1024]{1,0:T(8,128)(2,1)} %get-tuple-element.50), channel_id=1, source_target_pairs={{0,8},{8,16},{16,24},{1,9},{9,17},{17,25},{2,10},{10,18},{18,26},{... | collective-permute-start | bytes 393224 | tf_op jit(solution)/shard_map/ppermute | solution.py:575
  12.9 1.3 collective-permute-start.1
  14.2 4.3 %collective-permute-start.2 = (bf16[64,1024]{1,0:T(8,128)(2,1)}, bf16[64,1024]{1,0:T(8,128)(2,1)S(1)}, u32[]{:S(2)}, u32[]{:S(2)}) collective-permute-start(bf16[64,1024]{1,0:T(8,128)(2,1)} %get-tuple-element.52), channel_id=1, source_target_pairs={{0,2},{2,4},{4,6},{1,3},{3,5},{5,7},{8,10},{10,12},{12,14},{9,11},... | collective-permute-start | bytes 393224 | tf_op jit(solution)/shard_map/ppermute | solution.py:575
  18.5 1.9 collective-permute-start.3
  22.1 2.9 %collective-permute-done.3.refs_3_ = bf16[64,1024]{1,0:T(8,128)(2,1)S(1)} collective-permute-done((bf16[64,1024]{1,0:T(8,128)(2,1)}, bf16[64,1024]{1,0:T(8,128)(2,1)S(1)}, u32[]{:S(2)}, u32[]{:S(2)}) %collective-permute-start.3) | collective-permute-done | bytes 131104 | tf_op jit(solution)/shard_map/ppermute | solution.py:576
  25.6 9.2 %shard_map.78 = (bf16[512,1024]{1,0:T(8,128)(2,1)}, f32[640,128]{1,0:T(8,128)}, f32[640,128]{1,0:T(8,128)}, f32[1664,128]{1,0:T(8,128)}, f32[1664,128]{1,0:T(8,128)}) custom-call(s32[38]{0:T(128)} %stack.163.table_ref, bf16[512,8192]{1,0:T(8,128)(2,1)} %bitcast.47, f32[512,128]{1,0:T(8,128)} %get-tuple-element.48.conduct_ref, ...), custom_call_target="tpu_custom_call" | custom-call | flops 1 | bytes 1 | tf_op jit(solution)/shard_map/pallas_call | solution.py:583
  34.8 5.6 %shard_map.79 = bf16[512,4096]{1,0:T(8,128)(2,1)} custom-call(s32[38]{0:T(128)} %stack.163.table_ref, bf16[512,8192]{1,0:T(8,128)(2,1)} %bitcast.48), custom_call_target="tpu_custom_call" | custom-call | flops 1 | bytes 1 | tf_op jit(solution)/shard_map/pallas_call | solution.py:337
  41.4 8.8 %collective-permute-done.7 = f32[640,128]{1,0:T(8,128)S(1)} collective-permute-done((f32[640,128]{1,0:T(8,128)S(1)}, f32[640,128]{1,0:T(8,128)S(1)}, u32[]{:S(2)}, u32[]{:S(2)}) %collective-permute-start.7) | collective-permute-done | bytes 327712 | tf_op jit(solution)/shard_map/ppermute | solution.py:606
  51.0 5.8 %all-to-all-start = ((f32[16,40,128]{2,1,0:T(8,128)}), f32[16,40,128]{2,1,0:T(8,128)S(1)}, u32[]{:S(2)}, u32[]{:S(2)}) async-start(f32[16,40,128]{2,1,0:T(8,128)} %bitcast.40), calls=%async_computation | async-start | bytes 655360 | tf_op jit(solution)/shard_map/all_to_all | solution.py:610
  57.7 1.5 add.271
  59.2 4.4 %shard_map.81 = bf16[1024,1024]{1,0:T(8,128)(2,1)S(1)} custom-call(s32[38]{0:T(128)S(1)} %copy-done.13, bf16[512,8192]{1,0:T(8,128)(2,1)} %bitcast.49, bf16[512,4096]{1,0:T(8,128)(2,1)} %collective-permute-done.5.refs_1_, bf16[512,1024]{1,0:T(8,128)(2,1)S(1)} %copy-done.2, bf16[512,1024]{1,0:T(8,128)(2,1)S(1)} %collective-permute-done.6.refs_3_), custom_call_target="tpu_custom_call" | custom-call | flops 1 | bytes 1 | tf_op jit(solution)/shard_map/pallas_call | solution.py:376
  63.6 1.3 copy-done.7
  64.9 4.4 %shard_map.80 = bf16[1024,1024]{1,0:T(8,128)(2,1)S(1)} custom-call(s32[38]{0:T(128)S(1)} %copy-done.13, bf16[512,8192]{1,0:T(8,128)(2,1)} %bitcast.50, bf16[512,4096]{1,0:T(8,128)(2,1)} %collective-permute-done.5.refs_1_, bf16[512,1024]{1,0:T(8,128)(2,1)S(1)} %copy-done.2, bf16[512,1024]{1,0:T(8,128)(2,1)S(1)} %collective-permute-done.6.refs_3_), custom_call_target="tpu_custom_call" | custom-call | flops 1 | bytes 1 | tf_op jit(solution)/shard_map/pallas_call | solution.py:376
  69.4 1.3 copy-done.8
  71.8 6.4 %all-to-all-start.1 = ((f32[16,144,128]{2,1,0:T(8,128)}), f32[16,144,128]{2,1,0:T(8,128)}, u32[]{:S(2)}, u32[]{:S(2)}) async-start(f32[16,144,128]{2,1,0:T(8,128)} %pad_maximum_fusion.1), calls=%async_computation.1 | async-start | bytes 2359296 | tf_op jit(solution)/shard_map/all_to_all | solution.py:632
  78.3 1.3 collective-permute-start.8
  80.8 5.8 %shard_map.84.refs_0_.refs_3_ = f32[1024,1024]{1,0:T(8,128)} custom-call(s32[38]{0:T(128)S(1)} %copy-done.13, bf16[512,8192]{1,0:T(8,128)(2,1)} %bitcast.51, bf16[512,4096]{1,0:T(8,128)(2,1)} %collective-permute-done.5.refs_1_, bf16[512,1024]{1,0:T(8,128)(2,1)S(1)} %copy-done.2, bf16[512,1024]{1,0:T(8,128)(2,1)S(1)} %collective-permute-done.6.refs_3_), custom_call_target="tpu_custom_call" | custom-call | flops 1 | bytes 1 | tf_op jit(solution)/shard_map/pallas_call | solution.py:376
  86.6 5.7 %shard_map.82.refs_0_ = f32[1024,1024]{1,0:T(8,128)} custom-call(s32[38]{0:T(128)S(1)} %copy-done.13, bf16[512,8192]{1,0:T(8,128)(2,1)} %bitcast.52, bf16[512,4096]{1,0:T(8,128)(2,1)} %collective-permute-done.5.refs_1_, bf16[512,1024]{1,0:T(8,128)(2,1)S(1)} %copy-done.2, bf16[512,1024]{1,0:T(8,128)(2,1)S(1)} %collective-permute-done.6.refs_3_), custom_call_target="tpu_custom_call" | custom-call | flops 1 | bytes 1 | tf_op jit(solution)/shard_map/pallas_call | solution.py:376
  92.3 44.6 %collective-permute-done.8.refs_1_ = bf16[1024,1024]{1,0:T(8,128)(2,1)S(1)} collective-permute-done((bf16[1024,1024]{1,0:T(8,128)(2,1)}, bf16[1024,1024]{1,0:T(8,128)(2,1)S(1)}, u32[]{:S(2)}, u32[]{:S(2)}) %collective-permute-start.8) | collective-permute-done | bytes 2097184 | tf_op jit(solution)/shard_map/ppermute | solution.py:537
  136.9 2.2 copy-done.1
  139.1 1.7 shard_map.83
  140.8 1.6 shard_map.85
  142.4 1.3 copy-done.5
  144.7 2.2 collective-permute-start.13
  146.9 1.2 slice.6
  150.2 5.3 %all-to-all-start.2 = ((f32[16,104,128]{2,1,0:T(8,128)}), f32[16,104,128]{2,1,0:T(8,128)}, u32[]{:S(2)}, u32[]{:S(2)}) async-start(f32[16,104,128]{2,1,0:T(8,128)} %broadcast_in_dim.25), calls=%async_computation.2 | async-start | bytes 1703936 | tf_op jit(solution)/shard_map/all_to_all | solution.py:610
  155.5 1.4 collective-permute-start.11
  159.2 27.0 %shard_map.86.w0_ref.refs_4_ = f32[512,512]{1,0:T(8,128)S(1)} custom-call(f32[1280,128]{1,0:T(8,128)S(1)} %copy-done.6), custom_call_target="tpu_custom_call" | custom-call | flops 1 | bytes 1 | tf_op jit(solution)/shard_map/pallas_call | solution.py:160
  186.2 2.5 collective-permute-done.11.refs_5_
  190.7 1.5 collective-permute-start.19
  192.2 1.2 copy-done.10
  193.4 1.2 copy-done.12
  194.7 4.3 %shard_map.87 = (bf16[256,1024]{1,0:T(8,128)(2,1)S(1)}, bf16[256,1024]{1,0:T(8,128)(2,1)S(1)}, bf16[256,1024]{1,0:T(8,128)(2,1)S(1)}, bf16[256,1024]{1,0:T(8,128...) custom-call(s32[38]{0:T(128)S(1)} %copy-done.13, f32[1024,1024]{1,0:T(8,128)} %shard_map.82.refs_0_, ...), custom_call_target="tpu_custom_call" | custom-call | flops 1 | bytes 1 | tf_op jit(solution)/shard_map/pallas_call | solution.py:442
  199.0 3.9 %collective-permute-start.14 = (bf16[256,1024]{1,0:T(8,128)(2,1)S(1)}, bf16[256,1024]{1,0:T(8,128)(2,1)S(1)}, u32[]{:S(2)}, u32[]{:S(2)}) collective-permute-start(bf16[256,1024]{1,0:T(8,128)(2,1)S(1)} %get-tuple-element.74), channel_id=1, source_target_pairs={{2,16},{6,20},{8,2},{10,18},{12,6},{14,22},{16,8},{18,24},{20,12},... | collective-permute-start | bytes 1572872 | tf_op jit(solution)/shard_map/ppermute | solution.py:672
  202.9 3.1 %collective-permute-start.15 = (bf16[256,1024]{1,0:T(8,128)(2,1)S(1)}, bf16[256,1024]{1,0:T(8,128)(2,1)S(1)}, u32[]{:S(2)}, u32[]{:S(2)}) collective-permute-start(bf16[256,1024]{1,0:T(8,128)(2,1)S(1)} %get-tuple-element.75), channel_id=1, source_target_pairs={{2,18},{6,22},{10,24},{14,28},{16,10},{18,26},{20,14},{22,30},{24,... | collective-permute-start | bytes 1572872 | tf_op jit(solution)/shard_map/ppermute | solution.py:672
  206.0 2.3 collective-permute-start.16
  208.3 2.9 %collective-permute-start.17 = (bf16[256,1024]{1,0:T(8,128)(2,1)S(1)}, bf16[256,1024]{1,0:T(8,128)(2,1)S(1)}, u32[]{:S(2)}, u32[]{:S(2)}) collective-permute-start(bf16[256,1024]{1,0:T(8,128)(2,1)S(1)} %get-tuple-element.77), channel_id=1, source_target_pairs={{0,10},{2,26},{4,14},{6,30},{8,0},{10,16},{12,4},{14,20},{16,2},{2... | collective-permute-start | bytes 1572872 | tf_op jit(solution)/shard_map/ppermute | solution.py:672
  211.4 1.3 broadcast_select_fusion.1
  212.8 28.8 %shard_map.88 = (f32[512,512]{1,0:T(8,128)S(1)}, f32[512,512]{1,0:T(8,128)S(1)}) custom-call(f32[3328,128]{1,0:T(8,128)S(1)} %pad_maximum_fusion.packed_ref, f32[512,512]{1,0:T(8,128)S(1)} %shard_map.86.w0_ref.refs_4_), custom_call_target="tpu_custom_call" | custom-call | flops 1 | bytes 1 | tf_op jit(solution)/shard_map/pallas_call | solution.py:160
  241.6 8.0 %collective-permute-done.17.refs_3_ = bf16[256,1024]{1,0:T(8,128)(2,1)S(1)} collective-permute-done((bf16[256,1024]{1,0:T(8,128)(2,1)S(1)}, bf16[256,1024]{1,0:T(8,128)(2,1)S(1)}, u32[]{:S(2)}, u32[]{:S(2)}) %collective-permute-start.17) | collective-permute-done | bytes 524320 | tf_op jit(solution)/shard_map/ppermute | solution.py:672
  249.6 2.6 shard_map.89
  252.3 1.3 collective-permute-start.21
  254.3 7.5 %collective-permute-done.20.refs_1_ = f32[2,256,256]{2,1,0:T(8,128)S(1)} collective-permute-done((f32[2,256,256]{2,1,0:T(8,128)S(1)}, f32[2,256,256]{2,1,0:T(8,128)S(1)}, u32[]{:S(2)}, u32[]{:S(2)}) %collective-permute-start.20) | collective-permute-done | bytes 524320 | tf_op jit(solution)/shard_map/ppermute | solution.py:694
  261.8 13.8 %collective-permute-done.21.refs_2_ = f32[2,256,256]{2,1,0:T(8,128)S(1)} collective-permute-done((f32[2,256,256]{2,1,0:T(8,128)S(1)}, f32[2,256,256]{2,1,0:T(8,128)S(1)}, u32[]{:S(2)}, u32[]{:S(2)}) %collective-permute-start.21) | collective-permute-done | bytes 524320 | tf_op jit(solution)/shard_map/ppermute | solution.py:694
  275.6 1.3 collective-permute-done.22.refs_3_
  276.9 2.0 shard_map.90
  (84 shorter events, 18.3 us)
Async XLA Ops:
  7.6 13.7 %collective-permute-start.4 = (bf16[64,1024]{1,0:T(8,128)(2,1)S(1)}, bf16[64,1024]{1,0:T(8,128)(2,1)S(1)}, u32[]{:S(2)}, u32[]{:S(2)}) collective-permute-start(bf16[64,1024]{1,0:T(8,128)(2,1)S(1)} %broadcast_select_fusion.6), channel_id=1, source_target_pairs={{0,1},{1,0},{2,3},{3,2},{4,5},{5,4},{6,7},{7,6},{8,9},{9,8},{10,11... | collective-permute-start | bytes 393224 | tf_op jit(solution)/shard_map/ppermute | solution.py:571
  9.7 12.3 %collective-permute-start = (bf16[64,1024]{1,0:T(8,128)(2,1)}, bf16[64,1024]{1,0:T(8,128)(2,1)S(1)}, u32[]{:S(2)}, u32[]{:S(2)}) collective-permute-start(bf16[64,1024]{1,0:T(8,128)(2,1)} %get-tuple-element.50), channel_id=1, source_target_pairs={{0,8},{8,16},{16,24},{1,9},{9,17},{17,25},{2,10},{10,18},{18,26},{... | collective-permute-start | bytes 393224 | tf_op jit(solution)/shard_map/ppermute | solution.py:575
  12.9 9.1 %collective-permute-start.1 = (bf16[64,1024]{1,0:T(8,128)(2,1)}, bf16[64,1024]{1,0:T(8,128)(2,1)S(1)}, u32[]{:S(2)}, u32[]{:S(2)}) collective-permute-start(bf16[64,1024]{1,0:T(8,128)(2,1)} %get-tuple-element.51), channel_id=1, source_target_pairs={{8,0},{16,8},{24,16},{9,1},{17,9},{25,17},{10,2},{18,10},{26,18},{... | collective-permute-start | bytes 393224 | tf_op jit(solution)/shard_map/ppermute | solution.py:576
  14.2 7.8 %collective-permute-start.2 = (bf16[64,1024]{1,0:T(8,128)(2,1)}, bf16[64,1024]{1,0:T(8,128)(2,1)S(1)}, u32[]{:S(2)}, u32[]{:S(2)}) collective-permute-start(bf16[64,1024]{1,0:T(8,128)(2,1)} %get-tuple-element.52), channel_id=1, source_target_pairs={{0,2},{2,4},{4,6},{1,3},{3,5},{5,7},{8,10},{10,12},{12,14},{9,11},... | collective-permute-start | bytes 393224 | tf_op jit(solution)/shard_map/ppermute | solution.py:575
  18.5 6.5 %collective-permute-start.3 = (bf16[64,1024]{1,0:T(8,128)(2,1)}, bf16[64,1024]{1,0:T(8,128)(2,1)S(1)}, u32[]{:S(2)}, u32[]{:S(2)}) collective-permute-start(bf16[64,1024]{1,0:T(8,128)(2,1)} %get-tuple-element.53), channel_id=1, source_target_pairs={{2,0},{4,2},{6,4},{3,1},{5,3},{7,5},{10,8},{12,10},{14,12},{11,9},... | collective-permute-start | bytes 393224 | tf_op jit(solution)/shard_map/ppermute | solution.py:576
  22.0 3.0 %copy-start.16 = (bf16[64,1024]{1,0:T(8,128)(2,1)}, bf16[64,1024]{1,0:T(8,128)(2,1)S(1)}, u32[]{:S(2)}) copy-start(bf16[64,1024]{1,0:T(8,128)(2,1)S(1)} %collective-permute-done.refs_0_) | copy-start | bytes 393220
  22.0 3.0 %copy-start.17 = (bf16[64,1024]{1,0:T(8,128)(2,1)}, bf16[64,1024]{1,0:T(8,128)(2,1)S(1)}, u32[]{:S(2)}) copy-start(bf16[64,1024]{1,0:T(8,128)(2,1)S(1)} %collective-permute-done.1.refs_1_) | copy-start | bytes 393220
  22.1 2.9 %copy-start.18 = (bf16[64,1024]{1,0:T(8,128)(2,1)}, bf16[64,1024]{1,0:T(8,128)(2,1)S(1)}, u32[]{:S(2)}) copy-start(bf16[64,1024]{1,0:T(8,128)(2,1)S(1)} %collective-permute-done.2.refs_2_) | copy-start | bytes 393220
  25.0 0.7 copy-start.19
  34.8 5.6 %copy-start.2 = (bf16[512,1024]{1,0:T(8,128)(2,1)S(1)}, bf16[512,1024]{1,0:T(8,128)(2,1)}, u32[]{:S(2)}) copy-start(bf16[512,1024]{1,0:T(8,128)(2,1)} %get-tuple-element.63.refs_2_) | copy-start | bytes 3145732
  34.8 6.1 %copy-start.20 = (f32[640,128]{1,0:T(8,128)S(1)}, f32[640,128]{1,0:T(8,128)}, u32[]{:S(2)}) copy-start(f32[640,128]{1,0:T(8,128)} %get-tuple-element.59) | copy-start | bytes 983044
  34.8 15.4 %copy-start.15 = (f32[640,128]{1,0:T(8,128)S(1)}, f32[640,128]{1,0:T(8,128)}, u32[]{:S(2)}) copy-start(f32[640,128]{1,0:T(8,128)} %get-tuple-element.58) | copy-start | bytes 983044
  40.4 18.8 %collective-permute-start.5 = (bf16[512,4096]{1,0:T(8,128)(2,1)}, bf16[512,4096]{1,0:T(8,128)(2,1)}, u32[]{:S(2)}, u32[]{:S(2)}) collective-permute-start(bf16[512,4096]{1,0:T(8,128)(2,1)} %shard_map.79), channel_id=1, source_target_pairs={{0,2},{2,0},{1,3},{3,1},{4,6},{6,4},{5,7},{7,5},{8,10},{10,8},{9,1... | collective-permute-start | bytes 12582920 | tf_op jit(solution)/shard_map/ppermute | solution.py:600
  40.4 18.8 %collective-permute-start.6 = (bf16[512,1024]{1,0:T(8,128)(2,1)S(1)}, bf16[512,1024]{1,0:T(8,128)(2,1)S(1)}, u32[]{:S(2)}, u32[]{:S(2)}) collective-permute-start(bf16[512,1024]{1,0:T(8,128)(2,1)S(1)} %copy-done.2), channel_id=1, source_target_pairs={{0,2},{2,0},{1,3},{3,1},{4,6},{6,4},{5,7},{7,5},{8,10},{10,8},{9,1... | collective-permute-start | bytes 3145736 | tf_op jit(solution)/shard_map/ppermute | solution.py:597
  40.9 9.3 %collective-permute-start.7 = (f32[640,128]{1,0:T(8,128)S(1)}, f32[640,128]{1,0:T(8,128)S(1)}, u32[]{:S(2)}, u32[]{:S(2)}) collective-permute-start(f32[640,128]{1,0:T(8,128)S(1)} %copy-done.20), channel_id=1, source_target_pairs={{0,2},{2,0},{1,3},{3,1},{4,6},{6,4},{5,7},{7,5},{8,10},{10,8},{9,1... | collective-permute-start | bytes 983048 | tf_op jit(solution)/shard_map/ppermute | solution.py:606
  41.0 15.8 %collective-permute-start.12 = (f32[1664,128]{1,0:T(8,128)}, f32[1664,128]{1,0:T(8,128)S(1)}, u32[]{:S(2)}, u32[]{:S(2)}) collective-permute-start(f32[1664,128]{1,0:T(8,128)} %get-tuple-element.66), channel_id=1, source_target_pairs={{0,2},{2,0},{1,3},{3,1},{4,6},{6,4},{5,7},{7,5},{8,10},{10,8},{9,1... | collective-permute-start | bytes 2555912 | tf_op jit(solution)/shard_map/ppermute | solution.py:606
  50.2 9.0 %copy-start.13 = (s32[38]{0:T(128)S(1)}, s32[38]{0:T(128)}, u32[]{:S(2)}) copy-start(s32[38]{0:T(128)} %stack.163.table_ref) | copy-start | bytes 460
  51.0 19.7 %all-to-all-start = ((f32[16,40,128]{2,1,0:T(8,128)}), f32[16,40,128]{2,1,0:T(8,128)S(1)}, u32[]{:S(2)}, u32[]{:S(2)}) async-start(f32[16,40,128]{2,1,0:T(8,128)} %bitcast.40), calls=%async_computation | async-start | bytes 655360 | tf_op jit(solution)/shard_map/all_to_all | solution.py:610
  56.8 0.9 copy-start.14
  63.6 1.3 copy-start.7
  69.4 1.3 copy-start.8
  71.8 71.9 %all-to-all-start.1 = ((f32[16,144,128]{2,1,0:T(8,128)}), f32[16,144,128]{2,1,0:T(8,128)}, u32[]{:S(2)}, u32[]{:S(2)}) async-start(f32[16,144,128]{2,1,0:T(8,128)} %pad_maximum_fusion.1), calls=%async_computation.1 | async-start | bytes 2359296 | tf_op jit(solution)/shard_map/all_to_all | solution.py:632
  78.3 58.6 %collective-permute-start.8 = (bf16[1024,1024]{1,0:T(8,128)(2,1)}, bf16[1024,1024]{1,0:T(8,128)(2,1)S(1)}, u32[]{:S(2)}, u32[]{:S(2)}) collective-permute-start(bf16[1024,1024]{1,0:T(8,128)(2,1)} %copy-done.8), channel_id=1, source_target_pairs={{0,1},{1,0},{2,3},{3,2},{4,5},{5,4},{6,7},{7,6},{8,9},{9,8},{10,11... | collective-permute-start | bytes 6291464 | tf_op jit(solution)/shard_map/ppermute | solution.py:537
  79.6 61.2 %collective-permute-start.10 = (bf16[1024,1024]{1,0:T(8,128)(2,1)}, bf16[1024,1024]{1,0:T(8,128)(2,1)S(1)}, u32[]{:S(2)}, u32[]{:S(2)}) collective-permute-start(bf16[1024,1024]{1,0:T(8,128)(2,1)} %copy-done.7), channel_id=1, source_target_pairs={{0,4},{4,0},{1,5},{5,1},{2,6},{6,2},{3,7},{7,3},{8,12},{12,8},{9,1... | collective-permute-start | bytes 6291464 | tf_op jit(solution)/shard_map/ppermute | solution.py:537
  92.3 48.5 %copy-start = (f32[1024,1024]{1,0:T(8,128)S(1)}, f32[1024,1024]{1,0:T(8,128)}, u32[]{:S(2)}) copy-start(f32[1024,1024]{1,0:T(8,128)} %shard_map.84.refs_0_.refs_3_) | copy-start | bytes 12582916
  136.9 2.2 copy-start.1
  139.1 1.7 copy-start.3
  142.4 1.3 copy-start.5
  144.7 3.5 %collective-permute-start.13 = (f32[640,128]{1,0:T(8,128)S(1)}, f32[640,128]{1,0:T(8,128)S(1)}, u32[]{:S(2)}, u32[]{:S(2)}) collective-permute-start(f32[640,128]{1,0:T(8,128)S(1)} %bitcast.54), channel_id=1, source_target_pairs={{0,2},{2,0},{1,3},{3,1},{4,6},{6,4},{5,7},{7,5},{8,10},{10,8},{9,1... | collective-permute-start | bytes 983048 | tf_op jit(solution)/shard_map/ppermute | solution.py:462
  149.2 43.0 %copy-start.4 = (bf16[1024,1024]{1,0:T(8,128)(2,1)S(1)}, bf16[1024,1024]{1,0:T(8,128)(2,1)}, u32[]{:S(2)}) copy-start(bf16[1024,1024]{1,0:T(8,128)(2,1)} %copy-done.3) | copy-start | bytes 6291460
  150.2 40.5 %all-to-all-start.2 = ((f32[16,104,128]{2,1,0:T(8,128)}), f32[16,104,128]{2,1,0:T(8,128)}, u32[]{:S(2)}, u32[]{:S(2)}) async-start(f32[16,104,128]{2,1,0:T(8,128)} %broadcast_in_dim.25), calls=%async_computation.2 | async-start | bytes 1703936 | tf_op jit(solution)/shard_map/all_to_all | solution.py:610
  155.5 33.2 %collective-permute-start.11 = (bf16[512,1024]{1,0:T(8,128)(2,1)}, bf16[512,1024]{1,0:T(8,128)(2,1)S(1)}, u32[]{:S(2)}, u32[]{:S(2)}) collective-permute-start(bf16[512,1024]{1,0:T(8,128)(2,1)} %shard_map.85), channel_id=1, source_target_pairs={{0,1},{1,0},{2,3},{3,2},{4,5},{5,4},{6,7},{7,6},{8,9},{9,8},{10,11... | collective-permute-start | bytes 3145736 | tf_op jit(solution)/shard_map/ppermute | solution.py:537
  156.9 32.8 %collective-permute-start.9 = (bf16[512,1024]{1,0:T(8,128)(2,1)}, bf16[512,1024]{1,0:T(8,128)(2,1)S(1)}, u32[]{:S(2)}, u32[]{:S(2)}) collective-permute-start(bf16[512,1024]{1,0:T(8,128)(2,1)} %shard_map.83), channel_id=1, source_target_pairs={{0,4},{4,0},{1,5},{5,1},{2,6},{6,2},{3,7},{7,3},{8,12},{12,8},{9,1... | collective-permute-start | bytes 3145736 | tf_op jit(solution)/shard_map/ppermute | solution.py:537
  158.1 1.1 copy-start.6
  188.7 1.0 copy-start.9
  189.7 1.0 copy-start.11
  190.7 20.6 %collective-permute-start.19 = (f32[1664,128]{1,0:T(8,128)}, f32[1664,128]{1,0:T(8,128)S(1)}, u32[]{:S(2)}, u32[]{:S(2)}) collective-permute-start(f32[1664,128]{1,0:T(8,128)} %bitcast.43), channel_id=1, source_target_pairs={{0,2},{2,0},{1,3},{3,1},{4,6},{6,4},{5,7},{7,5},{8,10},{10,8},{9,1... | collective-permute-start | bytes 2555912 | tf_op jit(solution)/shard_map/ppermute | solution.py:462
  192.2 1.2 copy-start.10
  193.4 1.2 copy-start.12
  199.0 42.6 %collective-permute-start.14 = (bf16[256,1024]{1,0:T(8,128)(2,1)S(1)}, bf16[256,1024]{1,0:T(8,128)(2,1)S(1)}, u32[]{:S(2)}, u32[]{:S(2)}) collective-permute-start(bf16[256,1024]{1,0:T(8,128)(2,1)S(1)} %get-tuple-element.74), channel_id=1, source_target_pairs={{2,16},{6,20},{8,2},{10,18},{12,6},{14,22},{16,8},{18,24},{20,12},... | collective-permute-start | bytes 1572872 | tf_op jit(solution)/shard_map/ppermute | solution.py:672
  202.9 38.7 %collective-permute-start.15 = (bf16[256,1024]{1,0:T(8,128)(2,1)S(1)}, bf16[256,1024]{1,0:T(8,128)(2,1)S(1)}, u32[]{:S(2)}, u32[]{:S(2)}) collective-permute-start(bf16[256,1024]{1,0:T(8,128)(2,1)S(1)} %get-tuple-element.75), channel_id=1, source_target_pairs={{2,18},{6,22},{10,24},{14,28},{16,10},{18,26},{20,14},{22,30},{24,... | collective-permute-start | bytes 1572872 | tf_op jit(solution)/shard_map/ppermute | solution.py:672
  206.0 35.6 %collective-permute-start.16 = (bf16[256,1024]{1,0:T(8,128)(2,1)S(1)}, bf16[256,1024]{1,0:T(8,128)(2,1)S(1)}, u32[]{:S(2)}, u32[]{:S(2)}) collective-permute-start(bf16[256,1024]{1,0:T(8,128)(2,1)S(1)} %get-tuple-element.76), channel_id=1, source_target_pairs={{0,8},{2,24},{4,12},{6,28},{10,26},{14,30},{16,0},{20,4},{24,2},{2... | collective-permute-start | bytes 1572872 | tf_op jit(solution)/shard_map/ppermute | solution.py:672
  208.3 41.3 %collective-permute-start.17 = (bf16[256,1024]{1,0:T(8,128)(2,1)S(1)}, bf16[256,1024]{1,0:T(8,128)(2,1)S(1)}, u32[]{:S(2)}, u32[]{:S(2)}) collective-permute-start(bf16[256,1024]{1,0:T(8,128)(2,1)S(1)} %get-tuple-element.77), channel_id=1, source_target_pairs={{0,10},{2,26},{4,14},{6,30},{8,0},{10,16},{12,4},{14,20},{16,2},{2... | collective-permute-start | bytes 1572872 | tf_op jit(solution)/shard_map/ppermute | solution.py:672
  211.3 38.4 %collective-permute-start.18 = (f32[256,1024]{1,0:T(8,128)S(1)}, f32[256,1024]{1,0:T(8,128)S(1)}, u32[]{:S(2)}, u32[]{:S(2)}) collective-permute-start(f32[256,1024]{1,0:T(8,128)S(1)} %get-tuple-element.78), channel_id=1, source_target_pairs={{0,2},{2,0},{1,3},{3,1},{4,6},{6,4},{5,7},{7,5},{8,10},{10,8},{9,1... | collective-permute-start | bytes 3145736 | tf_op jit(solution)/shard_map/ppermute | solution.py:673
  252.2 9.6 %collective-permute-start.20 = (f32[2,256,256]{2,1,0:T(8,128)S(1)}, f32[2,256,256]{2,1,0:T(8,128)S(1)}, u32[]{:S(2)}, u32[]{:S(2)}) collective-permute-start(f32[2,256,256]{2,1,0:T(8,128)S(1)} %get-tuple-element.91), channel_id=1, source_target_pairs={{0,2},{2,4},{4,6},{6,0},{1,3},{3,5},{5,7},{7,1},{8,10},{10,12},{12... | collective-permute-start | bytes 1572872 | tf_op jit(solution)/shard_map/ppermute | solution.py:694
  252.3 23.3 %collective-permute-start.21 = (f32[2,256,256]{2,1,0:T(8,128)S(1)}, f32[2,256,256]{2,1,0:T(8,128)S(1)}, u32[]{:S(2)}, u32[]{:S(2)}) collective-permute-start(f32[2,256,256]{2,1,0:T(8,128)S(1)} %get-tuple-element.92), channel_id=1, source_target_pairs={{0,4},{2,6},{4,0},{6,2},{1,5},{3,7},{5,1},{7,3},{8,12},{10,14},{12... | collective-permute-start | bytes 1572872 | tf_op jit(solution)/shard_map/ppermute | solution.py:694
  253.5 23.3 %collective-permute-start.22 = (f32[2,256,256]{2,1,0:T(8,128)S(1)}, f32[2,256,256]{2,1,0:T(8,128)S(1)}, u32[]{:S(2)}, u32[]{:S(2)}) collective-permute-start(f32[2,256,256]{2,1,0:T(8,128)S(1)} %get-tuple-element.93), channel_id=1, source_target_pairs={{0,6},{2,0},{4,2},{6,4},{1,7},{3,1},{5,3},{7,5},{8,14},{10,8},{12,... | collective-permute-start | bytes 1572872 | tf_op jit(solution)/shard_map/ppermute | solution.py:694

commit v6 on v4

--- a/solution.py
+++ b/solution.py
@@ -185,8 +185,14 @@
     return pl.BlockSpec(array.shape, lambda *_: (0,) * array.ndim, memory_space=memory)
 
 
-def faces_kernel(cond_ref, ground_ref, info_ref, cells_ref, load_ref, panel_ref, *refs, sides):
-    outs, (conduct_ref, grounds_ref, scaled_ref) = refs[:6], refs[6:]
+def faces_kernel(
+    table_ref, cond_ref, ground_ref, info_ref, cells_ref, load_ref, panel_ref, basis_ref, *refs, sides, at
+):
+    outs, (conduct_ref, grounds_ref, given_ref, scaled_ref, copy_sem) = refs[:6], refs[6:]
+    half = given_ref.shape[1]
+    start = pl.multiple_of(table_ref[at] * half, half)
+    copy = pltpu.make_async_copy(basis_ref.at[:, pl.ds(start, half)], given_ref, copy_sem)
+    copy.start()
     size_x, size_y, size_z = sides
     count, width = panel_ref.shape
     tile = 64
@@ -229,10 +235,11 @@
         for out, at in ((outs[4], 0), (outs[5], size_z - 1)):
             face = scaled_ref[p, pl.ds(at, size_x * size_y, stride=size_z), :]
             out[:, lanes] = face.astype(jnp.bfloat16)
+    copy.wait()
 
 
 def image_kernel(table_ref, panel_ref, conduct_ref, grounds_ref, *refs, sides, nb, at):
-    halos, (image_ref, *lead_refs, scaled_ref, square_ref) = refs[:6], refs[6:]
+    halos, (image_ref, kept_ref, sent_ref, scaled_ref, square_ref) = refs[:6], refs[6:]
     core = table_ref[at]
     size_x, size_y, size_z = sides
     width = panel_ref.shape[1]
@@ -293,62 +300,38 @@
 
     blocks = nb // LEAF
 
-    def put_block(refs, number, value):
-        half = refs[0].shape[0] // LEAF
-        rows = slice(number % half * LEAF, (number % half + 1) * LEAF)
-        kept = core == number // half
-
-        @pl.when(kept)
-        def _():
-            refs[0][rows, :] = value
-
-        @pl.when(jnp.logical_not(kept))
-        def _():
-            refs[1][rows, :] = value
-
-    def lower(refs):
-        number = 0
+    first_blocks = blocks * (blocks + 1) // 2
+    half = kept_ref.shape[0] // LEAF - 1
+
+    def put_block(number, value):
+        if number < first_blocks:
+            owner, place = divmod(number, first_blocks // 2)
+        else:
+            owner, place = divmod(number - first_blocks, half - first_blocks // 2)
+            place += first_blocks // 2
+        kept = core == owner
+        for ref, here in ((kept_ref, kept), (sent_ref, jnp.logical_not(kept))):
+            at_row = pl.multiple_of(jnp.where(here, place, half) * LEAF, LEAF)
+            ref[pl.ds(at_row, LEAF), :] = value
+
+    def lower(number):
         for i in range(blocks):
             for j in range(i + 1):
                 row, col = slice(i * LEAF, (i + 1) * LEAF), slice(j * LEAF, (j + 1) * LEAF)
-                put_block(refs, number, 0.5 * (square_ref[row, col] + square_ref[col, row].T))
+                put_block(number, 0.5 * (square_ref[row, col] + square_ref[col, row].T))
                 number += 1
         return number
 
     head, tail = slice(0, nb), slice(nb, 2 * nb)
     square_ref[...] = product(head, head)
-    lower(lead_refs[:2])
+    number = lower(0)
     square_ref[...] = product(tail, tail)
-    number = lower(lead_refs[2:])
+    number = lower(number)
     square_ref[...] = product(tail, head)
     for j in range(blocks):
         for i in range(blocks):
             row, col = slice(i * LEAF, (i + 1) * LEAF), slice(j * LEAF, (j + 1) * LEAF)
-            put_block(lead_refs[2:], number + j * blocks + i, square_ref[row, col])
-
-
-def copy_kernel(table_ref, in_ref, out_ref):
-    del table_ref
-    out_ref[...] = in_ref[...]
-
-
-def take_columns(table, at, array, width):
-    rows = array.shape[0]
-    tile = min(128, rows)
-    return pl.pallas_call(
-        copy_kernel,
-        grid_spec=pltpu.PrefetchScalarGridSpec(
-            num_scalar_prefetch=1,
-            grid=(rows // tile,),
-            in_specs=[pl.BlockSpec((tile, width), lambda t, tab: (t, tab[at]))],
-            out_specs=pl.BlockSpec((tile, width), lambda t, tab: (t, 0)),
-        ),
-        out_shape=jax.ShapeDtypeStruct((rows, width), array.dtype),
-        compiler_params=pltpu.CompilerParams(vmem_limit_bytes=58 * 2**20),
-        cost_estimate=pl.CostEstimate(
-            flops=0, transcendentals=0, bytes_accessed=4 * rows * width
-        ),
-    )(table, array)
+            put_block(number + j * blocks + i, square_ref[row, col])
 
 
 def products_kernel(table_ref, *refs):
@@ -469,12 +452,6 @@
 
 def swap_pairs():
     return [(0, 1), (1, 0)]
-
-
-def other_half(half, core):
-    other = lax.ppermute(half, "core", swap_pairs())
-    first = core == 0
-    return jnp.concatenate([jnp.where(first, half, other), jnp.where(first, other, half)], 0)
 
 
 def join_kernel(table_ref, *refs, at):
@@ -563,18 +540,24 @@
     face_rows = [cells_y * cells_z] * 2 + [cells_x * cells_z] * 2 + [cells_x * cells_y] * 2
     outs = [jax.ShapeDtypeStruct((n, cols), bf16) for n in face_rows]
     outs += [jax.ShapeDtypeStruct((count, LEAF), f32)] * 2
-    *faces, conduct, grounds = pl.pallas_call(
-        functools.partial(faces_kernel, sides=sides),
-        out_shape=outs,
-        grid=(1,),
-        in_specs=[block_of(cond_table, pltpu.SMEM), block_of(ground_table, pltpu.SMEM)]
-        + [block_of(info), block_of(port_rows), block_of(load_rows), panel_spec],
-        out_specs=[block_of(a) for a in outs],
-        scratch_shapes=[pltpu.VMEM((cols // LEAF, count, LEAF), f32)],
+    given = jax.ShapeDtypeStruct((count, width_k // 2), basis.dtype)
+    *faces, conduct, grounds, given = pl.pallas_call(
+        functools.partial(faces_kernel, sides=sides, at=given_at),
+        out_shape=[*outs, given],
+        grid_spec=pltpu.PrefetchScalarGridSpec(
+            num_scalar_prefetch=1,
+            grid=(1,),
+            in_specs=[block_of(cond_table, pltpu.SMEM), block_of(ground_table, pltpu.SMEM)]
+            + [block_of(info), block_of(port_rows), block_of(load_rows), panel_spec]
+            + [pl.BlockSpec(memory_space=pl.ANY)],
+            out_specs=[block_of(a) for a in outs] + [pl.BlockSpec(memory_space=pl.ANY)],
+            scratch_shapes=[
+                pltpu.VMEM((cols // LEAF, count, LEAF), f32),
+                pltpu.SemaphoreType.DMA,
+            ],
+        ),
         compiler_params=pltpu.CompilerParams(vmem_limit_bytes=58 * 2**20),
-    )(cond_table, ground_table, info, port_rows, load_rows, flat_basis)
-    later_table, _ = lax.optimization_barrier((table, faces))
-    given = take_columns(later_table, given_at, flat_basis, width_k // 2)
+    )(table, cond_table, ground_table, info, port_rows, load_rows, flat_basis, flat_basis)
     halos = []
     for i, (axis, size) in enumerate(
         (("gx", devices_x), (("gy", "core"), devices_y), ("gz", devices_z))
@@ -592,72 +575,70 @@
 
     blocks = NB // LEAF
     lower_rows = blocks * (blocks + 1) // 2 * LEAF
-    halos, _ = lax.optimization_barrier((halos, given))
-    first_part = jax.ShapeDtypeStruct((lower_rows // 2, LEAF), f32)
-    later_part = jax.ShapeDtypeStruct(((lower_rows + blocks * NB) // 2, LEAF), f32)
-    lead_parts = [first_part] * 2 + [later_part] * 2
+    half_rows = lower_rows + blocks * NB // 2
+    lead_parts = [jax.ShapeDtypeStruct((half_rows + LEAF, LEAF), f32)] * 2
     outs = [jax.ShapeDtypeStruct((count, cols), bf16), *lead_parts]
-    image, first_kept, first_sent, later_kept, later_sent = pl.pallas_call(
+    image, lead_kept, lead_sent = pl.pallas_call(
         functools.partial(image_kernel, sides=sides, nb=NB, at=core_at),
         out_shape=outs,
         grid_spec=pltpu.PrefetchScalarGridSpec(
             num_scalar_prefetch=1,
             grid=(1,),
-            in_specs=[panel_spec] + [block_of(a) for a in (conduct, grounds, *halos)],
-            out_specs=[block_of(a) for a in outs],
+            in_specs=[panel_spec] + [whole()] * 8,
+            out_specs=[whole()] * 3,
             scratch_shapes=[pltpu.VMEM((count, LEAF), f32), pltpu.VMEM((NB, NB), f32)],
         ),
-        compiler_params=pltpu.CompilerParams(vmem_limit_bytes=58 * 2**20),
+        compiler_params=pltpu.CompilerParams(vmem_limit_bytes=54 * 2**20),
     )(table, flat_basis, conduct, grounds, *halos)
 
     other_image = lax.ppermute(image, "core", swap_pairs())
-
-    axes = ("gx", "gy", "gz")
-    chips = devices_x * chips_y * devices_z
-
-    def halved(kept, sent):
-        return kept + lax.ppermute(sent, "core", swap_pairs())
-
-    def exchanged(rows):
-        rows = rows.reshape(chips, -1, LEAF)
+    other_basis = lax.ppermute(given, "core", swap_pairs())
+
+    plane_axes = ("gy", "gz")
+    chips = chips_y * devices_z
+
+    def exchanged(rows, axes):
         return lax.all_to_all(rows, axes, split_axis=0, concat_axis=0, tiled=True)
 
-    def for_all(own):
-        return jnp.broadcast_to(own, (chips, *own.shape))
-
-    first_half, later_half = halved(first_kept, first_sent), halved(later_kept, later_sent)
-    first_terms = exchanged(first_half)
+    def for_all(own, size):
+        return jnp.broadcast_to(own, (size, *own.shape))
+
+    lead_got = lax.ppermute(lead_sent, "core", swap_pairs())
+    lead_half = lead_kept[:half_rows] + lead_got[:half_rows]
+    lead_terms = exchanged(lead_half.reshape(chips, -1, LEAF), plane_axes)
 
     def chip_products(images, lists, dtype):
         return products(table, [flat_basis, other_basis], images, lists, narrow, dtype)
 
-    images, _ = lax.optimization_barrier(([image, other_image], first_half))
+    images, _ = lax.optimization_barrier(([image, other_image], lead_half))
     sent_a = [chip_products(images, lists_a[d], bf16) for d in range(1, devices_z)]
     sent_b = [chip_products(images, lists_b[d], bf16) for d in range(1, chips_y)]
     got_a = [move(a, "gz", d) for d, a in enumerate(sent_a, 1)]
     got_b = [move(a, "gy", d) for d, a in enumerate(sent_b, 1)]
-    first_terms, _ = lax.optimization_barrier((first_terms, (sent_a, sent_b)))
-    own = jnp.sum(first_terms, axis=0)
-    share = own.shape[0]
-    images, _ = lax.optimization_barrier((images, own))
     own_a, own_b = (chip_products(images, lists[0], f32) for lists in (lists_a, lists_b))
-    both = jnp.concatenate([for_all(own), later_half.reshape(chips, -1, LEAF)], 1)
-    both = lax.all_to_all(both, axes, split_axis=0, concat_axis=0, tiled=True)
-    both, _ = lax.optimization_barrier((both, (own_a, own_b)))
+    lead_terms, _ = lax.optimization_barrier((lead_terms, (own_a, own_b)))
+    own = jnp.sum(lead_terms, axis=0).reshape(devices_x, -1, LEAF)
+    own = jnp.sum(exchanged(own, "gx"), axis=0)
+    own = exchanged(for_all(own, devices_x), "gx").reshape(-1, LEAF)
+    own = for_all(own, chips)
+    (got_a, got_b), _ = lax.optimization_barrier(((got_a, got_b), own))
+    lead_half = exchanged(own, plane_axes).reshape(-1, LEAF)
     sums_a, sums_b = [own_a, *got_a], [own_b, *got_b]
 
     further_a = [add_blocks(table, sums_a, *next_a[d], narrow, bf16) for d in range(1, chips_y)]
     further_b = [add_blocks(table, sums_b, *next_b[d], narrow, bf16) for d in range(1, devices_z)]
-    both, _ = lax.optimization_barrier((both, (further_a, further_b)))
+    lead_half, _ = lax.optimization_barrier((lead_half, (further_a, further_b)))
     further_a = [move(a, "gy", d) for d, a in enumerate(further_a, 1)]
     further_b = [move(a, "gz", d) for d, a in enumerate(further_b, 1)]
-    first_rows = other_half(both[:, :share].reshape(-1, LEAF), core)
-    later_half = exchanged(for_all(jnp.sum(both[:, share:], axis=0))).reshape(-1, LEAF)
+    other = lax.ppermute(lead_half, "core", swap_pairs())
+    lower_half, upper_half = jnp.where(core == 0, lead_half, other), jnp.where(core == 0, other, lead_half)
+    first = lower_rows // 2
+    first_rows = jnp.concatenate([lower_half[:first], upper_half[:first]], 0)
+    later_rows = jnp.concatenate([lower_half[first:], upper_half[first:]], 0)
     inverse_0 = first_panel(first_rows, NB)
-    (further_a, further_b, later_half), inverse_0 = lax.optimization_barrier(
-        ((further_a, further_b, later_half), inverse_0)
+    (further_a, further_b), inverse_0 = lax.optimization_barrier(
+        ((further_a, further_b), inverse_0)
     )
-    later_rows = other_half(later_half, core)
 
     terms = []
     for zz in range(split):

time: 269 us -> 363 us (1.35)
  Pallas kernels: 108 us -> 229 us
  waiting for transfers between devices: 81.6 us -> 50.5 us
  blocking collectives: 0 us -> 24.3 us
  starting transfers between devices: 54.9 us -> 43.8 us
  local copies, waits for them, and re-layouts: 13.9 us -> 6.9 us
    pallas_call x2 -> x1, Pallas kernels: 9.67 us -> 131 us  [local(): pl.pallas_call(functools.partial(faces_kernel, sides=sides, at=given_at),...]
    ppermute x4, waiting for transfers between devices: 44.5 us -> 6.09 us  [move(): return lax.ppermute(array, axis, [(i, (i + d) % size) for i in range(size)])]
    all_to_all x0 -> x2, blocking collectives: none -> 24.3 us  [exchanged(): return lax.all_to_all(rows, axes, split_axis=0, concat_axis=0, tiled=True)]
    all_to_all x1 -> x0, starting transfers between devices: 6.36 us -> none  [local(): both = lax.all_to_all(both, axes, split_axis=0, concat_axis=0, tiled=True)]
    unnamed x40 -> x16, local copies, waits for them, and re-layouts: 9.4 us -> 3.17 us
    all_to_all x2, waiting for transfers between devices: 0.01 us -> 5.97 us  [exchanged(): return lax.all_to_all(rows, axes, split_axis=0, concat_axis=0, tiled=True)]
    all_to_all x2, starting transfers between devices: 11.8 us -> 7.37 us  [exchanged(): return lax.all_to_all(rows, axes, split_axis=0, concat_axis=0, tiled=True)]
    ppermute x2, waiting for transfers between devices: 0.01 us -> 3.8 us  [local(): halos.append(lax.ppermute(low, axis, [(k + 1, k) for k in range(size - 1)]))]
  transfers between devices with their start and end apart: 26 -> 23, of which waited for: 8 -> 9; matrix products, arithmetic and copies ran while one was open for 2% -> 2% of each run, Pallas kernels for 35% -> 25%
where the time goes in v6:
time: 363 us; the launch traced here: 362 us
  Pallas kernels  229 us (63%)
  waiting for transfers between devices  50.5 us (14%)
  starting transfers between devices  43.8 us (12%)
  blocking collectives  24.3 us (7%)
  local copies, waits for them, and re-layouts  6.9 us (2%)
  other arithmetic  5.95 us (2%)
    pallas_call x1, Pallas kernels, local(): pl.pallas_call(functools.partial(faces_kernel, sides=sides, at=given_at),...  131 us
    pallas_call x2, Pallas kernels, panel_call(): pl.pallas_call(kernel, out_shape=[jax.ShapeDtypeStruct((nb, nb), jnp.floa...  55.9 us
    all_to_all x2, blocking collectives, exchanged(): return lax.all_to_all(rows, axes, split_axis=0, concat_axis=0, tiled=True)  24.3 us
    ppermute x3, waiting for transfers between devices, local(): pairs[d] = lax.ppermute(pairs[d], ('gy', 'core'), route)  22.6 us
    pallas_call x4, Pallas kernels, products(): pl.pallas_call(products_kernel, grid_spec=pltpu.PrefetchScalarGridSpec(nu...  22.1 us
    ppermute x4, starting transfers between devices, local(): x_got.append(lax.ppermute(x_sent[step], ('gx', 'gy', 'core'), pairs))  13.7 us
    ppermute x4, waiting for transfers between devices, local(): x_got.append(lax.ppermute(x_sent[step], ('gx', 'gy', 'core'), pairs))  9.03 us
    all_to_all x2, starting transfers between devices, exchanged(): return lax.all_to_all(rows, axes, split_axis=0, concat_axis=0, tiled=True)  7.37 us
  transfers between devices with their start and end apart: 23, of which 9 were waited for; matrix products, arithmetic and copies ran while one was open for 2% of the time, Pallas kernels for 25%

profile of v6, /device:TPU:1, one launch (start us, length us, event | category | flops | bytes accessed | tf_op | source)
XLA Modules:
  0.0 361.7 jit_solution(1421831374788780203)
XLA Ops:
  0.8 0.8 stack.164
  2.0 0.9 copy.11.info_ref
  3.5 131.2 %shard_map.77 = (bf16[64,1024]{1,0:T(8,128)(2,1)}, bf16[64,1024]{1,0:T(8,128)(2,1)}, bf16[64,1024]{1,0:T(8,128)(2,1)}, bf16[64,1024]{1,0:T(8,128)(2,1)}, bf16[64...) custom-call(s32[38]{0:T(128)} %stack.163.table_ref, ...), custom_call_target="tpu_custom_call" | custom-call | tf_op jit(solution)/shard_map/pallas_call | solution.py:544
  134.8 0.9 broadcast_select_fusion.4
  135.8 2.7 collective-permute-start.5
  138.5 3.2 collective-permute-start.1
  141.7 1.3 collective-permute-start.2
  143.0 3.6 collective-permute-start.3
  146.6 1.9 collective-permute-start.4
  148.5 0.7 broadcast_select_fusion.2
  149.3 3.8 %collective-permute-done.4.refs_3_ = bf16[64,1024]{1,0:T(8,128)(2,1)S(1)} collective-permute-done((bf16[64,1024]{1,0:T(8,128)(2,1)}, bf16[64,1024]{1,0:T(8,128)(2,1)S(1)}, u32[]{:S(2)}, u32[]{:S(2)}) %collective-permute-start.4) | collective-permute-done | bytes 131104 | tf_op jit(solution)/shard_map/ppermute | solution.py:573
  153.8 6.6 %shard_map.78 = (bf16[512,1024]{1,0:T(8,128)(2,1)}, f32[2432,128]{1,0:T(8,128)}, f32[2432,128]{1,0:T(8,128)}) custom-call(s32[38]{0:T(128)} %stack.163.table_ref, bf16[512,8192]{1,0:T(8,128)(2,1)} %bitcast.46, f32[512,128]{1,0:T(8,128)} %get-tuple-element.43.conduct_ref, f32[512,128]{1,0:T(8,128)} %get-tuple-element.44.grounds_ref, ...), custom_call_target="tpu_custom_call" | custom-call | tf_op jit(solution)/shard_map/pallas_call | solution.py:581
  160.8 2.6 collective-permute-done.7
  163.5 2.4 slice_add_fusion
  165.9 3.7 %all-to-all-start = ((f32[4,576,128]{2,1,0:T(8,128)}), f32[4,576,128]{2,1,0:T(8,128)S(1)}, u32[]{:S(2)}, u32[]{:S(2)}) async-start(f32[4,576,128]{2,1,0:T(8,128)} %bitcast.40), calls=%async_computation | async-start | bytes 2359296 | tf_op jit(solution)/shard_map/all_to_all | solution.py:601
  169.6 5.3 %shard_map.80 = bf16[1024,1024]{1,0:T(8,128)(2,1)} custom-call(s32[38]{0:T(128)S(1)} %copy-done.3, bf16[512,8192]{1,0:T(8,128)(2,1)} %bitcast.47, bf16[512,4096]{1,0:T(8,128)(2,1)} %collective-permute-done.refs_1_, bf16[512,1024]{1,0:T(8,128)(2,1)S(1)} %copy-done.2, bf16[512,1024]{1,0:T(8,128)(2,1)S(1)} %collective-permute-done.6.refs_3_), custom_call_target="tpu_custom_call" | custom-call | flops 2147483648 | bytes 8388608 | tf_op jit(solution)/shard_map/pallas_call | solution.py:362
  175.0 1.4 collective-permute-start.8
  176.4 5.3 %shard_map.81 = bf16[1024,1024]{1,0:T(8,128)(2,1)} custom-call(s32[38]{0:T(128)S(1)} %copy-done.3, bf16[512,8192]{1,0:T(8,128)(2,1)} %bitcast.48, bf16[512,4096]{1,0:T(8,128)(2,1)} %collective-permute-done.refs_1_, bf16[512,1024]{1,0:T(8,128)(2,1)S(1)} %copy-done.2, bf16[512,1024]{1,0:T(8,128)(2,1)S(1)} %collective-permute-done.6.refs_3_), custom_call_target="tpu_custom_call" | custom-call | flops 2147483648 | bytes 8388608 | tf_op jit(solution)/shard_map/pallas_call | solution.py:362
  181.7 1.2 collective-permute-start.9
  182.9 5.7 %shard_map.82.refs_0_.refs_3_ = f32[1024,1024]{1,0:T(8,128)} custom-call(s32[38]{0:T(128)S(1)} %copy-done.3, bf16[512,8192]{1,0:T(8,128)(2,1)} %bitcast.49, bf16[512,4096]{1,0:T(8,128)(2,1)} %collective-permute-done.refs_1_, bf16[512,1024]{1,0:T(8,128)(2,1)S(1)} %copy-done.2, bf16[512,1024]{1,0:T(8,128)(2,1)S(1)} %collective-permute-done.6.refs_3_), custom_call_target="tpu_custom_call" | custom-call | flops 2147483648 | bytes 8388608 | tf_op jit(solution)/shard_map/pallas_call | solution.py:362
  188.6 5.7 %shard_map.79.refs_0_ = f32[1024,1024]{1,0:T(8,128)} custom-call(s32[38]{0:T(128)S(1)} %copy-done.3, bf16[512,8192]{1,0:T(8,128)(2,1)} %bitcast.50, bf16[512,4096]{1,0:T(8,128)(2,1)} %collective-permute-done.refs_1_, bf16[512,1024]{1,0:T(8,128)(2,1)S(1)} %copy-done.2, bf16[512,1024]{1,0:T(8,128)(2,1)S(1)} %collective-permute-done.6.refs_3_), custom_call_target="tpu_custom_call" | custom-call | flops 2147483648 | bytes 8388608 | tf_op jit(solution)/shard_map/pallas_call | solution.py:362
  194.4 12.7 %all_to_all.20 = f32[4,144,128]{2,1,0:T(8,128)S(1)} all-to-all(f32[4,144,128]{2,1,0:T(8,128)S(1)} %bitcast.53), channel_id=1, replica_groups=mesh['gx'=4,'gy'=2,'core'=2,'gz'=2] {'gx'}, dimensions={0} | all-to-all | bytes 589824 | tf_op jit(solution)/shard_map/all_to_all | solution.py:601
  207.2 11.6 %all_to_all.21 = f32[4,144,128]{2,1,0:T(8,128)S(1)} all-to-all(f32[4,144,128]{2,1,0:T(8,128)S(1)} %broadcast_in_dim.24), channel_id=1, replica_groups=mesh['gx'=4,'gy'=2,'core'=2,'gz'=2] {'gx'}, dimensions={0} | all-to-all | bytes 589824 | tf_op jit(solution)/shard_map/all_to_all | solution.py:601
  218.7 1.1 broadcast_in_dim.25
  219.9 3.7 %all-to-all-start.3 = ((f32[4,576,128]{2,1,0:T(8,128)}), f32[4,576,128]{2,1,0:T(8,128)S(1)}, u32[]{:S(2)}, u32[]{:S(2)}) async-start(f32[4,576,128]{2,1,0:T(8,128)} %broadcast_in_dim.25), calls=%async_computation.3 | async-start | bytes 2359296 | tf_op jit(solution)/shard_map/all_to_all | solution.py:601
  223.6 6.1 %collective-permute-done.8.refs_1_ = bf16[1024,1024]{1,0:T(8,128)(2,1)} collective-permute-done((bf16[1024,1024]{1,0:T(8,128)(2,1)}, bf16[1024,1024]{1,0:T(8,128)(2,1)}, u32[]{:S(2)}, u32[]{:S(2)}) %collective-permute-start.8) | collective-permute-done | bytes 2097184 | tf_op jit(solution)/shard_map/ppermute | solution.py:527
  229.7 2.2 copy-done.1
  231.8 2.2 shard_map.83
  234.3 1.9 shard_map.84
  236.3 6.0 %all-to-all-done.3 = f32[4,576,128]{2,1,0:T(8,128)S(1)} async-done(((f32[4,576,128]{2,1,0:T(8,128)}), f32[4,576,128]{2,1,0:T(8,128)S(1)}, u32[]{:S(2)}, u32[]{:S(2)}) %all-to-all-start.3) | async-done | bytes 1179680 | tf_op jit(solution)/shard_map/all_to_all | solution.py:601
  242.2 1.0 collective-permute-start.12
  243.2 1.1 collective-permute-start.11
  244.3 1.2 collective-permute-start.10
  245.8 1.4 broadcast_select_fusion.1
  247.3 27.0 %shard_map.85.w0_ref.refs_4_ = f32[512,512]{1,0:T(8,128)S(1)} custom-call(f32[1280,128]{1,0:T(8,128)S(1)} %pad_maximum_fusion.1.packed_ref), custom_call_target="tpu_custom_call" | custom-call | flops 512 | bytes 512 | tf_op jit(solution)/shard_map/pallas_call | solution.py:159
  274.4 4.7 %shard_map.86 = (bf16[256,1024]{1,0:T(8,128)(2,1)S(1)}, bf16[256,1024]{1,0:T(8,128)(2,1)S(1)}, bf16[256,1024]{1,0:T(8,128)(2,1)S(1)}, bf16[256,1024]{1,0:T(8,128...) custom-call(s32[38]{0:T(128)S(1)} %copy-done.3, f32[1024,1024]{1,0:T(8,128)} %shard_map.79.refs_0_, ...), custom_call_target="tpu_custom_call" | custom-call | bytes 14680064 | tf_op jit(solution)/shard_map/pallas_call | solution.py:436
  279.5 5.3 %collective-permute-start.13 = (bf16[256,1024]{1,0:T(8,128)(2,1)S(1)}, bf16[256,1024]{1,0:T(8,128)(2,1)S(1)}, u32[]{:S(2)}, u32[]{:S(2)}) collective-permute-start(bf16[256,1024]{1,0:T(8,128)(2,1)S(1)} %get-tuple-element.63), channel_id=1, source_target_pairs={{2,16},{6,20},{8,2},{10,18},{12,6},{14,22},{16,8},{18,24},{20,12},... | collective-permute-start | bytes 1572872 | tf_op jit(solution)/shard_map/ppermute | solution.py:663
  284.8 3.2 collective-permute-start.14
  288.0 1.9 collective-permute-start.15
  290.0 3.3 collective-permute-start.16
  293.5 28.8 %shard_map.87 = (f32[512,512]{1,0:T(8,128)S(1)}, f32[512,512]{1,0:T(8,128)S(1)}) custom-call(f32[3328,128]{1,0:T(8,128)S(1)} %pad_maximum_fusion.packed_ref, f32[512,512]{1,0:T(8,128)S(1)} %shard_map.85.w0_ref.refs_4_), custom_call_target="tpu_custom_call" | custom-call | flops 512 | bytes 512 | tf_op jit(solution)/shard_map/pallas_call | solution.py:159
  322.4 9.0 %collective-permute-done.16.refs_3_ = bf16[256,1024]{1,0:T(8,128)(2,1)S(1)} collective-permute-done((bf16[256,1024]{1,0:T(8,128)(2,1)S(1)}, bf16[256,1024]{1,0:T(8,128)(2,1)S(1)}, u32[]{:S(2)}, u32[]{:S(2)}) %collective-permute-start.16) | collective-permute-done | bytes 524320 | tf_op jit(solution)/shard_map/ppermute | solution.py:663
  331.4 2.6 shard_map.88
  334.1 2.3 collective-permute-start.19
  336.4 0.7 collective-permute-start.20
  337.1 5.4 %collective-permute-done.18.refs_1_ = f32[2,256,256]{2,1,0:T(8,128)S(1)} collective-permute-done((f32[2,256,256]{2,1,0:T(8,128)S(1)}, f32[2,256,256]{2,1,0:T(8,128)S(1)}, u32[]{:S(2)}, u32[]{:S(2)}) %collective-permute-start.18) | collective-permute-done | bytes 524320 | tf_op jit(solution)/shard_map/ppermute | solution.py:684
  342.5 16.6 %collective-permute-done.19.refs_2_ = f32[2,256,256]{2,1,0:T(8,128)S(1)} collective-permute-done((f32[2,256,256]{2,1,0:T(8,128)S(1)}, f32[2,256,256]{2,1,0:T(8,128)S(1)}, u32[]{:S(2)}, u32[]{:S(2)}) %collective-permute-start.19) | collective-permute-done | bytes 524320 | tf_op jit(solution)/shard_map/ppermute | solution.py:684
  359.7 2.0 shard_map.89
  (52 shorter events, 4.5 us)
Async XLA Ops:
  134.7 34.9 %collective-permute-start = (bf16[512,4096]{1,0:T(8,128)(2,1)}, bf16[512,4096]{1,0:T(8,128)(2,1)}, u32[]{:S(2)}, u32[]{:S(2)}) collective-permute-start(bf16[512,4096]{1,0:T(8,128)(2,1)} %get-tuple-element.42), channel_id=1, source_target_pairs={{0,2},{2,0},{1,3},{3,1},{4,6},{6,4},{5,7},{7,5},{8,10},{10,8},{9,1... | collective-permute-start | bytes 12582920 | tf_op jit(solution)/shard_map/ppermute | solution.py:595
  135.8 10.9 %collective-permute-start.5 = (bf16[64,1024]{1,0:T(8,128)(2,1)S(1)}, bf16[64,1024]{1,0:T(8,128)(2,1)S(1)}, u32[]{:S(2)}, u32[]{:S(2)}) collective-permute-start(bf16[64,1024]{1,0:T(8,128)(2,1)S(1)} %broadcast_select_fusion.4), channel_id=1, source_target_pairs={{0,1},{1,0},{2,3},{3,2},{4,5},{5,4},{6,7},{7,6},{8,9},{9,8},{10,11... | collective-permute-start | bytes 393224 | tf_op jit(solution)/shard_map/ppermute | solution.py:568
  138.5 10.8 %collective-permute-start.1 = (bf16[64,1024]{1,0:T(8,128)(2,1)}, bf16[64,1024]{1,0:T(8,128)(2,1)S(1)}, u32[]{:S(2)}, u32[]{:S(2)}) collective-permute-start(bf16[64,1024]{1,0:T(8,128)(2,1)} %get-tuple-element.45), channel_id=1, source_target_pairs={{0,8},{8,16},{16,24},{1,9},{9,17},{17,25},{2,10},{10,18},{18,26},{... | collective-permute-start | bytes 393224 | tf_op jit(solution)/shard_map/ppermute | solution.py:572
  141.7 7.6 %collective-permute-start.2 = (bf16[64,1024]{1,0:T(8,128)(2,1)}, bf16[64,1024]{1,0:T(8,128)(2,1)S(1)}, u32[]{:S(2)}, u32[]{:S(2)}) collective-permute-start(bf16[64,1024]{1,0:T(8,128)(2,1)} %get-tuple-element.46), channel_id=1, source_target_pairs={{8,0},{16,8},{24,16},{9,1},{17,9},{25,17},{10,2},{18,10},{26,18},{... | collective-permute-start | bytes 393224 | tf_op jit(solution)/shard_map/ppermute | solution.py:573
  143.0 6.3 %collective-permute-start.3 = (bf16[64,1024]{1,0:T(8,128)(2,1)}, bf16[64,1024]{1,0:T(8,128)(2,1)S(1)}, u32[]{:S(2)}, u32[]{:S(2)}) collective-permute-start(bf16[64,1024]{1,0:T(8,128)(2,1)} %get-tuple-element.47), channel_id=1, source_target_pairs={{0,2},{2,4},{4,6},{1,3},{3,5},{5,7},{8,10},{10,12},{12,14},{9,11},... | collective-permute-start | bytes 393224 | tf_op jit(solution)/shard_map/ppermute | solution.py:572
  146.6 6.5 %collective-permute-start.4 = (bf16[64,1024]{1,0:T(8,128)(2,1)}, bf16[64,1024]{1,0:T(8,128)(2,1)S(1)}, u32[]{:S(2)}, u32[]{:S(2)}) collective-permute-start(bf16[64,1024]{1,0:T(8,128)(2,1)} %get-tuple-element.48), channel_id=1, source_target_pairs={{2,0},{4,2},{6,4},{3,1},{5,3},{7,5},{10,8},{12,10},{14,12},{11,9},... | collective-permute-start | bytes 393224 | tf_op jit(solution)/shard_map/ppermute | solution.py:573
  149.3 3.8 %copy-start.4 = (bf16[64,1024]{1,0:T(8,128)(2,1)}, bf16[64,1024]{1,0:T(8,128)(2,1)S(1)}, u32[]{:S(2)}) copy-start(bf16[64,1024]{1,0:T(8,128)(2,1)S(1)} %collective-permute-done.1.refs_0_) | copy-start | bytes 393220
  149.3 3.8 %copy-start.5 = (bf16[64,1024]{1,0:T(8,128)(2,1)}, bf16[64,1024]{1,0:T(8,128)(2,1)S(1)}, u32[]{:S(2)}) copy-start(bf16[64,1024]{1,0:T(8,128)(2,1)S(1)} %collective-permute-done.2.refs_1_) | copy-start | bytes 393220
  149.3 3.8 %copy-start.6 = (bf16[64,1024]{1,0:T(8,128)(2,1)}, bf16[64,1024]{1,0:T(8,128)(2,1)S(1)}, u32[]{:S(2)}) copy-start(bf16[64,1024]{1,0:T(8,128)(2,1)S(1)} %collective-permute-done.3.refs_2_) | copy-start | bytes 393220
  153.1 0.7 copy-start.7
  160.3 3.2 collective-permute-start.7
  160.3 9.3 %collective-permute-start.6 = (bf16[512,1024]{1,0:T(8,128)(2,1)}, bf16[512,1024]{1,0:T(8,128)(2,1)S(1)}, u32[]{:S(2)}, u32[]{:S(2)}) collective-permute-start(bf16[512,1024]{1,0:T(8,128)(2,1)} %get-tuple-element.54.refs_2_), channel_id=1, source_target_pairs={{0,2},{2,0},{1,3},{3,1},{4,6},{6,4},{5,7},{7,5},{8,10},{10,8},{9,1... | collective-permute-start | bytes 3145736 | tf_op jit(solution)/shard_map/ppermute | solution.py:594
  165.9 3.7 %copy-start.2 = (bf16[512,1024]{1,0:T(8,128)(2,1)S(1)}, bf16[512,1024]{1,0:T(8,128)(2,1)}, u32[]{:S(2)}) copy-start(bf16[512,1024]{1,0:T(8,128)(2,1)} %get-tuple-element.54.refs_2_) | copy-start | bytes 3145732
  165.9 3.7 %copy-start.3 = (s32[38]{0:T(128)S(1)}, s32[38]{0:T(128)}, u32[]{:S(2)}) copy-start(s32[38]{0:T(128)} %stack.163.table_ref) | copy-start | bytes 460
  165.9 28.4 %all-to-all-start = ((f32[4,576,128]{2,1,0:T(8,128)}), f32[4,576,128]{2,1,0:T(8,128)S(1)}, u32[]{:S(2)}, u32[]{:S(2)}) async-start(f32[4,576,128]{2,1,0:T(8,128)} %bitcast.40), calls=%async_computation | async-start | bytes 2359296 | tf_op jit(solution)/shard_map/all_to_all | solution.py:601
  175.0 54.7 %collective-permute-start.8 = (bf16[1024,1024]{1,0:T(8,128)(2,1)}, bf16[1024,1024]{1,0:T(8,128)(2,1)}, u32[]{:S(2)}, u32[]{:S(2)}) collective-permute-start(bf16[1024,1024]{1,0:T(8,128)(2,1)} %shard_map.80), channel_id=1, source_target_pairs={{0,1},{1,0},{2,3},{3,2},{4,5},{5,4},{6,7},{7,6},{8,9},{9,8},{10,11... | collective-permute-start | bytes 6291464 | tf_op jit(solution)/shard_map/ppermute | solution.py:527
  181.7 48.0 %collective-permute-start.9 = (bf16[1024,1024]{1,0:T(8,128)(2,1)}, bf16[1024,1024]{1,0:T(8,128)(2,1)}, u32[]{:S(2)}, u32[]{:S(2)}) collective-permute-start(bf16[1024,1024]{1,0:T(8,128)(2,1)} %shard_map.81), channel_id=1, source_target_pairs={{0,4},{4,0},{1,5},{5,1},{2,6},{6,2},{3,7},{7,3},{8,12},{12,8},{9,1... | collective-permute-start | bytes 6291464 | tf_op jit(solution)/shard_map/ppermute | solution.py:527
  219.9 22.4 %all-to-all-start.3 = ((f32[4,576,128]{2,1,0:T(8,128)}), f32[4,576,128]{2,1,0:T(8,128)S(1)}, u32[]{:S(2)}, u32[]{:S(2)}) async-start(f32[4,576,128]{2,1,0:T(8,128)} %broadcast_in_dim.25), calls=%async_computation.3 | async-start | bytes 2359296 | tf_op jit(solution)/shard_map/all_to_all | solution.py:601
  229.7 2.2 copy-start.1
  231.8 2.5 copy-start
  242.2 3.6 collective-permute-start.12
  243.2 31.2 %collective-permute-start.11 = (bf16[512,1024]{1,0:T(8,128)(2,1)S(1)}, bf16[512,1024]{1,0:T(8,128)(2,1)S(1)}, u32[]{:S(2)}, u32[]{:S(2)}) collective-permute-start(bf16[512,1024]{1,0:T(8,128)(2,1)S(1)} %shard_map.84), channel_id=1, source_target_pairs={{0,1},{1,0},{2,3},{3,2},{4,5},{5,4},{6,7},{7,6},{8,9},{9,8},{10,11... | collective-permute-start | bytes 3145736 | tf_op jit(solution)/shard_map/ppermute | solution.py:527
  244.3 30.1 %collective-permute-start.10 = (bf16[512,1024]{1,0:T(8,128)(2,1)S(1)}, bf16[512,1024]{1,0:T(8,128)(2,1)S(1)}, u32[]{:S(2)}, u32[]{:S(2)}) collective-permute-start(bf16[512,1024]{1,0:T(8,128)(2,1)S(1)} %shard_map.83), channel_id=1, source_target_pairs={{0,4},{4,0},{1,5},{5,1},{2,6},{6,2},{3,7},{7,3},{8,12},{12,8},{9,1... | collective-permute-start | bytes 3145736 | tf_op jit(solution)/shard_map/ppermute | solution.py:527
  279.1 52.4 %collective-permute-start.17 = (f32[256,1024]{1,0:T(8,128)S(1)}, f32[256,1024]{1,0:T(8,128)S(1)}, u32[]{:S(2)}, u32[]{:S(2)}) collective-permute-start(f32[256,1024]{1,0:T(8,128)S(1)} %get-tuple-element.67), channel_id=1, source_target_pairs={{0,2},{2,0},{1,3},{3,1},{4,6},{6,4},{5,7},{7,5},{8,10},{10,8},{9,1... | collective-permute-start | bytes 3145736 | tf_op jit(solution)/shard_map/ppermute | solution.py:664
  279.5 42.9 %collective-permute-start.13 = (bf16[256,1024]{1,0:T(8,128)(2,1)S(1)}, bf16[256,1024]{1,0:T(8,128)(2,1)S(1)}, u32[]{:S(2)}, u32[]{:S(2)}) collective-permute-start(bf16[256,1024]{1,0:T(8,128)(2,1)S(1)} %get-tuple-element.63), channel_id=1, source_target_pairs={{2,16},{6,20},{8,2},{10,18},{12,6},{14,22},{16,8},{18,24},{20,12},... | collective-permute-start | bytes 1572872 | tf_op jit(solution)/shard_map/ppermute | solution.py:663
  284.8 37.6 %collective-permute-start.14 = (bf16[256,1024]{1,0:T(8,128)(2,1)S(1)}, bf16[256,1024]{1,0:T(8,128)(2,1)S(1)}, u32[]{:S(2)}, u32[]{:S(2)}) collective-permute-start(bf16[256,1024]{1,0:T(8,128)(2,1)S(1)} %get-tuple-element.64), channel_id=1, source_target_pairs={{2,18},{6,22},{10,24},{14,28},{16,10},{18,26},{20,14},{22,30},{24,... | collective-permute-start | bytes 1572872 | tf_op jit(solution)/shard_map/ppermute | solution.py:663
  288.0 34.3 %collective-permute-start.15 = (bf16[256,1024]{1,0:T(8,128)(2,1)S(1)}, bf16[256,1024]{1,0:T(8,128)(2,1)S(1)}, u32[]{:S(2)}, u32[]{:S(2)}) collective-permute-start(bf16[256,1024]{1,0:T(8,128)(2,1)S(1)} %get-tuple-element.65), channel_id=1, source_target_pairs={{0,8},{2,24},{4,12},{6,28},{10,26},{14,30},{16,0},{20,4},{24,2},{2... | collective-permute-start | bytes 1572872 | tf_op jit(solution)/shard_map/ppermute | solution.py:663
  290.0 41.4 %collective-permute-start.16 = (bf16[256,1024]{1,0:T(8,128)(2,1)S(1)}, bf16[256,1024]{1,0:T(8,128)(2,1)S(1)}, u32[]{:S(2)}, u32[]{:S(2)}) collective-permute-start(bf16[256,1024]{1,0:T(8,128)(2,1)S(1)} %get-tuple-element.66), channel_id=1, source_target_pairs={{0,10},{2,26},{4,14},{6,30},{8,0},{10,16},{12,4},{14,20},{16,2},{2... | collective-permute-start | bytes 1572872 | tf_op jit(solution)/shard_map/ppermute | solution.py:663
  334.0 8.5 %collective-permute-start.18 = (f32[2,256,256]{2,1,0:T(8,128)S(1)}, f32[2,256,256]{2,1,0:T(8,128)S(1)}, u32[]{:S(2)}, u32[]{:S(2)}) collective-permute-start(f32[2,256,256]{2,1,0:T(8,128)S(1)} %get-tuple-element.79), channel_id=1, source_target_pairs={{0,2},{2,4},{4,6},{6,0},{1,3},{3,5},{5,7},{7,1},{8,10},{10,12},{12... | collective-permute-start | bytes 1572872 | tf_op jit(solution)/shard_map/ppermute | solution.py:684
  334.1 25.0 %collective-permute-start.19 = (f32[2,256,256]{2,1,0:T(8,128)S(1)}, f32[2,256,256]{2,1,0:T(8,128)S(1)}, u32[]{:S(2)}, u32[]{:S(2)}) collective-permute-start(f32[2,256,256]{2,1,0:T(8,128)S(1)} %get-tuple-element.80), channel_id=1, source_target_pairs={{0,4},{2,6},{4,0},{6,2},{1,5},{3,7},{5,1},{7,3},{8,12},{10,14},{12... | collective-permute-start | bytes 1572872 | tf_op jit(solution)/shard_map/ppermute | solution.py:684
  336.4 23.3 %collective-permute-start.20 = (f32[2,256,256]{2,1,0:T(8,128)S(1)}, f32[2,256,256]{2,1,0:T(8,128)S(1)}, u32[]{:S(2)}, u32[]{:S(2)}) collective-permute-start(f32[2,256,256]{2,1,0:T(8,128)S(1)} %get-tuple-element.81), channel_id=1, source_target_pairs={{0,6},{2,0},{4,2},{6,4},{1,7},{3,1},{5,3},{7,5},{8,14},{10,8},{12,... | collective-permute-start | bytes 1572872 | tf_op jit(solution)/shard_map/ppermute | solution.py:684

commit v7 on v6

--- a/solution.py
+++ b/solution.py
@@ -188,11 +188,21 @@
 def faces_kernel(
     table_ref, cond_ref, ground_ref, info_ref, cells_ref, load_ref, panel_ref, basis_ref, *refs, sides, at
 ):
-    outs, (conduct_ref, grounds_ref, given_ref, scaled_ref, copy_sem) = refs[:6], refs[6:]
+    outs, (conduct_ref, grounds_ref, given_ref, scaled_ref, held_ref, in_sems, out_sems) = refs[:6], refs[6:]
     half = given_ref.shape[1]
-    start = pl.multiple_of(table_ref[at] * half, half)
-    copy = pltpu.make_async_copy(basis_ref.at[:, pl.ds(start, half)], given_ref, copy_sem)
-    copy.start()
+    lanes = pl.ds(pl.multiple_of(table_ref[at] * half, half), half)
+    pieces = in_sems.shape[0]
+    height = given_ref.shape[0] // pieces
+    copies_in, copies_out = [], []
+    for i in range(pieces):
+        rows = pl.ds(i * height, height)
+        copies_in.append(
+            pltpu.make_async_copy(basis_ref.at[rows, lanes], held_ref.at[rows], in_sems.at[i])
+        )
+        copies_out.append(
+            pltpu.make_async_copy(held_ref.at[rows], given_ref.at[rows], out_sems.at[i])
+        )
+        copies_in[i].start()
     size_x, size_y, size_z = sides
     count, width = panel_ref.shape
     tile = 64
@@ -222,6 +232,9 @@
         return carry
 
     lax.fori_loop(0, count // tile, by_tile, 0)
+    for copy_in, copy_out in zip(copies_in, copies_out):
+        copy_in.wait()
+        copy_out.start()
     plane = size_y * size_z
     for p in range(width // LEAF):
         lanes = slice(p * LEAF, (p + 1) * LEAF)
@@ -235,7 +248,8 @@
         for out, at in ((outs[4], 0), (outs[5], size_z - 1)):
             face = scaled_ref[p, pl.ds(at, size_x * size_y, stride=size_z), :]
             out[:, lanes] = face.astype(jnp.bfloat16)
-    copy.wait()
+    for copy_out in copies_out:
+        copy_out.wait()
 
 
 def image_kernel(table_ref, panel_ref, conduct_ref, grounds_ref, *refs, sides, nb, at):
@@ -553,7 +567,9 @@
             out_specs=[block_of(a) for a in outs] + [pl.BlockSpec(memory_space=pl.ANY)],
             scratch_shapes=[
                 pltpu.VMEM((cols // LEAF, count, LEAF), f32),
-                pltpu.SemaphoreType.DMA,
+                pltpu.VMEM((count, width_k // 2), basis.dtype),
+                pltpu.SemaphoreType.DMA((4,)),
+                pltpu.SemaphoreType.DMA((4,)),
             ],
         ),
         compiler_params=pltpu.CompilerParams(vmem_limit_bytes=58 * 2**20),

time: 363 us -> 238 us (0.66)
  Pallas kernels: 229 us -> 105 us
    pallas_call x1, Pallas kernels: 131 us -> 6.79 us  [local(): pl.pallas_call(functools.partial(faces_kernel, sides=sides, at=given_at),...]
  transfers between devices with their start and end apart: 23 -> 23, of which waited for: 9 -> 9; matrix products, arithmetic and copies ran while one was open for 2% -> 3% of each run, Pallas kernels for 25% -> 37%
where the time goes in v7:
time: 238 us; the launch traced here: 237 us
  Pallas kernels  105 us (44%)
  waiting for transfers between devices  50.5 us (21%)
  starting transfers between devices  43.8 us (18%)
  blocking collectives  24.3 us (10%)
  local copies, waits for them, and re-layouts  6.9 us (3%)
  other arithmetic  5.95 us (2%)
    pallas_call x2, Pallas kernels, panel_call(): pl.pallas_call(kernel, out_shape=[jax.ShapeDtypeStruct((nb, nb), jnp.floa...  55.9 us
    all_to_all x2, blocking collectives, exchanged(): return lax.all_to_all(rows, axes, split_axis=0, concat_axis=0, tiled=True)  24.3 us
    ppermute x3, waiting for transfers between devices, local(): pairs[d] = lax.ppermute(pairs[d], ('gy', 'core'), route)  22.6 us
    pallas_call x4, Pallas kernels, products(): pl.pallas_call(products_kernel, grid_spec=pltpu.PrefetchScalarGridSpec(nu...  22.1 us
    ppermute x4, starting transfers between devices, local(): x_got.append(lax.ppermute(x_sent[step], ('gx', 'gy', 'core'), pairs))  13.7 us
    ppermute x4, waiting for transfers between devices, local(): x_got.append(lax.ppermute(x_sent[step], ('gx', 'gy', 'core'), pairs))  9.04 us
    all_to_all x2, starting transfers between devices, exchanged(): return lax.all_to_all(rows, axes, split_axis=0, concat_axis=0, tiled=True)  7.37 us
    ppermute x2, starting transfers between devices, local(): lax.ppermute(high, axis, [(k, k + 1) for k in range(size - 1)])  6.81 us
  transfers between devices with their start and end apart: 23, of which 9 were waited for; matrix products, arithmetic and copies ran while one was open for 3% of the time, Pallas kernels for 37%

profile of v7, /device:TPU:1, one launch (start us, length us, event | category | flops | bytes accessed | tf_op | source)
XLA Modules:
  0.0 237.3 jit_solution(9018471594338905205)
XLA Ops:
  0.8 0.8 stack.164
  2.0 0.9 copy.11.info_ref
  3.5 6.8 %shard_map.77 = (bf16[64,1024]{1,0:T(8,128)(2,1)}, bf16[64,1024]{1,0:T(8,128)(2,1)}, bf16[64,1024]{1,0:T(8,128)(2,1)}, bf16[64,1024]{1,0:T(8,128)(2,1)}, bf16[64...) custom-call(s32[38]{0:T(128)} %stack.163.table_ref, ...), custom_call_target="tpu_custom_call" | custom-call | tf_op jit(solution)/shard_map/pallas_call | solution.py:558
  10.4 0.9 broadcast_select_fusion.4
  11.3 2.7 %collective-permute-start.5 = (bf16[64,1024]{1,0:T(8,128)(2,1)S(1)}, bf16[64,1024]{1,0:T(8,128)(2,1)S(1)}, u32[]{:S(2)}, u32[]{:S(2)}) collective-permute-start(bf16[64,1024]{1,0:T(8,128)(2,1)S(1)} %broadcast_select_fusion.4), channel_id=1, source_target_pairs={{0,1},{1,0},{2,3},{3,2},{4,5},{5,4},{6,7},{7,6},{8,9},{9,8},{10,11... | collective-permute-start | bytes 393224 | tf_op jit(solution)/shard_map/ppermute | solution.py:584
  14.0 3.2 %collective-permute-start.1 = (bf16[64,1024]{1,0:T(8,128)(2,1)}, bf16[64,1024]{1,0:T(8,128)(2,1)S(1)}, u32[]{:S(2)}, u32[]{:S(2)}) collective-permute-start(bf16[64,1024]{1,0:T(8,128)(2,1)} %get-tuple-element.45), channel_id=1, source_target_pairs={{0,8},{8,16},{16,24},{1,9},{9,17},{17,25},{2,10},{10,18},{18,26},{... | collective-permute-start | bytes 393224 | tf_op jit(solution)/shard_map/ppermute | solution.py:588
  17.2 1.3 collective-permute-start.2
  18.5 3.6 %collective-permute-start.3 = (bf16[64,1024]{1,0:T(8,128)(2,1)}, bf16[64,1024]{1,0:T(8,128)(2,1)S(1)}, u32[]{:S(2)}, u32[]{:S(2)}) collective-permute-start(bf16[64,1024]{1,0:T(8,128)(2,1)} %get-tuple-element.47), channel_id=1, source_target_pairs={{0,2},{2,4},{4,6},{1,3},{3,5},{5,7},{8,10},{10,12},{12,14},{9,11},... | collective-permute-start | bytes 393224 | tf_op jit(solution)/shard_map/ppermute | solution.py:588
  22.2 1.9 collective-permute-start.4
  24.1 0.7 broadcast_select_fusion.2
  24.9 3.8 %collective-permute-done.4.refs_3_ = bf16[64,1024]{1,0:T(8,128)(2,1)S(1)} collective-permute-done((bf16[64,1024]{1,0:T(8,128)(2,1)}, bf16[64,1024]{1,0:T(8,128)(2,1)S(1)}, u32[]{:S(2)}, u32[]{:S(2)}) %collective-permute-start.4) | collective-permute-done | bytes 131104 | tf_op jit(solution)/shard_map/ppermute | solution.py:589
  29.3 6.6 %shard_map.78 = (bf16[512,1024]{1,0:T(8,128)(2,1)}, f32[2432,128]{1,0:T(8,128)}, f32[2432,128]{1,0:T(8,128)}) custom-call(s32[38]{0:T(128)} %stack.163.table_ref, bf16[512,8192]{1,0:T(8,128)(2,1)} %bitcast.46, f32[512,128]{1,0:T(8,128)} %get-tuple-element.43.conduct_ref, f32[512,128]{1,0:T(8,128)} %get-tuple-element.44.grounds_ref, ...), custom_call_target="tpu_custom_call" | custom-call | tf_op jit(solution)/shard_map/pallas_call | solution.py:597
  36.4 2.6 %collective-permute-done.7 = f32[2432,128]{1,0:T(8,128)S(1)} collective-permute-done((f32[2432,128]{1,0:T(8,128)}, f32[2432,128]{1,0:T(8,128)S(1)}, u32[]{:S(2)}, u32[]{:S(2)}) %collective-permute-start.7) | collective-permute-done | bytes 1245216 | tf_op jit(solution)/shard_map/ppermute | solution.py:622
  39.0 2.4 %slice_add_fusion = f32[2304,128]{1,0:T(8,128)} fusion(f32[2432,128]{1,0:T(8,128)S(1)} %collective-permute-done.7, f32[2432,128]{1,0:T(8,128)} %get-tuple-element.52), kind=kLoop, calls=%fused_computation.1 | loop fusion | flops 294912 | bytes 3538944 | tf_op jit(solution)/shard_map/add | solution.py:623
  41.5 3.7 %all-to-all-start = ((f32[4,576,128]{2,1,0:T(8,128)}), f32[4,576,128]{2,1,0:T(8,128)S(1)}, u32[]{:S(2)}, u32[]{:S(2)}) async-start(f32[4,576,128]{2,1,0:T(8,128)} %bitcast.40), calls=%async_computation | async-start | bytes 2359296 | tf_op jit(solution)/shard_map/all_to_all | solution.py:617
  45.2 5.3 %shard_map.80 = bf16[1024,1024]{1,0:T(8,128)(2,1)} custom-call(s32[38]{0:T(128)S(1)} %copy-done.3, bf16[512,8192]{1,0:T(8,128)(2,1)} %bitcast.47, bf16[512,4096]{1,0:T(8,128)(2,1)} %collective-permute-done.refs_1_, bf16[512,1024]{1,0:T(8,128)(2,1)S(1)} %copy-done.2, bf16[512,1024]{1,0:T(8,128)(2,1)S(1)} %collective-permute-done.6.refs_3_), custom_call_target="tpu_custom_call" | custom-call | flops 2147483648 | bytes 8388608 | tf_op jit(solution)/shard_map/pallas_call | solution.py:376
  50.5 1.4 collective-permute-start.8
  51.9 5.3 %shard_map.81 = bf16[1024,1024]{1,0:T(8,128)(2,1)} custom-call(s32[38]{0:T(128)S(1)} %copy-done.3, bf16[512,8192]{1,0:T(8,128)(2,1)} %bitcast.48, bf16[512,4096]{1,0:T(8,128)(2,1)} %collective-permute-done.refs_1_, bf16[512,1024]{1,0:T(8,128)(2,1)S(1)} %copy-done.2, bf16[512,1024]{1,0:T(8,128)(2,1)S(1)} %collective-permute-done.6.refs_3_), custom_call_target="tpu_custom_call" | custom-call | flops 2147483648 | bytes 8388608 | tf_op jit(solution)/shard_map/pallas_call | solution.py:376
  57.3 1.2 collective-permute-start.9
  58.5 5.7 %shard_map.82.refs_0_.refs_3_ = f32[1024,1024]{1,0:T(8,128)} custom-call(s32[38]{0:T(128)S(1)} %copy-done.3, bf16[512,8192]{1,0:T(8,128)(2,1)} %bitcast.49, bf16[512,4096]{1,0:T(8,128)(2,1)} %collective-permute-done.refs_1_, bf16[512,1024]{1,0:T(8,128)(2,1)S(1)} %copy-done.2, bf16[512,1024]{1,0:T(8,128)(2,1)S(1)} %collective-permute-done.6.refs_3_), custom_call_target="tpu_custom_call" | custom-call | flops 2147483648 | bytes 8388608 | tf_op jit(solution)/shard_map/pallas_call | solution.py:376
  64.2 5.7 %shard_map.79.refs_0_ = f32[1024,1024]{1,0:T(8,128)} custom-call(s32[38]{0:T(128)S(1)} %copy-done.3, bf16[512,8192]{1,0:T(8,128)(2,1)} %bitcast.50, bf16[512,4096]{1,0:T(8,128)(2,1)} %collective-permute-done.refs_1_, bf16[512,1024]{1,0:T(8,128)(2,1)S(1)} %copy-done.2, bf16[512,1024]{1,0:T(8,128)(2,1)S(1)} %collective-permute-done.6.refs_3_), custom_call_target="tpu_custom_call" | custom-call | flops 2147483648 | bytes 8388608 | tf_op jit(solution)/shard_map/pallas_call | solution.py:376
  70.0 12.7 %all_to_all.20 = f32[4,144,128]{2,1,0:T(8,128)S(1)} all-to-all(f32[4,144,128]{2,1,0:T(8,128)S(1)} %bitcast.53), channel_id=1, replica_groups=mesh['gx'=4,'gy'=2,'core'=2,'gz'=2] {'gx'}, dimensions={0} | all-to-all | bytes 589824 | tf_op jit(solution)/shard_map/all_to_all | solution.py:617
  82.7 11.6 %all_to_all.21 = f32[4,144,128]{2,1,0:T(8,128)S(1)} all-to-all(f32[4,144,128]{2,1,0:T(8,128)S(1)} %broadcast_in_dim.24), channel_id=1, replica_groups=mesh['gx'=4,'gy'=2,'core'=2,'gz'=2] {'gx'}, dimensions={0} | all-to-all | bytes 589824 | tf_op jit(solution)/shard_map/all_to_all | solution.py:617
  94.3 1.1 broadcast_in_dim.25
  95.4 3.7 %all-to-all-start.3 = ((f32[4,576,128]{2,1,0:T(8,128)}), f32[4,576,128]{2,1,0:T(8,128)S(1)}, u32[]{:S(2)}, u32[]{:S(2)}) async-start(f32[4,576,128]{2,1,0:T(8,128)} %broadcast_in_dim.25), calls=%async_computation.3 | async-start | bytes 2359296 | tf_op jit(solution)/shard_map/all_to_all | solution.py:617
  99.1 6.1 %collective-permute-done.8.refs_1_ = bf16[1024,1024]{1,0:T(8,128)(2,1)} collective-permute-done((bf16[1024,1024]{1,0:T(8,128)(2,1)}, bf16[1024,1024]{1,0:T(8,128)(2,1)}, u32[]{:S(2)}, u32[]{:S(2)}) %collective-permute-start.8) | collective-permute-done | bytes 2097184 | tf_op jit(solution)/shard_map/ppermute | solution.py:541
  105.2 2.2 copy-done.1
  107.4 2.2 shard_map.83
  109.9 1.9 shard_map.84
  111.8 6.0 %all-to-all-done.3 = f32[4,576,128]{2,1,0:T(8,128)S(1)} async-done(((f32[4,576,128]{2,1,0:T(8,128)}), f32[4,576,128]{2,1,0:T(8,128)S(1)}, u32[]{:S(2)}, u32[]{:S(2)}) %all-to-all-start.3) | async-done | bytes 1179680 | tf_op jit(solution)/shard_map/all_to_all | solution.py:617
  117.8 1.0 collective-permute-start.12
  118.7 1.1 collective-permute-start.11
  119.8 1.2 collective-permute-start.10
  121.4 1.4 broadcast_select_fusion.1
  122.9 27.0 %shard_map.85.w0_ref.refs_4_ = f32[512,512]{1,0:T(8,128)S(1)} custom-call(f32[1280,128]{1,0:T(8,128)S(1)} %pad_maximum_fusion.1.packed_ref), custom_call_target="tpu_custom_call" | custom-call | flops 512 | bytes 512 | tf_op jit(solution)/shard_map/pallas_call | solution.py:159
  150.0 4.7 %shard_map.86 = (bf16[256,1024]{1,0:T(8,128)(2,1)S(1)}, bf16[256,1024]{1,0:T(8,128)(2,1)S(1)}, bf16[256,1024]{1,0:T(8,128)(2,1)S(1)}, bf16[256,1024]{1,0:T(8,128...) custom-call(s32[38]{0:T(128)S(1)} %copy-done.3, f32[1024,1024]{1,0:T(8,128)} %shard_map.79.refs_0_, ...), custom_call_target="tpu_custom_call" | custom-call | bytes 14680064 | tf_op jit(solution)/shard_map/pallas_call | solution.py:450
  155.1 5.3 %collective-permute-start.13 = (bf16[256,1024]{1,0:T(8,128)(2,1)S(1)}, bf16[256,1024]{1,0:T(8,128)(2,1)S(1)}, u32[]{:S(2)}, u32[]{:S(2)}) collective-permute-start(bf16[256,1024]{1,0:T(8,128)(2,1)S(1)} %get-tuple-element.63), channel_id=1, source_target_pairs={{2,16},{6,20},{8,2},{10,18},{12,6},{14,22},{16,8},{18,24},{20,12},... | collective-permute-start | bytes 1572872 | tf_op jit(solution)/shard_map/ppermute | solution.py:679
  160.4 3.2 %collective-permute-start.14 = (bf16[256,1024]{1,0:T(8,128)(2,1)S(1)}, bf16[256,1024]{1,0:T(8,128)(2,1)S(1)}, u32[]{:S(2)}, u32[]{:S(2)}) collective-permute-start(bf16[256,1024]{1,0:T(8,128)(2,1)S(1)} %get-tuple-element.64), channel_id=1, source_target_pairs={{2,18},{6,22},{10,24},{14,28},{16,10},{18,26},{20,14},{22,30},{24,... | collective-permute-start | bytes 1572872 | tf_op jit(solution)/shard_map/ppermute | solution.py:679
  163.6 1.9 collective-permute-start.15
  165.5 3.3 %collective-permute-start.16 = (bf16[256,1024]{1,0:T(8,128)(2,1)S(1)}, bf16[256,1024]{1,0:T(8,128)(2,1)S(1)}, u32[]{:S(2)}, u32[]{:S(2)}) collective-permute-start(bf16[256,1024]{1,0:T(8,128)(2,1)S(1)} %get-tuple-element.66), channel_id=1, source_target_pairs={{0,10},{2,26},{4,14},{6,30},{8,0},{10,16},{12,4},{14,20},{16,2},{2... | collective-permute-start | bytes 1572872 | tf_op jit(solution)/shard_map/ppermute | solution.py:679
  169.1 28.8 %shard_map.87 = (f32[512,512]{1,0:T(8,128)S(1)}, f32[512,512]{1,0:T(8,128)S(1)}) custom-call(f32[3328,128]{1,0:T(8,128)S(1)} %pad_maximum_fusion.packed_ref, f32[512,512]{1,0:T(8,128)S(1)} %shard_map.85.w0_ref.refs_4_), custom_call_target="tpu_custom_call" | custom-call | flops 512 | bytes 512 | tf_op jit(solution)/shard_map/pallas_call | solution.py:159
  197.9 9.0 %collective-permute-done.16.refs_3_ = bf16[256,1024]{1,0:T(8,128)(2,1)S(1)} collective-permute-done((bf16[256,1024]{1,0:T(8,128)(2,1)S(1)}, bf16[256,1024]{1,0:T(8,128)(2,1)S(1)}, u32[]{:S(2)}, u32[]{:S(2)}) %collective-permute-start.16) | collective-permute-done | bytes 524320 | tf_op jit(solution)/shard_map/ppermute | solution.py:679
  207.0 2.6 %shard_map.88 = (f32[2,256,256]{2,1,0:T(8,128)S(1)}, f32[2,256,256]{2,1,0:T(8,128)S(1)}, f32[2,256,256]{2,1,0:T(8,128)S(1)}, f32[2,256,256]{2,1,0:T(8,128)S(1)}) custom-call(s32[38]{0:T(128)S(1)} %copy-done.3, f32[256,1024]{1,0:T(8,128)S(1)} %get-tuple-element.62.own_ref, f32[256,1024]{1,0:T(8,128)S(1)} %collective-permute-done.17.swapped_ref, ...), custom_call_target="tpu_custom_call" | custom-call | tf_op jit(solution)/shard_map/pallas_call | solution.py:686
  209.6 2.3 collective-permute-start.19
  211.9 0.7 collective-permute-start.20
  212.7 5.4 %collective-permute-done.18.refs_1_ = f32[2,256,256]{2,1,0:T(8,128)S(1)} collective-permute-done((f32[2,256,256]{2,1,0:T(8,128)S(1)}, f32[2,256,256]{2,1,0:T(8,128)S(1)}, u32[]{:S(2)}, u32[]{:S(2)}) %collective-permute-start.18) | collective-permute-done | bytes 524320 | tf_op jit(solution)/shard_map/ppermute | solution.py:700
  218.1 16.5 %collective-permute-done.19.refs_2_ = f32[2,256,256]{2,1,0:T(8,128)S(1)} collective-permute-done((f32[2,256,256]{2,1,0:T(8,128)S(1)}, f32[2,256,256]{2,1,0:T(8,128)S(1)}, u32[]{:S(2)}, u32[]{:S(2)}) %collective-permute-start.19) | collective-permute-done | bytes 524320 | tf_op jit(solution)/shard_map/ppermute | solution.py:700
  235.3 2.0 shard_map.89
  (52 shorter events, 4.5 us)
Async XLA Ops:
  10.3 34.9 %collective-permute-start = (bf16[512,4096]{1,0:T(8,128)(2,1)}, bf16[512,4096]{1,0:T(8,128)(2,1)}, u32[]{:S(2)}, u32[]{:S(2)}) collective-permute-start(bf16[512,4096]{1,0:T(8,128)(2,1)} %get-tuple-element.42), channel_id=1, source_target_pairs={{0,2},{2,0},{1,3},{3,1},{4,6},{6,4},{5,7},{7,5},{8,10},{10,8},{9,1... | collective-permute-start | bytes 12582920 | tf_op jit(solution)/shard_map/ppermute | solution.py:611
  11.3 10.9 %collective-permute-start.5 = (bf16[64,1024]{1,0:T(8,128)(2,1)S(1)}, bf16[64,1024]{1,0:T(8,128)(2,1)S(1)}, u32[]{:S(2)}, u32[]{:S(2)}) collective-permute-start(bf16[64,1024]{1,0:T(8,128)(2,1)S(1)} %broadcast_select_fusion.4), channel_id=1, source_target_pairs={{0,1},{1,0},{2,3},{3,2},{4,5},{5,4},{6,7},{7,6},{8,9},{9,8},{10,11... | collective-permute-start | bytes 393224 | tf_op jit(solution)/shard_map/ppermute | solution.py:584
  14.0 10.8 %collective-permute-start.1 = (bf16[64,1024]{1,0:T(8,128)(2,1)}, bf16[64,1024]{1,0:T(8,128)(2,1)S(1)}, u32[]{:S(2)}, u32[]{:S(2)}) collective-permute-start(bf16[64,1024]{1,0:T(8,128)(2,1)} %get-tuple-element.45), channel_id=1, source_target_pairs={{0,8},{8,16},{16,24},{1,9},{9,17},{17,25},{2,10},{10,18},{18,26},{... | collective-permute-start | bytes 393224 | tf_op jit(solution)/shard_map/ppermute | solution.py:588
  17.2 7.6 %collective-permute-start.2 = (bf16[64,1024]{1,0:T(8,128)(2,1)}, bf16[64,1024]{1,0:T(8,128)(2,1)S(1)}, u32[]{:S(2)}, u32[]{:S(2)}) collective-permute-start(bf16[64,1024]{1,0:T(8,128)(2,1)} %get-tuple-element.46), channel_id=1, source_target_pairs={{8,0},{16,8},{24,16},{9,1},{17,9},{25,17},{10,2},{18,10},{26,18},{... | collective-permute-start | bytes 393224 | tf_op jit(solution)/shard_map/ppermute | solution.py:589
  18.5 6.3 %collective-permute-start.3 = (bf16[64,1024]{1,0:T(8,128)(2,1)}, bf16[64,1024]{1,0:T(8,128)(2,1)S(1)}, u32[]{:S(2)}, u32[]{:S(2)}) collective-permute-start(bf16[64,1024]{1,0:T(8,128)(2,1)} %get-tuple-element.47), channel_id=1, source_target_pairs={{0,2},{2,4},{4,6},{1,3},{3,5},{5,7},{8,10},{10,12},{12,14},{9,11},... | collective-permute-start | bytes 393224 | tf_op jit(solution)/shard_map/ppermute | solution.py:588
  22.2 6.5 %collective-permute-start.4 = (bf16[64,1024]{1,0:T(8,128)(2,1)}, bf16[64,1024]{1,0:T(8,128)(2,1)S(1)}, u32[]{:S(2)}, u32[]{:S(2)}) collective-permute-start(bf16[64,1024]{1,0:T(8,128)(2,1)} %get-tuple-element.48), channel_id=1, source_target_pairs={{2,0},{4,2},{6,4},{3,1},{5,3},{7,5},{10,8},{12,10},{14,12},{11,9},... | collective-permute-start | bytes 393224 | tf_op jit(solution)/shard_map/ppermute | solution.py:589
  24.8 3.8 %copy-start.4 = (bf16[64,1024]{1,0:T(8,128)(2,1)}, bf16[64,1024]{1,0:T(8,128)(2,1)S(1)}, u32[]{:S(2)}) copy-start(bf16[64,1024]{1,0:T(8,128)(2,1)S(1)} %collective-permute-done.1.refs_0_) | copy-start | bytes 393220
  24.8 3.8 %copy-start.5 = (bf16[64,1024]{1,0:T(8,128)(2,1)}, bf16[64,1024]{1,0:T(8,128)(2,1)S(1)}, u32[]{:S(2)}) copy-start(bf16[64,1024]{1,0:T(8,128)(2,1)S(1)} %collective-permute-done.2.refs_1_) | copy-start | bytes 393220
  24.9 3.8 %copy-start.6 = (bf16[64,1024]{1,0:T(8,128)(2,1)}, bf16[64,1024]{1,0:T(8,128)(2,1)S(1)}, u32[]{:S(2)}) copy-start(bf16[64,1024]{1,0:T(8,128)(2,1)S(1)} %collective-permute-done.3.refs_2_) | copy-start | bytes 393220
  28.7 0.7 copy-start.7
  35.9 3.2 %collective-permute-start.7 = (f32[2432,128]{1,0:T(8,128)}, f32[2432,128]{1,0:T(8,128)S(1)}, u32[]{:S(2)}, u32[]{:S(2)}) collective-permute-start(f32[2432,128]{1,0:T(8,128)} %get-tuple-element.53), channel_id=1, source_target_pairs={{0,2},{2,0},{1,3},{3,1},{4,6},{6,4},{5,7},{7,5},{8,10},{10,8},{9,1... | collective-permute-start | bytes 3735560 | tf_op jit(solution)/shard_map/ppermute | solution.py:622
  35.9 9.3 %collective-permute-start.6 = (bf16[512,1024]{1,0:T(8,128)(2,1)}, bf16[512,1024]{1,0:T(8,128)(2,1)S(1)}, u32[]{:S(2)}, u32[]{:S(2)}) collective-permute-start(bf16[512,1024]{1,0:T(8,128)(2,1)} %get-tuple-element.54.refs_2_), channel_id=1, source_target_pairs={{0,2},{2,0},{1,3},{3,1},{4,6},{6,4},{5,7},{7,5},{8,10},{10,8},{9,1... | collective-permute-start | bytes 3145736 | tf_op jit(solution)/shard_map/ppermute | solution.py:610
  41.5 3.7 %copy-start.2 = (bf16[512,1024]{1,0:T(8,128)(2,1)S(1)}, bf16[512,1024]{1,0:T(8,128)(2,1)}, u32[]{:S(2)}) copy-start(bf16[512,1024]{1,0:T(8,128)(2,1)} %get-tuple-element.54.refs_2_) | copy-start | bytes 3145732
  41.5 3.7 %copy-start.3 = (s32[38]{0:T(128)S(1)}, s32[38]{0:T(128)}, u32[]{:S(2)}) copy-start(s32[38]{0:T(128)} %stack.163.table_ref) | copy-start | bytes 460
  41.5 28.4 %all-to-all-start = ((f32[4,576,128]{2,1,0:T(8,128)}), f32[4,576,128]{2,1,0:T(8,128)S(1)}, u32[]{:S(2)}, u32[]{:S(2)}) async-start(f32[4,576,128]{2,1,0:T(8,128)} %bitcast.40), calls=%async_computation | async-start | bytes 2359296 | tf_op jit(solution)/shard_map/all_to_all | solution.py:617
  50.5 54.7 %collective-permute-start.8 = (bf16[1024,1024]{1,0:T(8,128)(2,1)}, bf16[1024,1024]{1,0:T(8,128)(2,1)}, u32[]{:S(2)}, u32[]{:S(2)}) collective-permute-start(bf16[1024,1024]{1,0:T(8,128)(2,1)} %shard_map.80), channel_id=1, source_target_pairs={{0,1},{1,0},{2,3},{3,2},{4,5},{5,4},{6,7},{7,6},{8,9},{9,8},{10,11... | collective-permute-start | bytes 6291464 | tf_op jit(solution)/shard_map/ppermute | solution.py:541
  57.3 48.0 %collective-permute-start.9 = (bf16[1024,1024]{1,0:T(8,128)(2,1)}, bf16[1024,1024]{1,0:T(8,128)(2,1)}, u32[]{:S(2)}, u32[]{:S(2)}) collective-permute-start(bf16[1024,1024]{1,0:T(8,128)(2,1)} %shard_map.81), channel_id=1, source_target_pairs={{0,4},{4,0},{1,5},{5,1},{2,6},{6,2},{3,7},{7,3},{8,12},{12,8},{9,1... | collective-permute-start | bytes 6291464 | tf_op jit(solution)/shard_map/ppermute | solution.py:541
  95.4 22.4 %all-to-all-start.3 = ((f32[4,576,128]{2,1,0:T(8,128)}), f32[4,576,128]{2,1,0:T(8,128)S(1)}, u32[]{:S(2)}, u32[]{:S(2)}) async-start(f32[4,576,128]{2,1,0:T(8,128)} %broadcast_in_dim.25), calls=%async_computation.3 | async-start | bytes 2359296 | tf_op jit(solution)/shard_map/all_to_all | solution.py:617
  105.2 2.2 copy-start.1
  107.4 2.5 %copy-start = (f32[1024,1024]{1,0:T(8,128)S(1)}, f32[1024,1024]{1,0:T(8,128)}, u32[]{:S(2)}) copy-start(f32[1024,1024]{1,0:T(8,128)} %shard_map.82.refs_0_.refs_3_) | copy-start | bytes 12582916
  117.8 3.6 %collective-permute-start.12 = (f32[2304,128]{1,0:T(8,128)S(1)}, f32[2304,128]{1,0:T(8,128)}, u32[]{:S(2)}, u32[]{:S(2)}) collective-permute-start(f32[2304,128]{1,0:T(8,128)S(1)} %bitcast.51), channel_id=1, source_target_pairs={{0,2},{2,0},{1,3},{3,1},{4,6},{6,4},{5,7},{7,5},{8,10},{10,8},{9,1... | collective-permute-start | bytes 3538952 | tf_op jit(solution)/shard_map/ppermute | solution.py:649
  118.7 31.2 %collective-permute-start.11 = (bf16[512,1024]{1,0:T(8,128)(2,1)S(1)}, bf16[512,1024]{1,0:T(8,128)(2,1)S(1)}, u32[]{:S(2)}, u32[]{:S(2)}) collective-permute-start(bf16[512,1024]{1,0:T(8,128)(2,1)S(1)} %shard_map.84), channel_id=1, source_target_pairs={{0,1},{1,0},{2,3},{3,2},{4,5},{5,4},{6,7},{7,6},{8,9},{9,8},{10,11... | collective-permute-start | bytes 3145736 | tf_op jit(solution)/shard_map/ppermute | solution.py:541
  119.8 30.1 %collective-permute-start.10 = (bf16[512,1024]{1,0:T(8,128)(2,1)S(1)}, bf16[512,1024]{1,0:T(8,128)(2,1)S(1)}, u32[]{:S(2)}, u32[]{:S(2)}) collective-permute-start(bf16[512,1024]{1,0:T(8,128)(2,1)S(1)} %shard_map.83), channel_id=1, source_target_pairs={{0,4},{4,0},{1,5},{5,1},{2,6},{6,2},{3,7},{7,3},{8,12},{12,8},{9,1... | collective-permute-start | bytes 3145736 | tf_op jit(solution)/shard_map/ppermute | solution.py:541
  154.6 52.4 %collective-permute-start.17 = (f32[256,1024]{1,0:T(8,128)S(1)}, f32[256,1024]{1,0:T(8,128)S(1)}, u32[]{:S(2)}, u32[]{:S(2)}) collective-permute-start(f32[256,1024]{1,0:T(8,128)S(1)} %get-tuple-element.67), channel_id=1, source_target_pairs={{0,2},{2,0},{1,3},{3,1},{4,6},{6,4},{5,7},{7,5},{8,10},{10,8},{9,1... | collective-permute-start | bytes 3145736 | tf_op jit(solution)/shard_map/ppermute | solution.py:680
  155.1 42.9 %collective-permute-start.13 = (bf16[256,1024]{1,0:T(8,128)(2,1)S(1)}, bf16[256,1024]{1,0:T(8,128)(2,1)S(1)}, u32[]{:S(2)}, u32[]{:S(2)}) collective-permute-start(bf16[256,1024]{1,0:T(8,128)(2,1)S(1)} %get-tuple-element.63), channel_id=1, source_target_pairs={{2,16},{6,20},{8,2},{10,18},{12,6},{14,22},{16,8},{18,24},{20,12},... | collective-permute-start | bytes 1572872 | tf_op jit(solution)/shard_map/ppermute | solution.py:679
  160.4 37.6 %collective-permute-start.14 = (bf16[256,1024]{1,0:T(8,128)(2,1)S(1)}, bf16[256,1024]{1,0:T(8,128)(2,1)S(1)}, u32[]{:S(2)}, u32[]{:S(2)}) collective-permute-start(bf16[256,1024]{1,0:T(8,128)(2,1)S(1)} %get-tuple-element.64), channel_id=1, source_target_pairs={{2,18},{6,22},{10,24},{14,28},{16,10},{18,26},{20,14},{22,30},{24,... | collective-permute-start | bytes 1572872 | tf_op jit(solution)/shard_map/ppermute | solution.py:679
  163.6 34.3 %collective-permute-start.15 = (bf16[256,1024]{1,0:T(8,128)(2,1)S(1)}, bf16[256,1024]{1,0:T(8,128)(2,1)S(1)}, u32[]{:S(2)}, u32[]{:S(2)}) collective-permute-start(bf16[256,1024]{1,0:T(8,128)(2,1)S(1)} %get-tuple-element.65), channel_id=1, source_target_pairs={{0,8},{2,24},{4,12},{6,28},{10,26},{14,30},{16,0},{20,4},{24,2},{2... | collective-permute-start | bytes 1572872 | tf_op jit(solution)/shard_map/ppermute | solution.py:679
  165.5 41.4 %collective-permute-start.16 = (bf16[256,1024]{1,0:T(8,128)(2,1)S(1)}, bf16[256,1024]{1,0:T(8,128)(2,1)S(1)}, u32[]{:S(2)}, u32[]{:S(2)}) collective-permute-start(bf16[256,1024]{1,0:T(8,128)(2,1)S(1)} %get-tuple-element.66), channel_id=1, source_target_pairs={{0,10},{2,26},{4,14},{6,30},{8,0},{10,16},{12,4},{14,20},{16,2},{2... | collective-permute-start | bytes 1572872 | tf_op jit(solution)/shard_map/ppermute | solution.py:679
  209.6 8.5 %collective-permute-start.18 = (f32[2,256,256]{2,1,0:T(8,128)S(1)}, f32[2,256,256]{2,1,0:T(8,128)S(1)}, u32[]{:S(2)}, u32[]{:S(2)}) collective-permute-start(f32[2,256,256]{2,1,0:T(8,128)S(1)} %get-tuple-element.79), channel_id=1, source_target_pairs={{0,2},{2,4},{4,6},{6,0},{1,3},{3,5},{5,7},{7,1},{8,10},{10,12},{12... | collective-permute-start | bytes 1572872 | tf_op jit(solution)/shard_map/ppermute | solution.py:700
  209.6 25.0 %collective-permute-start.19 = (f32[2,256,256]{2,1,0:T(8,128)S(1)}, f32[2,256,256]{2,1,0:T(8,128)S(1)}, u32[]{:S(2)}, u32[]{:S(2)}) collective-permute-start(f32[2,256,256]{2,1,0:T(8,128)S(1)} %get-tuple-element.80), channel_id=1, source_target_pairs={{0,4},{2,6},{4,0},{6,2},{1,5},{3,7},{5,1},{7,3},{8,12},{10,14},{12... | collective-permute-start | bytes 1572872 | tf_op jit(solution)/shard_map/ppermute | solution.py:700
  211.9 23.3 %collective-permute-start.20 = (f32[2,256,256]{2,1,0:T(8,128)S(1)}, f32[2,256,256]{2,1,0:T(8,128)S(1)}, u32[]{:S(2)}, u32[]{:S(2)}) collective-permute-start(f32[2,256,256]{2,1,0:T(8,128)S(1)} %get-tuple-element.81), channel_id=1, source_target_pairs={{0,6},{2,0},{4,2},{6,4},{1,7},{3,1},{5,3},{7,5},{8,14},{10,8},{12,... | collective-permute-start | bytes 1572872 | tf_op jit(solution)/shard_map/ppermute | solution.py:700

commit v8 on v7

--- a/solution.py
+++ b/solution.py
@@ -34,38 +34,54 @@
     lanes = lax.broadcasted_iota(jnp.int32, (SUB, LEAF), 1)
     subs = lax.broadcasted_iota(jnp.int32, (SUB, LEAF), 0)
     shape = (SUB, LEAF)
-    for t in range(LEAF // SUB):
+    panels = LEAF // SUB
+    rows = block_ref[0:SUB, :]
+    for t in range(panels):
         j0 = t * SUB
-        rows = block_ref[j0 : j0 + SUB, :]
-        cols = [jnp.broadcast_to(rows[:, j0 + k : j0 + k + 1], shape) for k in range(SUB)]
+        after = t + 1 < panels
+
+        def columns(array):
+            return [jnp.broadcast_to(array[:, j0 + k : j0 + k + 1], shape) for k in range(SUB)]
+
+        cols = columns(rows)
         p = [[jnp.broadcast_to(cols[k][i : i + 1, :], shape) for k in range(i + 1)] for i in range(SUB)]
         in_block = jnp.logical_and(lanes >= j0, lanes < j0 + SUB)
         start = jnp.where(in_block, (lanes - j0 == subs).astype(jnp.float32), rows)
         u = [jnp.broadcast_to(start[k : k + 1, :], shape) for k in range(SUB)]
+        if after:
+            below = block_ref[j0 + SUB : j0 + 2 * SUB, :]
+            c = columns(below)
+            rows = jnp.where(in_block, 0.0, below)
         inv = [None] * SUB
         factor = [[None] * SUB for _ in range(SUB)]
         for k in range(SUB):
+            products = {(i, j): p[i][k] * p[j][k] for i in range(k + 1, SUB) for j in range(k + 1, i + 1)}
             inv[k] = inverse_of(p[k][k])
+            for (i, j), product in products.items():
+                p[i][j] = p[i][j] - product * inv[k]
+            if after:
+                step = c[k] * inv[k]
+                rows = rows - step * u[k]
             for i in range(k + 1, SUB):
                 factor[i][k] = p[i][k] * inv[k]
-                for j in range(k + 1, i + 1):
-                    p[i][j] = p[i][j] - factor[i][k] * p[j][k] if j < i else p[i][j] - factor[i][k] * p[i][k]
                 u[i] = u[i] - factor[i][k] * u[k]
+                if after:
+                    c[i] = c[i] - step * p[i][k]
         out = u[0] * lax.rsqrt(p[0][0])
         for k in range(1, SUB):
             out = jnp.where(subs == k, u[k] * lax.rsqrt(p[k][k]), out)
         block_ref[j0 : j0 + SUB, :] = out
-        if t + 1 == LEAF // SUB:
-            break
+        if t + 2 >= panels:
+            continue
         z = [None] * SUB
         for k in reversed(range(SUB)):
             z[k] = u[k] * inv[k]
             for i in range(k + 1, SUB):
                 z[k] = z[k] - factor[i][k] * z[i]
-        for v in range(t + 1, LEAF // SUB):
+        for v in range(t + 2, panels):
             below = block_ref[v * SUB : (v + 1) * SUB, :]
             upd = jnp.where(in_block, 0.0, below)
-            for k in range(SUB):
+            for k in reversed(range(SUB)):
                 upd = upd - jnp.broadcast_to(below[:, j0 + k : j0 + k + 1], shape) * z[k]
             block_ref[v * SUB : (v + 1) * SUB, :] = upd
 
@@ -87,12 +103,16 @@
         s_ref[span, span] = (leaf_rows == leaf_cols).astype(jnp.float32)
         upper = dot3(inverse, s_ref[span, :], ((1,), (0,)))
         s_ref[span, :] = upper
-        tail = jnp.where(wide_cols >= off + LEAF, upper, 0.0)
-        current = s_ref[...]
-        dead = jnp.logical_and(
-            row_ids >= off + LEAF, jnp.logical_and(col_ids >= off, col_ids < off + LEAF)
-        )
-        s_ref[...] = jnp.where(dead, 0.0, current) - dot3(tail, upper, ((0,), (0,)))
+
+        @pl.when(b < width // LEAF - 1)
+        def _():
+            tail = jnp.where(wide_cols >= off + LEAF, upper, 0.0)
+            current = s_ref[...]
+            dead = jnp.logical_and(
+                row_ids >= off + LEAF, jnp.logical_and(col_ids >= off, col_ids < off + LEAF)
+            )
+            s_ref[...] = jnp.where(dead, 0.0, current) - dot3(tail, upper, ((0,), (0,)))
+
         return carry
 
     lax.fori_loop(0, width // LEAF, step, 0)
@@ -186,9 +206,10 @@
 
 
 def faces_kernel(
-    table_ref, cond_ref, ground_ref, info_ref, cells_ref, load_ref, panel_ref, basis_ref, *refs, sides, at
+    table_ref, cond_ref, ground_ref, info_ref, cells_ref, load_ref, panel_ref, basis_ref, *refs, sides, at, last_at
 ):
-    outs, (conduct_ref, grounds_ref, given_ref, scaled_ref, held_ref, in_sems, out_sems) = refs[:6], refs[6:]
+    *outs, conduct_ref, grounds_ref, given_ref, scaled_ref, held_ref, in_sems, out_sems = refs
+    last = table_ref[last_at] != 0
     half = given_ref.shape[1]
     lanes = pl.ds(pl.multiple_of(table_ref[at] * half, half), half)
     pieces = in_sems.shape[0]
@@ -245,16 +266,22 @@
                 scaled_ref[p, x * plane + at : x * plane + at + size_z, :] for x in range(size_x)
             ]
             out[:, lanes] = jnp.concatenate(face, 0).astype(jnp.bfloat16)
-        for out, at in ((outs[4], 0), (outs[5], size_z - 1)):
-            face = scaled_ref[p, pl.ds(at, size_x * size_y, stride=size_z), :]
-            out[:, lanes] = face.astype(jnp.bfloat16)
+        low, high = (
+            scaled_ref[p, pl.ds(at, size_x * size_y, stride=size_z), :] for at in (0, size_z - 1)
+        )
+        if len(outs) == 5:
+            outs[4][:, lanes] = jnp.where(last, low, high).astype(jnp.bfloat16)
+        else:
+            outs[4][:, lanes] = low.astype(jnp.bfloat16)
+            outs[5][:, lanes] = high.astype(jnp.bfloat16)
     for copy_out in copies_out:
         copy_out.wait()
 
 
-def image_kernel(table_ref, panel_ref, conduct_ref, grounds_ref, *refs, sides, nb, at):
-    halos, (image_ref, kept_ref, sent_ref, scaled_ref, square_ref) = refs[:6], refs[6:]
+def image_kernel(table_ref, panel_ref, conduct_ref, grounds_ref, *refs, sides, nb, at, last_at):
+    *halos, image_ref, kept_ref, sent_ref, scaled_ref, square_ref = refs
     core = table_ref[at]
+    last = table_ref[last_at] != 0
     size_x, size_y, size_z = sides
     width = panel_ref.shape[1]
     plane = size_y * size_z
@@ -262,9 +289,10 @@
 
     def by_lane(p, carry):
         lanes = pl.ds(pl.multiple_of(p * LEAF, LEAF), LEAF)
-        x_low, x_high, y_low, y_high, z_low, z_high = (
-            h[:, lanes].astype(jnp.float32) for h in halos
-        )
+        x_low, x_high, y_low, y_high, *z_halos = (h[:, lanes].astype(jnp.float32) for h in halos)
+        if len(z_halos) == 1:
+            z_halos = [jnp.where(last, z_halos[0], 0.0), jnp.where(last, 0.0, z_halos[0])]
+        z_low, z_high = z_halos
         scaled_ref[...] = (
             (conduct_ref[...] * panel_ref[:, lanes].astype(jnp.float32))
             .astype(jnp.bfloat16)
@@ -382,7 +410,7 @@
             out_specs=pl.BlockSpec((step, cols), lambda t, tab: (t, 0)),
         ),
         out_shape=jax.ShapeDtypeStruct((total, cols), dtype),
-        compiler_params=pltpu.CompilerParams(vmem_limit_bytes=48 * 2**20),
+        compiler_params=pltpu.CompilerParams(vmem_limit_bytes=32 * 2**20),
         cost_estimate=pl.CostEstimate(
             flops=2 * total * cols * rows * len(bases),
             transcendentals=0,
@@ -457,7 +485,7 @@
             scratch_shapes=[pltpu.VMEM((height * len(sums), cols), jnp.float32)],
         ),
         out_shape=outs,
-        compiler_params=pltpu.CompilerParams(vmem_limit_bytes=44 * 2**20),
+        compiler_params=pltpu.CompilerParams(vmem_limit_bytes=34 * 2**20),
         cost_estimate=pl.CostEstimate(
             flops=0, transcendentals=0, bytes_accessed=height * len(sums) * cols * 14
         ),
@@ -530,6 +558,7 @@
     leaving_at, _ = put(leaving + [at_x % spans * 2 + core, at_x % spans * 2 + 1 - core])
     given_at, _ = put([1 - core])
     core_at, _ = put([core])
+    last_at, _ = put([at_z == 1])
     places_at, _ = put([(at_y - d) % devices_y for d in range(devices_y)])
     order_at, _ = put([(at_y + d) % devices_y for d in range(devices_y)])
     home_at, _ = put([at_x // spans == core])
@@ -551,12 +580,13 @@
         + global_z[None, None, :]
     )
     info = jnp.stack([classes, flat_ids], -1).reshape(count, 2)
-    face_rows = [cells_y * cells_z] * 2 + [cells_x * cells_z] * 2 + [cells_x * cells_y] * 2
+    face_rows = [cells_y * cells_z] * 2 + [cells_x * cells_z] * 2
+    face_rows += [cells_x * cells_y] * (1 if devices_z == 2 else 2)
     outs = [jax.ShapeDtypeStruct((n, cols), bf16) for n in face_rows]
     outs += [jax.ShapeDtypeStruct((count, LEAF), f32)] * 2
     given = jax.ShapeDtypeStruct((count, width_k // 2), basis.dtype)
     *faces, conduct, grounds, given = pl.pallas_call(
-        functools.partial(faces_kernel, sides=sides, at=given_at),
+        functools.partial(faces_kernel, sides=sides, at=given_at, last_at=last_at),
         out_shape=[*outs, given],
         grid_spec=pltpu.PrefetchScalarGridSpec(
             num_scalar_prefetch=1,
@@ -578,16 +608,12 @@
     for i, (axis, size) in enumerate(
         (("gx", devices_x), (("gy", "core"), devices_y), ("gz", devices_z))
     ):
+        if i == 2 and size == 2:
+            halos.append(lax.ppermute(faces[4], axis, swap_pairs()))
+            continue
         low, high = faces[2 * i : 2 * i + 2]
-        if size == 2:
-            last = lax.axis_index(axis) == 1
-            got = lax.ppermute(jnp.where(last, low, high), axis, swap_pairs())
-            halos.append(jnp.where(last, got, 0))
-            halos.append(jnp.where(last, 0, got))
-        else:
-            halos.append(lax.ppermute(high, axis, [(k, k + 1) for k in range(size - 1)]))
-            halos.append(lax.ppermute(low, axis, [(k + 1, k) for k in range(size - 1)]))
-    other_basis = lax.ppermute(given, "core", swap_pairs())
+        halos.append(lax.ppermute(high, axis, [(k, k + 1) for k in range(size - 1)]))
+        halos.append(lax.ppermute(low, axis, [(k + 1, k) for k in range(size - 1)]))
 
     blocks = NB // LEAF
     lower_rows = blocks * (blocks + 1) // 2 * LEAF
@@ -595,12 +621,12 @@
     lead_parts = [jax.ShapeDtypeStruct((half_rows + LEAF, LEAF), f32)] * 2
     outs = [jax.ShapeDtypeStruct((count, cols), bf16), *lead_parts]
     image, lead_kept, lead_sent = pl.pallas_call(
-        functools.partial(image_kernel, sides=sides, nb=NB, at=core_at),
+        functools.partial(image_kernel, sides=sides, nb=NB, at=core_at, last_at=last_at),
         out_shape=outs,
         grid_spec=pltpu.PrefetchScalarGridSpec(
             num_scalar_prefetch=1,
             grid=(1,),
-            in_specs=[panel_spec] + [whole()] * 8,
+            in_specs=[panel_spec] + [whole()] * (2 + len(halos)),
             out_specs=[whole()] * 3,
             scratch_shapes=[pltpu.VMEM((count, LEAF), f32), pltpu.VMEM((NB, NB), f32)],
         ),

time: 238 us -> 234 us (0.983)
  Pallas kernels: 105 us -> 90.5 us
  local copies, waits for them, and re-layouts: 6.9 us -> 14.3 us
  starting transfers between devices: 43.8 us -> 46.2 us
    pallas_call x2, Pallas kernels: 55.9 us -> 46.2 us  [panel_call(): pl.pallas_call(kernel, out_shape=[jax.ShapeDtypeStruct((nb, nb), jnp.floa...]
    unnamed x16 -> x28, local copies, waits for them, and re-layouts: 3.17 us -> 10.6 us
    ppermute x4, waiting for transfers between devices: 9.04 us -> 13.9 us  [local(): x_got.append(lax.ppermute(x_sent[step], ('gx', 'gy', 'core'), pairs))]
    pallas_call x4, Pallas kernels: 22.1 us -> 18.9 us  [products(): pl.pallas_call(products_kernel, grid_spec=pltpu.PrefetchScalarGridSpec(nu...]
    ppermute x1, starting transfers between devices: 0.95 us -> 3.75 us  [local(): other = lax.ppermute(lead_half, 'core', swap_pairs())]
  transfers between devices with their start and end apart: 23 -> 23, of which waited for: 9 -> 10; matrix products, arithmetic and copies ran while one was open for 3% -> 2% of each run, Pallas kernels for 37% -> 32%
where the time goes in v8:
time: 234 us; the launch traced here: 233 us
  Pallas kernels  90.5 us (39%)
  waiting for transfers between devices  52.5 us (22%)
  starting transfers between devices  46.2 us (20%)
  blocking collectives  24.3 us (10%)
  local copies, waits for them, and re-layouts  14.3 us (6%)
  other arithmetic  4.43 us (2%)
    pallas_call x2, Pallas kernels, panel_call(): pl.pallas_call(kernel, out_shape=[jax.ShapeDtypeStruct((nb, nb), jnp.floa...  46.2 us
    all_to_all x2, blocking collectives, exchanged(): return lax.all_to_all(rows, axes, split_axis=0, concat_axis=0, tiled=True)  24.3 us
    ppermute x3, waiting for transfers between devices, local(): pairs[d] = lax.ppermute(pairs[d], ('gy', 'core'), route)  22.6 us
    pallas_call x4, Pallas kernels, products(): pl.pallas_call(products_kernel, grid_spec=pltpu.PrefetchScalarGridSpec(nu...  18.9 us
    ppermute x4, starting transfers between devices, local(): x_got.append(lax.ppermute(x_sent[step], ('gx', 'gy', 'core'), pairs))  14.3 us
    ppermute x4, waiting for transfers between devices, local(): x_got.append(lax.ppermute(x_sent[step], ('gx', 'gy', 'core'), pairs))  13.9 us
    unnamed x28, local copies, waits for them, and re-layouts  10.6 us
    all_to_all x2, starting transfers between devices, exchanged(): return lax.all_to_all(rows, axes, split_axis=0, concat_axis=0, tiled=True)  8.15 us
  transfers between devices with their start and end apart: 23, of which 10 were waited for; matrix products, arithmetic and copies ran while one was open for 2% of the time, Pallas kernels for 32%

profile of v8, /device:TPU:1, one launch (start us, length us, event | category | flops | bytes accessed | tf_op | source)
XLA Modules:
  0.0 233.5 jit_solution(6160682277077735490)
XLA Ops:
  2.0 0.9 copy.11.info_ref
  3.4 6.8 %shard_map.77 = (bf16[64,1024]{1,0:T(8,128)(2,1)}, bf16[64,1024]{1,0:T(8,128)(2,1)}, bf16[64,1024]{1,0:T(8,128)(2,1)}, bf16[64,1024]{1,0:T(8,128)(2,1)}, bf16[64...) custom-call(s32[39]{0:T(128)} %stack.171.table_ref, f32[16]{0:T(128)} %cond_ref.1, ...), custom_call_target="tpu_custom_call" | custom-call | tf_op jit(solution)/shard_map/pallas_call | solution.py:588
  10.3 4.6 %collective-permute-start.1 = (bf16[64,1024]{1,0:T(8,128)(2,1)}, bf16[64,1024]{1,0:T(8,128)(2,1)S(1)}, u32[]{:S(2)}, u32[]{:S(2)}) collective-permute-start(bf16[64,1024]{1,0:T(8,128)(2,1)} %get-tuple-element.44), channel_id=1, source_target_pairs={{0,8},{8,16},{16,24},{1,9},{9,17},{17,25},{2,10},{10,18},{18,26},{... | collective-permute-start | bytes 393224 | tf_op jit(solution)/shard_map/ppermute | solution.py:615
  15.0 1.3 collective-permute-start.2
  16.3 3.3 %collective-permute-start.3 = (bf16[64,1024]{1,0:T(8,128)(2,1)}, bf16[64,1024]{1,0:T(8,128)(2,1)S(1)}, u32[]{:S(2)}, u32[]{:S(2)}) collective-permute-start(bf16[64,1024]{1,0:T(8,128)(2,1)} %get-tuple-element.46), channel_id=1, source_target_pairs={{0,2},{2,4},{4,6},{1,3},{3,5},{5,7},{8,10},{10,12},{12,14},{9,11},... | collective-permute-start | bytes 393224 | tf_op jit(solution)/shard_map/ppermute | solution.py:615
  19.6 1.9 collective-permute-start.4
  21.6 1.3 collective-permute-start.5
  22.9 3.3 %collective-permute-done.4.refs_3_ = bf16[64,1024]{1,0:T(8,128)(2,1)S(1)} collective-permute-done((bf16[64,1024]{1,0:T(8,128)(2,1)}, bf16[64,1024]{1,0:T(8,128)(2,1)S(1)}, u32[]{:S(2)}, u32[]{:S(2)}) %collective-permute-start.4) | collective-permute-done | bytes 131104 | tf_op jit(solution)/shard_map/ppermute | solution.py:616
  26.8 6.5 %shard_map.78 = (bf16[512,1024]{1,0:T(8,128)(2,1)}, f32[2432,128]{1,0:T(8,128)}, f32[2432,128]{1,0:T(8,128)}) custom-call(s32[39]{0:T(128)} %stack.171.table_ref, bf16[512,8192]{1,0:T(8,128)(2,1)} %bitcast.47, f32[512,128]{1,0:T(8,128)} %get-tuple-element.42.conduct_ref, f32[512,128]{1,0:T(8,128)} %get-tuple-element.43.grounds_ref, ...), custom_call_target="tpu_custom_call" | custom-call | tf_op jit(solution)/shard_map/pallas_call | solution.py:623
  33.9 2.6 %collective-permute-done.7 = f32[2432,128]{1,0:T(8,128)S(1)} collective-permute-done((f32[2432,128]{1,0:T(8,128)}, f32[2432,128]{1,0:T(8,128)S(1)}, u32[]{:S(2)}, u32[]{:S(2)}) %collective-permute-start.7) | collective-permute-done | bytes 1245216 | tf_op jit(solution)/shard_map/ppermute | solution.py:648
  36.5 2.4 %slice_add_fusion = f32[2304,128]{1,0:T(8,128)} fusion(f32[2432,128]{1,0:T(8,128)S(1)} %collective-permute-done.7, f32[2432,128]{1,0:T(8,128)} %get-tuple-element.50), kind=kLoop, calls=%fused_computation.1 | loop fusion | flops 294912 | bytes 3538944 | tf_op jit(solution)/shard_map/add | solution.py:649
  39.0 4.4 %all-to-all-start = ((f32[4,576,128]{2,1,0:T(8,128)}), f32[4,576,128]{2,1,0:T(8,128)S(1)}, u32[]{:S(2)}, u32[]{:S(2)}) async-start(f32[4,576,128]{2,1,0:T(8,128)} %bitcast.41), calls=%async_computation | async-start | bytes 2359296 | tf_op jit(solution)/shard_map/all_to_all | solution.py:643
  43.4 3.4 %copy-done = bf16[8,8,8,8192]{3,2,1,0:T(8,128)(2,1)S(1)} copy-done((bf16[8,8,8,8192]{3,2,1,0:T(8,128)(2,1)S(1)}, bf16[8,8,8,8192]{3,2,1,0:T(8,128)(2,1)}, u32[]{:S(2)}) %copy-start) | copy-done | bytes 8388632
  46.8 5.2 %shard_map.80 = bf16[1024,1024]{1,0:T(8,128)(2,1)} custom-call(s32[39]{0:T(128)S(1)} %copy-done.8, bf16[512,8192]{1,0:T(8,128)(2,1)S(1)} %bitcast.48, bf16[512,4096]{1,0:T(8,128)(2,1)} %collective-permute-done.refs_1_, bf16[512,1024]{1,0:T(8,128)(2,1)S(1)} %copy-done.7, bf16[512,1024]{1,0:T(8,128)(2,1)S(1)} %collective-permute-done.6.refs_3_), custom_call_target="tpu_custom_call" | custom-call | flops 2147483648 | bytes 8388608 | tf_op jit(solution)/shard_map/pallas_call | solution.py:404
  52.0 1.5 collective-permute-start.8
  53.5 5.2 %shard_map.81 = bf16[1024,1024]{1,0:T(8,128)(2,1)} custom-call(s32[39]{0:T(128)S(1)} %copy-done.8, bf16[512,8192]{1,0:T(8,128)(2,1)S(1)} %bitcast.49, bf16[512,4096]{1,0:T(8,128)(2,1)} %collective-permute-done.refs_1_, bf16[512,1024]{1,0:T(8,128)(2,1)S(1)} %copy-done.7, bf16[512,1024]{1,0:T(8,128)(2,1)S(1)} %collective-permute-done.6.refs_3_), custom_call_target="tpu_custom_call" | custom-call | flops 2147483648 | bytes 8388608 | tf_op jit(solution)/shard_map/pallas_call | solution.py:404
  58.7 1.2 collective-permute-start.9
  59.9 4.2 %shard_map.82.refs_0_.refs_3_ = f32[1024,1024]{1,0:T(8,128)S(1)} custom-call(s32[39]{0:T(128)S(1)} %copy-done.8, bf16[512,8192]{1,0:T(8,128)(2,1)S(1)} %bitcast.50, bf16[512,4096]{1,0:T(8,128)(2,1)} %collective-permute-done.refs_1_, bf16[512,1024]{1,0:T(8,128)(2,1)S(1)} %copy-done.7, bf16[512,1024]{1,0:T(8,128)(2,1)S(1)} %collective-permute-done.6.refs_3_), custom_call_target="tpu_custom_call" | custom-call | flops 2147483648 | bytes 8388608 | tf_op jit(solution)/shard_map/pallas_call | solution.py:404
  64.1 2.0 copy-done.1
  66.1 4.2 %shard_map.79.refs_0_ = f32[1024,1024]{1,0:T(8,128)S(1)} custom-call(s32[39]{0:T(128)S(1)} %copy-done.8, bf16[512,8192]{1,0:T(8,128)(2,1)S(1)} %bitcast.51, bf16[512,4096]{1,0:T(8,128)(2,1)} %collective-permute-done.refs_1_, bf16[512,1024]{1,0:T(8,128)(2,1)S(1)} %copy-done.7, bf16[512,1024]{1,0:T(8,128)(2,1)S(1)} %collective-permute-done.6.refs_3_), custom_call_target="tpu_custom_call" | custom-call | flops 2147483648 | bytes 8388608 | tf_op jit(solution)/shard_map/pallas_call | solution.py:404
  70.4 2.0 copy-done.4
  72.4 12.9 %all_to_all.20 = f32[4,144,128]{2,1,0:T(8,128)S(1)} all-to-all(f32[4,144,128]{2,1,0:T(8,128)S(1)} %bitcast.54), channel_id=1, replica_groups=mesh['gx'=4,'gy'=2,'core'=2,'gz'=2] {'gx'}, dimensions={0} | all-to-all | bytes 589824 | tf_op jit(solution)/shard_map/all_to_all | solution.py:643
  85.4 11.4 %all_to_all.21 = f32[4,144,128]{2,1,0:T(8,128)S(1)} all-to-all(f32[4,144,128]{2,1,0:T(8,128)S(1)} %broadcast_in_dim.17), channel_id=1, replica_groups=mesh['gx'=4,'gy'=2,'core'=2,'gz'=2] {'gx'}, dimensions={0} | all-to-all | bytes 589824 | tf_op jit(solution)/shard_map/all_to_all | solution.py:643
  96.8 1.1 broadcast_in_dim.18
  97.9 3.7 %all-to-all-start.3 = ((f32[4,576,128]{2,1,0:T(8,128)}), f32[4,576,128]{2,1,0:T(8,128)S(1)}, u32[]{:S(2)}, u32[]{:S(2)}) async-start(f32[4,576,128]{2,1,0:T(8,128)} %broadcast_in_dim.18), calls=%async_computation.3 | async-start | bytes 2359296 | tf_op jit(solution)/shard_map/all_to_all | solution.py:643
  101.7 1.3 collective-permute-done.8.refs_1_
  103.0 4.0 %collective-permute-done.9.refs_1_.refs_4_ = bf16[1024,1024]{1,0:T(8,128)(2,1)} collective-permute-done((bf16[1024,1024]{1,0:T(8,128)(2,1)}, bf16[1024,1024]{1,0:T(8,128)(2,1)}, u32[]{:S(2)}, u32[]{:S(2)}) %collective-permute-start.9) | collective-permute-done | bytes 2097184 | tf_op jit(solution)/shard_map/ppermute | solution.py:570
  106.9 2.2 copy-done.5
  109.1 2.2 shard_map.83
  111.6 1.9 shard_map.84
  113.5 3.9 %all-to-all-done.3 = f32[4,576,128]{2,1,0:T(8,128)S(1)} async-done(((f32[4,576,128]{2,1,0:T(8,128)}), f32[4,576,128]{2,1,0:T(8,128)S(1)}, u32[]{:S(2)}, u32[]{:S(2)}) %all-to-all-start.3) | async-done | bytes 1179680 | tf_op jit(solution)/shard_map/all_to_all | solution.py:643
  117.5 3.7 %collective-permute-start.12 = (f32[2304,128]{1,0:T(8,128)S(1)}, f32[2304,128]{1,0:T(8,128)}, u32[]{:S(2)}, u32[]{:S(2)}) collective-permute-start(f32[2304,128]{1,0:T(8,128)S(1)} %bitcast.52), channel_id=1, source_target_pairs={{0,2},{2,0},{1,3},{3,1},{4,6},{6,4},{5,7},{7,5},{8,10},{10,8},{9,1... | collective-permute-start | bytes 3538952 | tf_op jit(solution)/shard_map/ppermute | solution.py:675
  121.2 1.8 collective-permute-start.10
  123.8 1.6 broadcast_select_fusion.1
  125.5 22.2 %shard_map.85.w0_ref.refs_4_ = f32[512,512]{1,0:T(8,128)S(1)} custom-call(f32[1280,128]{1,0:T(8,128)S(1)} %pad_maximum_fusion.1.packed_ref), custom_call_target="tpu_custom_call" | custom-call | flops 512 | bytes 512 | tf_op jit(solution)/shard_map/pallas_call | solution.py:179
  147.8 3.5 %shard_map.86 = (bf16[256,1024]{1,0:T(8,128)(2,1)S(1)}, bf16[256,1024]{1,0:T(8,128)(2,1)S(1)}, bf16[256,1024]{1,0:T(8,128)(2,1)S(1)}, bf16[256,1024]{1,0:T(8,128...) custom-call(s32[39]{0:T(128)S(1)} %copy-done.8, f32[1024,1024]{1,0:T(8,128)S(1)} %copy-done.6, ...), custom_call_target="tpu_custom_call" | custom-call | bytes 14680064 | tf_op jit(solution)/shard_map/pallas_call | solution.py:478
  151.7 5.9 %collective-permute-start.13 = (bf16[256,1024]{1,0:T(8,128)(2,1)S(1)}, bf16[256,1024]{1,0:T(8,128)(2,1)S(1)}, u32[]{:S(2)}, u32[]{:S(2)}) collective-permute-start(bf16[256,1024]{1,0:T(8,128)(2,1)S(1)} %get-tuple-element.61), channel_id=1, source_target_pairs={{2,16},{6,20},{8,2},{10,18},{12,6},{14,22},{16,8},{18,24},{20,12},... | collective-permute-start | bytes 1572872 | tf_op jit(solution)/shard_map/ppermute | solution.py:705
  157.6 3.2 %collective-permute-start.14 = (bf16[256,1024]{1,0:T(8,128)(2,1)S(1)}, bf16[256,1024]{1,0:T(8,128)(2,1)S(1)}, u32[]{:S(2)}, u32[]{:S(2)}) collective-permute-start(bf16[256,1024]{1,0:T(8,128)(2,1)S(1)} %get-tuple-element.62), channel_id=1, source_target_pairs={{2,18},{6,22},{10,24},{14,28},{16,10},{18,26},{20,14},{22,30},{24,... | collective-permute-start | bytes 1572872 | tf_op jit(solution)/shard_map/ppermute | solution.py:705
  160.8 1.9 collective-permute-start.15
  162.8 3.3 %collective-permute-start.16 = (bf16[256,1024]{1,0:T(8,128)(2,1)S(1)}, bf16[256,1024]{1,0:T(8,128)(2,1)S(1)}, u32[]{:S(2)}, u32[]{:S(2)}) collective-permute-start(bf16[256,1024]{1,0:T(8,128)(2,1)S(1)} %get-tuple-element.64), channel_id=1, source_target_pairs={{0,10},{2,26},{4,14},{6,30},{8,0},{10,16},{12,4},{14,20},{16,2},{2... | collective-permute-start | bytes 1572872 | tf_op jit(solution)/shard_map/ppermute | solution.py:705
  166.3 24.0 %shard_map.87 = (f32[512,512]{1,0:T(8,128)S(1)}, f32[512,512]{1,0:T(8,128)S(1)}) custom-call(f32[3328,128]{1,0:T(8,128)S(1)} %pad_maximum_fusion.packed_ref, f32[512,512]{1,0:T(8,128)S(1)} %shard_map.85.w0_ref.refs_4_), custom_call_target="tpu_custom_call" | custom-call | flops 512 | bytes 512 | tf_op jit(solution)/shard_map/pallas_call | solution.py:179
  190.3 13.9 %collective-permute-done.16.refs_3_ = bf16[256,1024]{1,0:T(8,128)(2,1)S(1)} collective-permute-done((bf16[256,1024]{1,0:T(8,128)(2,1)S(1)}, bf16[256,1024]{1,0:T(8,128)(2,1)S(1)}, u32[]{:S(2)}, u32[]{:S(2)}) %collective-permute-start.16) | collective-permute-done | bytes 524320 | tf_op jit(solution)/shard_map/ppermute | solution.py:705
  204.2 2.6 %shard_map.88 = (f32[2,256,256]{2,1,0:T(8,128)S(1)}, f32[2,256,256]{2,1,0:T(8,128)S(1)}, f32[2,256,256]{2,1,0:T(8,128)S(1)}, f32[2,256,256]{2,1,0:T(8,128)S(1)}) custom-call(s32[39]{0:T(128)S(1)} %copy-done.8, f32[256,1024]{1,0:T(8,128)S(1)} %get-tuple-element.60.own_ref, f32[256,1024]{1,0:T(8,128)S(1)} %collective-permute-done.17.swapped_ref, ...), custom_call_target="tpu_custom_call" | custom-call | tf_op jit(solution)/shard_map/pallas_call | solution.py:712
  206.9 1.3 collective-permute-start.19
  208.9 7.5 %collective-permute-done.18.refs_1_ = f32[2,256,256]{2,1,0:T(8,128)S(1)} collective-permute-done((f32[2,256,256]{2,1,0:T(8,128)S(1)}, f32[2,256,256]{2,1,0:T(8,128)S(1)}, u32[]{:S(2)}, u32[]{:S(2)}) %collective-permute-start.18) | collective-permute-done | bytes 524320 | tf_op jit(solution)/shard_map/ppermute | solution.py:726
  216.4 13.8 %collective-permute-done.19.refs_2_ = f32[2,256,256]{2,1,0:T(8,128)S(1)} collective-permute-done((f32[2,256,256]{2,1,0:T(8,128)S(1)}, f32[2,256,256]{2,1,0:T(8,128)S(1)}, u32[]{:S(2)}, u32[]{:S(2)}) %collective-permute-start.19) | collective-permute-done | bytes 524320 | tf_op jit(solution)/shard_map/ppermute | solution.py:726
  230.2 1.3 collective-permute-done.20.refs_3_
  231.5 2.0 shard_map.89
  (62 shorter events, 5.9 us)
Async XLA Ops:
  10.2 33.2 %collective-permute-start = (bf16[512,4096]{1,0:T(8,128)(2,1)}, bf16[512,4096]{1,0:T(8,128)(2,1)}, u32[]{:S(2)}, u32[]{:S(2)}) collective-permute-start(bf16[512,4096]{1,0:T(8,128)(2,1)} %get-tuple-element.41), channel_id=1, source_target_pairs={{0,2},{2,0},{1,3},{3,1},{4,6},{6,4},{5,7},{7,5},{8,10},{10,8},{9,1... | collective-permute-start | bytes 12582920 | tf_op jit(solution)/shard_map/ppermute | solution.py:637
  10.3 11.2 %collective-permute-start.1 = (bf16[64,1024]{1,0:T(8,128)(2,1)}, bf16[64,1024]{1,0:T(8,128)(2,1)S(1)}, u32[]{:S(2)}, u32[]{:S(2)}) collective-permute-start(bf16[64,1024]{1,0:T(8,128)(2,1)} %get-tuple-element.44), channel_id=1, source_target_pairs={{0,8},{8,16},{16,24},{1,9},{9,17},{17,25},{2,10},{10,18},{18,26},{... | collective-permute-start | bytes 393224 | tf_op jit(solution)/shard_map/ppermute | solution.py:615
  15.0 7.9 %collective-permute-start.2 = (bf16[64,1024]{1,0:T(8,128)(2,1)}, bf16[64,1024]{1,0:T(8,128)(2,1)S(1)}, u32[]{:S(2)}, u32[]{:S(2)}) collective-permute-start(bf16[64,1024]{1,0:T(8,128)(2,1)} %get-tuple-element.45), channel_id=1, source_target_pairs={{8,0},{16,8},{24,16},{9,1},{17,9},{25,17},{10,2},{18,10},{26,18},{... | collective-permute-start | bytes 393224 | tf_op jit(solution)/shard_map/ppermute | solution.py:616
  16.3 6.6 %collective-permute-start.3 = (bf16[64,1024]{1,0:T(8,128)(2,1)}, bf16[64,1024]{1,0:T(8,128)(2,1)S(1)}, u32[]{:S(2)}, u32[]{:S(2)}) collective-permute-start(bf16[64,1024]{1,0:T(8,128)(2,1)} %get-tuple-element.46), channel_id=1, source_target_pairs={{0,2},{2,4},{4,6},{1,3},{3,5},{5,7},{8,10},{10,12},{12,14},{9,11},... | collective-permute-start | bytes 393224 | tf_op jit(solution)/shard_map/ppermute | solution.py:615
  19.6 6.5 %collective-permute-start.4 = (bf16[64,1024]{1,0:T(8,128)(2,1)}, bf16[64,1024]{1,0:T(8,128)(2,1)S(1)}, u32[]{:S(2)}, u32[]{:S(2)}) collective-permute-start(bf16[64,1024]{1,0:T(8,128)(2,1)} %get-tuple-element.47), channel_id=1, source_target_pairs={{2,0},{4,2},{6,4},{3,1},{5,3},{7,5},{10,8},{12,10},{14,12},{11,9},... | collective-permute-start | bytes 393224 | tf_op jit(solution)/shard_map/ppermute | solution.py:616
  21.6 4.6 %copy-start.9 = (bf16[64,1024]{1,0:T(8,128)(2,1)}, bf16[64,1024]{1,0:T(8,128)(2,1)S(1)}, u32[]{:S(2)}) copy-start(bf16[64,1024]{1,0:T(8,128)(2,1)S(1)} %collective-permute-done.1.refs_0_) | copy-start | bytes 393220
  21.6 4.6 %collective-permute-start.5 = (bf16[64,1024]{1,0:T(8,128)(2,1)}, bf16[64,1024]{1,0:T(8,128)(2,1)S(1)}, u32[]{:S(2)}, u32[]{:S(2)}) collective-permute-start(bf16[64,1024]{1,0:T(8,128)(2,1)} %get-tuple-element.48), channel_id=1, source_target_pairs={{0,1},{1,0},{2,3},{3,2},{4,5},{5,4},{6,7},{7,6},{8,9},{9,8},{10,11... | collective-permute-start | bytes 393224 | tf_op jit(solution)/shard_map/ppermute | solution.py:612
  22.9 3.3 %copy-start.10 = (bf16[64,1024]{1,0:T(8,128)(2,1)}, bf16[64,1024]{1,0:T(8,128)(2,1)S(1)}, u32[]{:S(2)}) copy-start(bf16[64,1024]{1,0:T(8,128)(2,1)S(1)} %collective-permute-done.2.refs_1_) | copy-start | bytes 393220
  22.9 3.3 %copy-start.11 = (bf16[64,1024]{1,0:T(8,128)(2,1)}, bf16[64,1024]{1,0:T(8,128)(2,1)S(1)}, u32[]{:S(2)}) copy-start(bf16[64,1024]{1,0:T(8,128)(2,1)S(1)} %collective-permute-done.3.refs_2_) | copy-start | bytes 393220
  26.1 0.7 copy-start.12
  26.1 0.7 copy-start.13
  33.4 3.2 %collective-permute-start.7 = (f32[2432,128]{1,0:T(8,128)}, f32[2432,128]{1,0:T(8,128)S(1)}, u32[]{:S(2)}, u32[]{:S(2)}) collective-permute-start(f32[2432,128]{1,0:T(8,128)} %get-tuple-element.51), channel_id=1, source_target_pairs={{0,2},{2,0},{1,3},{3,1},{4,6},{6,4},{5,7},{7,5},{8,10},{10,8},{9,1... | collective-permute-start | bytes 3735560 | tf_op jit(solution)/shard_map/ppermute | solution.py:648
  33.4 10.0 %collective-permute-start.6 = (bf16[512,1024]{1,0:T(8,128)(2,1)}, bf16[512,1024]{1,0:T(8,128)(2,1)S(1)}, u32[]{:S(2)}, u32[]{:S(2)}) collective-permute-start(bf16[512,1024]{1,0:T(8,128)(2,1)} %get-tuple-element.52.refs_2_), channel_id=1, source_target_pairs={{0,2},{2,0},{1,3},{3,1},{4,6},{6,4},{5,7},{7,5},{8,10},{10,8},{9,1... | collective-permute-start | bytes 3145736 | tf_op jit(solution)/shard_map/ppermute | solution.py:636
  38.9 4.5 %copy-start.7 = (bf16[512,1024]{1,0:T(8,128)(2,1)S(1)}, bf16[512,1024]{1,0:T(8,128)(2,1)}, u32[]{:S(2)}) copy-start(bf16[512,1024]{1,0:T(8,128)(2,1)} %get-tuple-element.52.refs_2_) | copy-start | bytes 3145732
  39.0 4.5 %copy-start.8 = (s32[39]{0:T(128)S(1)}, s32[39]{0:T(128)}, u32[]{:S(2)}) copy-start(s32[39]{0:T(128)} %stack.171.table_ref) | copy-start | bytes 472
  39.0 33.4 %all-to-all-start = ((f32[4,576,128]{2,1,0:T(8,128)}), f32[4,576,128]{2,1,0:T(8,128)S(1)}, u32[]{:S(2)}, u32[]{:S(2)}) async-start(f32[4,576,128]{2,1,0:T(8,128)} %bitcast.41), calls=%async_computation | async-start | bytes 2359296 | tf_op jit(solution)/shard_map/all_to_all | solution.py:643
  43.4 3.4 %copy-start = (bf16[8,8,8,8192]{3,2,1,0:T(8,128)(2,1)S(1)}, bf16[8,8,8,8192]{3,2,1,0:T(8,128)(2,1)}, u32[]{:S(2)}) copy-start(bf16[8,8,8,8192]{3,2,1,0:T(8,128)(2,1)} %param.6) | copy-start | bytes 25165828
  52.0 50.9 %collective-permute-start.8 = (bf16[1024,1024]{1,0:T(8,128)(2,1)}, bf16[1024,1024]{1,0:T(8,128)(2,1)}, u32[]{:S(2)}, u32[]{:S(2)}) collective-permute-start(bf16[1024,1024]{1,0:T(8,128)(2,1)} %shard_map.80), channel_id=1, source_target_pairs={{0,1},{1,0},{2,3},{3,2},{4,5},{5,4},{6,7},{7,6},{8,9},{9,8},{10,11... | collective-permute-start | bytes 6291464 | tf_op jit(solution)/shard_map/ppermute | solution.py:570
  58.7 48.2 %collective-permute-start.9 = (bf16[1024,1024]{1,0:T(8,128)(2,1)}, bf16[1024,1024]{1,0:T(8,128)(2,1)}, u32[]{:S(2)}, u32[]{:S(2)}) collective-permute-start(bf16[1024,1024]{1,0:T(8,128)(2,1)} %shard_map.81), channel_id=1, source_target_pairs={{0,4},{4,0},{1,5},{5,1},{2,6},{6,2},{3,7},{7,3},{8,12},{12,8},{9,1... | collective-permute-start | bytes 6291464 | tf_op jit(solution)/shard_map/ppermute | solution.py:570
  64.1 2.0 copy-start.1
  70.4 2.0 copy-start.4
  97.9 19.5 %all-to-all-start.3 = ((f32[4,576,128]{2,1,0:T(8,128)}), f32[4,576,128]{2,1,0:T(8,128)S(1)}, u32[]{:S(2)}, u32[]{:S(2)}) async-start(f32[4,576,128]{2,1,0:T(8,128)} %broadcast_in_dim.18), calls=%async_computation.3 | async-start | bytes 2359296 | tf_op jit(solution)/shard_map/all_to_all | solution.py:643
  106.9 2.2 copy-start.5
  109.1 2.5 %copy-start.2 = (f32[1024,1024]{1,0:T(8,128)S(1)}, f32[1024,1024]{1,0:T(8,128)}, u32[]{:S(2)}) copy-start(f32[1024,1024]{1,0:T(8,128)} %copy-done.1) | copy-start | bytes 12582916
  117.5 6.4 %collective-permute-start.12 = (f32[2304,128]{1,0:T(8,128)S(1)}, f32[2304,128]{1,0:T(8,128)}, u32[]{:S(2)}, u32[]{:S(2)}) collective-permute-start(f32[2304,128]{1,0:T(8,128)S(1)} %bitcast.52), channel_id=1, source_target_pairs={{0,2},{2,0},{1,3},{3,1},{4,6},{6,4},{5,7},{7,5},{8,10},{10,8},{9,1... | collective-permute-start | bytes 3538952 | tf_op jit(solution)/shard_map/ppermute | solution.py:675
  121.2 26.5 %collective-permute-start.11 = (bf16[512,1024]{1,0:T(8,128)(2,1)S(1)}, bf16[512,1024]{1,0:T(8,128)(2,1)S(1)}, u32[]{:S(2)}, u32[]{:S(2)}) collective-permute-start(bf16[512,1024]{1,0:T(8,128)(2,1)S(1)} %shard_map.84), channel_id=1, source_target_pairs={{0,1},{1,0},{2,3},{3,2},{4,5},{5,4},{6,7},{7,6},{8,9},{9,8},{10,11... | collective-permute-start | bytes 3145736 | tf_op jit(solution)/shard_map/ppermute | solution.py:570
  121.2 26.5 %collective-permute-start.10 = (bf16[512,1024]{1,0:T(8,128)(2,1)S(1)}, bf16[512,1024]{1,0:T(8,128)(2,1)S(1)}, u32[]{:S(2)}, u32[]{:S(2)}) collective-permute-start(bf16[512,1024]{1,0:T(8,128)(2,1)S(1)} %shard_map.83), channel_id=1, source_target_pairs={{0,4},{4,0},{1,5},{5,1},{2,6},{6,2},{3,7},{7,3},{8,12},{12,8},{9,1... | collective-permute-start | bytes 3145736 | tf_op jit(solution)/shard_map/ppermute | solution.py:570
  123.8 23.9 %copy-start.6 = (f32[1024,1024]{1,0:T(8,128)S(1)}, f32[1024,1024]{1,0:T(8,128)}, u32[]{:S(2)}) copy-start(f32[1024,1024]{1,0:T(8,128)} %copy-done.4) | copy-start | bytes 12582916
  125.4 22.4 %copy-start.3 = (f32[1024,1024]{1,0:T(8,128)S(1)}, f32[1024,1024]{1,0:T(8,128)}, u32[]{:S(2)}) copy-start(f32[1024,1024]{1,0:T(8,128)} %copy-done.1) | copy-start | bytes 12582916
  151.3 52.9 %collective-permute-start.17 = (f32[256,1024]{1,0:T(8,128)S(1)}, f32[256,1024]{1,0:T(8,128)S(1)}, u32[]{:S(2)}, u32[]{:S(2)}) collective-permute-start(f32[256,1024]{1,0:T(8,128)S(1)} %get-tuple-element.65), channel_id=1, source_target_pairs={{0,2},{2,0},{1,3},{3,1},{4,6},{6,4},{5,7},{7,5},{8,10},{10,8},{9,1... | collective-permute-start | bytes 3145736 | tf_op jit(solution)/shard_map/ppermute | solution.py:706
  151.7 38.6 %collective-permute-start.13 = (bf16[256,1024]{1,0:T(8,128)(2,1)S(1)}, bf16[256,1024]{1,0:T(8,128)(2,1)S(1)}, u32[]{:S(2)}, u32[]{:S(2)}) collective-permute-start(bf16[256,1024]{1,0:T(8,128)(2,1)S(1)} %get-tuple-element.61), channel_id=1, source_target_pairs={{2,16},{6,20},{8,2},{10,18},{12,6},{14,22},{16,8},{18,24},{20,12},... | collective-permute-start | bytes 1572872 | tf_op jit(solution)/shard_map/ppermute | solution.py:705
  157.6 32.7 %collective-permute-start.14 = (bf16[256,1024]{1,0:T(8,128)(2,1)S(1)}, bf16[256,1024]{1,0:T(8,128)(2,1)S(1)}, u32[]{:S(2)}, u32[]{:S(2)}) collective-permute-start(bf16[256,1024]{1,0:T(8,128)(2,1)S(1)} %get-tuple-element.62), channel_id=1, source_target_pairs={{2,18},{6,22},{10,24},{14,28},{16,10},{18,26},{20,14},{22,30},{24,... | collective-permute-start | bytes 1572872 | tf_op jit(solution)/shard_map/ppermute | solution.py:705
  160.8 29.5 %collective-permute-start.15 = (bf16[256,1024]{1,0:T(8,128)(2,1)S(1)}, bf16[256,1024]{1,0:T(8,128)(2,1)S(1)}, u32[]{:S(2)}, u32[]{:S(2)}) collective-permute-start(bf16[256,1024]{1,0:T(8,128)(2,1)S(1)} %get-tuple-element.63), channel_id=1, source_target_pairs={{0,8},{2,24},{4,12},{6,28},{10,26},{14,30},{16,0},{20,4},{24,2},{2... | collective-permute-start | bytes 1572872 | tf_op jit(solution)/shard_map/ppermute | solution.py:705
  162.8 41.4 %collective-permute-start.16 = (bf16[256,1024]{1,0:T(8,128)(2,1)S(1)}, bf16[256,1024]{1,0:T(8,128)(2,1)S(1)}, u32[]{:S(2)}, u32[]{:S(2)}) collective-permute-start(bf16[256,1024]{1,0:T(8,128)(2,1)S(1)} %get-tuple-element.64), channel_id=1, source_target_pairs={{0,10},{2,26},{4,14},{6,30},{8,0},{10,16},{12,4},{14,20},{16,2},{2... | collective-permute-start | bytes 1572872 | tf_op jit(solution)/shard_map/ppermute | solution.py:705
  206.8 9.6 %collective-permute-start.18 = (f32[2,256,256]{2,1,0:T(8,128)S(1)}, f32[2,256,256]{2,1,0:T(8,128)S(1)}, u32[]{:S(2)}, u32[]{:S(2)}) collective-permute-start(f32[2,256,256]{2,1,0:T(8,128)S(1)} %get-tuple-element.77), channel_id=1, source_target_pairs={{0,2},{2,4},{4,6},{6,0},{1,3},{3,5},{5,7},{7,1},{8,10},{10,12},{12... | collective-permute-start | bytes 1572872 | tf_op jit(solution)/shard_map/ppermute | solution.py:726
  206.9 23.3 %collective-permute-start.19 = (f32[2,256,256]{2,1,0:T(8,128)S(1)}, f32[2,256,256]{2,1,0:T(8,128)S(1)}, u32[]{:S(2)}, u32[]{:S(2)}) collective-permute-start(f32[2,256,256]{2,1,0:T(8,128)S(1)} %get-tuple-element.78), channel_id=1, source_target_pairs={{0,4},{2,6},{4,0},{6,2},{1,5},{3,7},{5,1},{7,3},{8,12},{10,14},{12... | collective-permute-start | bytes 1572872 | tf_op jit(solution)/shard_map/ppermute | solution.py:726
  208.1 23.3 %collective-permute-start.20 = (f32[2,256,256]{2,1,0:T(8,128)S(1)}, f32[2,256,256]{2,1,0:T(8,128)S(1)}, u32[]{:S(2)}, u32[]{:S(2)}) collective-permute-start(f32[2,256,256]{2,1,0:T(8,128)S(1)} %get-tuple-element.79), channel_id=1, source_target_pairs={{0,6},{2,0},{4,2},{6,4},{1,7},{3,1},{5,3},{7,5},{8,14},{10,8},{12,... | collective-permute-start | bytes 1572872 | tf_op jit(solution)/shard_map/ppermute | solution.py:726

commit v9 on v8

--- a/solution.py
+++ b/solution.py
@@ -379,12 +379,11 @@
 def products_kernel(table_ref, *refs):
     del table_ref
     out, count = refs[-1], len(refs) // 2
-    total = None
-    for b, image in zip(refs[:count], refs[count:-1]):
-        term = lax.dot_general(
-            b[...], image[...], (((0,), (0,)), ((), ())), preferred_element_type=jnp.float32
-        )
-        total = term if total is None else total + term
+    bases = jnp.concatenate([ref[...] for ref in refs[:count]], 0)
+    images = jnp.concatenate([ref[...] for ref in refs[count:-1]], 0)
+    total = lax.dot_general(
+        bases, images, (((0,), (0,)), ((), ())), preferred_element_type=jnp.float32
+    )
     out[...] = total.astype(out.dtype)
 
 
@@ -410,7 +409,7 @@
             out_specs=pl.BlockSpec((step, cols), lambda t, tab: (t, 0)),
         ),
         out_shape=jax.ShapeDtypeStruct((total, cols), dtype),
-        compiler_params=pltpu.CompilerParams(vmem_limit_bytes=32 * 2**20),
+        compiler_params=pltpu.CompilerParams(vmem_limit_bytes=48 * 2**20),
         cost_estimate=pl.CostEstimate(
             flops=2 * total * cols * rows * len(bases),
             transcendentals=0,
@@ -594,7 +593,7 @@
             in_specs=[block_of(cond_table, pltpu.SMEM), block_of(ground_table, pltpu.SMEM)]
             + [block_of(info), block_of(port_rows), block_of(load_rows), panel_spec]
             + [pl.BlockSpec(memory_space=pl.ANY)],
-            out_specs=[block_of(a) for a in outs] + [pl.BlockSpec(memory_space=pl.ANY)],
+            out_specs=[whole()] * len(outs) + [pl.BlockSpec(memory_space=pl.ANY)],
             scratch_shapes=[
                 pltpu.VMEM((cols // LEAF, count, LEAF), f32),
                 pltpu.VMEM((count, width_k // 2), basis.dtype),
@@ -602,7 +601,7 @@
                 pltpu.SemaphoreType.DMA((4,)),
             ],
         ),
-        compiler_params=pltpu.CompilerParams(vmem_limit_bytes=58 * 2**20),
+        compiler_params=pltpu.CompilerParams(vmem_limit_bytes=56 * 2**20),
     )(table, cond_table, ground_table, info, port_rows, load_rows, flat_basis, flat_basis)
     halos = []
     for i, (axis, size) in enumerate(
@@ -630,7 +629,7 @@
             out_specs=[whole()] * 3,
             scratch_shapes=[pltpu.VMEM((count, LEAF), f32), pltpu.VMEM((NB, NB), f32)],
         ),
-        compiler_params=pltpu.CompilerParams(vmem_limit_bytes=54 * 2**20),
+        compiler_params=pltpu.CompilerParams(vmem_limit_bytes=56 * 2**20),
     )(table, flat_basis, conduct, grounds, *halos)
 
     other_image = lax.ppermute(image, "core", swap_pairs())
@@ -647,7 +646,7 @@
 
     lead_got = lax.ppermute(lead_sent, "core", swap_pairs())
     lead_half = lead_kept[:half_rows] + lead_got[:half_rows]
-    lead_terms = exchanged(lead_half.reshape(chips, -1, LEAF), plane_axes)
+    lead_terms = exchanged(lead_half.astype(bf16).reshape(chips, -1, LEAF), plane_axes)
 
     def chip_products(images, lists, dtype):
         return products(table, [flat_basis, other_basis], images, lists, narrow, dtype)
@@ -659,7 +658,7 @@
     got_b = [move(a, "gy", d) for d, a in enumerate(sent_b, 1)]
     own_a, own_b = (chip_products(images, lists[0], f32) for lists in (lists_a, lists_b))
     lead_terms, _ = lax.optimization_barrier((lead_terms, (own_a, own_b)))
-    own = jnp.sum(lead_terms, axis=0).reshape(devices_x, -1, LEAF)
+    own = jnp.sum(lead_terms.astype(f32), axis=0).reshape(devices_x, -1, LEAF)
     own = jnp.sum(exchanged(own, "gx"), axis=0)
     own = exchanged(for_all(own, devices_x), "gx").reshape(-1, LEAF)
     own = for_all(own, chips)

time: 234 us -> 231 us (0.987)
  local copies, waits for them, and re-layouts: 14.3 us -> 6.94 us
  Pallas kernels: 90.5 us -> 93.8 us
    unnamed x28 -> x22, local copies, waits for them, and re-layouts: 10.6 us -> 3.2 us
    pallas_call x4, Pallas kernels: 18.9 us -> 22.1 us  [products(): pl.pallas_call(products_kernel, grid_spec=pltpu.PrefetchScalarGridSpec(nu...]
  transfers between devices with their start and end apart: 23 -> 23, of which waited for: 10 -> 9; matrix products, arithmetic and copies ran while one was open for 2% -> 2% of each run, Pallas kernels for 32% -> 34%
where the time goes in v9:
time: 231 us; the launch traced here: 230 us
  Pallas kernels  93.8 us (41%)
  waiting for transfers between devices  54 us (23%)
  starting transfers between devices  45.6 us (20%)
  blocking collectives  24.3 us (11%)
  local copies, waits for them, and re-layouts  6.94 us (3%)
  other arithmetic  4.2 us (2%)
    pallas_call x2, Pallas kernels, panel_call(): pl.pallas_call(kernel, out_shape=[jax.ShapeDtypeStruct((nb, nb), jnp.floa...  46.1 us
    all_to_all x2, blocking collectives, exchanged(): return lax.all_to_all(rows, axes, split_axis=0, concat_axis=0, tiled=True)  24.3 us
    ppermute x3, waiting for transfers between devices, local(): pairs[d] = lax.ppermute(pairs[d], ('gy', 'core'), route)  22.6 us
    pallas_call x4, Pallas kernels, products(): pl.pallas_call(products_kernel, grid_spec=pltpu.PrefetchScalarGridSpec(nu...  22.1 us
    ppermute x4, waiting for transfers between devices, local(): x_got.append(lax.ppermute(x_sent[step], ('gx', 'gy', 'core'), pairs))  13.9 us
    ppermute x4, starting transfers between devices, local(): x_got.append(lax.ppermute(x_sent[step], ('gx', 'gy', 'core'), pairs))  13.7 us
    all_to_all x2, starting transfers between devices, exchanged(): return lax.all_to_all(rows, axes, split_axis=0, concat_axis=0, tiled=True)  8.17 us
    ppermute x2, starting transfers between devices, local(): lax.ppermute(high, axis, [(k, k + 1) for k in range(size - 1)])  7.98 us
  transfers between devices with their start and end apart: 23, of which 9 were waited for; matrix products, arithmetic and copies ran while one was open for 2% of the time, Pallas kernels for 34%

profile of v9, /device:TPU:1, one launch (start us, length us, event | category | flops | bytes accessed | tf_op | source)
XLA Modules:
  0.0 230.1 jit_solution(433212758661707497)
XLA Ops:
  0.8 0.8 stack.172
  2.0 0.9 copy.11.info_ref
  2.8 0.6 stack.171.table_ref
  3.5 6.8 %shard_map.77 = (bf16[64,1024]{1,0:T(8,128)(2,1)}, bf16[64,1024]{1,0:T(8,128)(2,1)}, bf16[64,1024]{1,0:T(8,128)(2,1)}, bf16[64,1024]{1,0:T(8,128)(2,1)}, bf16[64...) custom-call(s32[39]{0:T(128)} %stack.171.table_ref, f32[16]{0:T(128)} %cond_ref.1, ...), custom_call_target="tpu_custom_call" | custom-call | tf_op jit(solution)/shard_map/pallas_call | solution.py:587
  10.4 4.6 %collective-permute-start.1 = (bf16[64,1024]{1,0:T(8,128)(2,1)}, bf16[64,1024]{1,0:T(8,128)(2,1)S(1)}, u32[]{:S(2)}, u32[]{:S(2)}) collective-permute-start(bf16[64,1024]{1,0:T(8,128)(2,1)} %get-tuple-element.44), channel_id=1, source_target_pairs={{0,8},{8,16},{16,24},{1,9},{9,17},{17,25},{2,10},{10,18},{18,26},{... | collective-permute-start | bytes 393224 | tf_op jit(solution)/shard_map/ppermute | solution.py:614
  15.0 1.3 collective-permute-start.2
  16.3 3.3 %collective-permute-start.3 = (bf16[64,1024]{1,0:T(8,128)(2,1)}, bf16[64,1024]{1,0:T(8,128)(2,1)S(1)}, u32[]{:S(2)}, u32[]{:S(2)}) collective-permute-start(bf16[64,1024]{1,0:T(8,128)(2,1)} %get-tuple-element.46), channel_id=1, source_target_pairs={{0,2},{2,4},{4,6},{1,3},{3,5},{5,7},{8,10},{10,12},{12,14},{9,11},... | collective-permute-start | bytes 393224 | tf_op jit(solution)/shard_map/ppermute | solution.py:614
  19.7 1.9 collective-permute-start.4
  21.6 1.3 collective-permute-start.5
  22.9 3.3 %collective-permute-done.4.refs_3_ = bf16[64,1024]{1,0:T(8,128)(2,1)S(1)} collective-permute-done((bf16[64,1024]{1,0:T(8,128)(2,1)}, bf16[64,1024]{1,0:T(8,128)(2,1)S(1)}, u32[]{:S(2)}, u32[]{:S(2)}) %collective-permute-start.4) | collective-permute-done | bytes 131104 | tf_op jit(solution)/shard_map/ppermute | solution.py:615
  26.9 6.5 %shard_map.78 = (bf16[512,1024]{1,0:T(8,128)(2,1)}, f32[2432,128]{1,0:T(8,128)}, f32[2432,128]{1,0:T(8,128)}) custom-call(s32[39]{0:T(128)} %stack.171.table_ref, bf16[512,8192]{1,0:T(8,128)(2,1)} %bitcast.47, f32[512,128]{1,0:T(8,128)} %get-tuple-element.42.conduct_ref, f32[512,128]{1,0:T(8,128)} %get-tuple-element.43.grounds_ref, ...), custom_call_target="tpu_custom_call" | custom-call | tf_op jit(solution)/shard_map/pallas_call | solution.py:622
  33.9 2.6 %collective-permute-done.7 = f32[2432,128]{1,0:T(8,128)S(1)} collective-permute-done((f32[2432,128]{1,0:T(8,128)}, f32[2432,128]{1,0:T(8,128)S(1)}, u32[]{:S(2)}, u32[]{:S(2)}) %collective-permute-start.7) | collective-permute-done | bytes 1245216 | tf_op jit(solution)/shard_map/ppermute | solution.py:647
  36.6 2.2 slice_add_fusion
  38.8 4.5 %all-to-all-start = ((bf16[4,576,128]{2,1,0:T(8,128)(2,1)}), bf16[4,576,128]{2,1,0:T(8,128)(2,1)S(1)}, u32[]{:S(2)}, u32[]{:S(2)}) async-start(bf16[4,576,128]{2,1,0:T(8,128)(2,1)} %bitcast.41), calls=%async_computation | async-start | bytes 1179648 | tf_op jit(solution)/shard_map/all_to_all | solution.py:642
  43.2 5.3 %shard_map.80 = bf16[1024,1024]{1,0:T(8,128)(2,1)} custom-call(s32[39]{0:T(128)S(1)} %copy-done.5, bf16[512,8192]{1,0:T(8,128)(2,1)} %bitcast.48, bf16[512,4096]{1,0:T(8,128)(2,1)} %collective-permute-done.refs_1_, bf16[512,1024]{1,0:T(8,128)(2,1)S(1)} %copy-done.4, bf16[512,1024]{1,0:T(8,128)(2,1)S(1)} %collective-permute-done.6.refs_3_), custom_call_target="tpu_custom_call" | custom-call | flops 2147483648 | bytes 8388608 | tf_op jit(solution)/shard_map/pallas_call | solution.py:403
  48.6 1.5 collective-permute-start.8
  50.0 5.3 %shard_map.81 = bf16[1024,1024]{1,0:T(8,128)(2,1)} custom-call(s32[39]{0:T(128)S(1)} %copy-done.5, bf16[512,8192]{1,0:T(8,128)(2,1)} %bitcast.49, bf16[512,4096]{1,0:T(8,128)(2,1)} %collective-permute-done.refs_1_, bf16[512,1024]{1,0:T(8,128)(2,1)S(1)} %copy-done.4, bf16[512,1024]{1,0:T(8,128)(2,1)S(1)} %collective-permute-done.6.refs_3_), custom_call_target="tpu_custom_call" | custom-call | flops 2147483648 | bytes 8388608 | tf_op jit(solution)/shard_map/pallas_call | solution.py:403
  55.4 1.2 collective-permute-start.9
  56.5 5.8 %shard_map.82.refs_0_.refs_3_ = f32[1024,1024]{1,0:T(8,128)} custom-call(s32[39]{0:T(128)S(1)} %copy-done.5, bf16[512,8192]{1,0:T(8,128)(2,1)} %bitcast.50, bf16[512,4096]{1,0:T(8,128)(2,1)} %collective-permute-done.refs_1_, bf16[512,1024]{1,0:T(8,128)(2,1)S(1)} %copy-done.4, bf16[512,1024]{1,0:T(8,128)(2,1)S(1)} %collective-permute-done.6.refs_3_), custom_call_target="tpu_custom_call" | custom-call | flops 2147483648 | bytes 8388608 | tf_op jit(solution)/shard_map/pallas_call | solution.py:403
  62.3 5.7 %shard_map.79.refs_0_ = f32[1024,1024]{1,0:T(8,128)} custom-call(s32[39]{0:T(128)S(1)} %copy-done.5, bf16[512,8192]{1,0:T(8,128)(2,1)} %bitcast.51, bf16[512,4096]{1,0:T(8,128)(2,1)} %collective-permute-done.refs_1_, bf16[512,1024]{1,0:T(8,128)(2,1)S(1)} %copy-done.4, bf16[512,1024]{1,0:T(8,128)(2,1)S(1)} %collective-permute-done.6.refs_3_), custom_call_target="tpu_custom_call" | custom-call | flops 2147483648 | bytes 8388608 | tf_op jit(solution)/shard_map/pallas_call | solution.py:403
  68.1 12.9 %all_to_all.20 = f32[4,144,128]{2,1,0:T(8,128)S(1)} all-to-all(f32[4,144,128]{2,1,0:T(8,128)S(1)} %bitcast.54), channel_id=1, replica_groups=mesh['gx'=4,'gy'=2,'core'=2,'gz'=2] {'gx'}, dimensions={0} | all-to-all | bytes 589824 | tf_op jit(solution)/shard_map/all_to_all | solution.py:642
  81.0 11.4 %all_to_all.21 = f32[4,144,128]{2,1,0:T(8,128)S(1)} all-to-all(f32[4,144,128]{2,1,0:T(8,128)S(1)} %broadcast_in_dim.17), channel_id=1, replica_groups=mesh['gx'=4,'gy'=2,'core'=2,'gz'=2] {'gx'}, dimensions={0} | all-to-all | bytes 589824 | tf_op jit(solution)/shard_map/all_to_all | solution.py:642
  92.5 1.1 broadcast_in_dim.18
  93.6 3.7 %all-to-all-start.3 = ((f32[4,576,128]{2,1,0:T(8,128)}), f32[4,576,128]{2,1,0:T(8,128)S(1)}, u32[]{:S(2)}, u32[]{:S(2)}) async-start(f32[4,576,128]{2,1,0:T(8,128)} %broadcast_in_dim.18), calls=%async_computation.3 | async-start | bytes 2359296 | tf_op jit(solution)/shard_map/all_to_all | solution.py:642
  97.3 7.5 %collective-permute-done.9.refs_1_.refs_4_ = bf16[1024,1024]{1,0:T(8,128)(2,1)} collective-permute-done((bf16[1024,1024]{1,0:T(8,128)(2,1)}, bf16[1024,1024]{1,0:T(8,128)(2,1)}, u32[]{:S(2)}, u32[]{:S(2)}) %collective-permute-start.9) | collective-permute-done | bytes 2097184 | tf_op jit(solution)/shard_map/ppermute | solution.py:569
  104.9 2.2 copy-done.2
  107.0 2.2 shard_map.83
  109.5 1.9 shard_map.84
  111.5 2.7 %all-to-all-done.3 = f32[4,576,128]{2,1,0:T(8,128)S(1)} async-done(((f32[4,576,128]{2,1,0:T(8,128)}), f32[4,576,128]{2,1,0:T(8,128)S(1)}, u32[]{:S(2)}, u32[]{:S(2)}) %all-to-all-start.3) | async-done | bytes 1179680 | tf_op jit(solution)/shard_map/all_to_all | solution.py:642
  114.1 4.3 %collective-permute-start.12 = (f32[2304,128]{1,0:T(8,128)S(1)}, f32[2304,128]{1,0:T(8,128)}, u32[]{:S(2)}, u32[]{:S(2)}) collective-permute-start(f32[2304,128]{1,0:T(8,128)S(1)} %bitcast.52), channel_id=1, source_target_pairs={{0,2},{2,0},{1,3},{3,1},{4,6},{6,4},{5,7},{7,5},{8,10},{10,8},{9,1... | collective-permute-start | bytes 3538952 | tf_op jit(solution)/shard_map/ppermute | solution.py:674
  118.5 1.2 collective-permute-start.10
  119.7 1.4 collective-permute-done.12
  121.1 1.6 broadcast_select_fusion.1
  122.8 22.2 %shard_map.85.w0_ref.refs_4_ = f32[512,512]{1,0:T(8,128)S(1)} custom-call(f32[1280,128]{1,0:T(8,128)S(1)} %pad_maximum_fusion.1.packed_ref), custom_call_target="tpu_custom_call" | custom-call | flops 512 | bytes 512 | tf_op jit(solution)/shard_map/pallas_call | solution.py:179
  145.0 3.5 %shard_map.86 = (bf16[256,1024]{1,0:T(8,128)(2,1)S(1)}, bf16[256,1024]{1,0:T(8,128)(2,1)S(1)}, bf16[256,1024]{1,0:T(8,128)(2,1)S(1)}, bf16[256,1024]{1,0:T(8,128...) custom-call(s32[39]{0:T(128)S(1)} %copy-done.5, f32[1024,1024]{1,0:T(8,128)S(1)} %copy-done.3, ...), custom_call_target="tpu_custom_call" | custom-call | bytes 14680064 | tf_op jit(solution)/shard_map/pallas_call | solution.py:477
  149.0 5.3 %collective-permute-start.13 = (bf16[256,1024]{1,0:T(8,128)(2,1)S(1)}, bf16[256,1024]{1,0:T(8,128)(2,1)S(1)}, u32[]{:S(2)}, u32[]{:S(2)}) collective-permute-start(bf16[256,1024]{1,0:T(8,128)(2,1)S(1)} %get-tuple-element.61), channel_id=1, source_target_pairs={{2,16},{6,20},{8,2},{10,18},{12,6},{14,22},{16,8},{18,24},{20,12},... | collective-permute-start | bytes 1572872 | tf_op jit(solution)/shard_map/ppermute | solution.py:704
  154.3 3.2 %collective-permute-start.14 = (bf16[256,1024]{1,0:T(8,128)(2,1)S(1)}, bf16[256,1024]{1,0:T(8,128)(2,1)S(1)}, u32[]{:S(2)}, u32[]{:S(2)}) collective-permute-start(bf16[256,1024]{1,0:T(8,128)(2,1)S(1)} %get-tuple-element.62), channel_id=1, source_target_pairs={{2,18},{6,22},{10,24},{14,28},{16,10},{18,26},{20,14},{22,30},{24,... | collective-permute-start | bytes 1572872 | tf_op jit(solution)/shard_map/ppermute | solution.py:704
  157.5 1.9 collective-permute-start.15
  159.5 3.3 %collective-permute-start.16 = (bf16[256,1024]{1,0:T(8,128)(2,1)S(1)}, bf16[256,1024]{1,0:T(8,128)(2,1)S(1)}, u32[]{:S(2)}, u32[]{:S(2)}) collective-permute-start(bf16[256,1024]{1,0:T(8,128)(2,1)S(1)} %get-tuple-element.64), channel_id=1, source_target_pairs={{0,10},{2,26},{4,14},{6,30},{8,0},{10,16},{12,4},{14,20},{16,2},{2... | collective-permute-start | bytes 1572872 | tf_op jit(solution)/shard_map/ppermute | solution.py:704
  163.0 24.0 %shard_map.87 = (f32[512,512]{1,0:T(8,128)S(1)}, f32[512,512]{1,0:T(8,128)S(1)}) custom-call(f32[3328,128]{1,0:T(8,128)S(1)} %pad_maximum_fusion.packed_ref, f32[512,512]{1,0:T(8,128)S(1)} %shard_map.85.w0_ref.refs_4_), custom_call_target="tpu_custom_call" | custom-call | flops 512 | bytes 512 | tf_op jit(solution)/shard_map/pallas_call | solution.py:179
  187.0 13.9 %collective-permute-done.16.refs_3_ = bf16[256,1024]{1,0:T(8,128)(2,1)S(1)} collective-permute-done((bf16[256,1024]{1,0:T(8,128)(2,1)S(1)}, bf16[256,1024]{1,0:T(8,128)(2,1)S(1)}, u32[]{:S(2)}, u32[]{:S(2)}) %collective-permute-start.16) | collective-permute-done | bytes 524320 | tf_op jit(solution)/shard_map/ppermute | solution.py:704
  200.9 2.6 %shard_map.88 = (f32[2,256,256]{2,1,0:T(8,128)S(1)}, f32[2,256,256]{2,1,0:T(8,128)S(1)}, f32[2,256,256]{2,1,0:T(8,128)S(1)}, f32[2,256,256]{2,1,0:T(8,128)S(1)}) custom-call(s32[39]{0:T(128)S(1)} %copy-done.5, f32[256,1024]{1,0:T(8,128)S(1)} %get-tuple-element.60.own_ref, f32[256,1024]{1,0:T(8,128)S(1)} %collective-permute-done.17.swapped_ref, ...), custom_call_target="tpu_custom_call" | custom-call | tf_op jit(solution)/shard_map/pallas_call | solution.py:711
  203.6 1.2 collective-permute-start.19
  204.8 0.7 collective-permute-start.20
  205.5 7.5 %collective-permute-done.18.refs_1_ = f32[2,256,256]{2,1,0:T(8,128)S(1)} collective-permute-done((f32[2,256,256]{2,1,0:T(8,128)S(1)}, f32[2,256,256]{2,1,0:T(8,128)S(1)}, u32[]{:S(2)}, u32[]{:S(2)}) %collective-permute-start.18) | collective-permute-done | bytes 524320 | tf_op jit(solution)/shard_map/ppermute | solution.py:725
  213.1 13.8 %collective-permute-done.19.refs_2_ = f32[2,256,256]{2,1,0:T(8,128)S(1)} collective-permute-done((f32[2,256,256]{2,1,0:T(8,128)S(1)}, f32[2,256,256]{2,1,0:T(8,128)S(1)}, u32[]{:S(2)}, u32[]{:S(2)}) %collective-permute-start.19) | collective-permute-done | bytes 524320 | tf_op jit(solution)/shard_map/ppermute | solution.py:725
  226.8 1.3 collective-permute-done.20.refs_3_
  228.1 2.0 shard_map.89
  (56 shorter events, 2.9 us)
Async XLA Ops:
  10.2 33.0 %collective-permute-start = (bf16[512,4096]{1,0:T(8,128)(2,1)}, bf16[512,4096]{1,0:T(8,128)(2,1)}, u32[]{:S(2)}, u32[]{:S(2)}) collective-permute-start(bf16[512,4096]{1,0:T(8,128)(2,1)} %get-tuple-element.41), channel_id=1, source_target_pairs={{0,2},{2,0},{1,3},{3,1},{4,6},{6,4},{5,7},{7,5},{8,10},{10,8},{9,1... | collective-permute-start | bytes 12582920 | tf_op jit(solution)/shard_map/ppermute | solution.py:636
  10.4 11.2 %collective-permute-start.1 = (bf16[64,1024]{1,0:T(8,128)(2,1)}, bf16[64,1024]{1,0:T(8,128)(2,1)S(1)}, u32[]{:S(2)}, u32[]{:S(2)}) collective-permute-start(bf16[64,1024]{1,0:T(8,128)(2,1)} %get-tuple-element.44), channel_id=1, source_target_pairs={{0,8},{8,16},{16,24},{1,9},{9,17},{17,25},{2,10},{10,18},{18,26},{... | collective-permute-start | bytes 393224 | tf_op jit(solution)/shard_map/ppermute | solution.py:614
  15.0 7.9 %collective-permute-start.2 = (bf16[64,1024]{1,0:T(8,128)(2,1)}, bf16[64,1024]{1,0:T(8,128)(2,1)S(1)}, u32[]{:S(2)}, u32[]{:S(2)}) collective-permute-start(bf16[64,1024]{1,0:T(8,128)(2,1)} %get-tuple-element.45), channel_id=1, source_target_pairs={{8,0},{16,8},{24,16},{9,1},{17,9},{25,17},{10,2},{18,10},{26,18},{... | collective-permute-start | bytes 393224 | tf_op jit(solution)/shard_map/ppermute | solution.py:615
  16.3 6.6 %collective-permute-start.3 = (bf16[64,1024]{1,0:T(8,128)(2,1)}, bf16[64,1024]{1,0:T(8,128)(2,1)S(1)}, u32[]{:S(2)}, u32[]{:S(2)}) collective-permute-start(bf16[64,1024]{1,0:T(8,128)(2,1)} %get-tuple-element.46), channel_id=1, source_target_pairs={{0,2},{2,4},{4,6},{1,3},{3,5},{5,7},{8,10},{10,12},{12,14},{9,11},... | collective-permute-start | bytes 393224 | tf_op jit(solution)/shard_map/ppermute | solution.py:614
  19.7 6.5 %collective-permute-start.4 = (bf16[64,1024]{1,0:T(8,128)(2,1)}, bf16[64,1024]{1,0:T(8,128)(2,1)S(1)}, u32[]{:S(2)}, u32[]{:S(2)}) collective-permute-start(bf16[64,1024]{1,0:T(8,128)(2,1)} %get-tuple-element.47), channel_id=1, source_target_pairs={{2,0},{4,2},{6,4},{3,1},{5,3},{7,5},{10,8},{12,10},{14,12},{11,9},... | collective-permute-start | bytes 393224 | tf_op jit(solution)/shard_map/ppermute | solution.py:615
  21.6 4.6 %copy-start.6 = (bf16[64,1024]{1,0:T(8,128)(2,1)}, bf16[64,1024]{1,0:T(8,128)(2,1)S(1)}, u32[]{:S(2)}) copy-start(bf16[64,1024]{1,0:T(8,128)(2,1)S(1)} %collective-permute-done.1.refs_0_) | copy-start | bytes 393220
  21.6 4.6 %collective-permute-start.5 = (bf16[64,1024]{1,0:T(8,128)(2,1)}, bf16[64,1024]{1,0:T(8,128)(2,1)S(1)}, u32[]{:S(2)}, u32[]{:S(2)}) collective-permute-start(bf16[64,1024]{1,0:T(8,128)(2,1)} %get-tuple-element.48), channel_id=1, source_target_pairs={{0,1},{1,0},{2,3},{3,2},{4,5},{5,4},{6,7},{7,6},{8,9},{9,8},{10,11... | collective-permute-start | bytes 393224 | tf_op jit(solution)/shard_map/ppermute | solution.py:611
  22.9 3.3 %copy-start.7 = (bf16[64,1024]{1,0:T(8,128)(2,1)}, bf16[64,1024]{1,0:T(8,128)(2,1)S(1)}, u32[]{:S(2)}) copy-start(bf16[64,1024]{1,0:T(8,128)(2,1)S(1)} %collective-permute-done.2.refs_1_) | copy-start | bytes 393220
  22.9 3.3 %copy-start.8 = (bf16[64,1024]{1,0:T(8,128)(2,1)}, bf16[64,1024]{1,0:T(8,128)(2,1)S(1)}, u32[]{:S(2)}) copy-start(bf16[64,1024]{1,0:T(8,128)(2,1)S(1)} %collective-permute-done.3.refs_2_) | copy-start | bytes 393220
  26.2 0.7 copy-start.9
  26.2 0.7 copy-start.10
  33.4 3.2 %collective-permute-start.7 = (f32[2432,128]{1,0:T(8,128)}, f32[2432,128]{1,0:T(8,128)S(1)}, u32[]{:S(2)}, u32[]{:S(2)}) collective-permute-start(f32[2432,128]{1,0:T(8,128)} %get-tuple-element.51), channel_id=1, source_target_pairs={{0,2},{2,0},{1,3},{3,1},{4,6},{6,4},{5,7},{7,5},{8,10},{10,8},{9,1... | collective-permute-start | bytes 3735560 | tf_op jit(solution)/shard_map/ppermute | solution.py:647
  33.4 5.4 %collective-permute-start.6 = (bf16[512,1024]{1,0:T(8,128)(2,1)}, bf16[512,1024]{1,0:T(8,128)(2,1)S(1)}, u32[]{:S(2)}, u32[]{:S(2)}) collective-permute-start(bf16[512,1024]{1,0:T(8,128)(2,1)} %get-tuple-element.52.refs_2_), channel_id=1, source_target_pairs={{0,2},{2,0},{1,3},{3,1},{4,6},{6,4},{5,7},{7,5},{8,10},{10,8},{9,1... | collective-permute-start | bytes 3145736 | tf_op jit(solution)/shard_map/ppermute | solution.py:635
  36.5 6.7 %copy-start.5 = (s32[39]{0:T(128)S(1)}, s32[39]{0:T(128)}, u32[]{:S(2)}) copy-start(s32[39]{0:T(128)} %stack.171.table_ref) | copy-start | bytes 472
  38.8 4.5 %copy-start.4 = (bf16[512,1024]{1,0:T(8,128)(2,1)S(1)}, bf16[512,1024]{1,0:T(8,128)(2,1)}, u32[]{:S(2)}) copy-start(bf16[512,1024]{1,0:T(8,128)(2,1)} %get-tuple-element.52.refs_2_) | copy-start | bytes 3145732
  38.8 29.2 %all-to-all-start = ((bf16[4,576,128]{2,1,0:T(8,128)(2,1)}), bf16[4,576,128]{2,1,0:T(8,128)(2,1)S(1)}, u32[]{:S(2)}, u32[]{:S(2)}) async-start(bf16[4,576,128]{2,1,0:T(8,128)(2,1)} %bitcast.41), calls=%async_computation | async-start | bytes 1179648 | tf_op jit(solution)/shard_map/all_to_all | solution.py:642
  48.6 48.8 %collective-permute-start.8 = (bf16[1024,1024]{1,0:T(8,128)(2,1)}, bf16[1024,1024]{1,0:T(8,128)(2,1)}, u32[]{:S(2)}, u32[]{:S(2)}) collective-permute-start(bf16[1024,1024]{1,0:T(8,128)(2,1)} %shard_map.80), channel_id=1, source_target_pairs={{0,1},{1,0},{2,3},{3,2},{4,5},{5,4},{6,7},{7,6},{8,9},{9,8},{10,11... | collective-permute-start | bytes 6291464 | tf_op jit(solution)/shard_map/ppermute | solution.py:569
  55.4 49.5 %collective-permute-start.9 = (bf16[1024,1024]{1,0:T(8,128)(2,1)}, bf16[1024,1024]{1,0:T(8,128)(2,1)}, u32[]{:S(2)}, u32[]{:S(2)}) collective-permute-start(bf16[1024,1024]{1,0:T(8,128)(2,1)} %shard_map.81), channel_id=1, source_target_pairs={{0,4},{4,0},{1,5},{5,1},{2,6},{6,2},{3,7},{7,3},{8,12},{12,8},{9,1... | collective-permute-start | bytes 6291464 | tf_op jit(solution)/shard_map/ppermute | solution.py:569
  93.6 20.5 %all-to-all-start.3 = ((f32[4,576,128]{2,1,0:T(8,128)}), f32[4,576,128]{2,1,0:T(8,128)S(1)}, u32[]{:S(2)}, u32[]{:S(2)}) async-start(f32[4,576,128]{2,1,0:T(8,128)} %broadcast_in_dim.18), calls=%async_computation.3 | async-start | bytes 2359296 | tf_op jit(solution)/shard_map/all_to_all | solution.py:642
  104.9 2.2 copy-start.2
  107.0 2.5 %copy-start = (f32[1024,1024]{1,0:T(8,128)S(1)}, f32[1024,1024]{1,0:T(8,128)}, u32[]{:S(2)}) copy-start(f32[1024,1024]{1,0:T(8,128)} %shard_map.82.refs_0_.refs_3_) | copy-start | bytes 12582916
  114.1 6.9 %collective-permute-start.12 = (f32[2304,128]{1,0:T(8,128)S(1)}, f32[2304,128]{1,0:T(8,128)}, u32[]{:S(2)}, u32[]{:S(2)}) collective-permute-start(f32[2304,128]{1,0:T(8,128)S(1)} %bitcast.52), channel_id=1, source_target_pairs={{0,2},{2,0},{1,3},{3,1},{4,6},{6,4},{5,7},{7,5},{8,10},{10,8},{9,1... | collective-permute-start | bytes 3538952 | tf_op jit(solution)/shard_map/ppermute | solution.py:674
  118.5 26.5 %collective-permute-start.11 = (bf16[512,1024]{1,0:T(8,128)(2,1)S(1)}, bf16[512,1024]{1,0:T(8,128)(2,1)S(1)}, u32[]{:S(2)}, u32[]{:S(2)}) collective-permute-start(bf16[512,1024]{1,0:T(8,128)(2,1)S(1)} %shard_map.84), channel_id=1, source_target_pairs={{0,1},{1,0},{2,3},{3,2},{4,5},{5,4},{6,7},{7,6},{8,9},{9,8},{10,11... | collective-permute-start | bytes 3145736 | tf_op jit(solution)/shard_map/ppermute | solution.py:569
  118.5 26.5 %collective-permute-start.10 = (bf16[512,1024]{1,0:T(8,128)(2,1)S(1)}, bf16[512,1024]{1,0:T(8,128)(2,1)S(1)}, u32[]{:S(2)}, u32[]{:S(2)}) collective-permute-start(bf16[512,1024]{1,0:T(8,128)(2,1)S(1)} %shard_map.83), channel_id=1, source_target_pairs={{0,4},{4,0},{1,5},{5,1},{2,6},{6,2},{3,7},{7,3},{8,12},{12,8},{9,1... | collective-permute-start | bytes 3145736 | tf_op jit(solution)/shard_map/ppermute | solution.py:569
  121.1 23.9 %copy-start.3 = (f32[1024,1024]{1,0:T(8,128)S(1)}, f32[1024,1024]{1,0:T(8,128)}, u32[]{:S(2)}) copy-start(f32[1024,1024]{1,0:T(8,128)} %shard_map.79.refs_0_) | copy-start | bytes 12582916
  122.6 22.3 %copy-start.1 = (f32[1024,1024]{1,0:T(8,128)S(1)}, f32[1024,1024]{1,0:T(8,128)}, u32[]{:S(2)}) copy-start(f32[1024,1024]{1,0:T(8,128)} %shard_map.82.refs_0_.refs_3_) | copy-start | bytes 12582916
  148.5 52.4 %collective-permute-start.17 = (f32[256,1024]{1,0:T(8,128)S(1)}, f32[256,1024]{1,0:T(8,128)S(1)}, u32[]{:S(2)}, u32[]{:S(2)}) collective-permute-start(f32[256,1024]{1,0:T(8,128)S(1)} %get-tuple-element.65), channel_id=1, source_target_pairs={{0,2},{2,0},{1,3},{3,1},{4,6},{6,4},{5,7},{7,5},{8,10},{10,8},{9,1... | collective-permute-start | bytes 3145736 | tf_op jit(solution)/shard_map/ppermute | solution.py:705
  149.0 38.0 %collective-permute-start.13 = (bf16[256,1024]{1,0:T(8,128)(2,1)S(1)}, bf16[256,1024]{1,0:T(8,128)(2,1)S(1)}, u32[]{:S(2)}, u32[]{:S(2)}) collective-permute-start(bf16[256,1024]{1,0:T(8,128)(2,1)S(1)} %get-tuple-element.61), channel_id=1, source_target_pairs={{2,16},{6,20},{8,2},{10,18},{12,6},{14,22},{16,8},{18,24},{20,12},... | collective-permute-start | bytes 1572872 | tf_op jit(solution)/shard_map/ppermute | solution.py:704
  154.3 32.7 %collective-permute-start.14 = (bf16[256,1024]{1,0:T(8,128)(2,1)S(1)}, bf16[256,1024]{1,0:T(8,128)(2,1)S(1)}, u32[]{:S(2)}, u32[]{:S(2)}) collective-permute-start(bf16[256,1024]{1,0:T(8,128)(2,1)S(1)} %get-tuple-element.62), channel_id=1, source_target_pairs={{2,18},{6,22},{10,24},{14,28},{16,10},{18,26},{20,14},{22,30},{24,... | collective-permute-start | bytes 1572872 | tf_op jit(solution)/shard_map/ppermute | solution.py:704
  157.5 29.5 %collective-permute-start.15 = (bf16[256,1024]{1,0:T(8,128)(2,1)S(1)}, bf16[256,1024]{1,0:T(8,128)(2,1)S(1)}, u32[]{:S(2)}, u32[]{:S(2)}) collective-permute-start(bf16[256,1024]{1,0:T(8,128)(2,1)S(1)} %get-tuple-element.63), channel_id=1, source_target_pairs={{0,8},{2,24},{4,12},{6,28},{10,26},{14,30},{16,0},{20,4},{24,2},{2... | collective-permute-start | bytes 1572872 | tf_op jit(solution)/shard_map/ppermute | solution.py:704
  159.5 41.4 %collective-permute-start.16 = (bf16[256,1024]{1,0:T(8,128)(2,1)S(1)}, bf16[256,1024]{1,0:T(8,128)(2,1)S(1)}, u32[]{:S(2)}, u32[]{:S(2)}) collective-permute-start(bf16[256,1024]{1,0:T(8,128)(2,1)S(1)} %get-tuple-element.64), channel_id=1, source_target_pairs={{0,10},{2,26},{4,14},{6,30},{8,0},{10,16},{12,4},{14,20},{16,2},{2... | collective-permute-start | bytes 1572872 | tf_op jit(solution)/shard_map/ppermute | solution.py:704
  203.5 9.6 %collective-permute-start.18 = (f32[2,256,256]{2,1,0:T(8,128)S(1)}, f32[2,256,256]{2,1,0:T(8,128)S(1)}, u32[]{:S(2)}, u32[]{:S(2)}) collective-permute-start(f32[2,256,256]{2,1,0:T(8,128)S(1)} %get-tuple-element.77), channel_id=1, source_target_pairs={{0,2},{2,4},{4,6},{6,0},{1,3},{3,5},{5,7},{7,1},{8,10},{10,12},{12... | collective-permute-start | bytes 1572872 | tf_op jit(solution)/shard_map/ppermute | solution.py:725
  203.6 23.3 %collective-permute-start.19 = (f32[2,256,256]{2,1,0:T(8,128)S(1)}, f32[2,256,256]{2,1,0:T(8,128)S(1)}, u32[]{:S(2)}, u32[]{:S(2)}) collective-permute-start(f32[2,256,256]{2,1,0:T(8,128)S(1)} %get-tuple-element.78), channel_id=1, source_target_pairs={{0,4},{2,6},{4,0},{6,2},{1,5},{3,7},{5,1},{7,3},{8,12},{10,14},{12... | collective-permute-start | bytes 1572872 | tf_op jit(solution)/shard_map/ppermute | solution.py:725
  204.8 23.3 %collective-permute-start.20 = (f32[2,256,256]{2,1,0:T(8,128)S(1)}, f32[2,256,256]{2,1,0:T(8,128)S(1)}, u32[]{:S(2)}, u32[]{:S(2)}) collective-permute-start(f32[2,256,256]{2,1,0:T(8,128)S(1)} %get-tuple-element.79), channel_id=1, source_target_pairs={{0,6},{2,0},{4,2},{6,4},{1,7},{3,1},{5,3},{7,5},{8,14},{10,8},{12,... | collective-permute-start | bytes 1572872 | tf_op jit(solution)/shard_map/ppermute | solution.py:725

commit v10 on v9

--- a/solution.py
+++ b/solution.py
@@ -278,9 +278,8 @@
         copy_out.wait()
 
 
-def image_kernel(table_ref, panel_ref, conduct_ref, grounds_ref, *refs, sides, nb, at, last_at):
-    *halos, image_ref, kept_ref, sent_ref, scaled_ref, square_ref = refs
-    core = table_ref[at]
+def image_kernel(table_ref, panel_ref, conduct_ref, grounds_ref, *refs, sides, nb, last_at):
+    *halos, image_ref, lead_ref, scaled_ref, square_ref = refs
     last = table_ref[last_at] != 0
     size_x, size_y, size_z = sides
     width = panel_ref.shape[1]
@@ -342,19 +341,8 @@
 
     blocks = nb // LEAF
 
-    first_blocks = blocks * (blocks + 1) // 2
-    half = kept_ref.shape[0] // LEAF - 1
-
     def put_block(number, value):
-        if number < first_blocks:
-            owner, place = divmod(number, first_blocks // 2)
-        else:
-            owner, place = divmod(number - first_blocks, half - first_blocks // 2)
-            place += first_blocks // 2
-        kept = core == owner
-        for ref, here in ((kept_ref, kept), (sent_ref, jnp.logical_not(kept))):
-            at_row = pl.multiple_of(jnp.where(here, place, half) * LEAF, LEAF)
-            ref[pl.ds(at_row, LEAF), :] = value
+        lead_ref[number * LEAF : (number + 1) * LEAF, :] = value.astype(lead_ref.dtype)
 
     def lower(number):
         for i in range(blocks):
@@ -369,11 +357,13 @@
     number = lower(0)
     square_ref[...] = product(tail, tail)
     number = lower(number)
-    square_ref[...] = product(tail, head)
+    below = product(tail, head)
     for j in range(blocks):
         for i in range(blocks):
-            row, col = slice(i * LEAF, (i + 1) * LEAF), slice(j * LEAF, (j + 1) * LEAF)
-            put_block(number + j * blocks + i, square_ref[row, col])
+            put_block(
+                number + j * blocks + i,
+                below[i * LEAF : (i + 1) * LEAF, j * LEAF : (j + 1) * LEAF],
+            )
 
 
 def products_kernel(table_ref, *refs):
@@ -556,7 +546,6 @@
     leaving = [(at_x + step) % devices_x for step in range(devices_x)]
     leaving_at, _ = put(leaving + [at_x % spans * 2 + core, at_x % spans * 2 + 1 - core])
     given_at, _ = put([1 - core])
-    core_at, _ = put([core])
     last_at, _ = put([at_z == 1])
     places_at, _ = put([(at_y - d) % devices_y for d in range(devices_y)])
     order_at, _ = put([(at_y + d) % devices_y for d in range(devices_y)])
@@ -616,17 +605,16 @@
 
     blocks = NB // LEAF
     lower_rows = blocks * (blocks + 1) // 2 * LEAF
-    half_rows = lower_rows + blocks * NB // 2
-    lead_parts = [jax.ShapeDtypeStruct((half_rows + LEAF, LEAF), f32)] * 2
-    outs = [jax.ShapeDtypeStruct((count, cols), bf16), *lead_parts]
-    image, lead_kept, lead_sent = pl.pallas_call(
-        functools.partial(image_kernel, sides=sides, nb=NB, at=core_at, last_at=last_at),
+    lead_rows = 2 * lower_rows + blocks * NB
+    outs = [jax.ShapeDtypeStruct((n, width), bf16) for n, width in ((count, cols), (lead_rows, LEAF))]
+    image, lead = pl.pallas_call(
+        functools.partial(image_kernel, sides=sides, nb=NB, last_at=last_at),
         out_shape=outs,
         grid_spec=pltpu.PrefetchScalarGridSpec(
             num_scalar_prefetch=1,
             grid=(1,),
             in_specs=[panel_spec] + [whole()] * (2 + len(halos)),
-            out_specs=[whole()] * 3,
+            out_specs=[whole()] * 2,
             scratch_shapes=[pltpu.VMEM((count, LEAF), f32), pltpu.VMEM((NB, NB), f32)],
         ),
         compiler_params=pltpu.CompilerParams(vmem_limit_bytes=56 * 2**20),
@@ -644,26 +632,28 @@
     def for_all(own, size):
         return jnp.broadcast_to(own, (size, *own.shape))
 
-    lead_got = lax.ppermute(lead_sent, "core", swap_pairs())
-    lead_half = lead_kept[:half_rows] + lead_got[:half_rows]
-    lead_terms = exchanged(lead_half.astype(bf16).reshape(chips, -1, LEAF), plane_axes)
+    lead_terms = exchanged(lead.reshape(chips, -1, LEAF), plane_axes)
 
     def chip_products(images, lists, dtype):
         return products(table, [flat_basis, other_basis], images, lists, narrow, dtype)
 
-    images, _ = lax.optimization_barrier(([image, other_image], lead_half))
+    images, _ = lax.optimization_barrier(([image, other_image], lead))
     sent_a = [chip_products(images, lists_a[d], bf16) for d in range(1, devices_z)]
     sent_b = [chip_products(images, lists_b[d], bf16) for d in range(1, chips_y)]
     got_a = [move(a, "gz", d) for d, a in enumerate(sent_a, 1)]
     got_b = [move(a, "gy", d) for d, a in enumerate(sent_b, 1)]
+    images, _ = lax.optimization_barrier((images, (sent_a, sent_b)))
     own_a, own_b = (chip_products(images, lists[0], f32) for lists in (lists_a, lists_b))
     lead_terms, _ = lax.optimization_barrier((lead_terms, (own_a, own_b)))
-    own = jnp.sum(lead_terms.astype(f32), axis=0).reshape(devices_x, -1, LEAF)
+    own = jnp.sum(lead_terms.astype(f32), axis=0).reshape(2, -1, LEAF)
+    kept = lax.dynamic_index_in_dim(own, core, 0, keepdims=False)
+    sent = lax.dynamic_index_in_dim(own, 1 - core, 0, keepdims=False)
+    own = (kept + lax.ppermute(sent, "core", swap_pairs())).reshape(devices_x, -1, LEAF)
     own = jnp.sum(exchanged(own, "gx"), axis=0)
     own = exchanged(for_all(own, devices_x), "gx").reshape(-1, LEAF)
     own = for_all(own, chips)
     (got_a, got_b), _ = lax.optimization_barrier(((got_a, got_b), own))
-    lead_half = exchanged(own, plane_axes).reshape(-1, LEAF)
+    lead_half = exchanged(own, plane_axes)
     sums_a, sums_b = [own_a, *got_a], [own_b, *got_b]
 
     further_a = [add_blocks(table, sums_a, *next_a[d], narrow, bf16) for d in range(1, chips_y)]
@@ -672,10 +662,9 @@
     further_a = [move(a, "gy", d) for d, a in enumerate(further_a, 1)]
     further_b = [move(a, "gz", d) for d, a in enumerate(further_b, 1)]
     other = lax.ppermute(lead_half, "core", swap_pairs())
-    lower_half, upper_half = jnp.where(core == 0, lead_half, other), jnp.where(core == 0, other, lead_half)
-    first = lower_rows // 2
-    first_rows = jnp.concatenate([lower_half[:first], upper_half[:first]], 0)
-    later_rows = jnp.concatenate([lower_half[first:], upper_half[first:]], 0)
+    halves = jnp.where(core == 0, lead_half, other), jnp.where(core == 0, other, lead_half)
+    lead = jnp.stack(halves, 1).reshape(lead_rows, LEAF)
+    first_rows, later_rows = lead[:lower_rows], lead[lower_rows:]
     inverse_0 = first_panel(first_rows, NB)
     (further_a, further_b), inverse_0 = lax.optimization_barrier(
         ((further_a, further_b), inverse_0)

time: 231 us -> 240 us (1.039)
  waiting for transfers between devices: 54 us -> 62.1 us
    ppermute x4, waiting for transfers between devices: 7.54 us -> 20.6 us  [move(): return lax.ppermute(array, axis, [(i, (i + d) % size) for i in range(size)])]
    ppermute x1, waiting for transfers between devices: 2.64 us -> 0.01 us  [local(): lax.ppermute(sent, 'core', swap_pairs())]
    unnamed x22 -> x26, local copies, waits for them, and re-layouts: 3.2 us -> 5.54 us
  transfers between devices with their start and end apart: 23 -> 23, of which waited for: 9 -> 9; matrix products, arithmetic and copies ran while one was open for 2% -> 1% of each run, Pallas kernels for 34% -> 32%
where the time goes in v10:
time: 240 us; the launch traced here: 239 us
  Pallas kernels  92 us (38%)
  waiting for transfers between devices  62.1 us (26%)
  starting transfers between devices  46.7 us (19%)
  blocking collectives  24.3 us (10%)
  local copies, waits for them, and re-layouts  9.31 us (4%)
  other arithmetic  3.84 us (2%)
    pallas_call x2, Pallas kernels, panel_call(): pl.pallas_call(kernel, out_shape=[jax.ShapeDtypeStruct((nb, nb), jnp.floa...  46.1 us
    all_to_all x2, blocking collectives, exchanged(): return lax.all_to_all(rows, axes, split_axis=0, concat_axis=0, tiled=True)  24.3 us
    ppermute x3, waiting for transfers between devices, local(): pairs[d] = lax.ppermute(pairs[d], ('gy', 'core'), route)  22.6 us
    pallas_call x4, Pallas kernels, products(): pl.pallas_call(products_kernel, grid_spec=pltpu.PrefetchScalarGridSpec(nu...  22.4 us
    ppermute x4, waiting for transfers between devices, move(): return lax.ppermute(array, axis, [(i, (i + d) % size) for i in range(size)])  20.6 us
    ppermute x4, waiting for transfers between devices, local(): x_got.append(lax.ppermute(x_sent[step], ('gx', 'gy', 'core'), pairs))  14.1 us
    ppermute x4, starting transfers between devices, local(): x_got.append(lax.ppermute(x_sent[step], ('gx', 'gy', 'core'), pairs))  13.8 us
    all_to_all x2, starting transfers between devices, exchanged(): return lax.all_to_all(rows, axes, split_axis=0, concat_axis=0, tiled=True)  9.12 us
  transfers between devices with their start and end apart: 23, of which 9 were waited for; matrix products, arithmetic and copies ran while one was open for 1% of the time, Pallas kernels for 32%

profile of v10, /device:TPU:1, one launch (start us, length us, event | category | flops | bytes accessed | tf_op | source)
XLA Modules:
  0.0 239.5 jit_solution(2481178270437622088)
XLA Ops:
  0.8 0.8 stack.177
  2.0 0.9 copy.14.info_ref
  3.5 6.8 %shard_map.77 = (bf16[64,1024]{1,0:T(8,128)(2,1)}, bf16[64,1024]{1,0:T(8,128)(2,1)}, bf16[64,1024]{1,0:T(8,128)(2,1)}, bf16[64,1024]{1,0:T(8,128)(2,1)}, bf16[64...) custom-call(s32[38]{0:T(128)} %stack.176.table_ref, f32[16]{0:T(128)} %cond_ref.1, ...), custom_call_target="tpu_custom_call" | custom-call | tf_op jit(solution)/shard_map/pallas_call | solution.py:576
  10.4 4.6 %collective-permute-start.1 = (bf16[64,1024]{1,0:T(8,128)(2,1)}, bf16[64,1024]{1,0:T(8,128)(2,1)S(1)}, u32[]{:S(2)}, u32[]{:S(2)}) collective-permute-start(bf16[64,1024]{1,0:T(8,128)(2,1)} %get-tuple-element.45), channel_id=1, source_target_pairs={{0,8},{8,16},{16,24},{1,9},{9,17},{17,25},{2,10},{10,18},{18,26},{... | collective-permute-start | bytes 393224 | tf_op jit(solution)/shard_map/ppermute | solution.py:603
  15.1 1.3 collective-permute-start.2
  16.4 3.3 %collective-permute-start.3 = (bf16[64,1024]{1,0:T(8,128)(2,1)}, bf16[64,1024]{1,0:T(8,128)(2,1)S(1)}, u32[]{:S(2)}, u32[]{:S(2)}) collective-permute-start(bf16[64,1024]{1,0:T(8,128)(2,1)} %get-tuple-element.47), channel_id=1, source_target_pairs={{0,2},{2,4},{4,6},{1,3},{3,5},{5,7},{8,10},{10,12},{12,14},{9,11},... | collective-permute-start | bytes 393224 | tf_op jit(solution)/shard_map/ppermute | solution.py:603
  19.7 1.9 collective-permute-start.4
  21.6 1.3 collective-permute-start.5
  22.9 3.3 %collective-permute-done.4.refs_3_ = bf16[64,1024]{1,0:T(8,128)(2,1)S(1)} collective-permute-done((bf16[64,1024]{1,0:T(8,128)(2,1)}, bf16[64,1024]{1,0:T(8,128)(2,1)S(1)}, u32[]{:S(2)}, u32[]{:S(2)}) %collective-permute-start.4) | collective-permute-done | bytes 131104 | tf_op jit(solution)/shard_map/ppermute | solution.py:604
  26.9 5.9 %shard_map.78 = (bf16[512,1024]{1,0:T(8,128)(2,1)}, bf16[4608,128]{1,0:T(8,128)(2,1)}) custom-call(s32[38]{0:T(128)} %stack.176.table_ref, bf16[512,8192]{1,0:T(8,128)(2,1)} %bitcast.57, f32[512,128]{1,0:T(8,128)} %get-tuple-element.43.conduct_ref, f32[512,128]{1,0:T(8,128)} %get-tuple-element.44.grounds_ref, bf16[64,1024]{1,0:T(8,128)(2,1)} %copy-done.8, ...), custom_call_target="tpu_custom_call" | custom-call | tf_op jit(solution)/shard_map/pallas_call | solution.py:610
  32.9 4.7 %all-to-all-start = ((bf16[4,1152,128]{2,1,0:T(8,128)(2,1)}), bf16[4,1152,128]{2,1,0:T(8,128)(2,1)}, u32[]{:S(2)}, u32[]{:S(2)}) async-start(bf16[4,1152,128]{2,1,0:T(8,128)(2,1)} %bitcast.67), calls=%async_computation | async-start | bytes 2359296 | tf_op jit(solution)/shard_map/all_to_all | solution.py:630
  37.6 5.4 %shard_map.80 = bf16[1024,1024]{1,0:T(8,128)(2,1)} custom-call(s32[38]{0:T(128)S(1)} %copy-done.7, bf16[512,8192]{1,0:T(8,128)(2,1)} %bitcast.58, bf16[512,4096]{1,0:T(8,128)(2,1)} %collective-permute-done.refs_1_, bf16[512,1024]{1,0:T(8,128)(2,1)S(1)} %copy-done.4, bf16[512,1024]{1,0:T(8,128)(2,1)S(1)} %collective-permute-done.6.refs_3_), custom_call_target="tpu_custom_call" | custom-call | flops 2147483648 | bytes 8388608 | tf_op jit(solution)/shard_map/pallas_call | solution.py:393
  43.0 5.4 %shard_map.79 = bf16[1024,1024]{1,0:T(8,128)(2,1)} custom-call(s32[38]{0:T(128)S(1)} %copy-done.7, bf16[512,8192]{1,0:T(8,128)(2,1)} %bitcast.59, bf16[512,4096]{1,0:T(8,128)(2,1)} %collective-permute-done.refs_1_, bf16[512,1024]{1,0:T(8,128)(2,1)S(1)} %copy-done.4, bf16[512,1024]{1,0:T(8,128)(2,1)S(1)} %collective-permute-done.6.refs_3_), custom_call_target="tpu_custom_call" | custom-call | flops 2147483648 | bytes 8388608 | tf_op jit(solution)/shard_map/pallas_call | solution.py:393
  48.3 5.8 %shard_map.82.refs_0_.refs_3_ = f32[1024,1024]{1,0:T(8,128)} custom-call(s32[38]{0:T(128)S(1)} %copy-done.7, bf16[512,8192]{1,0:T(8,128)(2,1)} %bitcast.60, bf16[512,4096]{1,0:T(8,128)(2,1)} %collective-permute-done.refs_1_, bf16[512,1024]{1,0:T(8,128)(2,1)S(1)} %copy-done.4, bf16[512,1024]{1,0:T(8,128)(2,1)S(1)} %collective-permute-done.6.refs_3_), custom_call_target="tpu_custom_call" | custom-call | flops 2147483648 | bytes 8388608 | tf_op jit(solution)/shard_map/pallas_call | solution.py:393
  54.2 5.8 %shard_map.81.refs_0_ = f32[1024,1024]{1,0:T(8,128)} custom-call(s32[38]{0:T(128)S(1)} %copy-done.7, bf16[512,8192]{1,0:T(8,128)(2,1)} %bitcast.61, bf16[512,4096]{1,0:T(8,128)(2,1)} %collective-permute-done.refs_1_, bf16[512,1024]{1,0:T(8,128)(2,1)S(1)} %copy-done.4, bf16[512,1024]{1,0:T(8,128)(2,1)S(1)} %collective-permute-done.6.refs_3_), custom_call_target="tpu_custom_call" | custom-call | flops 2147483648 | bytes 8388608 | tf_op jit(solution)/shard_map/pallas_call | solution.py:393
  59.9 1.5 convert_reduce_fusion
  62.0 1.7 collective-permute-start.7
  63.7 1.3 collective-permute-start.8
  65.0 12.7 %all_to_all.20 = f32[4,144,128]{2,1,0:T(8,128)S(1)} all-to-all(f32[4,144,128]{2,1,0:T(8,128)S(1)} %bitcast.66), channel_id=1, replica_groups=mesh['gx'=4,'gy'=2,'core'=2,'gz'=2] {'gx'}, dimensions={0} | all-to-all | bytes 589824 | tf_op jit(solution)/shard_map/all_to_all | solution.py:630
  77.8 11.6 %all_to_all.21 = f32[4,144,128]{2,1,0:T(8,128)S(1)} all-to-all(f32[4,144,128]{2,1,0:T(8,128)S(1)} %broadcast_in_dim.17), channel_id=1, replica_groups=mesh['gx'=4,'gy'=2,'core'=2,'gz'=2] {'gx'}, dimensions={0} | all-to-all | bytes 589824 | tf_op jit(solution)/shard_map/all_to_all | solution.py:630
  89.4 1.1 broadcast_in_dim.18
  90.5 4.5 %all-to-all-start.3 = ((f32[4,576,128]{2,1,0:T(8,128)}), f32[4,576,128]{2,1,0:T(8,128)}, u32[]{:S(2)}, u32[]{:S(2)}) async-start(f32[4,576,128]{2,1,0:T(8,128)} %broadcast_in_dim.18), calls=%async_computation.3 | async-start | bytes 2359296 | tf_op jit(solution)/shard_map/all_to_all | solution.py:630
  94.9 15.0 %collective-permute-done.7.refs_1_ = bf16[1024,1024]{1,0:T(8,128)(2,1)S(1)} collective-permute-done((bf16[1024,1024]{1,0:T(8,128)(2,1)}, bf16[1024,1024]{1,0:T(8,128)(2,1)S(1)}, u32[]{:S(2)}, u32[]{:S(2)}) %collective-permute-start.7) | collective-permute-done | bytes 2097184 | tf_op jit(solution)/shard_map/ppermute | solution.py:558
  109.9 5.6 %collective-permute-done.8.refs_1_.refs_4_ = bf16[1024,1024]{1,0:T(8,128)(2,1)} collective-permute-done((bf16[1024,1024]{1,0:T(8,128)(2,1)}, bf16[1024,1024]{1,0:T(8,128)(2,1)}, u32[]{:S(2)}, u32[]{:S(2)}) %collective-permute-start.8) | collective-permute-done | bytes 2097184 | tf_op jit(solution)/shard_map/ppermute | solution.py:558
  115.5 2.2 copy-done.2
  117.7 0.9 shard_map.83
  118.6 1.0 copy-done.5
  120.3 1.9 shard_map.84
  122.2 1.0 copy-done.6
  123.5 3.3 %collective-permute-start.12 = (f32[4,576,128]{2,1,0:T(8,128)}, f32[4,576,128]{2,1,0:T(8,128)}, u32[]{:S(2)}, u32[]{:S(2)}) collective-permute-start(f32[4,576,128]{2,1,0:T(8,128)} %all-to-all-done.3), channel_id=1, source_target_pairs={{0,2},{2,0},{1,3},{3,1},{4,6},{6,4},{5,7},{7,5},{8,10},{10,8},{9,1... | collective-permute-start | bytes 3538952 | tf_op jit(solution)/shard_map/ppermute | solution.py:664
  126.8 1.6 collective-permute-start.10
  128.4 1.2 collective-permute-done.12
  129.6 2.0 select_bitcast_fusion.1
  131.8 22.2 %shard_map.85.w0_ref.refs_4_ = f32[512,512]{1,0:T(8,128)S(1)} custom-call(f32[1280,128]{1,0:T(8,128)S(1)} %slice.8.packed_ref), custom_call_target="tpu_custom_call" | custom-call | flops 512 | bytes 512 | tf_op jit(solution)/shard_map/pallas_call | solution.py:179
  154.0 3.5 %shard_map.86 = (bf16[256,1024]{1,0:T(8,128)(2,1)S(1)}, bf16[256,1024]{1,0:T(8,128)(2,1)S(1)}, bf16[256,1024]{1,0:T(8,128)(2,1)S(1)}, bf16[256,1024]{1,0:T(8,128...) custom-call(s32[38]{0:T(128)S(1)} %copy-done.7, f32[1024,1024]{1,0:T(8,128)S(1)} %copy-done.3, ...), custom_call_target="tpu_custom_call" | custom-call | bytes 14680064 | tf_op jit(solution)/shard_map/pallas_call | solution.py:467
  157.9 5.3 %collective-permute-start.13 = (bf16[256,1024]{1,0:T(8,128)(2,1)S(1)}, bf16[256,1024]{1,0:T(8,128)(2,1)S(1)}, u32[]{:S(2)}, u32[]{:S(2)}) collective-permute-start(bf16[256,1024]{1,0:T(8,128)(2,1)S(1)} %get-tuple-element.63), channel_id=1, source_target_pairs={{2,16},{6,20},{8,2},{10,18},{12,6},{14,22},{16,8},{18,24},{20,12},... | collective-permute-start | bytes 1572872 | tf_op jit(solution)/shard_map/ppermute | solution.py:693
  163.2 3.3 %collective-permute-start.14 = (bf16[256,1024]{1,0:T(8,128)(2,1)S(1)}, bf16[256,1024]{1,0:T(8,128)(2,1)S(1)}, u32[]{:S(2)}, u32[]{:S(2)}) collective-permute-start(bf16[256,1024]{1,0:T(8,128)(2,1)S(1)} %get-tuple-element.64), channel_id=1, source_target_pairs={{2,18},{6,22},{10,24},{14,28},{16,10},{18,26},{20,14},{22,30},{24,... | collective-permute-start | bytes 1572872 | tf_op jit(solution)/shard_map/ppermute | solution.py:693
  166.5 1.9 collective-permute-start.15
  168.4 3.3 %collective-permute-start.16 = (bf16[256,1024]{1,0:T(8,128)(2,1)S(1)}, bf16[256,1024]{1,0:T(8,128)(2,1)S(1)}, u32[]{:S(2)}, u32[]{:S(2)}) collective-permute-start(bf16[256,1024]{1,0:T(8,128)(2,1)S(1)} %get-tuple-element.66), channel_id=1, source_target_pairs={{0,10},{2,26},{4,14},{6,30},{8,0},{10,16},{12,4},{14,20},{16,2},{2... | collective-permute-start | bytes 1572872 | tf_op jit(solution)/shard_map/ppermute | solution.py:693
  171.9 23.9 %shard_map.87 = (f32[512,512]{1,0:T(8,128)S(1)}, f32[512,512]{1,0:T(8,128)S(1)}) custom-call(f32[3328,128]{1,0:T(8,128)S(1)} %slice.9.packed_ref, f32[512,512]{1,0:T(8,128)S(1)} %shard_map.85.w0_ref.refs_4_), custom_call_target="tpu_custom_call" | custom-call | flops 512 | bytes 512 | tf_op jit(solution)/shard_map/pallas_call | solution.py:179
  195.8 14.1 %collective-permute-done.16.refs_3_ = bf16[256,1024]{1,0:T(8,128)(2,1)S(1)} collective-permute-done((bf16[256,1024]{1,0:T(8,128)(2,1)S(1)}, bf16[256,1024]{1,0:T(8,128)(2,1)S(1)}, u32[]{:S(2)}, u32[]{:S(2)}) %collective-permute-start.16) | collective-permute-done | bytes 524320 | tf_op jit(solution)/shard_map/ppermute | solution.py:693
  209.9 2.5 %shard_map.88 = (f32[2,256,256]{2,1,0:T(8,128)S(1)}, f32[2,256,256]{2,1,0:T(8,128)S(1)}, f32[2,256,256]{2,1,0:T(8,128)S(1)}, f32[2,256,256]{2,1,0:T(8,128)S(1)}) custom-call(s32[38]{0:T(128)S(1)} %copy-done.7, f32[256,1024]{1,0:T(8,128)S(1)} %get-tuple-element.62.own_ref, f32[256,1024]{1,0:T(8,128)S(1)} %collective-permute-done.17.swapped_ref, ...), custom_call_target="tpu_custom_call" | custom-call | tf_op jit(solution)/shard_map/pallas_call | solution.py:700
  212.5 1.7 collective-permute-start.19
  214.1 0.7 collective-permute-start.20
  214.8 6.7 %collective-permute-done.18.refs_1_ = f32[2,256,256]{2,1,0:T(8,128)S(1)} collective-permute-done((f32[2,256,256]{2,1,0:T(8,128)S(1)}, f32[2,256,256]{2,1,0:T(8,128)S(1)}, u32[]{:S(2)}, u32[]{:S(2)}) %collective-permute-start.18) | collective-permute-done | bytes 524320 | tf_op jit(solution)/shard_map/ppermute | solution.py:714
  221.6 15.1 %collective-permute-done.19.refs_2_ = f32[2,256,256]{2,1,0:T(8,128)S(1)} collective-permute-done((f32[2,256,256]{2,1,0:T(8,128)S(1)}, f32[2,256,256]{2,1,0:T(8,128)S(1)}, u32[]{:S(2)}, u32[]{:S(2)}) %collective-permute-start.19) | collective-permute-done | bytes 524320 | tf_op jit(solution)/shard_map/ppermute | solution.py:714
  236.7 0.8 collective-permute-done.20.refs_3_
  237.5 2.0 shard_map.89
  (58 shorter events, 4.3 us)
Async XLA Ops:
  10.3 27.3 %collective-permute-start = (bf16[512,4096]{1,0:T(8,128)(2,1)}, bf16[512,4096]{1,0:T(8,128)(2,1)}, u32[]{:S(2)}, u32[]{:S(2)}) collective-permute-start(bf16[512,4096]{1,0:T(8,128)(2,1)} %get-tuple-element.42), channel_id=1, source_target_pairs={{0,2},{2,0},{1,3},{3,1},{4,6},{6,4},{5,7},{7,5},{8,10},{10,8},{9,1... | collective-permute-start | bytes 12582920 | tf_op jit(solution)/shard_map/ppermute | solution.py:624
  10.4 11.2 %collective-permute-start.1 = (bf16[64,1024]{1,0:T(8,128)(2,1)}, bf16[64,1024]{1,0:T(8,128)(2,1)S(1)}, u32[]{:S(2)}, u32[]{:S(2)}) collective-permute-start(bf16[64,1024]{1,0:T(8,128)(2,1)} %get-tuple-element.45), channel_id=1, source_target_pairs={{0,8},{8,16},{16,24},{1,9},{9,17},{17,25},{2,10},{10,18},{18,26},{... | collective-permute-start | bytes 393224 | tf_op jit(solution)/shard_map/ppermute | solution.py:603
  15.1 7.9 %collective-permute-start.2 = (bf16[64,1024]{1,0:T(8,128)(2,1)}, bf16[64,1024]{1,0:T(8,128)(2,1)S(1)}, u32[]{:S(2)}, u32[]{:S(2)}) collective-permute-start(bf16[64,1024]{1,0:T(8,128)(2,1)} %get-tuple-element.46), channel_id=1, source_target_pairs={{8,0},{16,8},{24,16},{9,1},{17,9},{25,17},{10,2},{18,10},{26,18},{... | collective-permute-start | bytes 393224 | tf_op jit(solution)/shard_map/ppermute | solution.py:604
  16.4 6.6 %collective-permute-start.3 = (bf16[64,1024]{1,0:T(8,128)(2,1)}, bf16[64,1024]{1,0:T(8,128)(2,1)S(1)}, u32[]{:S(2)}, u32[]{:S(2)}) collective-permute-start(bf16[64,1024]{1,0:T(8,128)(2,1)} %get-tuple-element.47), channel_id=1, source_target_pairs={{0,2},{2,4},{4,6},{1,3},{3,5},{5,7},{8,10},{10,12},{12,14},{9,11},... | collective-permute-start | bytes 393224 | tf_op jit(solution)/shard_map/ppermute | solution.py:603
  19.7 6.5 %collective-permute-start.4 = (bf16[64,1024]{1,0:T(8,128)(2,1)}, bf16[64,1024]{1,0:T(8,128)(2,1)S(1)}, u32[]{:S(2)}, u32[]{:S(2)}) collective-permute-start(bf16[64,1024]{1,0:T(8,128)(2,1)} %get-tuple-element.48), channel_id=1, source_target_pairs={{2,0},{4,2},{6,4},{3,1},{5,3},{7,5},{10,8},{12,10},{14,12},{11,9},... | collective-permute-start | bytes 393224 | tf_op jit(solution)/shard_map/ppermute | solution.py:604
  21.6 4.6 %copy-start.8 = (bf16[64,1024]{1,0:T(8,128)(2,1)}, bf16[64,1024]{1,0:T(8,128)(2,1)S(1)}, u32[]{:S(2)}) copy-start(bf16[64,1024]{1,0:T(8,128)(2,1)S(1)} %collective-permute-done.1.refs_0_) | copy-start | bytes 393220
  21.6 4.6 %collective-permute-start.5 = (bf16[64,1024]{1,0:T(8,128)(2,1)}, bf16[64,1024]{1,0:T(8,128)(2,1)S(1)}, u32[]{:S(2)}, u32[]{:S(2)}) collective-permute-start(bf16[64,1024]{1,0:T(8,128)(2,1)} %get-tuple-element.49), channel_id=1, source_target_pairs={{0,1},{1,0},{2,3},{3,2},{4,5},{5,4},{6,7},{7,6},{8,9},{9,8},{10,11... | collective-permute-start | bytes 393224 | tf_op jit(solution)/shard_map/ppermute | solution.py:600
  22.9 3.3 %copy-start.9 = (bf16[64,1024]{1,0:T(8,128)(2,1)}, bf16[64,1024]{1,0:T(8,128)(2,1)S(1)}, u32[]{:S(2)}) copy-start(bf16[64,1024]{1,0:T(8,128)(2,1)S(1)} %collective-permute-done.2.refs_1_) | copy-start | bytes 393220
  22.9 3.3 %copy-start.10 = (bf16[64,1024]{1,0:T(8,128)(2,1)}, bf16[64,1024]{1,0:T(8,128)(2,1)S(1)}, u32[]{:S(2)}) copy-start(bf16[64,1024]{1,0:T(8,128)(2,1)S(1)} %collective-permute-done.3.refs_2_) | copy-start | bytes 393220
  26.2 0.7 copy-start.11
  26.2 0.7 copy-start.12
  32.9 4.7 %copy-start.4 = (bf16[512,1024]{1,0:T(8,128)(2,1)S(1)}, bf16[512,1024]{1,0:T(8,128)(2,1)}, u32[]{:S(2)}) copy-start(bf16[512,1024]{1,0:T(8,128)(2,1)} %get-tuple-element.54.refs_2_) | copy-start | bytes 3145732
  32.9 4.7 %copy-start.7 = (s32[38]{0:T(128)S(1)}, s32[38]{0:T(128)}, u32[]{:S(2)}) copy-start(s32[38]{0:T(128)} %stack.176.table_ref) | copy-start | bytes 460
  32.9 4.7 %collective-permute-start.6 = (bf16[512,1024]{1,0:T(8,128)(2,1)}, bf16[512,1024]{1,0:T(8,128)(2,1)S(1)}, u32[]{:S(2)}, u32[]{:S(2)}) collective-permute-start(bf16[512,1024]{1,0:T(8,128)(2,1)} %get-tuple-element.54.refs_2_), channel_id=1, source_target_pairs={{0,2},{2,0},{1,3},{3,1},{4,6},{6,4},{5,7},{7,5},{8,10},{10,8},{9,1... | collective-permute-start | bytes 3145736 | tf_op jit(solution)/shard_map/ppermute | solution.py:623
  32.9 27.1 %all-to-all-start = ((bf16[4,1152,128]{2,1,0:T(8,128)(2,1)}), bf16[4,1152,128]{2,1,0:T(8,128)(2,1)}, u32[]{:S(2)}, u32[]{:S(2)}) async-start(bf16[4,1152,128]{2,1,0:T(8,128)(2,1)} %bitcast.67), calls=%async_computation | async-start | bytes 2359296 | tf_op jit(solution)/shard_map/all_to_all | solution.py:630
  61.5 3.5 %collective-permute-start.9 = (f32[576,128]{1,0:T(8,128)S(1)}, f32[576,128]{1,0:T(8,128)S(1)}, u32[]{:S(2)}, u32[]{:S(2)}) collective-permute-start(f32[576,128]{1,0:T(8,128)S(1)} %dynamic-slice_bitcast_fusion), channel_id=1, source_target_pairs={{0,2},{2,0},{1,3},{3,1},{4,6},{6,4},{5,7},{7,5},{8,10},{10,8},{9,1... | collective-permute-start | bytes 884744 | tf_op jit(solution)/shard_map/ppermute | solution.py:651
  62.0 47.9 %collective-permute-start.7 = (bf16[1024,1024]{1,0:T(8,128)(2,1)}, bf16[1024,1024]{1,0:T(8,128)(2,1)S(1)}, u32[]{:S(2)}, u32[]{:S(2)}) collective-permute-start(bf16[1024,1024]{1,0:T(8,128)(2,1)} %shard_map.79), channel_id=1, source_target_pairs={{0,1},{1,0},{2,3},{3,2},{4,5},{5,4},{6,7},{7,6},{8,9},{9,8},{10,11... | collective-permute-start | bytes 6291464 | tf_op jit(solution)/shard_map/ppermute | solution.py:558
  63.7 51.8 %collective-permute-start.8 = (bf16[1024,1024]{1,0:T(8,128)(2,1)}, bf16[1024,1024]{1,0:T(8,128)(2,1)}, u32[]{:S(2)}, u32[]{:S(2)}) collective-permute-start(bf16[1024,1024]{1,0:T(8,128)(2,1)} %shard_map.80), channel_id=1, source_target_pairs={{0,4},{4,0},{1,5},{5,1},{2,6},{6,2},{3,7},{7,3},{8,12},{12,8},{9,1... | collective-permute-start | bytes 6291464 | tf_op jit(solution)/shard_map/ppermute | solution.py:558
  90.5 33.1 %all-to-all-start.3 = ((f32[4,576,128]{2,1,0:T(8,128)}), f32[4,576,128]{2,1,0:T(8,128)}, u32[]{:S(2)}, u32[]{:S(2)}) async-start(f32[4,576,128]{2,1,0:T(8,128)} %broadcast_in_dim.18), calls=%async_computation.3 | async-start | bytes 2359296 | tf_op jit(solution)/shard_map/all_to_all | solution.py:630
  115.5 2.2 copy-start.2
  117.7 2.6 %copy-start = (f32[1024,1024]{1,0:T(8,128)S(1)}, f32[1024,1024]{1,0:T(8,128)}, u32[]{:S(2)}) copy-start(f32[1024,1024]{1,0:T(8,128)} %shard_map.82.refs_0_.refs_3_) | copy-start | bytes 12582916
  118.6 1.0 copy-start.5
  122.2 1.0 copy-start.6
  123.5 6.1 %collective-permute-start.12 = (f32[4,576,128]{2,1,0:T(8,128)}, f32[4,576,128]{2,1,0:T(8,128)}, u32[]{:S(2)}, u32[]{:S(2)}) collective-permute-start(f32[4,576,128]{2,1,0:T(8,128)} %all-to-all-done.3), channel_id=1, source_target_pairs={{0,2},{2,0},{1,3},{3,1},{4,6},{6,4},{5,7},{7,5},{8,10},{10,8},{9,1... | collective-permute-start | bytes 3538952 | tf_op jit(solution)/shard_map/ppermute | solution.py:664
  126.8 27.2 %collective-permute-start.11 = (bf16[512,1024]{1,0:T(8,128)(2,1)}, bf16[512,1024]{1,0:T(8,128)(2,1)S(1)}, u32[]{:S(2)}, u32[]{:S(2)}) collective-permute-start(bf16[512,1024]{1,0:T(8,128)(2,1)} %copy-done.6), channel_id=1, source_target_pairs={{0,1},{1,0},{2,3},{3,2},{4,5},{5,4},{6,7},{7,6},{8,9},{9,8},{10,11... | collective-permute-start | bytes 3145736 | tf_op jit(solution)/shard_map/ppermute | solution.py:558
  126.8 27.2 %collective-permute-start.10 = (bf16[512,1024]{1,0:T(8,128)(2,1)}, bf16[512,1024]{1,0:T(8,128)(2,1)}, u32[]{:S(2)}, u32[]{:S(2)}) collective-permute-start(bf16[512,1024]{1,0:T(8,128)(2,1)} %copy-done.5), channel_id=1, source_target_pairs={{0,4},{4,0},{1,5},{5,1},{2,6},{6,2},{3,7},{7,3},{8,12},{12,8},{9,1... | collective-permute-start | bytes 3145736 | tf_op jit(solution)/shard_map/ppermute | solution.py:558
  129.6 24.4 %copy-start.3 = (f32[1024,1024]{1,0:T(8,128)S(1)}, f32[1024,1024]{1,0:T(8,128)}, u32[]{:S(2)}) copy-start(f32[1024,1024]{1,0:T(8,128)} %shard_map.81.refs_0_) | copy-start | bytes 12582916
  131.6 22.4 %copy-start.1 = (f32[1024,1024]{1,0:T(8,128)S(1)}, f32[1024,1024]{1,0:T(8,128)}, u32[]{:S(2)}) copy-start(f32[1024,1024]{1,0:T(8,128)} %shard_map.82.refs_0_.refs_3_) | copy-start | bytes 12582916
  157.5 52.4 %collective-permute-start.17 = (f32[256,1024]{1,0:T(8,128)S(1)}, f32[256,1024]{1,0:T(8,128)S(1)}, u32[]{:S(2)}, u32[]{:S(2)}) collective-permute-start(f32[256,1024]{1,0:T(8,128)S(1)} %get-tuple-element.67), channel_id=1, source_target_pairs={{0,2},{2,0},{1,3},{3,1},{4,6},{6,4},{5,7},{7,5},{8,10},{10,8},{9,1... | collective-permute-start | bytes 3145736 | tf_op jit(solution)/shard_map/ppermute | solution.py:694
  157.9 37.9 %collective-permute-start.13 = (bf16[256,1024]{1,0:T(8,128)(2,1)S(1)}, bf16[256,1024]{1,0:T(8,128)(2,1)S(1)}, u32[]{:S(2)}, u32[]{:S(2)}) collective-permute-start(bf16[256,1024]{1,0:T(8,128)(2,1)S(1)} %get-tuple-element.63), channel_id=1, source_target_pairs={{2,16},{6,20},{8,2},{10,18},{12,6},{14,22},{16,8},{18,24},{20,12},... | collective-permute-start | bytes 1572872 | tf_op jit(solution)/shard_map/ppermute | solution.py:693
  163.2 32.6 %collective-permute-start.14 = (bf16[256,1024]{1,0:T(8,128)(2,1)S(1)}, bf16[256,1024]{1,0:T(8,128)(2,1)S(1)}, u32[]{:S(2)}, u32[]{:S(2)}) collective-permute-start(bf16[256,1024]{1,0:T(8,128)(2,1)S(1)} %get-tuple-element.64), channel_id=1, source_target_pairs={{2,18},{6,22},{10,24},{14,28},{16,10},{18,26},{20,14},{22,30},{24,... | collective-permute-start | bytes 1572872 | tf_op jit(solution)/shard_map/ppermute | solution.py:693
  166.5 29.3 %collective-permute-start.15 = (bf16[256,1024]{1,0:T(8,128)(2,1)S(1)}, bf16[256,1024]{1,0:T(8,128)(2,1)S(1)}, u32[]{:S(2)}, u32[]{:S(2)}) collective-permute-start(bf16[256,1024]{1,0:T(8,128)(2,1)S(1)} %get-tuple-element.65), channel_id=1, source_target_pairs={{0,8},{2,24},{4,12},{6,28},{10,26},{14,30},{16,0},{20,4},{24,2},{2... | collective-permute-start | bytes 1572872 | tf_op jit(solution)/shard_map/ppermute | solution.py:693
  168.4 41.4 %collective-permute-start.16 = (bf16[256,1024]{1,0:T(8,128)(2,1)S(1)}, bf16[256,1024]{1,0:T(8,128)(2,1)S(1)}, u32[]{:S(2)}, u32[]{:S(2)}) collective-permute-start(bf16[256,1024]{1,0:T(8,128)(2,1)S(1)} %get-tuple-element.66), channel_id=1, source_target_pairs={{0,10},{2,26},{4,14},{6,30},{8,0},{10,16},{12,4},{14,20},{16,2},{2... | collective-permute-start | bytes 1572872 | tf_op jit(solution)/shard_map/ppermute | solution.py:693
  212.4 9.2 %collective-permute-start.18 = (f32[2,256,256]{2,1,0:T(8,128)S(1)}, f32[2,256,256]{2,1,0:T(8,128)S(1)}, u32[]{:S(2)}, u32[]{:S(2)}) collective-permute-start(f32[2,256,256]{2,1,0:T(8,128)S(1)} %get-tuple-element.79), channel_id=1, source_target_pairs={{0,2},{2,4},{4,6},{6,0},{1,3},{3,5},{5,7},{7,1},{8,10},{10,12},{12... | collective-permute-start | bytes 1572872 | tf_op jit(solution)/shard_map/ppermute | solution.py:714
  212.5 24.2 %collective-permute-start.19 = (f32[2,256,256]{2,1,0:T(8,128)S(1)}, f32[2,256,256]{2,1,0:T(8,128)S(1)}, u32[]{:S(2)}, u32[]{:S(2)}) collective-permute-start(f32[2,256,256]{2,1,0:T(8,128)S(1)} %get-tuple-element.80), channel_id=1, source_target_pairs={{0,4},{2,6},{4,0},{6,2},{1,5},{3,7},{5,1},{7,3},{8,12},{10,14},{12... | collective-permute-start | bytes 1572872 | tf_op jit(solution)/shard_map/ppermute | solution.py:714
  214.1 23.3 %collective-permute-start.20 = (f32[2,256,256]{2,1,0:T(8,128)S(1)}, f32[2,256,256]{2,1,0:T(8,128)S(1)}, u32[]{:S(2)}, u32[]{:S(2)}) collective-permute-start(f32[2,256,256]{2,1,0:T(8,128)S(1)} %get-tuple-element.81), channel_id=1, source_target_pairs={{0,6},{2,0},{4,2},{6,4},{1,7},{3,1},{5,3},{7,5},{8,14},{10,8},{12,... | collective-permute-start | bytes 1572872 | tf_op jit(solution)/shard_map/ppermute | solution.py:714

commit v11 on v10

--- a/solution.py
+++ b/solution.py
@@ -644,11 +644,13 @@
     got_b = [move(a, "gy", d) for d, a in enumerate(sent_b, 1)]
     images, _ = lax.optimization_barrier((images, (sent_a, sent_b)))
     own_a, own_b = (chip_products(images, lists[0], f32) for lists in (lists_a, lists_b))
-    lead_terms, _ = lax.optimization_barrier((lead_terms, (own_a, own_b)))
+    lead_terms, _ = lax.optimization_barrier((lead_terms, (sent_a, sent_b)))
     own = jnp.sum(lead_terms.astype(f32), axis=0).reshape(2, -1, LEAF)
     kept = lax.dynamic_index_in_dim(own, core, 0, keepdims=False)
     sent = lax.dynamic_index_in_dim(own, 1 - core, 0, keepdims=False)
-    own = (kept + lax.ppermute(sent, "core", swap_pairs())).reshape(devices_x, -1, LEAF)
+    own = kept + lax.ppermute(sent, "core", swap_pairs())
+    own, _ = lax.optimization_barrier((own, (own_a, own_b)))
+    own = own.reshape(devices_x, -1, LEAF)
     own = jnp.sum(exchanged(own, "gx"), axis=0)
     own = exchanged(for_all(own, devices_x), "gx").reshape(-1, LEAF)
     own = for_all(own, chips)

time: 240 us -> 226 us (0.942)
  waiting for transfers between devices: 62.1 us -> 50 us
  starting transfers between devices: 46.7 us -> 43.6 us
    ppermute x4, waiting for transfers between devices: 20.6 us -> 0.01 us  [move(): return lax.ppermute(array, axis, [(i, (i + d) % size) for i in range(size)])]
    all_to_all x2, waiting for transfers between devices: 0.38 us -> 8.81 us  [exchanged(): return lax.all_to_all(rows, axes, split_axis=0, concat_axis=0, tiled=True)]
    unnamed x26 -> x22, local copies, waits for them, and re-layouts: 5.54 us -> 3.21 us
  transfers between devices with their start and end apart: 23 -> 23, of which waited for: 9 -> 8; matrix products, arithmetic and copies ran while one was open for 1% -> 2% of each run, Pallas kernels for 32% -> 35%
where the time goes in v11:
time: 226 us; the launch traced here: 225 us
  Pallas kernels  93.9 us (42%)
  waiting for transfers between devices  50 us (22%)
  starting transfers between devices  43.6 us (19%)
  blocking collectives  25.1 us (11%)
  local copies, waits for them, and re-layouts  7.01 us (3%)
  other arithmetic  3.83 us (2%)
    pallas_call x2, Pallas kernels, panel_call(): pl.pallas_call(kernel, out_shape=[jax.ShapeDtypeStruct((nb, nb), jnp.floa...  46.1 us
    all_to_all x2, blocking collectives, exchanged(): return lax.all_to_all(rows, axes, split_axis=0, concat_axis=0, tiled=True)  25.1 us
    ppermute x3, waiting for transfers between devices, local(): pairs[d] = lax.ppermute(pairs[d], ('gy', 'core'), route)  22.6 us
    pallas_call x4, Pallas kernels, products(): pl.pallas_call(products_kernel, grid_spec=pltpu.PrefetchScalarGridSpec(nu...  22.3 us
    ppermute x4, waiting for transfers between devices, local(): x_got.append(lax.ppermute(x_sent[step], ('gx', 'gy', 'core'), pairs))  14 us
    ppermute x4, starting transfers between devices, local(): x_got.append(lax.ppermute(x_sent[step], ('gx', 'gy', 'core'), pairs))  12 us
    all_to_all x2, starting transfers between devices, exchanged(): return lax.all_to_all(rows, axes, split_axis=0, concat_axis=0, tiled=True)  9.11 us
    all_to_all x2, waiting for transfers between devices, exchanged(): return lax.all_to_all(rows, axes, split_axis=0, concat_axis=0, tiled=True)  8.81 us
  transfers between devices with their start and end apart: 23, of which 8 were waited for; matrix products, arithmetic and copies ran while one was open for 2% of the time, Pallas kernels for 35%

profile of v11, /device:TPU:1, one launch (start us, length us, event | category | flops | bytes accessed | tf_op | source)
XLA Modules:
  0.0 224.8 jit_solution(18384704975581494249)
XLA Ops:
  0.8 0.8 stack.177
  2.0 0.9 copy.14.info_ref
  2.8 0.7 stack.176.table_ref
  3.5 6.8 %shard_map.77 = (bf16[64,1024]{1,0:T(8,128)(2,1)}, bf16[64,1024]{1,0:T(8,128)(2,1)}, bf16[64,1024]{1,0:T(8,128)(2,1)}, bf16[64,1024]{1,0:T(8,128)(2,1)}, bf16[64...) custom-call(s32[38]{0:T(128)} %stack.176.table_ref, f32[16]{0:T(128)} %cond_ref.1, ...), custom_call_target="tpu_custom_call" | custom-call | tf_op jit(solution)/shard_map/pallas_call | solution.py:576
  10.4 4.6 %collective-permute-start.1 = (bf16[64,1024]{1,0:T(8,128)(2,1)}, bf16[64,1024]{1,0:T(8,128)(2,1)S(1)}, u32[]{:S(2)}, u32[]{:S(2)}) collective-permute-start(bf16[64,1024]{1,0:T(8,128)(2,1)} %get-tuple-element.46), channel_id=1, source_target_pairs={{0,8},{8,16},{16,24},{1,9},{9,17},{17,25},{2,10},{10,18},{18,26},{... | collective-permute-start | bytes 393224 | tf_op jit(solution)/shard_map/ppermute | solution.py:603
  15.1 1.3 collective-permute-start.2
  16.4 3.3 %collective-permute-start.3 = (bf16[64,1024]{1,0:T(8,128)(2,1)}, bf16[64,1024]{1,0:T(8,128)(2,1)S(1)}, u32[]{:S(2)}, u32[]{:S(2)}) collective-permute-start(bf16[64,1024]{1,0:T(8,128)(2,1)} %get-tuple-element.48), channel_id=1, source_target_pairs={{0,2},{2,4},{4,6},{1,3},{3,5},{5,7},{8,10},{10,12},{12,14},{9,11},... | collective-permute-start | bytes 393224 | tf_op jit(solution)/shard_map/ppermute | solution.py:603
  19.7 1.9 collective-permute-start.4
  21.7 1.3 collective-permute-start.5
  23.0 3.3 %collective-permute-done.4.refs_3_ = bf16[64,1024]{1,0:T(8,128)(2,1)S(1)} collective-permute-done((bf16[64,1024]{1,0:T(8,128)(2,1)}, bf16[64,1024]{1,0:T(8,128)(2,1)S(1)}, u32[]{:S(2)}, u32[]{:S(2)}) %collective-permute-start.4) | collective-permute-done | bytes 131104 | tf_op jit(solution)/shard_map/ppermute | solution.py:604
  26.9 5.9 %shard_map.78 = (bf16[512,1024]{1,0:T(8,128)(2,1)}, bf16[4608,128]{1,0:T(8,128)(2,1)}) custom-call(s32[38]{0:T(128)} %stack.176.table_ref, bf16[512,8192]{1,0:T(8,128)(2,1)} %bitcast.57, f32[512,128]{1,0:T(8,128)} %get-tuple-element.44.conduct_ref, f32[512,128]{1,0:T(8,128)} %get-tuple-element.45.grounds_ref, bf16[64,1024]{1,0:T(8,128)(2,1)} %copy-done.6, ...), custom_call_target="tpu_custom_call" | custom-call | tf_op jit(solution)/shard_map/pallas_call | solution.py:610
  32.9 4.7 %all-to-all-start = ((bf16[4,1152,128]{2,1,0:T(8,128)(2,1)}), bf16[4,1152,128]{2,1,0:T(8,128)(2,1)}, u32[]{:S(2)}, u32[]{:S(2)}) async-start(bf16[4,1152,128]{2,1,0:T(8,128)(2,1)} %bitcast.67), calls=%async_computation | async-start | bytes 2359296 | tf_op jit(solution)/shard_map/all_to_all | solution.py:630
  37.6 5.4 %shard_map.79 = bf16[1024,1024]{1,0:T(8,128)(2,1)} custom-call(s32[38]{0:T(128)S(1)} %copy-done.5, bf16[512,8192]{1,0:T(8,128)(2,1)} %bitcast.58, bf16[512,4096]{1,0:T(8,128)(2,1)} %collective-permute-done.refs_1_, bf16[512,1024]{1,0:T(8,128)(2,1)S(1)} %copy-done.4, bf16[512,1024]{1,0:T(8,128)(2,1)S(1)} %collective-permute-done.6.refs_3_), custom_call_target="tpu_custom_call" | custom-call | flops 2147483648 | bytes 8388608 | tf_op jit(solution)/shard_map/pallas_call | solution.py:393
  42.9 1.5 collective-permute-start.7
  44.4 5.4 %shard_map.80 = bf16[1024,1024]{1,0:T(8,128)(2,1)} custom-call(s32[38]{0:T(128)S(1)} %copy-done.5, bf16[512,8192]{1,0:T(8,128)(2,1)} %bitcast.59, bf16[512,4096]{1,0:T(8,128)(2,1)} %collective-permute-done.refs_1_, bf16[512,1024]{1,0:T(8,128)(2,1)S(1)} %copy-done.4, bf16[512,1024]{1,0:T(8,128)(2,1)S(1)} %collective-permute-done.6.refs_3_), custom_call_target="tpu_custom_call" | custom-call | flops 2147483648 | bytes 8388608 | tf_op jit(solution)/shard_map/pallas_call | solution.py:393
  49.8 1.8 collective-permute-start.8
  51.6 1.8 all-to-all-done
  53.5 1.5 convert_reduce_fusion
  55.0 1.1 collective-permute-start.9
  56.1 5.8 %shard_map.82.refs_0_.refs_3_ = f32[1024,1024]{1,0:T(8,128)} custom-call(s32[38]{0:T(128)S(1)} %copy-done.5, bf16[512,8192]{1,0:T(8,128)(2,1)} %bitcast.60, bf16[512,4096]{1,0:T(8,128)(2,1)} %collective-permute-done.refs_1_, bf16[512,1024]{1,0:T(8,128)(2,1)S(1)} %copy-done.4, bf16[512,1024]{1,0:T(8,128)(2,1)S(1)} %collective-permute-done.6.refs_3_), custom_call_target="tpu_custom_call" | custom-call | flops 2147483648 | bytes 8388608 | tf_op jit(solution)/shard_map/pallas_call | solution.py:393
  61.9 5.8 %shard_map.81.refs_0_ = f32[1024,1024]{1,0:T(8,128)} custom-call(s32[38]{0:T(128)S(1)} %copy-done.5, bf16[512,8192]{1,0:T(8,128)(2,1)} %bitcast.61, bf16[512,4096]{1,0:T(8,128)(2,1)} %collective-permute-done.refs_1_, bf16[512,1024]{1,0:T(8,128)(2,1)S(1)} %copy-done.4, bf16[512,1024]{1,0:T(8,128)(2,1)S(1)} %collective-permute-done.6.refs_3_), custom_call_target="tpu_custom_call" | custom-call | flops 2147483648 | bytes 8388608 | tf_op jit(solution)/shard_map/pallas_call | solution.py:393
  67.7 14.7 %all_to_all.20 = f32[4,144,128]{2,1,0:T(8,128)S(1)} all-to-all(f32[4,144,128]{2,1,0:T(8,128)S(1)} %bitcast.66), channel_id=1, replica_groups=mesh['gx'=4,'gy'=2,'core'=2,'gz'=2] {'gx'}, dimensions={0} | all-to-all | bytes 589824 | tf_op jit(solution)/shard_map/all_to_all | solution.py:630
  82.5 10.4 %all_to_all.21 = f32[4,144,128]{2,1,0:T(8,128)S(1)} all-to-all(f32[4,144,128]{2,1,0:T(8,128)S(1)} %broadcast_in_dim.17), channel_id=1, replica_groups=mesh['gx'=4,'gy'=2,'core'=2,'gz'=2] {'gx'}, dimensions={0} | all-to-all | bytes 589824 | tf_op jit(solution)/shard_map/all_to_all | solution.py:630
  92.9 1.1 broadcast_in_dim.18
  94.0 4.4 %all-to-all-start.3 = ((f32[4,576,128]{2,1,0:T(8,128)}), f32[4,576,128]{2,1,0:T(8,128)}, u32[]{:S(2)}, u32[]{:S(2)}) async-start(f32[4,576,128]{2,1,0:T(8,128)} %broadcast_in_dim.18), calls=%async_computation.3 | async-start | bytes 2359296 | tf_op jit(solution)/shard_map/all_to_all | solution.py:630
  98.5 2.2 copy-done.2
  100.7 2.2 shard_map.83
  103.2 2.7 %shard_map.84 = bf16[512,1024]{1,0:T(8,128)(2,1)} custom-call(s32[38]{0:T(128)S(1)} %copy-done.5, f32[1024,1024]{1,0:T(8,128)S(1)} %copy-done, bf16[1024,1024]{1,0:T(8,128)(2,1)} %collective-permute-done.8.refs_1_.refs_4_), custom_call_target="tpu_custom_call" | custom-call | flops 524288 | bytes 4194304 | tf_op jit(solution)/shard_map/pallas_call | solution.py:425
  105.8 7.0 %all-to-all-done.3 = f32[4,576,128]{2,1,0:T(8,128)} async-done(((f32[4,576,128]{2,1,0:T(8,128)}), f32[4,576,128]{2,1,0:T(8,128)}, u32[]{:S(2)}, u32[]{:S(2)}) %all-to-all-start.3) | async-done | bytes 1179680 | tf_op jit(solution)/shard_map/all_to_all | solution.py:630
  112.8 1.5 collective-permute-start.12
  114.3 1.1 collective-permute-start.11
  115.8 1.3 collective-permute-done.12
  117.1 2.0 select_bitcast_fusion.1
  119.3 22.2 %shard_map.85.w0_ref.refs_4_ = f32[512,512]{1,0:T(8,128)S(1)} custom-call(f32[1280,128]{1,0:T(8,128)S(1)} %slice.8.packed_ref), custom_call_target="tpu_custom_call" | custom-call | flops 512 | bytes 512 | tf_op jit(solution)/shard_map/pallas_call | solution.py:179
  141.5 3.5 %shard_map.86 = (bf16[256,1024]{1,0:T(8,128)(2,1)S(1)}, bf16[256,1024]{1,0:T(8,128)(2,1)S(1)}, bf16[256,1024]{1,0:T(8,128)(2,1)S(1)}, bf16[256,1024]{1,0:T(8,128...) custom-call(s32[38]{0:T(128)S(1)} %copy-done.5, f32[1024,1024]{1,0:T(8,128)S(1)} %copy-done.3, ...), custom_call_target="tpu_custom_call" | custom-call | bytes 14680064 | tf_op jit(solution)/shard_map/pallas_call | solution.py:467
  145.5 3.9 %collective-permute-start.13 = (bf16[256,1024]{1,0:T(8,128)(2,1)S(1)}, bf16[256,1024]{1,0:T(8,128)(2,1)S(1)}, u32[]{:S(2)}, u32[]{:S(2)}) collective-permute-start(bf16[256,1024]{1,0:T(8,128)(2,1)S(1)} %get-tuple-element.65), channel_id=1, source_target_pairs={{2,16},{6,20},{8,2},{10,18},{12,6},{14,22},{16,8},{18,24},{20,12},... | collective-permute-start | bytes 1572872 | tf_op jit(solution)/shard_map/ppermute | solution.py:695
  149.4 2.9 %collective-permute-start.14 = (bf16[256,1024]{1,0:T(8,128)(2,1)S(1)}, bf16[256,1024]{1,0:T(8,128)(2,1)S(1)}, u32[]{:S(2)}, u32[]{:S(2)}) collective-permute-start(bf16[256,1024]{1,0:T(8,128)(2,1)S(1)} %get-tuple-element.66), channel_id=1, source_target_pairs={{2,18},{6,22},{10,24},{14,28},{16,10},{18,26},{20,14},{22,30},{24,... | collective-permute-start | bytes 1572872 | tf_op jit(solution)/shard_map/ppermute | solution.py:695
  152.3 1.9 collective-permute-start.15
  154.2 3.3 %collective-permute-start.16 = (bf16[256,1024]{1,0:T(8,128)(2,1)S(1)}, bf16[256,1024]{1,0:T(8,128)(2,1)S(1)}, u32[]{:S(2)}, u32[]{:S(2)}) collective-permute-start(bf16[256,1024]{1,0:T(8,128)(2,1)S(1)} %get-tuple-element.68), channel_id=1, source_target_pairs={{0,10},{2,26},{4,14},{6,30},{8,0},{10,16},{12,4},{14,20},{16,2},{2... | collective-permute-start | bytes 1572872 | tf_op jit(solution)/shard_map/ppermute | solution.py:695
  157.6 23.9 %shard_map.87 = (f32[512,512]{1,0:T(8,128)S(1)}, f32[512,512]{1,0:T(8,128)S(1)}) custom-call(f32[3328,128]{1,0:T(8,128)S(1)} %slice.9.packed_ref, f32[512,512]{1,0:T(8,128)S(1)} %shard_map.85.w0_ref.refs_4_), custom_call_target="tpu_custom_call" | custom-call | flops 512 | bytes 512 | tf_op jit(solution)/shard_map/pallas_call | solution.py:179
  181.6 14.0 %collective-permute-done.16.refs_3_ = bf16[256,1024]{1,0:T(8,128)(2,1)S(1)} collective-permute-done((bf16[256,1024]{1,0:T(8,128)(2,1)S(1)}, bf16[256,1024]{1,0:T(8,128)(2,1)S(1)}, u32[]{:S(2)}, u32[]{:S(2)}) %collective-permute-start.16) | collective-permute-done | bytes 524320 | tf_op jit(solution)/shard_map/ppermute | solution.py:695
  195.6 2.5 %shard_map.88 = (f32[2,256,256]{2,1,0:T(8,128)S(1)}, f32[2,256,256]{2,1,0:T(8,128)S(1)}, f32[2,256,256]{2,1,0:T(8,128)S(1)}, f32[2,256,256]{2,1,0:T(8,128)S(1)}) custom-call(s32[38]{0:T(128)S(1)} %copy-done.5, f32[256,1024]{1,0:T(8,128)S(1)} %get-tuple-element.64.own_ref, f32[256,1024]{1,0:T(8,128)S(1)} %collective-permute-done.17.swapped_ref, ...), custom_call_target="tpu_custom_call" | custom-call | tf_op jit(solution)/shard_map/pallas_call | solution.py:702
  198.2 1.3 collective-permute-start.19
  199.4 0.7 collective-permute-start.20
  200.1 7.5 %collective-permute-done.18.refs_1_ = f32[2,256,256]{2,1,0:T(8,128)S(1)} collective-permute-done((f32[2,256,256]{2,1,0:T(8,128)S(1)}, f32[2,256,256]{2,1,0:T(8,128)S(1)}, u32[]{:S(2)}, u32[]{:S(2)}) %collective-permute-start.18) | collective-permute-done | bytes 524320 | tf_op jit(solution)/shard_map/ppermute | solution.py:716
  207.7 13.8 %collective-permute-done.19.refs_2_ = f32[2,256,256]{2,1,0:T(8,128)S(1)} collective-permute-done((f32[2,256,256]{2,1,0:T(8,128)S(1)}, f32[2,256,256]{2,1,0:T(8,128)S(1)}, u32[]{:S(2)}, u32[]{:S(2)}) %collective-permute-start.19) | collective-permute-done | bytes 524320 | tf_op jit(solution)/shard_map/ppermute | solution.py:716
  221.5 1.3 collective-permute-done.20.refs_3_
  222.8 2.0 shard_map.89
  (54 shorter events, 2.7 us)
Async XLA Ops:
  10.3 27.2 %collective-permute-start = (bf16[512,4096]{1,0:T(8,128)(2,1)}, bf16[512,4096]{1,0:T(8,128)(2,1)}, u32[]{:S(2)}, u32[]{:S(2)}) collective-permute-start(bf16[512,4096]{1,0:T(8,128)(2,1)} %get-tuple-element.43), channel_id=1, source_target_pairs={{0,2},{2,0},{1,3},{3,1},{4,6},{6,4},{5,7},{7,5},{8,10},{10,8},{9,1... | collective-permute-start | bytes 12582920 | tf_op jit(solution)/shard_map/ppermute | solution.py:624
  10.4 11.2 %collective-permute-start.1 = (bf16[64,1024]{1,0:T(8,128)(2,1)}, bf16[64,1024]{1,0:T(8,128)(2,1)S(1)}, u32[]{:S(2)}, u32[]{:S(2)}) collective-permute-start(bf16[64,1024]{1,0:T(8,128)(2,1)} %get-tuple-element.46), channel_id=1, source_target_pairs={{0,8},{8,16},{16,24},{1,9},{9,17},{17,25},{2,10},{10,18},{18,26},{... | collective-permute-start | bytes 393224 | tf_op jit(solution)/shard_map/ppermute | solution.py:603
  15.1 7.9 %collective-permute-start.2 = (bf16[64,1024]{1,0:T(8,128)(2,1)}, bf16[64,1024]{1,0:T(8,128)(2,1)S(1)}, u32[]{:S(2)}, u32[]{:S(2)}) collective-permute-start(bf16[64,1024]{1,0:T(8,128)(2,1)} %get-tuple-element.47), channel_id=1, source_target_pairs={{8,0},{16,8},{24,16},{9,1},{17,9},{25,17},{10,2},{18,10},{26,18},{... | collective-permute-start | bytes 393224 | tf_op jit(solution)/shard_map/ppermute | solution.py:604
  16.4 6.6 %collective-permute-start.3 = (bf16[64,1024]{1,0:T(8,128)(2,1)}, bf16[64,1024]{1,0:T(8,128)(2,1)S(1)}, u32[]{:S(2)}, u32[]{:S(2)}) collective-permute-start(bf16[64,1024]{1,0:T(8,128)(2,1)} %get-tuple-element.48), channel_id=1, source_target_pairs={{0,2},{2,4},{4,6},{1,3},{3,5},{5,7},{8,10},{10,12},{12,14},{9,11},... | collective-permute-start | bytes 393224 | tf_op jit(solution)/shard_map/ppermute | solution.py:603
  19.7 6.5 %collective-permute-start.4 = (bf16[64,1024]{1,0:T(8,128)(2,1)}, bf16[64,1024]{1,0:T(8,128)(2,1)S(1)}, u32[]{:S(2)}, u32[]{:S(2)}) collective-permute-start(bf16[64,1024]{1,0:T(8,128)(2,1)} %get-tuple-element.49), channel_id=1, source_target_pairs={{2,0},{4,2},{6,4},{3,1},{5,3},{7,5},{10,8},{12,10},{14,12},{11,9},... | collective-permute-start | bytes 393224 | tf_op jit(solution)/shard_map/ppermute | solution.py:604
  21.7 4.6 %copy-start.6 = (bf16[64,1024]{1,0:T(8,128)(2,1)}, bf16[64,1024]{1,0:T(8,128)(2,1)S(1)}, u32[]{:S(2)}) copy-start(bf16[64,1024]{1,0:T(8,128)(2,1)S(1)} %collective-permute-done.1.refs_0_) | copy-start | bytes 393220
  21.7 4.6 %collective-permute-start.5 = (bf16[64,1024]{1,0:T(8,128)(2,1)}, bf16[64,1024]{1,0:T(8,128)(2,1)S(1)}, u32[]{:S(2)}, u32[]{:S(2)}) collective-permute-start(bf16[64,1024]{1,0:T(8,128)(2,1)} %get-tuple-element.50), channel_id=1, source_target_pairs={{0,1},{1,0},{2,3},{3,2},{4,5},{5,4},{6,7},{7,6},{8,9},{9,8},{10,11... | collective-permute-start | bytes 393224 | tf_op jit(solution)/shard_map/ppermute | solution.py:600
  23.0 3.3 %copy-start.7 = (bf16[64,1024]{1,0:T(8,128)(2,1)}, bf16[64,1024]{1,0:T(8,128)(2,1)S(1)}, u32[]{:S(2)}) copy-start(bf16[64,1024]{1,0:T(8,128)(2,1)S(1)} %collective-permute-done.2.refs_1_) | copy-start | bytes 393220
  23.0 3.3 %copy-start.8 = (bf16[64,1024]{1,0:T(8,128)(2,1)}, bf16[64,1024]{1,0:T(8,128)(2,1)S(1)}, u32[]{:S(2)}) copy-start(bf16[64,1024]{1,0:T(8,128)(2,1)S(1)} %collective-permute-done.3.refs_2_) | copy-start | bytes 393220
  26.2 0.7 copy-start.9
  26.2 0.7 copy-start.10
  32.8 4.7 %copy-start.4 = (bf16[512,1024]{1,0:T(8,128)(2,1)S(1)}, bf16[512,1024]{1,0:T(8,128)(2,1)}, u32[]{:S(2)}) copy-start(bf16[512,1024]{1,0:T(8,128)(2,1)} %get-tuple-element.55.refs_2_) | copy-start | bytes 3145732
  32.8 4.7 %copy-start.5 = (s32[38]{0:T(128)S(1)}, s32[38]{0:T(128)}, u32[]{:S(2)}) copy-start(s32[38]{0:T(128)} %stack.176.table_ref) | copy-start | bytes 460
  32.8 4.7 %collective-permute-start.6 = (bf16[512,1024]{1,0:T(8,128)(2,1)}, bf16[512,1024]{1,0:T(8,128)(2,1)S(1)}, u32[]{:S(2)}, u32[]{:S(2)}) collective-permute-start(bf16[512,1024]{1,0:T(8,128)(2,1)} %get-tuple-element.55.refs_2_), channel_id=1, source_target_pairs={{0,2},{2,0},{1,3},{3,1},{4,6},{6,4},{5,7},{7,5},{8,10},{10,8},{9,1... | collective-permute-start | bytes 3145736 | tf_op jit(solution)/shard_map/ppermute | solution.py:623
  32.9 20.6 %all-to-all-start = ((bf16[4,1152,128]{2,1,0:T(8,128)(2,1)}), bf16[4,1152,128]{2,1,0:T(8,128)(2,1)}, u32[]{:S(2)}, u32[]{:S(2)}) async-start(bf16[4,1152,128]{2,1,0:T(8,128)(2,1)} %bitcast.67), calls=%async_computation | async-start | bytes 2359296 | tf_op jit(solution)/shard_map/all_to_all | solution.py:630
  42.9 55.5 %collective-permute-start.7 = (bf16[1024,1024]{1,0:T(8,128)(2,1)}, bf16[1024,1024]{1,0:T(8,128)(2,1)}, u32[]{:S(2)}, u32[]{:S(2)}) collective-permute-start(bf16[1024,1024]{1,0:T(8,128)(2,1)} %shard_map.79), channel_id=1, source_target_pairs={{0,1},{1,0},{2,3},{3,2},{4,5},{5,4},{6,7},{7,6},{8,9},{9,8},{10,11... | collective-permute-start | bytes 6291464 | tf_op jit(solution)/shard_map/ppermute | solution.py:558
  49.8 48.7 %collective-permute-start.8 = (bf16[1024,1024]{1,0:T(8,128)(2,1)}, bf16[1024,1024]{1,0:T(8,128)(2,1)}, u32[]{:S(2)}, u32[]{:S(2)}) collective-permute-start(bf16[1024,1024]{1,0:T(8,128)(2,1)} %shard_map.80), channel_id=1, source_target_pairs={{0,4},{4,0},{1,5},{5,1},{2,6},{6,2},{3,7},{7,3},{8,12},{12,8},{9,1... | collective-permute-start | bytes 6291464 | tf_op jit(solution)/shard_map/ppermute | solution.py:558
  55.0 12.7 %collective-permute-start.9 = (f32[576,128]{1,0:T(8,128)S(1)}, f32[576,128]{1,0:T(8,128)S(1)}, u32[]{:S(2)}, u32[]{:S(2)}) collective-permute-start(f32[576,128]{1,0:T(8,128)S(1)} %dynamic-slice_bitcast_fusion), channel_id=1, source_target_pairs={{0,2},{2,0},{1,3},{3,1},{4,6},{6,4},{5,7},{7,5},{8,10},{10,8},{9,1... | collective-permute-start | bytes 884744 | tf_op jit(solution)/shard_map/ppermute | solution.py:651
  94.0 18.8 %all-to-all-start.3 = ((f32[4,576,128]{2,1,0:T(8,128)}), f32[4,576,128]{2,1,0:T(8,128)}, u32[]{:S(2)}, u32[]{:S(2)}) async-start(f32[4,576,128]{2,1,0:T(8,128)} %broadcast_in_dim.18), calls=%async_computation.3 | async-start | bytes 2359296 | tf_op jit(solution)/shard_map/all_to_all | solution.py:630
  98.5 2.2 copy-start.2
  100.6 2.5 %copy-start = (f32[1024,1024]{1,0:T(8,128)S(1)}, f32[1024,1024]{1,0:T(8,128)}, u32[]{:S(2)}) copy-start(f32[1024,1024]{1,0:T(8,128)} %shard_map.82.refs_0_.refs_3_) | copy-start | bytes 12582916
  112.8 4.3 %collective-permute-start.12 = (f32[4,576,128]{2,1,0:T(8,128)}, f32[4,576,128]{2,1,0:T(8,128)}, u32[]{:S(2)}, u32[]{:S(2)}) collective-permute-start(f32[4,576,128]{2,1,0:T(8,128)} %all-to-all-done.3), channel_id=1, source_target_pairs={{0,2},{2,0},{1,3},{3,1},{4,6},{6,4},{5,7},{7,5},{8,10},{10,8},{9,1... | collective-permute-start | bytes 3538952 | tf_op jit(solution)/shard_map/ppermute | solution.py:666
  114.3 27.2 %collective-permute-start.11 = (bf16[512,1024]{1,0:T(8,128)(2,1)}, bf16[512,1024]{1,0:T(8,128)(2,1)S(1)}, u32[]{:S(2)}, u32[]{:S(2)}) collective-permute-start(bf16[512,1024]{1,0:T(8,128)(2,1)} %shard_map.84), channel_id=1, source_target_pairs={{0,1},{1,0},{2,3},{3,2},{4,5},{5,4},{6,7},{7,6},{8,9},{9,8},{10,11... | collective-permute-start | bytes 3145736 | tf_op jit(solution)/shard_map/ppermute | solution.py:558
  115.5 26.0 %collective-permute-start.10 = (bf16[512,1024]{1,0:T(8,128)(2,1)S(1)}, bf16[512,1024]{1,0:T(8,128)(2,1)S(1)}, u32[]{:S(2)}, u32[]{:S(2)}) collective-permute-start(bf16[512,1024]{1,0:T(8,128)(2,1)S(1)} %shard_map.83), channel_id=1, source_target_pairs={{0,4},{4,0},{1,5},{5,1},{2,6},{6,2},{3,7},{7,3},{8,12},{12,8},{9,1... | collective-permute-start | bytes 3145736 | tf_op jit(solution)/shard_map/ppermute | solution.py:558
  117.1 24.4 %copy-start.3 = (f32[1024,1024]{1,0:T(8,128)S(1)}, f32[1024,1024]{1,0:T(8,128)}, u32[]{:S(2)}) copy-start(f32[1024,1024]{1,0:T(8,128)} %shard_map.81.refs_0_) | copy-start | bytes 12582916
  119.1 22.4 %copy-start.1 = (f32[1024,1024]{1,0:T(8,128)S(1)}, f32[1024,1024]{1,0:T(8,128)}, u32[]{:S(2)}) copy-start(f32[1024,1024]{1,0:T(8,128)} %shard_map.82.refs_0_.refs_3_) | copy-start | bytes 12582916
  145.0 50.6 %collective-permute-start.17 = (f32[256,1024]{1,0:T(8,128)S(1)}, f32[256,1024]{1,0:T(8,128)S(1)}, u32[]{:S(2)}, u32[]{:S(2)}) collective-permute-start(f32[256,1024]{1,0:T(8,128)S(1)} %get-tuple-element.69), channel_id=1, source_target_pairs={{0,2},{2,0},{1,3},{3,1},{4,6},{6,4},{5,7},{7,5},{8,10},{10,8},{9,1... | collective-permute-start | bytes 3145736 | tf_op jit(solution)/shard_map/ppermute | solution.py:696
  145.5 36.1 %collective-permute-start.13 = (bf16[256,1024]{1,0:T(8,128)(2,1)S(1)}, bf16[256,1024]{1,0:T(8,128)(2,1)S(1)}, u32[]{:S(2)}, u32[]{:S(2)}) collective-permute-start(bf16[256,1024]{1,0:T(8,128)(2,1)S(1)} %get-tuple-element.65), channel_id=1, source_target_pairs={{2,16},{6,20},{8,2},{10,18},{12,6},{14,22},{16,8},{18,24},{20,12},... | collective-permute-start | bytes 1572872 | tf_op jit(solution)/shard_map/ppermute | solution.py:695
  149.4 32.2 %collective-permute-start.14 = (bf16[256,1024]{1,0:T(8,128)(2,1)S(1)}, bf16[256,1024]{1,0:T(8,128)(2,1)S(1)}, u32[]{:S(2)}, u32[]{:S(2)}) collective-permute-start(bf16[256,1024]{1,0:T(8,128)(2,1)S(1)} %get-tuple-element.66), channel_id=1, source_target_pairs={{2,18},{6,22},{10,24},{14,28},{16,10},{18,26},{20,14},{22,30},{24,... | collective-permute-start | bytes 1572872 | tf_op jit(solution)/shard_map/ppermute | solution.py:695
  152.3 29.3 %collective-permute-start.15 = (bf16[256,1024]{1,0:T(8,128)(2,1)S(1)}, bf16[256,1024]{1,0:T(8,128)(2,1)S(1)}, u32[]{:S(2)}, u32[]{:S(2)}) collective-permute-start(bf16[256,1024]{1,0:T(8,128)(2,1)S(1)} %get-tuple-element.67), channel_id=1, source_target_pairs={{0,8},{2,24},{4,12},{6,28},{10,26},{14,30},{16,0},{20,4},{24,2},{2... | collective-permute-start | bytes 1572872 | tf_op jit(solution)/shard_map/ppermute | solution.py:695
  154.2 41.3 %collective-permute-start.16 = (bf16[256,1024]{1,0:T(8,128)(2,1)S(1)}, bf16[256,1024]{1,0:T(8,128)(2,1)S(1)}, u32[]{:S(2)}, u32[]{:S(2)}) collective-permute-start(bf16[256,1024]{1,0:T(8,128)(2,1)S(1)} %get-tuple-element.68), channel_id=1, source_target_pairs={{0,10},{2,26},{4,14},{6,30},{8,0},{10,16},{12,4},{14,20},{16,2},{2... | collective-permute-start | bytes 1572872 | tf_op jit(solution)/shard_map/ppermute | solution.py:695
  198.1 9.6 %collective-permute-start.18 = (f32[2,256,256]{2,1,0:T(8,128)S(1)}, f32[2,256,256]{2,1,0:T(8,128)S(1)}, u32[]{:S(2)}, u32[]{:S(2)}) collective-permute-start(f32[2,256,256]{2,1,0:T(8,128)S(1)} %get-tuple-element.81), channel_id=1, source_target_pairs={{0,2},{2,4},{4,6},{6,0},{1,3},{3,5},{5,7},{7,1},{8,10},{10,12},{12... | collective-permute-start | bytes 1572872 | tf_op jit(solution)/shard_map/ppermute | solution.py:716
  198.2 23.3 %collective-permute-start.19 = (f32[2,256,256]{2,1,0:T(8,128)S(1)}, f32[2,256,256]{2,1,0:T(8,128)S(1)}, u32[]{:S(2)}, u32[]{:S(2)}) collective-permute-start(f32[2,256,256]{2,1,0:T(8,128)S(1)} %get-tuple-element.82), channel_id=1, source_target_pairs={{0,4},{2,6},{4,0},{6,2},{1,5},{3,7},{5,1},{7,3},{8,12},{10,14},{12... | collective-permute-start | bytes 1572872 | tf_op jit(solution)/shard_map/ppermute | solution.py:716
  199.4 23.3 %collective-permute-start.20 = (f32[2,256,256]{2,1,0:T(8,128)S(1)}, f32[2,256,256]{2,1,0:T(8,128)S(1)}, u32[]{:S(2)}, u32[]{:S(2)}) collective-permute-start(f32[2,256,256]{2,1,0:T(8,128)S(1)} %get-tuple-element.83), channel_id=1, source_target_pairs={{0,6},{2,0},{4,2},{6,4},{1,7},{3,1},{5,3},{7,5},{8,14},{10,8},{12,... | collective-permute-start | bytes 1572872 | tf_op jit(solution)/shard_map/ppermute | solution.py:716

commit v12 on v11

--- a/solution.py
+++ b/solution.py
@@ -377,7 +377,7 @@
     out[...] = total.astype(out.dtype)
 
 
-def products(table, bases, images, lists, width, dtype):
+def products(table, bases, images, lists, width, dtype, weight=1):
     rows, cols = images[0].shape
     step = 512 if width % 512 == 0 else width
     parts = width // step
@@ -401,7 +401,7 @@
         out_shape=jax.ShapeDtypeStruct((total, cols), dtype),
         compiler_params=pltpu.CompilerParams(vmem_limit_bytes=48 * 2**20),
         cost_estimate=pl.CostEstimate(
-            flops=2 * total * cols * rows * len(bases),
+            flops=2 * total * cols * rows * len(bases) * weight,
             transcendentals=0,
             bytes_accessed=2 * rows * (total + cols) * len(bases) + 4 * total * cols,
         ),
@@ -634,8 +634,8 @@
 
     lead_terms = exchanged(lead.reshape(chips, -1, LEAF), plane_axes)
 
-    def chip_products(images, lists, dtype):
-        return products(table, [flat_basis, other_basis], images, lists, narrow, dtype)
+    def chip_products(images, lists, dtype, weight=1):
+        return products(table, [flat_basis, other_basis], images, lists, narrow, dtype, weight)
 
     images, _ = lax.optimization_barrier(([image, other_image], lead))
     sent_a = [chip_products(images, lists_a[d], bf16) for d in range(1, devices_z)]
@@ -643,15 +643,18 @@
     got_a = [move(a, "gz", d) for d, a in enumerate(sent_a, 1)]
     got_b = [move(a, "gy", d) for d, a in enumerate(sent_b, 1)]
     images, _ = lax.optimization_barrier((images, (sent_a, sent_b)))
-    own_a, own_b = (chip_products(images, lists[0], f32) for lists in (lists_a, lists_b))
+    own_a = chip_products(images, lists_a[0], f32, 4)
     lead_terms, _ = lax.optimization_barrier((lead_terms, (sent_a, sent_b)))
     own = jnp.sum(lead_terms.astype(f32), axis=0).reshape(2, -1, LEAF)
     kept = lax.dynamic_index_in_dim(own, core, 0, keepdims=False)
     sent = lax.dynamic_index_in_dim(own, 1 - core, 0, keepdims=False)
     own = kept + lax.ppermute(sent, "core", swap_pairs())
-    own, _ = lax.optimization_barrier((own, (own_a, own_b)))
+    own, _ = lax.optimization_barrier((own, own_a))
+    images, _ = lax.optimization_barrier((images, own))
+    own_b = chip_products(images, lists_b[0], f32)
     own = own.reshape(devices_x, -1, LEAF)
-    own = jnp.sum(exchanged(own, "gx"), axis=0)
+    terms, _ = lax.optimization_barrier((exchanged(own, "gx"), own_b))
+    own = jnp.sum(terms, axis=0)
     own = exchanged(for_all(own, devices_x), "gx").reshape(-1, LEAF)
     own = for_all(own, chips)
     (got_a, got_b), _ = lax.optimization_barrier(((got_a, got_b), own))

time: 226 us -> 227 us (level)
  blocking collectives: 25.1 us -> 10.5 us
  starting transfers between devices: 43.6 us -> 53.3 us
  waiting for transfers between devices: 50 us -> 55.1 us
    all_to_all x2 -> x1, blocking collectives: 25.1 us -> 10.5 us  [exchanged(): return lax.all_to_all(rows, axes, split_axis=0, concat_axis=0, tiled=True)]
    all_to_all x2 -> x3, starting transfers between devices: 9.11 us -> 14.8 us  [exchanged(): return lax.all_to_all(rows, axes, split_axis=0, concat_axis=0, tiled=True)]
    ppermute x4, waiting for transfers between devices: 0.01 us -> 5.25 us  [move(): return lax.ppermute(array, axis, [(i, (i + d) % size) for i in range(size)])]
    all_to_all x2 -> x3, waiting for transfers between devices: 8.81 us -> 9.7 us  [exchanged(): return lax.all_to_all(rows, axes, split_axis=0, concat_axis=0, tiled=True)]
  transfers between devices with their start and end apart: 23 -> 24, of which waited for: 8 -> 11; matrix products, arithmetic and copies ran while one was open for 2% -> 3% of each run, Pallas kernels for 35% -> 35%
where the time goes in v12:
time: 227 us; the launch traced here: 226 us
  Pallas kernels  94 us (41%)
  waiting for transfers between devices  55.1 us (24%)
  starting transfers between devices  53.3 us (23%)
  blocking collectives  10.5 us (5%)
  local copies, waits for them, and re-layouts  6.98 us (3%)
  other arithmetic  4.54 us (2%)
    pallas_call x2, Pallas kernels, panel_call(): pl.pallas_call(kernel, out_shape=[jax.ShapeDtypeStruct((nb, nb), jnp.floa...  46.1 us
    ppermute x3, waiting for transfers between devices, local(): pairs[d] = lax.ppermute(pairs[d], ('gy', 'core'), route)  22.6 us
    pallas_call x4, Pallas kernels, products(): pl.pallas_call(products_kernel, grid_spec=pltpu.PrefetchScalarGridSpec(nu...  22.4 us
    all_to_all x3, starting transfers between devices, exchanged(): return lax.all_to_all(rows, axes, split_axis=0, concat_axis=0, tiled=True)  14.8 us
    ppermute x4, waiting for transfers between devices, local(): x_got.append(lax.ppermute(x_sent[step], ('gx', 'gy', 'core'), pairs))  14.1 us
    ppermute x4, starting transfers between devices, local(): x_got.append(lax.ppermute(x_sent[step], ('gx', 'gy', 'core'), pairs))  14 us
    all_to_all x1, blocking collectives, exchanged(): return lax.all_to_all(rows, axes, split_axis=0, concat_axis=0, tiled=True)  10.5 us
    all_to_all x3, waiting for transfers between devices, exchanged(): return lax.all_to_all(rows, axes, split_axis=0, concat_axis=0, tiled=True)  9.7 us
  transfers between devices with their start and end apart: 24, of which 11 were waited for; matrix products, arithmetic and copies ran while one was open for 3% of the time, Pallas kernels for 35%

profile of v12, /device:TPU:1, one launch (start us, length us, event | category | flops | bytes accessed | tf_op | source)
XLA Modules:
  0.0 225.6 jit_solution(13607898240048946212)
XLA Ops:
  0.8 0.8 stack.177
  2.0 0.9 copy.12.info_ref
  3.5 6.8 %shard_map.77 = (bf16[64,1024]{1,0:T(8,128)(2,1)}, bf16[64,1024]{1,0:T(8,128)(2,1)}, bf16[64,1024]{1,0:T(8,128)(2,1)}, bf16[64,1024]{1,0:T(8,128)(2,1)}, bf16[64...) custom-call(s32[38]{0:T(128)} %stack.176.table_ref, f32[16]{0:T(128)} %cond_ref.1, ...), custom_call_target="tpu_custom_call" | custom-call | tf_op jit(solution)/shard_map/pallas_call | solution.py:576
  10.4 4.6 %collective-permute-start.1 = (bf16[64,1024]{1,0:T(8,128)(2,1)}, bf16[64,1024]{1,0:T(8,128)(2,1)S(1)}, u32[]{:S(2)}, u32[]{:S(2)}) collective-permute-start(bf16[64,1024]{1,0:T(8,128)(2,1)} %get-tuple-element.49), channel_id=1, source_target_pairs={{0,8},{8,16},{16,24},{1,9},{9,17},{17,25},{2,10},{10,18},{18,26},{... | collective-permute-start | bytes 393224 | tf_op jit(solution)/shard_map/ppermute | solution.py:603
  15.1 1.3 collective-permute-start.2
  16.4 3.3 %collective-permute-start.3 = (bf16[64,1024]{1,0:T(8,128)(2,1)}, bf16[64,1024]{1,0:T(8,128)(2,1)S(1)}, u32[]{:S(2)}, u32[]{:S(2)}) collective-permute-start(bf16[64,1024]{1,0:T(8,128)(2,1)} %get-tuple-element.51), channel_id=1, source_target_pairs={{0,2},{2,4},{4,6},{1,3},{3,5},{5,7},{8,10},{10,12},{12,14},{9,11},... | collective-permute-start | bytes 393224 | tf_op jit(solution)/shard_map/ppermute | solution.py:603
  19.7 1.9 collective-permute-start.4
  21.7 1.3 collective-permute-start.5
  23.0 3.3 %collective-permute-done.4.refs_3_ = bf16[64,1024]{1,0:T(8,128)(2,1)S(1)} collective-permute-done((bf16[64,1024]{1,0:T(8,128)(2,1)}, bf16[64,1024]{1,0:T(8,128)(2,1)S(1)}, u32[]{:S(2)}, u32[]{:S(2)}) %collective-permute-start.4) | collective-permute-done | bytes 131104 | tf_op jit(solution)/shard_map/ppermute | solution.py:604
  26.9 5.9 %shard_map.78 = (bf16[512,1024]{1,0:T(8,128)(2,1)}, bf16[4608,128]{1,0:T(8,128)(2,1)}) custom-call(s32[38]{0:T(128)} %stack.176.table_ref, bf16[512,8192]{1,0:T(8,128)(2,1)} %bitcast.57, f32[512,128]{1,0:T(8,128)} %get-tuple-element.47.conduct_ref, f32[512,128]{1,0:T(8,128)} %get-tuple-element.48.grounds_ref, bf16[64,1024]{1,0:T(8,128)(2,1)} %copy-done.6, ...), custom_call_target="tpu_custom_call" | custom-call | tf_op jit(solution)/shard_map/pallas_call | solution.py:610
  32.8 4.7 %all-to-all-start = ((bf16[4,1152,128]{2,1,0:T(8,128)(2,1)}), bf16[4,1152,128]{2,1,0:T(8,128)(2,1)}, u32[]{:S(2)}, u32[]{:S(2)}) async-start(bf16[4,1152,128]{2,1,0:T(8,128)(2,1)} %bitcast.66), calls=%async_computation | async-start | bytes 2359296 | tf_op jit(solution)/shard_map/all_to_all | solution.py:630
  37.6 5.4 %shard_map.79 = bf16[1024,1024]{1,0:T(8,128)(2,1)} custom-call(s32[38]{0:T(128)S(1)} %copy-done.5, bf16[512,8192]{1,0:T(8,128)(2,1)} %bitcast.58, bf16[512,4096]{1,0:T(8,128)(2,1)} %collective-permute-done.refs_1_, bf16[512,1024]{1,0:T(8,128)(2,1)S(1)} %copy-done.4, bf16[512,1024]{1,0:T(8,128)(2,1)S(1)} %collective-permute-done.6.refs_3_), custom_call_target="tpu_custom_call" | custom-call | flops 2147483648 | bytes 8388608 | tf_op jit(solution)/shard_map/pallas_call | solution.py:393
  43.0 1.4 collective-permute-start.7
  44.4 5.4 %shard_map.80 = bf16[1024,1024]{1,0:T(8,128)(2,1)} custom-call(s32[38]{0:T(128)S(1)} %copy-done.5, bf16[512,8192]{1,0:T(8,128)(2,1)} %bitcast.59, bf16[512,4096]{1,0:T(8,128)(2,1)} %collective-permute-done.refs_1_, bf16[512,1024]{1,0:T(8,128)(2,1)S(1)} %copy-done.4, bf16[512,1024]{1,0:T(8,128)(2,1)S(1)} %collective-permute-done.6.refs_3_), custom_call_target="tpu_custom_call" | custom-call | flops 2147483648 | bytes 8388608 | tf_op jit(solution)/shard_map/pallas_call | solution.py:393
  49.8 1.8 collective-permute-start.8
  51.6 1.8 all-to-all-done
  53.5 1.5 convert_reduce_fusion
  55.0 1.1 collective-permute-start.9
  56.1 5.8 %shard_map.81.refs_0_ = f32[1024,1024]{1,0:T(8,128)} custom-call(s32[38]{0:T(128)S(1)} %copy-done.5, bf16[512,8192]{1,0:T(8,128)(2,1)} %bitcast.60, bf16[512,4096]{1,0:T(8,128)(2,1)} %collective-permute-done.refs_1_, bf16[512,1024]{1,0:T(8,128)(2,1)S(1)} %copy-done.4, bf16[512,1024]{1,0:T(8,128)(2,1)S(1)} %collective-permute-done.6.refs_3_), custom_call_target="tpu_custom_call" | custom-call | flops 8589934592 | bytes 8388608 | tf_op jit(solution)/shard_map/pallas_call | solution.py:393
  62.7 5.7 %all-to-all-start.1 = ((f32[4,144,128]{2,1,0:T(8,128)}), f32[4,144,128]{2,1,0:T(8,128)S(1)}, u32[]{:S(2)}, u32[]{:S(2)}) async-start(f32[4,144,128]{2,1,0:T(8,128)} %bitcast.44), calls=%async_computation.1 | async-start | bytes 589824 | tf_op jit(solution)/shard_map/all_to_all | solution.py:630
  68.3 5.8 %shard_map.82.refs_0_.refs_3_ = f32[1024,1024]{1,0:T(8,128)} custom-call(s32[38]{0:T(128)S(1)} %copy-done.5, bf16[512,8192]{1,0:T(8,128)(2,1)} %bitcast.61, bf16[512,4096]{1,0:T(8,128)(2,1)} %collective-permute-done.refs_1_, bf16[512,1024]{1,0:T(8,128)(2,1)S(1)} %copy-done.4, bf16[512,1024]{1,0:T(8,128)(2,1)S(1)} %collective-permute-done.6.refs_3_), custom_call_target="tpu_custom_call" | custom-call | flops 2147483648 | bytes 8388608 | tf_op jit(solution)/shard_map/pallas_call | solution.py:393
  74.1 2.7 %all-to-all-done.1 = f32[4,144,128]{2,1,0:T(8,128)S(1)} async-done(((f32[4,144,128]{2,1,0:T(8,128)}), f32[4,144,128]{2,1,0:T(8,128)S(1)}, u32[]{:S(2)}, u32[]{:S(2)}) %all-to-all-start.1) | async-done | bytes 294944 | tf_op jit(solution)/shard_map/all_to_all | solution.py:630
  76.9 10.5 %all_to_all.20 = f32[4,144,128]{2,1,0:T(8,128)S(1)} all-to-all(f32[4,144,128]{2,1,0:T(8,128)S(1)} %broadcast_in_dim.17), channel_id=1, replica_groups=mesh['gx'=4,'gy'=2,'core'=2,'gz'=2] {'gx'}, dimensions={0} | all-to-all | bytes 589824 | tf_op jit(solution)/shard_map/all_to_all | solution.py:630
  87.4 1.1 broadcast_in_dim.18
  88.5 4.4 %all-to-all-start.3 = ((f32[4,576,128]{2,1,0:T(8,128)}), f32[4,576,128]{2,1,0:T(8,128)}, u32[]{:S(2)}, u32[]{:S(2)}) async-start(f32[4,576,128]{2,1,0:T(8,128)} %broadcast_in_dim.18), calls=%async_computation.3 | async-start | bytes 2359296 | tf_op jit(solution)/shard_map/all_to_all | solution.py:630
  92.9 4.4 %collective-permute-done.7.refs_1_ = bf16[1024,1024]{1,0:T(8,128)(2,1)} collective-permute-done((bf16[1024,1024]{1,0:T(8,128)(2,1)}, bf16[1024,1024]{1,0:T(8,128)(2,1)}, u32[]{:S(2)}, u32[]{:S(2)}) %collective-permute-start.7) | collective-permute-done | bytes 2097184 | tf_op jit(solution)/shard_map/ppermute | solution.py:558
  97.3 0.9 collective-permute-done.8.refs_1_.refs_4_
  98.2 2.2 copy-done.2
  100.4 2.2 shard_map.83
  102.9 2.7 %shard_map.84 = bf16[512,1024]{1,0:T(8,128)(2,1)} custom-call(s32[38]{0:T(128)S(1)} %copy-done.5, f32[1024,1024]{1,0:T(8,128)S(1)} %copy-done, bf16[1024,1024]{1,0:T(8,128)(2,1)} %collective-permute-done.8.refs_1_.refs_4_), custom_call_target="tpu_custom_call" | custom-call | flops 524288 | bytes 4194304 | tf_op jit(solution)/shard_map/pallas_call | solution.py:425
  105.5 5.1 %all-to-all-done.3 = f32[4,576,128]{2,1,0:T(8,128)} async-done(((f32[4,576,128]{2,1,0:T(8,128)}), f32[4,576,128]{2,1,0:T(8,128)}, u32[]{:S(2)}, u32[]{:S(2)}) %all-to-all-start.3) | async-done | bytes 1179680 | tf_op jit(solution)/shard_map/all_to_all | solution.py:630
  110.7 1.1 collective-permute-start.12
  111.8 1.2 collective-permute-start.11
  113.0 1.4 collective-permute-start.10
  114.6 2.0 select_bitcast_fusion.1
  116.8 22.2 %shard_map.85.w0_ref.refs_4_ = f32[512,512]{1,0:T(8,128)S(1)} custom-call(f32[1280,128]{1,0:T(8,128)S(1)} %slice.8.packed_ref), custom_call_target="tpu_custom_call" | custom-call | flops 512 | bytes 512 | tf_op jit(solution)/shard_map/pallas_call | solution.py:179
  139.0 3.5 %shard_map.86 = (bf16[256,1024]{1,0:T(8,128)(2,1)S(1)}, bf16[256,1024]{1,0:T(8,128)(2,1)S(1)}, bf16[256,1024]{1,0:T(8,128)(2,1)S(1)}, bf16[256,1024]{1,0:T(8,128...) custom-call(s32[38]{0:T(128)S(1)} %copy-done.5, f32[1024,1024]{1,0:T(8,128)S(1)} %copy-done.3, ...), custom_call_target="tpu_custom_call" | custom-call | bytes 14680064 | tf_op jit(solution)/shard_map/pallas_call | solution.py:467
  142.9 5.6 %collective-permute-start.13 = (bf16[256,1024]{1,0:T(8,128)(2,1)S(1)}, bf16[256,1024]{1,0:T(8,128)(2,1)S(1)}, u32[]{:S(2)}, u32[]{:S(2)}) collective-permute-start(bf16[256,1024]{1,0:T(8,128)(2,1)S(1)} %get-tuple-element.71), channel_id=1, source_target_pairs={{2,16},{6,20},{8,2},{10,18},{12,6},{14,22},{16,8},{18,24},{20,12},... | collective-permute-start | bytes 1572872 | tf_op jit(solution)/shard_map/ppermute | solution.py:698
  148.5 3.3 %collective-permute-start.14 = (bf16[256,1024]{1,0:T(8,128)(2,1)S(1)}, bf16[256,1024]{1,0:T(8,128)(2,1)S(1)}, u32[]{:S(2)}, u32[]{:S(2)}) collective-permute-start(bf16[256,1024]{1,0:T(8,128)(2,1)S(1)} %get-tuple-element.72), channel_id=1, source_target_pairs={{2,18},{6,22},{10,24},{14,28},{16,10},{18,26},{20,14},{22,30},{24,... | collective-permute-start | bytes 1572872 | tf_op jit(solution)/shard_map/ppermute | solution.py:698
  151.8 1.9 collective-permute-start.15
  153.7 3.3 %collective-permute-start.16 = (bf16[256,1024]{1,0:T(8,128)(2,1)S(1)}, bf16[256,1024]{1,0:T(8,128)(2,1)S(1)}, u32[]{:S(2)}, u32[]{:S(2)}) collective-permute-start(bf16[256,1024]{1,0:T(8,128)(2,1)S(1)} %get-tuple-element.74), channel_id=1, source_target_pairs={{0,10},{2,26},{4,14},{6,30},{8,0},{10,16},{12,4},{14,20},{16,2},{2... | collective-permute-start | bytes 1572872 | tf_op jit(solution)/shard_map/ppermute | solution.py:698
  157.1 23.9 %shard_map.87 = (f32[512,512]{1,0:T(8,128)S(1)}, f32[512,512]{1,0:T(8,128)S(1)}) custom-call(f32[3328,128]{1,0:T(8,128)S(1)} %slice.9.packed_ref, f32[512,512]{1,0:T(8,128)S(1)} %shard_map.85.w0_ref.refs_4_), custom_call_target="tpu_custom_call" | custom-call | flops 512 | bytes 512 | tf_op jit(solution)/shard_map/pallas_call | solution.py:179
  181.1 14.0 %collective-permute-done.16.refs_3_ = bf16[256,1024]{1,0:T(8,128)(2,1)S(1)} collective-permute-done((bf16[256,1024]{1,0:T(8,128)(2,1)S(1)}, bf16[256,1024]{1,0:T(8,128)(2,1)S(1)}, u32[]{:S(2)}, u32[]{:S(2)}) %collective-permute-start.16) | collective-permute-done | bytes 524320 | tf_op jit(solution)/shard_map/ppermute | solution.py:698
  195.1 2.5 %shard_map.88 = (f32[2,256,256]{2,1,0:T(8,128)S(1)}, f32[2,256,256]{2,1,0:T(8,128)S(1)}, f32[2,256,256]{2,1,0:T(8,128)S(1)}, f32[2,256,256]{2,1,0:T(8,128)S(1)}) custom-call(s32[38]{0:T(128)S(1)} %copy-done.5, f32[256,1024]{1,0:T(8,128)S(1)} %get-tuple-element.70.own_ref, f32[256,1024]{1,0:T(8,128)S(1)} %collective-permute-done.17.swapped_ref, ...), custom_call_target="tpu_custom_call" | custom-call | tf_op jit(solution)/shard_map/pallas_call | solution.py:705
  197.7 2.6 %collective-permute-start.19 = (f32[2,256,256]{2,1,0:T(8,128)S(1)}, f32[2,256,256]{2,1,0:T(8,128)S(1)}, u32[]{:S(2)}, u32[]{:S(2)}) collective-permute-start(f32[2,256,256]{2,1,0:T(8,128)S(1)} %get-tuple-element.88), channel_id=1, source_target_pairs={{0,4},{2,6},{4,0},{6,2},{1,5},{3,7},{5,1},{7,3},{8,12},{10,14},{12... | collective-permute-start | bytes 1572872 | tf_op jit(solution)/shard_map/ppermute | solution.py:719
  201.0 4.9 %collective-permute-done.18.refs_1_ = f32[2,256,256]{2,1,0:T(8,128)S(1)} collective-permute-done((f32[2,256,256]{2,1,0:T(8,128)S(1)}, f32[2,256,256]{2,1,0:T(8,128)S(1)}, u32[]{:S(2)}, u32[]{:S(2)}) %collective-permute-start.18) | collective-permute-done | bytes 524320 | tf_op jit(solution)/shard_map/ppermute | solution.py:719
  205.9 17.1 %collective-permute-done.19.refs_2_ = f32[2,256,256]{2,1,0:T(8,128)S(1)} collective-permute-done((f32[2,256,256]{2,1,0:T(8,128)S(1)}, f32[2,256,256]{2,1,0:T(8,128)S(1)}, u32[]{:S(2)}, u32[]{:S(2)}) %collective-permute-start.19) | collective-permute-done | bytes 524320 | tf_op jit(solution)/shard_map/ppermute | solution.py:719
  223.6 2.0 shard_map.89
  (55 shorter events, 5.3 us)
Async XLA Ops:
  10.3 27.3 %collective-permute-start = (bf16[512,4096]{1,0:T(8,128)(2,1)}, bf16[512,4096]{1,0:T(8,128)(2,1)}, u32[]{:S(2)}, u32[]{:S(2)}) collective-permute-start(bf16[512,4096]{1,0:T(8,128)(2,1)} %get-tuple-element.46), channel_id=1, source_target_pairs={{0,2},{2,0},{1,3},{3,1},{4,6},{6,4},{5,7},{7,5},{8,10},{10,8},{9,1... | collective-permute-start | bytes 12582920 | tf_op jit(solution)/shard_map/ppermute | solution.py:624
  10.4 11.2 %collective-permute-start.1 = (bf16[64,1024]{1,0:T(8,128)(2,1)}, bf16[64,1024]{1,0:T(8,128)(2,1)S(1)}, u32[]{:S(2)}, u32[]{:S(2)}) collective-permute-start(bf16[64,1024]{1,0:T(8,128)(2,1)} %get-tuple-element.49), channel_id=1, source_target_pairs={{0,8},{8,16},{16,24},{1,9},{9,17},{17,25},{2,10},{10,18},{18,26},{... | collective-permute-start | bytes 393224 | tf_op jit(solution)/shard_map/ppermute | solution.py:603
  15.1 7.9 %collective-permute-start.2 = (bf16[64,1024]{1,0:T(8,128)(2,1)}, bf16[64,1024]{1,0:T(8,128)(2,1)S(1)}, u32[]{:S(2)}, u32[]{:S(2)}) collective-permute-start(bf16[64,1024]{1,0:T(8,128)(2,1)} %get-tuple-element.50), channel_id=1, source_target_pairs={{8,0},{16,8},{24,16},{9,1},{17,9},{25,17},{10,2},{18,10},{26,18},{... | collective-permute-start | bytes 393224 | tf_op jit(solution)/shard_map/ppermute | solution.py:604
  16.4 6.6 %collective-permute-start.3 = (bf16[64,1024]{1,0:T(8,128)(2,1)}, bf16[64,1024]{1,0:T(8,128)(2,1)S(1)}, u32[]{:S(2)}, u32[]{:S(2)}) collective-permute-start(bf16[64,1024]{1,0:T(8,128)(2,1)} %get-tuple-element.51), channel_id=1, source_target_pairs={{0,2},{2,4},{4,6},{1,3},{3,5},{5,7},{8,10},{10,12},{12,14},{9,11},... | collective-permute-start | bytes 393224 | tf_op jit(solution)/shard_map/ppermute | solution.py:603
  19.7 6.5 %collective-permute-start.4 = (bf16[64,1024]{1,0:T(8,128)(2,1)}, bf16[64,1024]{1,0:T(8,128)(2,1)S(1)}, u32[]{:S(2)}, u32[]{:S(2)}) collective-permute-start(bf16[64,1024]{1,0:T(8,128)(2,1)} %get-tuple-element.52), channel_id=1, source_target_pairs={{2,0},{4,2},{6,4},{3,1},{5,3},{7,5},{10,8},{12,10},{14,12},{11,9},... | collective-permute-start | bytes 393224 | tf_op jit(solution)/shard_map/ppermute | solution.py:604
  21.6 4.6 %copy-start.6 = (bf16[64,1024]{1,0:T(8,128)(2,1)}, bf16[64,1024]{1,0:T(8,128)(2,1)S(1)}, u32[]{:S(2)}) copy-start(bf16[64,1024]{1,0:T(8,128)(2,1)S(1)} %collective-permute-done.1.refs_0_) | copy-start | bytes 393220
  21.7 4.6 %collective-permute-start.5 = (bf16[64,1024]{1,0:T(8,128)(2,1)}, bf16[64,1024]{1,0:T(8,128)(2,1)S(1)}, u32[]{:S(2)}, u32[]{:S(2)}) collective-permute-start(bf16[64,1024]{1,0:T(8,128)(2,1)} %get-tuple-element.53), channel_id=1, source_target_pairs={{0,1},{1,0},{2,3},{3,2},{4,5},{5,4},{6,7},{7,6},{8,9},{9,8},{10,11... | collective-permute-start | bytes 393224 | tf_op jit(solution)/shard_map/ppermute | solution.py:600
  22.9 3.3 %copy-start.7 = (bf16[64,1024]{1,0:T(8,128)(2,1)}, bf16[64,1024]{1,0:T(8,128)(2,1)S(1)}, u32[]{:S(2)}) copy-start(bf16[64,1024]{1,0:T(8,128)(2,1)S(1)} %collective-permute-done.2.refs_1_) | copy-start | bytes 393220
  22.9 3.3 %copy-start.8 = (bf16[64,1024]{1,0:T(8,128)(2,1)}, bf16[64,1024]{1,0:T(8,128)(2,1)S(1)}, u32[]{:S(2)}) copy-start(bf16[64,1024]{1,0:T(8,128)(2,1)S(1)} %collective-permute-done.3.refs_2_) | copy-start | bytes 393220
  26.2 0.7 copy-start.9
  26.2 0.7 copy-start.10
  32.8 4.7 %copy-start.4 = (bf16[512,1024]{1,0:T(8,128)(2,1)S(1)}, bf16[512,1024]{1,0:T(8,128)(2,1)}, u32[]{:S(2)}) copy-start(bf16[512,1024]{1,0:T(8,128)(2,1)} %get-tuple-element.62.refs_2_) | copy-start | bytes 3145732
  32.8 4.7 %copy-start.5 = (s32[38]{0:T(128)S(1)}, s32[38]{0:T(128)}, u32[]{:S(2)}) copy-start(s32[38]{0:T(128)} %stack.176.table_ref) | copy-start | bytes 460
  32.8 4.7 %collective-permute-start.6 = (bf16[512,1024]{1,0:T(8,128)(2,1)}, bf16[512,1024]{1,0:T(8,128)(2,1)S(1)}, u32[]{:S(2)}, u32[]{:S(2)}) collective-permute-start(bf16[512,1024]{1,0:T(8,128)(2,1)} %get-tuple-element.62.refs_2_), channel_id=1, source_target_pairs={{0,2},{2,0},{1,3},{3,1},{4,6},{6,4},{5,7},{7,5},{8,10},{10,8},{9,1... | collective-permute-start | bytes 3145736 | tf_op jit(solution)/shard_map/ppermute | solution.py:623
  32.8 20.6 %all-to-all-start = ((bf16[4,1152,128]{2,1,0:T(8,128)(2,1)}), bf16[4,1152,128]{2,1,0:T(8,128)(2,1)}, u32[]{:S(2)}, u32[]{:S(2)}) async-start(bf16[4,1152,128]{2,1,0:T(8,128)(2,1)} %bitcast.66), calls=%async_computation | async-start | bytes 2359296 | tf_op jit(solution)/shard_map/all_to_all | solution.py:630
  43.0 54.3 %collective-permute-start.7 = (bf16[1024,1024]{1,0:T(8,128)(2,1)}, bf16[1024,1024]{1,0:T(8,128)(2,1)}, u32[]{:S(2)}, u32[]{:S(2)}) collective-permute-start(bf16[1024,1024]{1,0:T(8,128)(2,1)} %shard_map.79), channel_id=1, source_target_pairs={{0,1},{1,0},{2,3},{3,2},{4,5},{5,4},{6,7},{7,6},{8,9},{9,8},{10,11... | collective-permute-start | bytes 6291464 | tf_op jit(solution)/shard_map/ppermute | solution.py:558
  49.8 48.4 %collective-permute-start.8 = (bf16[1024,1024]{1,0:T(8,128)(2,1)}, bf16[1024,1024]{1,0:T(8,128)(2,1)}, u32[]{:S(2)}, u32[]{:S(2)}) collective-permute-start(bf16[1024,1024]{1,0:T(8,128)(2,1)} %shard_map.80), channel_id=1, source_target_pairs={{0,4},{4,0},{1,5},{5,1},{2,6},{6,2},{3,7},{7,3},{8,12},{12,8},{9,1... | collective-permute-start | bytes 6291464 | tf_op jit(solution)/shard_map/ppermute | solution.py:558
  55.0 6.9 %collective-permute-start.9 = (f32[576,128]{1,0:T(8,128)S(1)}, f32[576,128]{1,0:T(8,128)S(1)}, u32[]{:S(2)}, u32[]{:S(2)}) collective-permute-start(f32[576,128]{1,0:T(8,128)S(1)} %dynamic-slice_bitcast_fusion), channel_id=1, source_target_pairs={{0,2},{2,0},{1,3},{3,1},{4,6},{6,4},{5,7},{7,5},{8,10},{10,8},{9,1... | collective-permute-start | bytes 884744 | tf_op jit(solution)/shard_map/ppermute | solution.py:651
  62.7 14.2 %all-to-all-start.1 = ((f32[4,144,128]{2,1,0:T(8,128)}), f32[4,144,128]{2,1,0:T(8,128)S(1)}, u32[]{:S(2)}, u32[]{:S(2)}) async-start(f32[4,144,128]{2,1,0:T(8,128)} %bitcast.44), calls=%async_computation.1 | async-start | bytes 589824 | tf_op jit(solution)/shard_map/all_to_all | solution.py:630
  88.5 22.2 %all-to-all-start.3 = ((f32[4,576,128]{2,1,0:T(8,128)}), f32[4,576,128]{2,1,0:T(8,128)}, u32[]{:S(2)}, u32[]{:S(2)}) async-start(f32[4,576,128]{2,1,0:T(8,128)} %broadcast_in_dim.18), calls=%async_computation.3 | async-start | bytes 2359296 | tf_op jit(solution)/shard_map/all_to_all | solution.py:630
  98.2 2.2 copy-start.2
  100.4 2.5 %copy-start = (f32[1024,1024]{1,0:T(8,128)S(1)}, f32[1024,1024]{1,0:T(8,128)}, u32[]{:S(2)}) copy-start(f32[1024,1024]{1,0:T(8,128)} %shard_map.82.refs_0_.refs_3_) | copy-start | bytes 12582916
  110.7 3.9 %collective-permute-start.12 = (f32[4,576,128]{2,1,0:T(8,128)}, f32[4,576,128]{2,1,0:T(8,128)}, u32[]{:S(2)}, u32[]{:S(2)}) collective-permute-start(f32[4,576,128]{2,1,0:T(8,128)} %all-to-all-done.3), channel_id=1, source_target_pairs={{0,2},{2,0},{1,3},{3,1},{4,6},{6,4},{5,7},{7,5},{8,10},{10,8},{9,1... | collective-permute-start | bytes 3538952 | tf_op jit(solution)/shard_map/ppermute | solution.py:669
  111.8 27.2 %collective-permute-start.11 = (bf16[512,1024]{1,0:T(8,128)(2,1)}, bf16[512,1024]{1,0:T(8,128)(2,1)S(1)}, u32[]{:S(2)}, u32[]{:S(2)}) collective-permute-start(bf16[512,1024]{1,0:T(8,128)(2,1)} %shard_map.84), channel_id=1, source_target_pairs={{0,1},{1,0},{2,3},{3,2},{4,5},{5,4},{6,7},{7,6},{8,9},{9,8},{10,11... | collective-permute-start | bytes 3145736 | tf_op jit(solution)/shard_map/ppermute | solution.py:558
  113.0 26.0 %collective-permute-start.10 = (bf16[512,1024]{1,0:T(8,128)(2,1)S(1)}, bf16[512,1024]{1,0:T(8,128)(2,1)S(1)}, u32[]{:S(2)}, u32[]{:S(2)}) collective-permute-start(bf16[512,1024]{1,0:T(8,128)(2,1)S(1)} %shard_map.83), channel_id=1, source_target_pairs={{0,4},{4,0},{1,5},{5,1},{2,6},{6,2},{3,7},{7,3},{8,12},{12,8},{9,1... | collective-permute-start | bytes 3145736 | tf_op jit(solution)/shard_map/ppermute | solution.py:558
  114.6 24.4 %copy-start.3 = (f32[1024,1024]{1,0:T(8,128)S(1)}, f32[1024,1024]{1,0:T(8,128)}, u32[]{:S(2)}) copy-start(f32[1024,1024]{1,0:T(8,128)} %shard_map.81.refs_0_) | copy-start | bytes 12582916
  116.6 22.4 %copy-start.1 = (f32[1024,1024]{1,0:T(8,128)S(1)}, f32[1024,1024]{1,0:T(8,128)}, u32[]{:S(2)}) copy-start(f32[1024,1024]{1,0:T(8,128)} %shard_map.82.refs_0_.refs_3_) | copy-start | bytes 12582916
  142.5 52.7 %collective-permute-start.17 = (f32[256,1024]{1,0:T(8,128)S(1)}, f32[256,1024]{1,0:T(8,128)S(1)}, u32[]{:S(2)}, u32[]{:S(2)}) collective-permute-start(f32[256,1024]{1,0:T(8,128)S(1)} %get-tuple-element.75), channel_id=1, source_target_pairs={{0,2},{2,0},{1,3},{3,1},{4,6},{6,4},{5,7},{7,5},{8,10},{10,8},{9,1... | collective-permute-start | bytes 3145736 | tf_op jit(solution)/shard_map/ppermute | solution.py:699
  142.9 38.1 %collective-permute-start.13 = (bf16[256,1024]{1,0:T(8,128)(2,1)S(1)}, bf16[256,1024]{1,0:T(8,128)(2,1)S(1)}, u32[]{:S(2)}, u32[]{:S(2)}) collective-permute-start(bf16[256,1024]{1,0:T(8,128)(2,1)S(1)} %get-tuple-element.71), channel_id=1, source_target_pairs={{2,16},{6,20},{8,2},{10,18},{12,6},{14,22},{16,8},{18,24},{20,12},... | collective-permute-start | bytes 1572872 | tf_op jit(solution)/shard_map/ppermute | solution.py:698
  148.5 32.5 %collective-permute-start.14 = (bf16[256,1024]{1,0:T(8,128)(2,1)S(1)}, bf16[256,1024]{1,0:T(8,128)(2,1)S(1)}, u32[]{:S(2)}, u32[]{:S(2)}) collective-permute-start(bf16[256,1024]{1,0:T(8,128)(2,1)S(1)} %get-tuple-element.72), channel_id=1, source_target_pairs={{2,18},{6,22},{10,24},{14,28},{16,10},{18,26},{20,14},{22,30},{24,... | collective-permute-start | bytes 1572872 | tf_op jit(solution)/shard_map/ppermute | solution.py:698
  151.8 29.3 %collective-permute-start.15 = (bf16[256,1024]{1,0:T(8,128)(2,1)S(1)}, bf16[256,1024]{1,0:T(8,128)(2,1)S(1)}, u32[]{:S(2)}, u32[]{:S(2)}) collective-permute-start(bf16[256,1024]{1,0:T(8,128)(2,1)S(1)} %get-tuple-element.73), channel_id=1, source_target_pairs={{0,8},{2,24},{4,12},{6,28},{10,26},{14,30},{16,0},{20,4},{24,2},{2... | collective-permute-start | bytes 1572872 | tf_op jit(solution)/shard_map/ppermute | solution.py:698
  153.7 41.4 %collective-permute-start.16 = (bf16[256,1024]{1,0:T(8,128)(2,1)S(1)}, bf16[256,1024]{1,0:T(8,128)(2,1)S(1)}, u32[]{:S(2)}, u32[]{:S(2)}) collective-permute-start(bf16[256,1024]{1,0:T(8,128)(2,1)S(1)} %get-tuple-element.74), channel_id=1, source_target_pairs={{0,10},{2,26},{4,14},{6,30},{8,0},{10,16},{12,4},{14,20},{16,2},{2... | collective-permute-start | bytes 1572872 | tf_op jit(solution)/shard_map/ppermute | solution.py:698
  197.7 8.3 %collective-permute-start.18 = (f32[2,256,256]{2,1,0:T(8,128)S(1)}, f32[2,256,256]{2,1,0:T(8,128)S(1)}, u32[]{:S(2)}, u32[]{:S(2)}) collective-permute-start(f32[2,256,256]{2,1,0:T(8,128)S(1)} %get-tuple-element.87), channel_id=1, source_target_pairs={{0,2},{2,4},{4,6},{6,0},{1,3},{3,5},{5,7},{7,1},{8,10},{10,12},{12... | collective-permute-start | bytes 1572872 | tf_op jit(solution)/shard_map/ppermute | solution.py:719
  197.7 25.3 %collective-permute-start.19 = (f32[2,256,256]{2,1,0:T(8,128)S(1)}, f32[2,256,256]{2,1,0:T(8,128)S(1)}, u32[]{:S(2)}, u32[]{:S(2)}) collective-permute-start(f32[2,256,256]{2,1,0:T(8,128)S(1)} %get-tuple-element.88), channel_id=1, source_target_pairs={{0,4},{2,6},{4,0},{6,2},{1,5},{3,7},{5,1},{7,3},{8,12},{10,14},{12... | collective-permute-start | bytes 1572872 | tf_op jit(solution)/shard_map/ppermute | solution.py:719
  200.3 23.3 %collective-permute-start.20 = (f32[2,256,256]{2,1,0:T(8,128)S(1)}, f32[2,256,256]{2,1,0:T(8,128)S(1)}, u32[]{:S(2)}, u32[]{:S(2)}) collective-permute-start(f32[2,256,256]{2,1,0:T(8,128)S(1)} %get-tuple-element.89), channel_id=1, source_target_pairs={{0,6},{2,0},{4,2},{6,4},{1,7},{3,1},{5,3},{7,5},{8,14},{10,8},{12,... | collective-permute-start | bytes 1572872 | tf_op jit(solution)/shard_map/ppermute | solution.py:719
